TPU v7x, 32 devices: a whole 2x2x4 slice. The times are simulated.
32 devices in a mesh: tm: 16 (over z, y, core), space: 2 (over x).
Axes of the slice: x: 2, y: 2, z: 4, core: 2. Of those that a mesh axis runs over, the one named last changes fastest.
Arguments:
- model: float32 [16, 2048, 1024], P('tm', 'space'), may hold values from -6 to 6
- kernels: float32 [3, 600, 2048], P(None, None, ('space', 'tm')), may hold values from -0.078125 to 0.078125
Outputs:
- data: float32 [16, 600, 1024], P('tm', None, 'space')
All inputs are finite; a program needn't handle non-finite values.
Results may differ from a plain program's by a relative error of at most 0.0003.
Values sent between devices are 32-bit elements; how exact they have to be, the bound alone decides.
No kernel may reach another device: no remote copies, remote signals or barrier semaphores. Data moves between devices by JAX's collectives and lax.ppermute only.
A program may use at most 64 MiB of HBM per device.

v0:
```python
import jax
import jax.numpy as jnp
from jax import lax
from jax.sharding import PartitionSpec as P


def passed_along(block, axis, distance):
    devices = range(lax.axis_size(axis))
    route = [(i - distance, i) for i in devices if i - distance in devices]
    return lax.ppermute(block, axis, route)


def on_device(model, kernels):
    local_model = model[0]
    lag_count = kernels.shape[0]
    products = jnp.einsum(
        "lsp,pc->lsc",
        lax.all_gather(kernels, "tm", axis=2, tiled=True),
        local_model,
        precision=lax.Precision.HIGHEST,
        preferred_element_type=jnp.float32,
    )
    running = products[lag_count - 1]
    for lag_index in range(lag_count - 2, -1, -1):
        running = passed_along(running, "tm", 1) + products[lag_index]
    result = lax.psum_scatter(running, "space", scatter_dimension=1, tiled=True)
    return result[None]


def solution(mesh):
    return jax.shard_map(
        on_device,
        mesh=mesh,
        in_specs=(P("tm", "space", None), P(None, None, ("space", "tm"))),
        out_specs=P("tm", None, "space"),
        check_vma=False,
    )
```

profile of v0, /device:TPU:0, one launch (start us, length us, event | category | flops | bytes accessed | tf_op | source)
XLA Modules:
  0.0 219.4 jit_solution(7558154374724874103)
XLA Ops:
  6.5 0.0 all-gather.2.cloned.1.call-start
  6.5 0.7 all-gather.2.cloned.1.call-update
  7.3 0.0 reduce-scatter.2.cloned.1.call-start
  7.3 76.7 %all-gather.2.cloned.1.call-done = f32[3,600,1024]{1,2,0:T(8,128)} async-done(((f32[3,600,64]{1,2,0:T(8,128)}), f32[3,600,1024]{1,2,0:T(8,128)}) %all-gather.2.cloned.1.call-update) | async-done | bytes 7372816 | tf_op jit(solution)/shard_map/all_gather | solution.py:18
  84.0 27.5 %fusion = f32[3,600,1024]{2,1,0:T(8,128)S(1)} fusion(f32[3,600,1024]{1,2,0:T(8,128)} %all-gather.2.cloned.1.call-done, f32[1,1024,1024]{2,1,0:T(8,128)} %param.2), kind=kOutput, calls=%fused_computation | convolution fusion | flops 22649241600 | bytes 18939904 | tf_op jit(solution)/shard_map/lsp,pc->lsc/dot_general | solution.py:16
  111.5 0.2 slice_bitcast_fusion.2
  111.7 2.3 %collective-permute-start = (f32[600,1024]{1,0:T(8,128)S(1)}, f32[600,1024]{1,0:T(8,128)S(1)}, u32[]{:S(2)}, u32[]{:S(2)}) collective-permute-start(f32[600,1024]{1,0:T(8,128)S(1)} %slice_bitcast_fusion.2), channel_id=1, source_target_pairs={{0,2},{2,4},{4,6},{6,8},{8,10},{10,12},{12,14},{14,16},{16,18},{18... | collective-permute-start | bytes 7372808 | tf_op jit(solution)/shard_map/ppermute | solution.py:10
  114.0 4.1 %collective-permute-done = f32[600,1024]{1,0:T(8,128)S(1)} collective-permute-done((f32[600,1024]{1,0:T(8,128)S(1)}, f32[600,1024]{1,0:T(8,128)S(1)}, u32[]{:S(2)}, u32[]{:S(2)}) %collective-permute-start) | collective-permute-done | bytes 2457632 | tf_op jit(solution)/shard_map/ppermute | solution.py:10
  118.2 0.5 fusion.3
  118.6 25.0 %collective-permute-start.1 = (f32[600,1024]{1,0:T(8,128)S(1)}, f32[600,1024]{1,0:T(8,128)S(1)}, u32[]{:S(2)}, u32[]{:S(2)}) collective-permute-start(f32[600,1024]{1,0:T(8,128)S(1)} %fusion.3), channel_id=1, source_target_pairs={{0,2},{2,4},{4,6},{6,8},{8,10},{10,12},{12,14},{14,16},{16,18},{18... | collective-permute-start | bytes 7372808 | tf_op jit(solution)/shard_map/ppermute | solution.py:10
  143.7 4.1 %collective-permute-done.1 = f32[600,1024]{1,0:T(8,128)S(1)} collective-permute-done((f32[600,1024]{1,0:T(8,128)S(1)}, f32[600,1024]{1,0:T(8,128)S(1)}, u32[]{:S(2)}, u32[]{:S(2)}) %collective-permute-start.1) | collective-permute-done | bytes 2457632 | tf_op jit(solution)/shard_map/ppermute | solution.py:10
  147.8 1.9 fusion.2
  149.7 0.0 reduce-scatter.2.cloned.1.call-update
  149.7 62.9 %reduce-scatter.2.cloned.1.call-done = f32[600,512]{1,0:T(8,128)} async-done(((f32[600,1024]{1,0:T(8,128)}), f32[600,512]{1,0:T(8,128)}) %reduce-scatter.2.cloned.1.call-update) | async-done | bytes 1228816 | tf_op jit(solution)/shard_map/reduce_scatter | solution.py:26
Async XLA Ops:
  6.5 77.5 %all-gather.2.cloned.1.call-start = ((), (), s32[]{:S(2)}) async-start(), calls=%async_computation.1 | async-start | bytes 8355840 | tf_op jit(solution)/shard_map/all_gather | solution.py:18
  7.3 205.3 %reduce-scatter.2.cloned.1.call-start = ((), (), s32[]{:S(2)}) async-start(), calls=%async_computation.2 | async-start | bytes 3686400 | tf_op jit(solution)/shard_map/reduce_scatter | solution.py:26
  111.7 6.5 %collective-permute-start = (f32[600,1024]{1,0:T(8,128)S(1)}, f32[600,1024]{1,0:T(8,128)S(1)}, u32[]{:S(2)}, u32[]{:S(2)}) collective-permute-start(f32[600,1024]{1,0:T(8,128)S(1)} %slice_bitcast_fusion.2), channel_id=1, source_target_pairs={{0,2},{2,4},{4,6},{6,8},{8,10},{10,12},{12,14},{14,16},{16,18},{18... | collective-permute-start | bytes 7372808 | tf_op jit(solution)/shard_map/ppermute | solution.py:10
  118.6 29.1 %collective-permute-start.1 = (f32[600,1024]{1,0:T(8,128)S(1)}, f32[600,1024]{1,0:T(8,128)S(1)}, u32[]{:S(2)}, u32[]{:S(2)}) collective-permute-start(f32[600,1024]{1,0:T(8,128)S(1)} %fusion.3), channel_id=1, source_target_pairs={{0,2},{2,4},{4,6},{6,8},{8,10},{10,12},{12,14},{14,16},{16,18},{18... | collective-permute-start | bytes 7372808 | tf_op jit(solution)/shard_map/ppermute | solution.py:10
Sparse Core Ops, SparseCore 0:
  9.6 74.2 all-gather.1
  149.8 62.7 reduce-scatter.1
where the time goes:
time: 220 us; the launch traced here: 219 us
  waiting for transfers between devices  149 us (68%)
  matrix products  27.5 us (12%)
  starting transfers between devices  27.4 us (12%)
  between operations  13.4 us (6%)
  other arithmetic  2.41 us (1%)
    all_gather x1, waiting for transfers between devices, on_device(): lax.all_gather(kernels, 'tm', axis=2, tiled=True)  76.7 us
    reduce_scatter x1, waiting for transfers between devices, on_device(): result = lax.psum_scatter(running, 'space', scatter_dimension=1, tiled=True)  62.9 us
    dot_general x1, matrix products, on_device(): jnp.einsum('lsp,pc->lsc', lax.all_gather(kernels, 'tm', axis=2, tiled=Tru...  27.5 us
    ppermute x2, starting transfers between devices, passed_along(): return lax.ppermute(block, axis, route)  27.3 us
    ppermute x2, waiting for transfers between devices, passed_along(): return lax.ppermute(block, axis, route)  8.25 us
  transfers between devices with their start and end apart: 4, of which 4 were waited for; matrix products, arithmetic and copies ran while one was open for 0% of the time, Pallas kernels for 0%

commit v1 on v0

v1 whole, which is shorter than its diff:
```python
import functools

import jax
import jax.numpy as jnp
from jax import lax
from jax.experimental import pallas as pl
from jax.experimental.pallas import tpu as pltpu
from jax.sharding import Mesh, PartitionSpec as P

F32, BF16 = jnp.float32, jnp.bfloat16
VMEM_LIMIT = 48 * 2**20


def split(values):
    high = values.astype(BF16)
    return high, (values - high.astype(F32)).astype(BF16)


def spread_kernel(half, core_ref, kt_ref, keep_ref, send_ref, scratch):
    core = core_ref[0]
    lags, _, sensors = kt_ref.shape
    for lag in range(lags):
        scratch[...] = kt_ref[lag].T
        low, high = scratch[:half, :], scratch[sensors - half :, :]
        keep_ref[lag] = jnp.where(core == 0, low, high)
        send_ref[lag] = jnp.where(core == 0, high, low)


def halves_kernel(core_ref, own_ref, other_ref, high_ref, low_ref):
    core = core_ref[0]
    high_ref[core], low_ref[core] = split(own_ref[...])
    high_ref[1 - core], low_ref[1 - core] = split(other_ref[...])


def product(kh, kl, mh, ml):
    dot = functools.partial(jnp.dot, preferred_element_type=F32)
    return dot(kh, mh) + (dot(kh, ml) + dot(kl, mh))


def fill(k_ref, kh, kl):
    chips, _, width = k_ref.shape
    for chip in range(chips):
        columns = slice(chip * width, (chip + 1) * width)
        kh[:, columns], kl[:, columns] = split(k_ref[chip])


def one_kernel(info, k_ref, mh, ml, keep_ref, send_ref, kh, kl):
    part = pl.program_id(0)

    @pl.when(part == 0)
    def _():
        fill(k_ref, kh, kl)

    total = product(kh[...], kl[...], mh[0], ml[0])

    @pl.when(part == 0)
    def _():
        keep_ref[...] = total

    @pl.when(part > 0)
    def _():
        send_ref[0] = total


def two_kernel(info, k1_ref, k2_ref, m1h, m1l, m0h, m0l, keep_ref, send_ref, k1h, k1l, k2h, k2l):
    part = pl.program_id(0)

    @pl.when(part == 0)
    def _():
        fill(k1_ref, k1h, k1l)
        fill(k2_ref, k2h, k2l)

    total = product(k1h[...], k1l[...], m1h[0], m1l[0]) + product(k2h[...], k2l[...], m0h[0], m0l[0])

    @pl.when(part == 0)
    def _():
        keep_ref[...] = total

    @pl.when(part > 0)
    def _():
        send_ref[0] = total


def own_kernel(info, k0_ref, k1_ref, mth, mtl, m0h, m0l, keep_ref, send_ref, chip_ref, cross_ref, k0h, k0l, k1h, k1l):
    turn, part = pl.program_id(0), pl.program_id(1)

    @pl.when((turn == 0) & (part == 0))
    def _():
        fill(k0_ref, k0h, k0l)
        fill(k1_ref, k1h, k1l)

    slot = lax.rem(info[0] + turn, 2)

    def store(total):
        @pl.when((turn == 0) & (part == 0))
        def _():
            keep_ref[...] = total

        @pl.when((turn == 0) & (part > 0))
        def _():
            send_ref[0] = total

        @pl.when((turn == 1) & (part == 0))
        def _():
            chip_ref[...] = total

        @pl.when((turn == 1) & (part > 0))
        def _():
            cross_ref[0] = total

    @pl.when(slot == 0)
    def _():
        store(product(k0h[...], k0l[...], mth[0], mtl[0]))

    @pl.when(slot == 1)
    def _():
        store(product(k0h[...], k0l[...], mth[0], mtl[0]) + product(k1h[...], k1l[...], m0h[0], m0l[0]))


def finish_kernel(core_ref, a1, a2, a3, b1, b2, b3, out_ref):
    core = core_ref[0]
    sensors, half = out_ref.shape[0], a1.shape[0]
    own = a1[...] + a2[...] + a3[...]
    other = b1[...] + b2[...] + b3[...]
    out_ref[:half, :] = jnp.where(core == 0, own, other)
    out_ref[half:, :] = jnp.where(core == 0, other, own)[2 * half - sensors :, :]


def on_device(model, kernels, chips, spaces):
    core, place = lax.axis_index("core"), lax.axis_index("space")
    core_info = jnp.reshape(core, (1,)).astype(jnp.int32)
    info = jnp.stack([core, place]).astype(jnp.int32)
    own_model = model[0]
    depth, columns = own_model.shape
    lags, sensors, width = kernels.shape
    half = -(-sensors // 16) * 8
    block = columns // spaces
    params = pltpu.CompilerParams(vmem_limit_bytes=VMEM_LIMIT)
    smem = pl.BlockSpec(memory_space=pltpu.SMEM)
    vmem = pl.BlockSpec(memory_space=pltpu.VMEM)

    def swap(values):
        return lax.ppermute(values, "core", [(0, 1), (1, 0)])

    def onward(values):
        return lax.ppermute(values, "chip", [(i, i + 1) for i in range(chips - 1)])

    keep, send = pl.pallas_call(
        functools.partial(spread_kernel, half),
        out_shape=[jax.ShapeDtypeStruct((lags, half, width), F32)] * 2,
        in_specs=[smem, vmem],
        out_specs=[vmem, vmem],
        scratch_shapes=[pltpu.VMEM((sensors, width), F32)],
        compiler_params=params,
        name="spread",
    )(core_info, jnp.swapaxes(kernels, 1, 2))
    received = swap(send)
    first, second = jnp.where(core == 0, keep, received), jnp.where(core == 0, received, keep)
    chip_columns = jnp.concatenate([first, second], axis=2)
    k2, k1, k0 = [lax.all_gather(chip_columns[lag], "chip") for lag in (2, 1, 0)]

    rows = 256
    high, low = pl.pallas_call(
        halves_kernel,
        grid=(depth // rows,),
        out_shape=[jax.ShapeDtypeStruct((2, depth, columns), BF16)] * 2,
        in_specs=[smem] + [pl.BlockSpec((rows, columns), lambda i: (i, 0))] * 2,
        out_specs=[pl.BlockSpec((2, rows, columns), lambda i: (0, i, 0))] * 2,
        compiler_params=params,
        name="halves",
    )(core_info, own_model, swap(own_model))

    gathered = (chips, half, 2 * width)
    k_scratch = [pltpu.VMEM((half, depth), BF16)] * 2
    block_shape = jax.ShapeDtypeStruct((half, block), F32)
    sent_shape = jax.ShapeDtypeStruct((spaces - 1, half, block), F32)

    def m_spec(slot):
        return pl.BlockSpec((1, depth, block), lambda d, info: (slot, 0, lax.rem(info[1] + d, spaces)))

    def k_spec():
        return pl.BlockSpec(gathered, lambda *_: (0, 0, 0))

    out_specs = [
        pl.BlockSpec((half, block), lambda d, info: (0, 0)),
        pl.BlockSpec((1, half, block), lambda d, info: (jnp.maximum(d - 1, 0), 0, 0)),
    ]

    def flops(terms):
        return pl.CostEstimate(
            flops=terms * 6 * half * depth * columns, bytes_accessed=terms * 4 * depth * columns, transcendentals=0
        )

    o1_keep, o1_send = pl.pallas_call(
        one_kernel,
        grid_spec=pltpu.PrefetchScalarGridSpec(
            num_scalar_prefetch=1,
            grid=(spaces,),
            in_specs=[k_spec(), m_spec(1), m_spec(1)],
            out_specs=out_specs,
            scratch_shapes=k_scratch,
        ),
        out_shape=[block_shape, sent_shape],
        compiler_params=params,
        cost_estimate=flops(1),
        name="second_next",
    )(info, k2, high, low)
    o0_keep, o0_send = pl.pallas_call(
        two_kernel,
        grid_spec=pltpu.PrefetchScalarGridSpec(
            num_scalar_prefetch=1,
            grid=(spaces,),
            in_specs=[k_spec(), k_spec(), m_spec(1), m_spec(1), m_spec(0), m_spec(0)],
            out_specs=out_specs,
            scratch_shapes=k_scratch * 2,
        ),
        out_shape=[block_shape, sent_shape],
        compiler_params=params,
        cost_estimate=flops(2),
        name="first_next",
    )(info, k1, k2, high, low, high, low)

    def own_m_spec():
        return pl.BlockSpec(
            (1, depth, block),
            lambda turn, d, info: (lax.rem(info[0] + turn, 2), 0, lax.rem(info[1] + d, spaces)),
        )

    def zero_m_spec():
        return pl.BlockSpec((1, depth, block), lambda turn, d, info: (0, 0, lax.rem(info[1] + d, spaces)))

    def sent_index(owner):
        def index(turn, d, info):
            at = jnp.maximum(d - 1, 0)
            if owner == 0:
                return jnp.where(turn == 0, at, spaces - 2), 0, 0
            return jnp.where(turn == 1, at, 0), 0, 0

        return index

    kept_index = lambda turn, d, info: (0, 0)
    d_keep, d_send, d_chip, d_cross = pl.pallas_call(
        own_kernel,
        grid_spec=pltpu.PrefetchScalarGridSpec(
            num_scalar_prefetch=1,
            grid=(2, spaces),
            in_specs=[k_spec(), k_spec(), own_m_spec(), own_m_spec(), zero_m_spec(), zero_m_spec()],
            out_specs=[
                pl.BlockSpec((half, block), kept_index),
                pl.BlockSpec((1, half, block), sent_index(0)),
                pl.BlockSpec((half, block), kept_index),
                pl.BlockSpec((1, half, block), sent_index(1)),
            ],
            scratch_shapes=k_scratch * 2,
        ),
        out_shape=[block_shape, sent_shape, block_shape, sent_shape],
        compiler_params=params,
        cost_estimate=flops(3),
        name="own_times",
    )(info, k0, k1, high, low, high, low)

    def over_space(sent):
        parts = [
            lax.ppermute(sent[d - 1], "space", [(i, (i + d) % spaces) for i in range(spaces)])
            for d in range(1, spaces)
        ]
        return functools.reduce(jnp.add, parts)

    def over_space_and_core(sent):
        parts = [
            lax.ppermute(
                sent[d - 1],
                ("core", "space"),
                [(c * spaces + i, (1 - c) * spaces + (i + d) % spaces) for c in range(2) for i in range(spaces)],
            )
            for d in range(1, spaces)
        ]
        return functools.reduce(jnp.add, parts)

    next1 = onward(o1_keep + over_space(o1_send))
    next0 = onward(o0_keep + over_space(o0_send))
    next_own = jnp.where(core == 0, next0, next1)
    next_other = swap(jnp.where(core == 0, next1, next0))
    result = pl.pallas_call(
        finish_kernel,
        out_shape=jax.ShapeDtypeStruct((sensors, block), F32),
        in_specs=[smem] + [vmem] * 6,
        out_specs=vmem,
        compiler_params=params,
        name="finish",
    )(core_info, d_keep, next_own, over_space(d_send), swap(d_chip), next_other, over_space_and_core(d_cross))
    return result[None]


def solution(mesh):
    times, spaces = mesh.shape["tm"], mesh.shape["space"]
    chips = times // 2
    chip_mesh = Mesh(mesh.devices.reshape(chips, 2, spaces), ("chip", "core", "space"))
    return jax.shard_map(
        functools.partial(on_device, chips=chips, spaces=spaces),
        mesh=chip_mesh,
        in_specs=(P(("chip", "core"), "space", None), P(None, None, ("space", "chip", "core"))),
        out_specs=P(("chip", "core"), None, "space"),
        check_vma=False,
    )
```

time: 220 us -> 195 us (0.89)
  Pallas kernels: 0 us -> 31.9 us
  matrix products: 27.5 us -> 0 us
  waiting for transfers between devices: 149 us -> 128 us
  starting transfers between devices: 27.4 us -> 10.5 us
  local copies, waits for them, and re-layouts: 0.17 us -> 6.94 us
    reduce_scatter x1 -> x0, waiting for transfers between devices: 62.9 us -> none  [on_device(): result = lax.psum_scatter(running, 'space', scatter_dimension=1, tiled=True)]
    ppermute x2 -> x10, waiting for transfers between devices: 8.25 us -> 51.5 us  [the longest x3 32.8 us: over_space(): lax.ppermute(sent[d - 1], 'space', [(i, (i + d) % spaces) for i in range(...]
    pallas_call x0 -> x6, Pallas kernels: none -> 31.9 us  [the longest x1 11.5 us: on_device(): pl.pallas_call(own_kernel, grid_spec=pltpu.PrefetchScalarGridSpec(num_sca...]
    dot_general x1 -> x0, matrix products: 27.5 us -> none  [on_device(): jnp.einsum('lsp,pc->lsc', lax.all_gather(kernels, 'tm', axis=2, tiled=Tru...]
    ppermute x2 -> x10, starting transfers between devices: 27.3 us -> 10.4 us  [the longest x2 4.81 us: onward(): return lax.ppermute(values, 'chip', [(i, i + 1) for i in range(chips - 1)])]
    unnamed x0 -> x14, local copies, waits for them, and re-layouts: none -> 6.94 us
    all_gather x1 -> x3, waiting for transfers between devices: 76.7 us -> 76 us  [on_device(): lax.all_gather(chip_columns[lag], 'chip')]
  transfers between devices with their start and end apart: 4 -> 13, of which waited for: 4 -> 9; matrix products, arithmetic and copies ran while one was open for 0% -> 1% of each run, Pallas kernels for 0% -> 16%
where the time goes in v1:
time: 195 us; the launch traced here: 193 us
  waiting for transfers between devices  128 us (66%)
  Pallas kernels  31.9 us (16%)
  between operations  13.2 us (7%)
  starting transfers between devices  10.5 us (5%)
  local copies, waits for them, and re-layouts  6.94 us (4%)
  other arithmetic  2.23 us (1%)
    all_gather x3, waiting for transfers between devices, on_device(): lax.all_gather(chip_columns[lag], 'chip')  76 us
    ppermute x3, waiting for transfers between devices, over_space(): lax.ppermute(sent[d - 1], 'space', [(i, (i + d) % spaces) for i in range(...  32.8 us
    pallas_call x1, Pallas kernels, on_device(): pl.pallas_call(own_kernel, grid_spec=pltpu.PrefetchScalarGridSpec(num_sca...  11.5 us
    ppermute x1, waiting for transfers between devices, over_space_and_core(): lax.ppermute(sent[d - 1], ('core', 'space'), [(c * spaces + i, (1 - c) *...  11.2 us
    pallas_call x1, Pallas kernels, on_device(): pl.pallas_call(two_kernel, grid_spec=pltpu.PrefetchScalarGridSpec(num_sca...  7.7 us
    ppermute x4, waiting for transfers between devices, swap(): return lax.ppermute(values, 'core', [(0, 1), (1, 0)])  7.51 us
    unnamed x14, local copies, waits for them, and re-layouts  6.94 us
    pallas_call x1, Pallas kernels, on_device(): pl.pallas_call(halves_kernel, grid=(depth // rows,), out_shape=[jax.Shape...  6.28 us
  transfers between devices with their start and end apart: 13, of which 9 were waited for; matrix products, arithmetic and copies ran while one was open for 1% of the time, Pallas kernels for 16%

profile of v1, /device:TPU:0, one launch (start us, length us, event | category | flops | bytes accessed | tf_op | source)
XLA Modules:
  0.0 193.2 jit_solution(2009435103711699395)
XLA Ops:
  6.5 1.0 copy-done.5
  8.5 1.5 collective-permute-done
  10.0 0.9 pad_maximum_fusion
  12.5 6.0 %collective-permute-done.1.other_ref = f32[1024,1024]{1,0:T(8,128)} collective-permute-done((f32[1024,1024]{1,0:T(8,128)}, f32[1024,1024]{1,0:T(8,128)}, u32[]{:S(2)}, u32[]{:S(2)}) %collective-permute-start.1) | collective-permute-done | bytes 4194336 | tf_op jit(solution)/shard_map/ppermute | solution.py:143
  18.6 6.3 %halves.1 = (bf16[2,1024,1024]{2,1,0:T(8,128)(2,1)S(1)}, bf16[2,1024,1024]{2,1,0:T(8,128)(2,1)}) custom-call(s32[1]{0:T(128)} %bitcast.core_ref, f32[1024,1024]{1,0:T(8,128)} %bitcast.15, f32[1024,1024]{1,0:T(8,128)} %collective-permute-done.1.other_ref), custom_call_target="tpu_custom_call" | custom-call | tf_op jit(solution)/shard_map/halves/pallas_call | solution.py:163
  24.9 2.0 %copy-done = bf16[2,1024,1024]{2,1,0:T(8,128)(2,1)} copy-done((bf16[2,1024,1024]{2,1,0:T(8,128)(2,1)}, bf16[2,1024,1024]{2,1,0:T(8,128)(2,1)S(1)}, u32[]{:S(2)}) %copy-start) | copy-done | bytes 4194328
  26.9 28.4 %all-gather.6.cloned.1.call-done.k1_ref = f32[8,304,128]{2,1,0:T(8,128)} async-done(((f32[1,304,128]{2,1,0:T(8,128)}), f32[8,304,128]{2,1,0:T(8,128)}) %all-gather.6.cloned.1.call-update) | async-done | bytes 1245200 | tf_op jit(solution)/shard_map/all_gather | solution.py:160
  55.3 42.5 %all-gather.8.cloned.1.call-done.k2_ref.k_ref = f32[8,304,128]{2,1,0:T(8,128)} async-done(((f32[1,304,128]{2,1,0:T(8,128)}), f32[8,304,128]{2,1,0:T(8,128)}) %all-gather.8.cloned.1.call-update) | async-done | bytes 1245200 | tf_op jit(solution)/shard_map/all_gather | solution.py:160
  97.8 1.3 copy-done.1
  99.0 1.3 copy-done.3
  100.3 7.7 %first_next.1 = (f32[304,512]{1,0:T(8,128)S(1)}, f32[1,304,512]{2,1,0:T(8,128)S(1)}) custom-call(s32[2]{0:T(128)S(1)} %pad_add_fusion.info, f32[8,304,128]{2,1,0:T(8,128)S(1)} %copy-done.3, f32[8,304,128]{2,1,0:T(8,128)S(1)} %copy-done.1, bf16[2,1024,1024]{2,1,0:T(8,128)(2,1)} %copy-done, bf16[2,1024,1024]{2,1,0:T(8,128)(2,1)} %get-tuple-element.20.mtl.m0l.m1l.ml, ...), custom_call_target="tpu_custom_call" | custom-call | flops 3825205248 | bytes 8388608 | tf_op jit(solution)/shard_map/first_next/pallas_call | solution.py:208
  108.1 1.5 collective-permute-start.2
  109.6 4.8 %second_next.1 = (f32[304,512]{1,0:T(8,128)S(1)}, f32[1,304,512]{2,1,0:T(8,128)S(1)}) custom-call(s32[2]{0:T(128)S(1)} %pad_add_fusion.info, f32[8,304,128]{2,1,0:T(8,128)S(1)} %copy-done.2, bf16[2,1024,1024]{2,1,0:T(8,128)(2,1)} %copy-done, bf16[2,1024,1024]{2,1,0:T(8,128)(2,1)} %get-tuple-element.20.mtl.m0l.m1l.ml), custom_call_target="tpu_custom_call" | custom-call | flops 1912602624 | bytes 4194304 | tf_op jit(solution)/shard_map/second_next/pallas_call | solution.py:194
  115.0 10.1 %collective-permute-done.2 = f32[304,512]{1,0:T(8,128)S(1)} collective-permute-done((f32[304,512]{1,0:T(8,128)S(1)}, f32[304,512]{1,0:T(8,128)S(1)}, u32[]{:S(2)}, u32[]{:S(2)}) %collective-permute-start.2) | collective-permute-done | bytes 622624 | tf_op jit(solution)/shard_map/ppermute | solution.py:264
  125.2 2.5 %collective-permute-start.3 = (f32[304,512]{1,0:T(8,128)S(1)}, f32[304,512]{1,0:T(8,128)S(1)}, u32[]{:S(2)}, u32[]{:S(2)}) collective-permute-start(f32[304,512]{1,0:T(8,128)S(1)} %add.6), channel_id=1, source_target_pairs={{0,4},{4,8},{8,12},{12,16},{16,20},{20,24},{24,28},{1,5},{5,9},{9,... | collective-permute-start | bytes 1867784 | tf_op jit(solution)/shard_map/ppermute | solution.py:146
  127.7 8.3 %collective-permute-done.4 = f32[304,512]{1,0:T(8,128)S(1)} collective-permute-done((f32[304,512]{1,0:T(8,128)S(1)}, f32[304,512]{1,0:T(8,128)S(1)}, u32[]{:S(2)}, u32[]{:S(2)}) %collective-permute-start.4) | collective-permute-done | bytes 622624 | tf_op jit(solution)/shard_map/ppermute | solution.py:264
  137.0 2.3 %collective-permute-start.5 = (f32[304,512]{1,0:T(8,128)}, f32[304,512]{1,0:T(8,128)S(1)}, u32[]{:S(2)}, u32[]{:S(2)}) collective-permute-start(f32[304,512]{1,0:T(8,128)} %add.7), channel_id=1, source_target_pairs={{0,4},{4,8},{8,12},{12,16},{16,20},{20,24},{24,28},{1,5},{5,9},{9,... | collective-permute-start | bytes 1867784 | tf_op jit(solution)/shard_map/ppermute | solution.py:146
  139.3 5.1 %all-gather.4.cloned.1.call-done.k0_ref = f32[8,304,128]{2,1,0:T(8,128)} async-done(((f32[1,304,128]{2,1,0:T(8,128)}), f32[8,304,128]{2,1,0:T(8,128)}) %all-gather.4.cloned.1.call-update) | async-done | bytes 1245200 | tf_op jit(solution)/shard_map/all_gather | solution.py:160
  144.4 1.3 copy-done.6
  145.7 11.5 %own_times.1 = (f32[304,512]{1,0:T(8,128)S(1)}, f32[1,304,512]{2,1,0:T(8,128)S(1)}, f32[304,512]{1,0:T(8,128)S(1)}, f32[1,304,512]{2,1,0:T(8,128)S(1)}) custom-call(s32[2]{0:T(128)S(1)} %pad_add_fusion.info, f32[8,304,128]{2,1,0:T(8,128)S(1)} %copy-done.6, f32[8,304,128]{2,1,0:T(8,128)S(1)} %copy-done.4, bf16[2,1024,1024]{2,1,0:T(8,128)(2,1)} %copy-done, ...), custom_call_target="tpu_custom_call" | custom-call | flops 5737807872 | bytes 12582912 | tf_op jit(solution)/shard_map/own_times/pallas_call | solution.py:242
  157.2 1.9 collective-permute-start.6
  159.8 14.4 %collective-permute-done.6.a3 = f32[304,512]{1,0:T(8,128)S(1)} collective-permute-done((f32[304,512]{1,0:T(8,128)S(1)}, f32[304,512]{1,0:T(8,128)S(1)}, u32[]{:S(2)}, u32[]{:S(2)}) %collective-permute-start.6) | collective-permute-done | bytes 622624 | tf_op jit(solution)/shard_map/ppermute | solution.py:264
  174.2 11.2 %collective-permute-done.9.b3 = f32[304,512]{1,0:T(8,128)S(1)} collective-permute-done((f32[304,512]{1,0:T(8,128)S(1)}, f32[304,512]{1,0:T(8,128)S(1)}, u32[]{:S(2)}, u32[]{:S(2)}) %collective-permute-start.9) | collective-permute-done | bytes 622624 | tf_op jit(solution)/shard_map/ppermute | solution.py:271
  185.4 1.2 finish.1
  (31 shorter events, 4.9 us)
Async XLA Ops:
  6.5 48.7 %all-gather.6.cloned.1.call-start = ((), (), s32[]{:S(2)}) async-start(), calls=%async_computation.1 | async-start | bytes 1400832 | tf_op jit(solution)/shard_map/all_gather | solution.py:160
  6.5 1.0 copy-start.5
  8.0 2.0 %collective-permute-start = (f32[3,304,64]{2,1,0:T(8,128)S(1)}, f32[3,304,64]{2,1,0:T(8,128)S(1)}, u32[]{:S(2)}, u32[]{:S(2)}) collective-permute-start(f32[3,304,64]{2,1,0:T(8,128)S(1)} %get-tuple-element.18), channel_id=1, source_target_pairs={{0,2},{2,0},{1,3},{3,1},{4,6},{6,4},{5,7},{7,5},{8,10},{10,8},{9,1... | collective-permute-start | bytes 700424 | tf_op jit(solution)/shard_map/ppermute | solution.py:143
  11.0 86.8 %all-gather.8.cloned.1.call-start = ((), (), s32[]{:S(2)}) async-start(), calls=%async_computation.2 | async-start | bytes 1400832 | tf_op jit(solution)/shard_map/all_gather | solution.py:160
  11.0 7.6 %collective-permute-start.1 = (f32[1024,1024]{1,0:T(8,128)}, f32[1024,1024]{1,0:T(8,128)}, u32[]{:S(2)}, u32[]{:S(2)}) collective-permute-start(f32[1024,1024]{1,0:T(8,128)} %bitcast.14), channel_id=1, source_target_pairs={{0,2},{2,0},{1,3},{3,1},{4,6},{6,4},{5,7},{7,5},{8,10},{10,8},{9,1... | collective-permute-start | bytes 12582920 | tf_op jit(solution)/shard_map/ppermute | solution.py:143
  11.7 132.7 %all-gather.4.cloned.1.call-start = ((), (), s32[]{:S(2)}) async-start(), calls=%async_computation | async-start | bytes 1400832 | tf_op jit(solution)/shard_map/all_gather | solution.py:160
  24.9 2.0 %copy-start = (bf16[2,1024,1024]{2,1,0:T(8,128)(2,1)}, bf16[2,1024,1024]{2,1,0:T(8,128)(2,1)S(1)}, u32[]{:S(2)}) copy-start(bf16[2,1024,1024]{2,1,0:T(8,128)(2,1)S(1)} %get-tuple-element.19.mth.m0h.m1h.mh) | copy-start | bytes 12582916
  97.8 1.3 copy-start.1
  99.0 1.3 copy-start.3
  100.3 9.3 %copy-start.2 = (f32[8,304,128]{2,1,0:T(8,128)S(1)}, f32[8,304,128]{2,1,0:T(8,128)}, u32[]{:S(2)}) copy-start(f32[8,304,128]{2,1,0:T(8,128)} %all-gather.8.cloned.1.call-done.k2_ref.k_ref) | copy-start | bytes 3735556
  108.0 36.4 %copy-start.4 = (f32[8,304,128]{2,1,0:T(8,128)S(1)}, f32[8,304,128]{2,1,0:T(8,128)}, u32[]{:S(2)}) copy-start(f32[8,304,128]{2,1,0:T(8,128)} %all-gather.6.cloned.1.call-done.k1_ref) | copy-start | bytes 3735556
  108.1 17.0 %collective-permute-start.2 = (f32[304,512]{1,0:T(8,128)S(1)}, f32[304,512]{1,0:T(8,128)S(1)}, u32[]{:S(2)}, u32[]{:S(2)}) collective-permute-start(f32[304,512]{1,0:T(8,128)S(1)} %bitcast.13), channel_id=1, source_target_pairs={{0,1},{1,0},{2,3},{3,2},{4,5},{5,4},{6,7},{7,6},{8,9},{9,8},{10,11... | collective-permute-start | bytes 1867784 | tf_op jit(solution)/shard_map/ppermute | solution.py:264
  114.4 21.6 %collective-permute-start.4 = (f32[304,512]{1,0:T(8,128)S(1)}, f32[304,512]{1,0:T(8,128)S(1)}, u32[]{:S(2)}, u32[]{:S(2)}) collective-permute-start(f32[304,512]{1,0:T(8,128)S(1)} %bitcast.12), channel_id=1, source_target_pairs={{0,1},{1,0},{2,3},{3,2},{4,5},{5,4},{6,7},{7,6},{8,9},{9,8},{10,11... | collective-permute-start | bytes 1867784 | tf_op jit(solution)/shard_map/ppermute | solution.py:264
  125.2 34.2 %collective-permute-start.3 = (f32[304,512]{1,0:T(8,128)S(1)}, f32[304,512]{1,0:T(8,128)S(1)}, u32[]{:S(2)}, u32[]{:S(2)}) collective-permute-start(f32[304,512]{1,0:T(8,128)S(1)} %add.6), channel_id=1, source_target_pairs={{0,4},{4,8},{8,12},{12,16},{16,20},{20,24},{24,28},{1,5},{5,9},{9,... | collective-permute-start | bytes 1867784 | tf_op jit(solution)/shard_map/ppermute | solution.py:146
  137.0 22.5 %collective-permute-start.5 = (f32[304,512]{1,0:T(8,128)}, f32[304,512]{1,0:T(8,128)S(1)}, u32[]{:S(2)}, u32[]{:S(2)}) collective-permute-start(f32[304,512]{1,0:T(8,128)} %add.7), channel_id=1, source_target_pairs={{0,4},{4,8},{8,12},{12,16},{16,20},{20,24},{24,28},{1,5},{5,9},{9,... | collective-permute-start | bytes 1867784 | tf_op jit(solution)/shard_map/ppermute | solution.py:146
  144.4 1.3 copy-start.6
  157.2 17.0 %collective-permute-start.6 = (f32[304,512]{1,0:T(8,128)S(1)}, f32[304,512]{1,0:T(8,128)S(1)}, u32[]{:S(2)}, u32[]{:S(2)}) collective-permute-start(f32[304,512]{1,0:T(8,128)S(1)} %bitcast.11), channel_id=1, source_target_pairs={{0,1},{1,0},{2,3},{3,2},{4,5},{5,4},{6,7},{7,6},{8,9},{9,8},{10,11... | collective-permute-start | bytes 1867784 | tf_op jit(solution)/shard_map/ppermute | solution.py:264
  159.1 15.1 %collective-permute-start.7 = (f32[304,512]{1,0:T(8,128)S(1)}, f32[304,512]{1,0:T(8,128)S(1)}, u32[]{:S(2)}, u32[]{:S(2)}) collective-permute-start(f32[304,512]{1,0:T(8,128)S(1)} %get-tuple-element.27), channel_id=1, source_target_pairs={{0,2},{2,0},{1,3},{3,1},{4,6},{6,4},{5,7},{7,5},{8,10},{10,8},{9,1... | collective-permute-start | bytes 1867784 | tf_op jit(solution)/shard_map/ppermute | solution.py:143
  159.1 26.3 %collective-permute-start.9 = (f32[304,512]{1,0:T(8,128)S(1)}, f32[304,512]{1,0:T(8,128)S(1)}, u32[]{:S(2)}, u32[]{:S(2)}) collective-permute-start(f32[304,512]{1,0:T(8,128)S(1)} %bitcast.10), channel_id=1, source_target_pairs={{0,3},{1,2},{2,1},{3,0},{4,7},{5,6},{6,5},{7,4},{8,11},{9,10},{10,... | collective-permute-start | bytes 1867784 | tf_op jit(solution)/shard_map/ppermute | solution.py:271
  159.6 25.8 %collective-permute-start.8 = (f32[304,512]{1,0:T(8,128)S(1)}, f32[304,512]{1,0:T(8,128)S(1)}, u32[]{:S(2)}, u32[]{:S(2)}) collective-permute-start(f32[304,512]{1,0:T(8,128)S(1)} %get-tuple-element.29), channel_id=1, source_target_pairs={{0,2},{2,0},{1,3},{3,1},{4,6},{6,4},{5,7},{7,5},{8,10},{10,8},{9,1... | collective-permute-start | bytes 1867784 | tf_op jit(solution)/shard_map/ppermute | solution.py:143
Sparse Core Ops, SparseCore 0:
  11.1 44.1 all-gather.5
  57.4 40.2 all-gather.7
  99.9 44.4 all-gather.3

commit v2 on v0

v2 whole, which is shorter than its diff:
```python
import functools

import jax
import jax.numpy as jnp
from jax import lax
from jax.experimental import pallas as pl
from jax.experimental.pallas import tpu as pltpu
from jax.sharding import Mesh, PartitionSpec as P

F32, BF16 = jnp.float32, jnp.bfloat16
VMEM_LIMIT = 28 * 2**20
SMEM_SPEC = pl.BlockSpec(memory_space=pltpu.SMEM)
VMEM_SPEC = pl.BlockSpec(memory_space=pltpu.VMEM)


def after(values, *others):
    return lax.optimization_barrier((values, *others))[0]


def split(values):
    high = values.astype(BF16)
    return high, (values - high.astype(F32)).astype(BF16)


def call(kernel, name, shapes, operands, flops=0):
    return pl.pallas_call(
        kernel,
        out_shape=shapes,
        in_specs=[SMEM_SPEC] + [VMEM_SPEC] * (len(operands) - 1),
        out_specs=[VMEM_SPEC] * len(shapes),
        compiler_params=pltpu.CompilerParams(vmem_limit_bytes=VMEM_LIMIT),
        cost_estimate=pl.CostEstimate(flops=flops, bytes_accessed=2**20, transcendentals=0),
        name=name,
    )(*operands)


def spread_kernel(info, own_ref, other_ref, *lag_refs):
    first = info[0] == 0
    half = lag_refs[0].shape[0]
    sensors = own_ref.shape[2]
    for lag, out_ref in enumerate(lag_refs):
        own, other = own_ref[lag], other_ref[lag]
        both = jnp.concatenate([jnp.where(first, own, other), jnp.where(first, other, own)], axis=0).T
        out_ref[...] = jnp.where(first, both[:half], both[sensors - half :])


def halves_kernel(info, own_ref, other_ref, high_ref, low_ref):
    core, place = info[0], info[1]
    spaces, block = high_ref.shape[1], high_ref.shape[3]
    for turn in range(spaces):
        columns = pl.ds(pl.multiple_of(lax.rem(place + turn, spaces) * block, block), block)
        high_ref[core, turn], low_ref[core, turn] = split(own_ref[:, columns])
        high_ref[1 - core, turn], low_ref[1 - core, turn] = split(other_ref[:, columns])


def chip_at(at, line, row, lines, rows):
    row_off, line_off = at // lines, at % lines
    return lax.rem(line - line_off + lines, lines) * rows + lax.rem(row + row_off, rows)


def fill(blocks, pair_ref):
    half, width = blocks[0].shape
    for at, block in enumerate(blocks):
        columns = slice(at * width, (at + 1) * width)
        pair_ref[:half, columns], pair_ref[half:, columns] = split(block[...])


def times(pair_ref, high_ref, low_ref, slot, turn, put):
    half = pair_ref.shape[0] // 2
    width = high_ref.shape[3]
    step = width if width % 256 else 256
    for start in range(0, width, step):
        columns = slice(start, start + step)
        both = jnp.dot(pair_ref[...], high_ref[slot, turn, :, columns], preferred_element_type=F32)
        low = jnp.dot(pair_ref[:half], low_ref[slot, turn, :, columns], preferred_element_type=F32)
        put(columns, both[:half] + (both[half:] + low))


def lead_two_kernel(info, high, low, *refs):
    blocks, (pair, send) = refs[:-2], refs[-2:]
    fill(blocks, pair)
    for turn in range(1, high.shape[1]):

        def put(columns, total):
            send[turn - 1, :, columns] = total

        times(pair, high, low, 1, turn, put)


def rest_kernel(info, high, low, pair, *refs):
    (*added, keep, other) = refs

    def put_keep(columns, total):
        keep[:, columns] = total + added[0][0, :, columns] if added else total

    times(pair, high, low, 1, 0, put_keep)
    for turn in range(high.shape[1]):

        def put(columns, total):
            other[turn, :, columns] = total

        times(pair, high, low, 0, turn, put)


def lead_one_kernel(info, high, low, added, *refs):
    blocks, (pair, send) = refs[:-2], refs[-2:]
    fill(blocks, pair)
    for turn in range(1, high.shape[1]):

        def put(columns, total):
            send[turn - 1, :, columns] = total + added[turn, :, columns]

        times(pair, high, low, 1, turn, put)


def both_times(info, high, low, pair, added, turn, own_put, other_put):
    first = info[0] == 0
    early = {}

    def put_early(columns, total):
        early[columns.start] = total

    def put_late(columns, total):
        late = total + added[turn, :, columns]
        own_put(columns, jnp.where(first, early[columns.start], late))
        other_put(columns, jnp.where(first, late, early[columns.start]))

    times(pair, high, low, 0, turn, put_early)
    times(pair, high, low, 1, turn, put_late)


def lead_zero_kernel(info, high, low, added, *refs):
    blocks, (pair, send, cross) = refs[:-3], refs[-3:]
    fill(blocks, pair)
    for turn in range(1, high.shape[1]):

        def own_put(columns, total):
            send[turn - 1, :, columns] = total

        def other_put(columns, total):
            cross[turn - 1, :, columns] = total

        both_times(info, high, low, pair, added, turn, own_put, other_put)


def last_kernel(info, high, low, pair, added, keep, chip):
    def own_put(columns, total):
        keep[:, columns] = total

    def other_put(columns, total):
        chip[:, columns] = total

    both_times(info, high, low, pair, added, 0, own_put, other_put)


def finish_kernel(info, a1, a2, a3, b1, b2, b3, out_ref):
    first = info[0] == 0
    sensors, half = out_ref.shape[0], a1.shape[0]
    own = a1[...] + a2[...] + a3[...]
    other = b1[...] + b2[...] + b3[...]
    out_ref[:half, :] = jnp.where(first, own, other)
    out_ref[half:, :] = jnp.where(first, other, own)[2 * half - sensors :, :]


def on_device(model, kernels, lines, rows, spaces):
    core = lax.axis_index("core")
    info = jnp.stack([core, lax.axis_index("space"), lax.axis_index("line"), lax.axis_index("row")]).astype(jnp.int32)
    own_model = model[0]
    depth, columns = own_model.shape
    lags, sensors, width = kernels.shape
    half = -(-sensors // 32) * 16
    block = columns // spaces

    def swap(values):
        return lax.ppermute(values, "core", [(0, 1), (1, 0)])

    def onward(values):
        return lax.ppermute(values, ("line", "row"), [(i, i + 1) for i in range(lines * rows - 1)])

    def over_space(sent):
        return [
            lax.ppermute(sent[d - 1], "space", [(i, (i + d) % spaces) for i in range(spaces)])
            for d in range(1, spaces)
        ]

    def over_space_and_core(sent):
        return [
            lax.ppermute(
                sent[d - 1],
                ("core", "space"),
                [(c * spaces + i, (1 - c) * spaces + (i + d) % spaces) for c in range(2) for i in range(spaces)],
            )
            for d in range(1, spaces)
        ]

    def total(parts):
        return functools.reduce(jnp.add, parts)

    kernels_t = jnp.swapaxes(kernels, 1, 2)
    other_t = swap(kernels_t)
    lag_blocks = call(
        spread_kernel, "spread", [jax.ShapeDtypeStruct((half, 2 * width), F32)] * lags, [info, kernels_t, other_t]
    )

    def arrived(at, info):
        return chip_at(at, info[2], info[3], lines, rows), 0

    high, low = pl.pallas_call(
        halves_kernel,
        grid_spec=pltpu.PrefetchScalarGridSpec(
            num_scalar_prefetch=1,
            grid=(lines * rows,),
            in_specs=[pl.BlockSpec((2 * width, columns), arrived)] * 2,
            out_specs=[pl.BlockSpec((2, spaces, 2 * width, block), lambda at, info: (0, 0, at, 0))] * 2,
        ),
        out_shape=[jax.ShapeDtypeStruct((2, spaces, depth, block), BF16)] * 2,
        compiler_params=pltpu.CompilerParams(vmem_limit_bytes=VMEM_LIMIT),
        name="halves",
    )(info, own_model, swap(after(own_model, other_t)))

    shifts = sorted(range(1, lines), key=lambda s: (min(s, lines - s), s))
    line_moves, row_moves = [], []

    def queued(moves, values, axis, route):
        if len(moves) >= 2:
            values = after(values, moves[-2])
        moved = lax.ppermute(values, axis, route)
        moves.append(moved)
        return moved

    gathered = {}
    for lag in (2, 1, 0):
        here = {0: lag_blocks[lag]}
        there = {}
        for shift in [0] + shifts:
            if shift:
                route = [(i, (i + shift) % lines) for i in range(lines)]
                here[shift] = queued(line_moves, lag_blocks[lag], "line", route)
            for off in range(1, rows):
                there[off, shift] = queued(
                    row_moves, here[shift], "row", [(i, (i - off) % rows) for i in range(rows)]
                )
        gathered[lag] = [here[s] for s in range(lines)] + [there[o, s] for o in range(1, rows) for s in range(lines)]

    pair = jax.ShapeDtypeStruct((2 * half, depth), BF16)
    one = jax.ShapeDtypeStruct((half, block), F32)
    sent = jax.ShapeDtypeStruct((spaces - 1, half, block), F32)
    whole = jax.ShapeDtypeStruct((spaces, half, block), F32)
    flops = 6 * half * depth * block

    pair2, send1 = call(lead_two_kernel, "lead2", [pair, sent], [info, high, low, *gathered[2]], flops)
    from1 = over_space(send1)
    keep1, early2 = call(rest_kernel, "rest2", [one, whole], [info, high, low, pair2], 3 * flops)

    pair1, send0 = call(lead_one_kernel, "lead1", [pair, sent], [info, high, low, early2, *gathered[1]], flops)
    from0 = over_space(send0)
    keep0, early1 = call(rest_kernel, "rest1", [one, whole], [info, high, low, pair1, early2], 3 * flops)

    pair0, d_send, d_cross = call(
        lead_zero_kernel, "lead0", [pair, sent, sent], [info, high, low, early1, *gathered[0]], 2 * flops
    )
    d_from, d_from_cross = over_space(d_send), over_space_and_core(d_cross)
    d_keep, d_chip = call(last_kernel, "last", [one, one], [info, high, low, pair0, early1], 2 * flops)

    next1 = onward(after(total([keep1, *from1]), row_moves[-1]))
    next0 = onward(after(total([keep0, *from0]), row_moves[-1]))
    next_own = jnp.where(core == 0, next0, next1)
    next_other = swap(jnp.where(core == 0, next1, next0))
    (result,) = call(
        finish_kernel,
        "finish",
        [jax.ShapeDtypeStruct((sensors, block), F32)],
        [info, d_keep, next_own, total(d_from), swap(d_chip), next_other, total(d_from_cross)],
    )
    return result[None]


def solution(mesh):
    chips, spaces = mesh.shape["tm"] // 2, mesh.shape["space"]
    rows = 1 if chips % 2 else 2
    lines = chips // rows
    grid = Mesh(mesh.devices.reshape(lines, rows, 2, spaces), ("line", "row", "core", "space"))
    return jax.shard_map(
        functools.partial(on_device, lines=lines, rows=rows, spaces=spaces),
        mesh=grid,
        in_specs=(P(("line", "row", "core"), "space", None), P(None, None, ("space", "line", "row", "core"))),
        out_specs=P(("line", "row", "core"), None, "space"),
        check_vma=False,
    )
```

time: 220 us -> 157 us (0.71)
  the two profiles are of different devices: /device:TPU:0 before, /device:TPU:19 now
where the time goes in v2:
time: 157 us; the launch traced here: 156 us
  starting transfers between devices  68.1 us (43%)
  waiting for transfers between devices  52.5 us (33%)
  Pallas kernels  24.8 us (16%)
  local copies, waits for them, and re-layouts  7.6 us (5%)
  other arithmetic  3.13 us (2%)
    ppermute x21, starting transfers between devices, queued(): moved = lax.ppermute(values, axis, route)  27.5 us
    ppermute x21, waiting for transfers between devices, queued(): moved = lax.ppermute(values, axis, route)  24.8 us
    ppermute x4, starting transfers between devices, swap(): return lax.ppermute(values, 'core', [(0, 1), (1, 0)])  24.7 us
    pallas_call x8, Pallas kernels, call(): pl.pallas_call(kernel, out_shape=shapes, in_specs=[SMEM_SPEC] + [VMEM_SPE...  18.6 us
    ppermute x1, waiting for transfers between devices, over_space_and_core(): lax.ppermute(sent[d - 1], ('core', 'space'), [(c * spaces + i, (1 - c) *...  13.5 us
    ppermute x2, starting transfers between devices, onward(): lax.ppermute(values, ('line', 'row'), [(i, i + 1) for i in range(lines *...  12.6 us
    ppermute x3, waiting for transfers between devices, over_space(): lax.ppermute(sent[d - 1], 'space', [(i, (i + d) % spaces) for i in range(...  12.5 us
    unnamed x12, local copies, waits for them, and re-layouts  7.6 us
  transfers between devices with their start and end apart: 31, of which 14 were waited for; matrix products, arithmetic and copies ran while one was open for 2% of the time, Pallas kernels for 14%

profile of v2, /device:TPU:19, one launch (start us, length us, event | category | flops | bytes accessed | tf_op | source)
XLA Modules:
  0.0 156.3 jit_solution(14446693150431786229)
XLA Ops:
  7.5 2.9 %collective-permute-done.2.refs_1_ = f32[304,128]{1,0:T(8,128)S(1)} collective-permute-done((f32[304,128]{1,0:T(8,128)S(1)}, f32[304,128]{1,0:T(8,128)S(1)}, u32[]{:S(2)}, u32[]{:S(2)}) %collective-permute-start.2) | collective-permute-done | bytes 155680 | tf_op jit(solution)/shard_map/ppermute | solution.py:227
  10.4 1.9 %collective-permute-start.3 = (f32[304,128]{1,0:T(8,128)S(1)}, f32[304,128]{1,0:T(8,128)S(1)}, u32[]{:S(2)}, u32[]{:S(2)}) collective-permute-start(f32[304,128]{1,0:T(8,128)S(1)} %get-tuple-element.47.refs_0_), channel_id=1, source_target_pairs={{0,16},{8,24},{16,0},{24,8},{1,17},{9,25},{17,1},{25,9},{2,18},{10... | collective-permute-start | bytes 466952 | tf_op jit(solution)/shard_map/ppermute | solution.py:227
  17.6 1.9 %collective-permute-done.9.refs_1_ = f32[304,128]{1,0:T(8,128)S(1)} collective-permute-done((f32[304,128]{1,0:T(8,128)S(1)}, f32[304,128]{1,0:T(8,128)S(1)}, u32[]{:S(2)}, u32[]{:S(2)}) %collective-permute-start.9) | collective-permute-done | bytes 155680 | tf_op jit(solution)/shard_map/ppermute | solution.py:227
  21.1 4.4 %collective-permute-start.10 = (f32[304,128]{1,0:T(8,128)S(1)}, f32[304,128]{1,0:T(8,128)S(1)}, u32[]{:S(2)}, u32[]{:S(2)}) collective-permute-start(f32[304,128]{1,0:T(8,128)S(1)} %get-tuple-element.56.refs_0_), channel_id=1, source_target_pairs={{0,16},{8,24},{16,0},{24,8},{1,17},{9,25},{17,1},{25,9},{2,18},{10... | collective-permute-start | bytes 466952 | tf_op jit(solution)/shard_map/ppermute | solution.py:227
  27.0 3.3 %collective-permute-done.10.refs_2_ = f32[304,128]{1,0:T(8,128)S(1)} collective-permute-done((f32[304,128]{1,0:T(8,128)S(1)}, f32[304,128]{1,0:T(8,128)S(1)}, u32[]{:S(2)}, u32[]{:S(2)}) %collective-permute-start.10) | collective-permute-done | bytes 155680 | tf_op jit(solution)/shard_map/ppermute | solution.py:227
  31.4 2.2 %copy-done.4 = f32[1,1024,1024]{2,1,0:T(8,128)S(1)} copy-done((f32[1,1024,1024]{2,1,0:T(8,128)S(1)}, f32[1,1024,1024]{2,1,0:T(8,128)}, u32[]{:S(2)}) %copy-start.4) | copy-done | bytes 4194328
  33.6 6.2 %halves.1 = (bf16[2,2,1024,512]{3,2,1,0:T(8,128)(2,1)S(1)}, bf16[2,2,1024,512]{3,2,1,0:T(8,128)(2,1)S(1)}) custom-call(s32[4]{0:T(128)S(1)} %pad_add_fusion.info, f32[1024,1024]{1,0:T(8,128)S(1)} %bitcast.12, f32[1024,1024]{1,0:T(8,128)} %collective-permute-done.1.other_ref), custom_call_target="tpu_custom_call" | custom-call | tf_op jit(solution)/shard_map/halves/pallas_call | solution.py:208
  41.5 3.6 %rest2.1 = (f32[304,512]{1,0:T(8,128)S(1)}, f32[2,304,512]{2,1,0:T(8,128)S(1)}) custom-call(s32[4]{0:T(128)S(1)} %pad_add_fusion.info, bf16[2,2,1024,512]{3,2,1,0:T(8,128)(2,1)S(1)} %get-tuple-element.44.high, bf16[2,2,1024,512]{3,2,1,0:T(8,128)(2,1)S(1)} %get-tuple-element.45.low, bf16[608,1024]{1,0:T(8,128)(2,1)S(1)} %get-tuple-element.50.pair), custom_call_target="tpu_custom_call" | custom-call | flops 2868903936 | bytes 1048576 | tf_op jit(solution)/shard_map/rest2/pallas_call | solution.py:26
  48.3 4.6 %collective-permute-start.16 = (f32[304,128]{1,0:T(8,128)S(1)}, f32[304,128]{1,0:T(8,128)S(1)}, u32[]{:S(2)}, u32[]{:S(2)}) collective-permute-start(f32[304,128]{1,0:T(8,128)S(1)} %get-tuple-element.66.refs_0_), channel_id=1, source_target_pairs={{0,8},{8,16},{16,24},{24,0},{1,9},{9,17},{17,25},{25,1},{2,10},{10... | collective-permute-start | bytes 466952 | tf_op jit(solution)/shard_map/ppermute | solution.py:227
  52.9 2.2 %collective-permute-done.16.refs_1_ = f32[304,128]{1,0:T(8,128)S(1)} collective-permute-done((f32[304,128]{1,0:T(8,128)S(1)}, f32[304,128]{1,0:T(8,128)S(1)}, u32[]{:S(2)}, u32[]{:S(2)}) %collective-permute-start.16) | collective-permute-done | bytes 155680 | tf_op jit(solution)/shard_map/ppermute | solution.py:227
  55.1 2.5 %collective-permute-start.17 = (f32[304,128]{1,0:T(8,128)S(1)}, f32[304,128]{1,0:T(8,128)S(1)}, u32[]{:S(2)}, u32[]{:S(2)}) collective-permute-start(f32[304,128]{1,0:T(8,128)S(1)} %get-tuple-element.66.refs_0_), channel_id=1, source_target_pairs={{0,16},{8,24},{16,0},{24,8},{1,17},{9,25},{17,1},{25,9},{2,18},{10... | collective-permute-start | bytes 466952 | tf_op jit(solution)/shard_map/ppermute | solution.py:227
  58.5 3.1 %collective-permute-done.17.refs_2_ = f32[304,128]{1,0:T(8,128)S(1)} collective-permute-done((f32[304,128]{1,0:T(8,128)S(1)}, f32[304,128]{1,0:T(8,128)S(1)}, u32[]{:S(2)}, u32[]{:S(2)}) %collective-permute-start.17) | collective-permute-done | bytes 155680 | tf_op jit(solution)/shard_map/ppermute | solution.py:227
  63.0 3.6 %rest1.1 = (f32[304,512]{1,0:T(8,128)S(1)}, f32[2,304,512]{2,1,0:T(8,128)S(1)}) custom-call(s32[4]{0:T(128)S(1)} %pad_add_fusion.info, bf16[2,2,1024,512]{3,2,1,0:T(8,128)(2,1)S(1)} %get-tuple-element.44.high, bf16[2,2,1024,512]{3,2,1,0:T(8,128)(2,1)S(1)} %get-tuple-element.45.low, bf16[608,1024]{1,0:T(8,128)(2,1)S(1)} %get-tuple-element.60.pair, ...), custom_call_target="tpu_custom_call" | custom-call | flops 2868903936 | bytes 1048576 | tf_op jit(solution)/shard_map/rest1/pallas_call | solution.py:26
  67.6 2.3 %collective-permute-start.24 = (f32[304,512]{1,0:T(8,128)}, f32[304,512]{1,0:T(8,128)S(1)}, u32[]{:S(2)}, u32[]{:S(2)}) collective-permute-start(f32[304,512]{1,0:T(8,128)} %add.6), channel_id=1, source_target_pairs={{0,4},{4,8},{8,12},{12,16},{16,20},{20,24},{24,28},{1,5},{5,9},{9,... | collective-permute-start | bytes 1867784 | tf_op jit(solution)/shard_map/ppermute | solution.py:178
  70.9 10.2 %collective-permute-start.26 = (f32[304,512]{1,0:T(8,128)}, f32[304,512]{1,0:T(8,128)}, u32[]{:S(2)}, u32[]{:S(2)}) collective-permute-start(f32[304,512]{1,0:T(8,128)} %add.7), channel_id=1, source_target_pairs={{0,4},{4,8},{8,12},{12,16},{16,20},{20,24},{24,28},{1,5},{5,9},{9,... | collective-permute-start | bytes 1867784 | tf_op jit(solution)/shard_map/ppermute | solution.py:178
  82.2 9.9 %collective-permute-done.22.refs_7_ = f32[304,128]{1,0:T(8,128)S(1)} collective-permute-done((f32[304,128]{1,0:T(8,128)S(1)}, f32[304,128]{1,0:T(8,128)S(1)}, u32[]{:S(2)}, u32[]{:S(2)}) %collective-permute-start.22) | collective-permute-done | bytes 155680 | tf_op jit(solution)/shard_map/ppermute | solution.py:227
  92.2 2.2 %copy-done.1 = bf16[2,2,1024,512]{3,2,1,0:T(8,128)(2,1)S(1)} copy-done((bf16[2,2,1024,512]{3,2,1,0:T(8,128)(2,1)S(1)}, bf16[2,2,1024,512]{3,2,1,0:T(8,128)(2,1)}, u32[]{:S(2)}) %copy-start.1) | copy-done | bytes 4194328
  94.4 2.2 %copy-done.3 = bf16[2,2,1024,512]{3,2,1,0:T(8,128)(2,1)S(1)} copy-done((bf16[2,2,1024,512]{3,2,1,0:T(8,128)(2,1)S(1)}, bf16[2,2,1024,512]{3,2,1,0:T(8,128)(2,1)}, u32[]{:S(2)}) %copy-start.3) | copy-done | bytes 4194328
  96.5 2.7 %lead0.1 = (bf16[608,1024]{1,0:T(8,128)(2,1)S(1)}, f32[1,304,512]{2,1,0:T(8,128)S(1)}, f32[1,304,512]{2,1,0:T(8,128)S(1)}) custom-call(s32[4]{0:T(128)S(1)} %pad_add_fusion.info, bf16[2,2,1024,512]{3,2,1,0:T(8,128)(2,1)S(1)} %copy-done.1, bf16[2,2,1024,512]{3,2,1,0:T(8,128)(2,1)S(1)} %copy-done.3, f32[2,304,512]{2,1,0:T(8,128)S(1)} %get-tuple-element.61.added, ...), custom_call_target="tpu_custom_call" | custom-call | flops 1912602624 | bytes 1048576 | tf_op jit(solution)/shard_map/lead0/pallas_call | solution.py:26
  99.2 2.6 %last.1 = (f32[304,512]{1,0:T(8,128)S(1)}, f32[304,512]{1,0:T(8,128)S(1)}) custom-call(s32[4]{0:T(128)S(1)} %pad_add_fusion.info, bf16[2,2,1024,512]{3,2,1,0:T(8,128)(2,1)S(1)} %copy-done.1, bf16[2,2,1024,512]{3,2,1,0:T(8,128)(2,1)S(1)} %copy-done.3, bf16[608,1024]{1,0:T(8,128)(2,1)S(1)} %get-tuple-element.70.pair, f32[2,304,512]{2,1,0:T(8,128)S(1)} %get-tuple-element.61.added), custom_call_target="tpu_custom_call" | custom-call | flops 1912602624 | bytes 1048576 | tf_op jit(solution)/shard_map/last/pallas_call | solution.py:26
  101.9 23.5 %collective-permute-start.28 = (f32[304,512]{1,0:T(8,128)S(1)}, f32[304,512]{1,0:T(8,128)S(1)}, u32[]{:S(2)}, u32[]{:S(2)}) collective-permute-start(f32[304,512]{1,0:T(8,128)S(1)} %get-tuple-element.79), channel_id=1, source_target_pairs={{0,2},{2,0},{1,3},{3,1},{4,6},{6,4},{5,7},{7,5},{8,10},{10,8},{9,1... | collective-permute-start | bytes 1867784 | tf_op jit(solution)/shard_map/ppermute | solution.py:175
  128.5 12.4 %collective-permute-done.27.a3 = f32[304,512]{1,0:T(8,128)S(1)} collective-permute-done((f32[304,512]{1,0:T(8,128)S(1)}, f32[304,512]{1,0:T(8,128)S(1)}, u32[]{:S(2)}, u32[]{:S(2)}) %collective-permute-start.27) | collective-permute-done | bytes 622624 | tf_op jit(solution)/shard_map/ppermute | solution.py:182
  141.0 13.5 %collective-permute-done.30.b3 = f32[304,512]{1,0:T(8,128)S(1)} collective-permute-done((f32[304,512]{1,0:T(8,128)S(1)}, f32[304,512]{1,0:T(8,128)S(1)}, u32[]{:S(2)}, u32[]{:S(2)}) %collective-permute-start.30) | collective-permute-done | bytes 622624 | tf_op jit(solution)/shard_map/ppermute | solution.py:188
  154.5 1.9 %finish.1 = f32[600,512]{1,0:T(8,128)} custom-call(s32[4]{0:T(128)S(1)} %pad_add_fusion.info, f32[304,512]{1,0:T(8,128)S(1)} %get-tuple-element.71.a1, f32[304,512]{1,0:T(8,128)S(1)} %get-tuple-element.82.a2, f32[304,512]{1,0:T(8,128)S(1)} %collective-permute-done.27.a3, f32[304,512]{1,0:T(8,128)S(1)} %collective-permute-done.28.b1, ...), custom_call_target="tpu_custom_call" | custom-call | bytes 1048576 | tf_op jit(solution)/shard_map/finish/pallas_call | solution.py:26
  (63 shorter events, 30.3 us)
Async XLA Ops:
  2.4 29.0 %collective-permute-start.1 = (f32[1024,1024]{1,0:T(8,128)}, f32[1024,1024]{1,0:T(8,128)}, u32[]{:S(2)}, u32[]{:S(2)}) collective-permute-start(f32[1024,1024]{1,0:T(8,128)} %bitcast.11), channel_id=1, source_target_pairs={{0,2},{2,0},{1,3},{3,1},{4,6},{6,4},{5,7},{7,5},{8,10},{10,8},{9,1... | collective-permute-start | bytes 12582920 | tf_op jit(solution)/shard_map/ppermute | solution.py:175
  6.1 7.5 %collective-permute-start.4 = (f32[304,128]{1,0:T(8,128)S(1)}, f32[304,128]{1,0:T(8,128)S(1)}, u32[]{:S(2)}, u32[]{:S(2)}) collective-permute-start(f32[304,128]{1,0:T(8,128)S(1)} %get-tuple-element.47.refs_0_), channel_id=1, source_target_pairs={{0,24},{8,0},{16,8},{24,16},{1,25},{9,1},{17,9},{25,17},{2,26},{10... | collective-permute-start | bytes 466952 | tf_op jit(solution)/shard_map/ppermute | solution.py:227
  6.3 8.5 %collective-permute-start.5 = (f32[304,128]{1,0:T(8,128)S(1)}, f32[304,128]{1,0:T(8,128)S(1)}, u32[]{:S(2)}, u32[]{:S(2)}) collective-permute-start(f32[304,128]{1,0:T(8,128)S(1)} %get-tuple-element.47.refs_0_), channel_id=1, source_target_pairs={{0,4},{4,0},{1,5},{5,1},{2,6},{6,2},{3,7},{7,3},{8,12},{12,8},{9,1... | collective-permute-start | bytes 466952 | tf_op jit(solution)/shard_map/ppermute | solution.py:227
  10.4 5.9 %collective-permute-start.3 = (f32[304,128]{1,0:T(8,128)S(1)}, f32[304,128]{1,0:T(8,128)S(1)}, u32[]{:S(2)}, u32[]{:S(2)}) collective-permute-start(f32[304,128]{1,0:T(8,128)S(1)} %get-tuple-element.47.refs_0_), channel_id=1, source_target_pairs={{0,16},{8,24},{16,0},{24,8},{1,17},{9,25},{17,1},{25,9},{2,18},{10... | collective-permute-start | bytes 466952 | tf_op jit(solution)/shard_map/ppermute | solution.py:227
  13.6 6.0 %collective-permute-start.9 = (f32[304,128]{1,0:T(8,128)S(1)}, f32[304,128]{1,0:T(8,128)S(1)}, u32[]{:S(2)}, u32[]{:S(2)}) collective-permute-start(f32[304,128]{1,0:T(8,128)S(1)} %get-tuple-element.56.refs_0_), channel_id=1, source_target_pairs={{0,8},{8,16},{16,24},{24,0},{1,9},{9,17},{17,25},{25,1},{2,10},{10... | collective-permute-start | bytes 466952 | tf_op jit(solution)/shard_map/ppermute | solution.py:227
  16.4 9.2 %collective-permute-start.7 = (f32[304,128]{1,0:T(8,128)S(1)}, f32[304,128]{1,0:T(8,128)S(1)}, u32[]{:S(2)}, u32[]{:S(2)}) collective-permute-start(f32[304,128]{1,0:T(8,128)S(1)} %collective-permute-done.3.refs_2_), channel_id=1, source_target_pairs={{0,4},{4,0},{1,5},{5,1},{2,6},{6,2},{3,7},{7,3},{8,12},{12,8},{9,1... | collective-permute-start | bytes 466952 | tf_op jit(solution)/shard_map/ppermute | solution.py:227
  19.5 6.0 %collective-permute-start.11 = (f32[304,128]{1,0:T(8,128)S(1)}, f32[304,128]{1,0:T(8,128)S(1)}, u32[]{:S(2)}, u32[]{:S(2)}) collective-permute-start(f32[304,128]{1,0:T(8,128)S(1)} %get-tuple-element.56.refs_0_), channel_id=1, source_target_pairs={{0,24},{8,0},{16,8},{24,16},{1,25},{9,1},{17,9},{25,17},{2,26},{10... | collective-permute-start | bytes 466952 | tf_op jit(solution)/shard_map/ppermute | solution.py:227
  19.8 6.0 %collective-permute-start.12 = (f32[304,128]{1,0:T(8,128)S(1)}, f32[304,128]{1,0:T(8,128)S(1)}, u32[]{:S(2)}, u32[]{:S(2)}) collective-permute-start(f32[304,128]{1,0:T(8,128)S(1)} %get-tuple-element.56.refs_0_), channel_id=1, source_target_pairs={{0,4},{4,0},{1,5},{5,1},{2,6},{6,2},{3,7},{7,3},{8,12},{12,8},{9,1... | collective-permute-start | bytes 466952 | tf_op jit(solution)/shard_map/ppermute | solution.py:227
  21.1 9.2 %collective-permute-start.10 = (f32[304,128]{1,0:T(8,128)S(1)}, f32[304,128]{1,0:T(8,128)S(1)}, u32[]{:S(2)}, u32[]{:S(2)}) collective-permute-start(f32[304,128]{1,0:T(8,128)S(1)} %get-tuple-element.56.refs_0_), channel_id=1, source_target_pairs={{0,16},{8,24},{16,0},{24,8},{1,17},{9,25},{17,1},{25,9},{2,18},{10... | collective-permute-start | bytes 466952 | tf_op jit(solution)/shard_map/ppermute | solution.py:227
  25.8 19.3 %collective-permute-start.15 = (f32[304,128]{1,0:T(8,128)S(1)}, f32[304,128]{1,0:T(8,128)S(1)}, u32[]{:S(2)}, u32[]{:S(2)}) collective-permute-start(f32[304,128]{1,0:T(8,128)S(1)} %collective-permute-done.11.refs_3_), channel_id=1, source_target_pairs={{0,4},{4,0},{1,5},{5,1},{2,6},{6,2},{3,7},{7,3},{8,12},{12,8},{9,1... | collective-permute-start | bytes 466952 | tf_op jit(solution)/shard_map/ppermute | solution.py:227
  30.8 14.3 %collective-permute-start.14 = (f32[304,128]{1,0:T(8,128)S(1)}, f32[304,128]{1,0:T(8,128)S(1)}, u32[]{:S(2)}, u32[]{:S(2)}) collective-permute-start(f32[304,128]{1,0:T(8,128)S(1)} %collective-permute-done.10.refs_2_), channel_id=1, source_target_pairs={{0,4},{4,0},{1,5},{5,1},{2,6},{6,2},{3,7},{7,3},{8,12},{12,8},{9,1... | collective-permute-start | bytes 466952 | tf_op jit(solution)/shard_map/ppermute | solution.py:227
  46.8 19.8 %collective-permute-start.23 = (f32[304,512]{1,0:T(8,128)S(1)}, f32[304,512]{1,0:T(8,128)S(1)}, u32[]{:S(2)}, u32[]{:S(2)}) collective-permute-start(f32[304,512]{1,0:T(8,128)S(1)} %bitcast.16), channel_id=1, source_target_pairs={{0,1},{1,0},{2,3},{3,2},{4,5},{5,4},{6,7},{7,6},{8,9},{9,8},{10,11... | collective-permute-start | bytes 1867784 | tf_op jit(solution)/shard_map/ppermute | solution.py:182
  47.1 22.8 %collective-permute-start.25 = (f32[304,512]{1,0:T(8,128)S(1)}, f32[304,512]{1,0:T(8,128)S(1)}, u32[]{:S(2)}, u32[]{:S(2)}) collective-permute-start(f32[304,512]{1,0:T(8,128)S(1)} %bitcast.15), channel_id=1, source_target_pairs={{0,1},{1,0},{2,3},{3,2},{4,5},{5,4},{6,7},{7,6},{8,9},{9,8},{10,11... | collective-permute-start | bytes 1867784 | tf_op jit(solution)/shard_map/ppermute | solution.py:182
  48.3 6.8 %collective-permute-start.16 = (f32[304,128]{1,0:T(8,128)S(1)}, f32[304,128]{1,0:T(8,128)S(1)}, u32[]{:S(2)}, u32[]{:S(2)}) collective-permute-start(f32[304,128]{1,0:T(8,128)S(1)} %get-tuple-element.66.refs_0_), channel_id=1, source_target_pairs={{0,8},{8,16},{16,24},{24,0},{1,9},{9,17},{17,25},{25,1},{2,10},{10... | collective-permute-start | bytes 466952 | tf_op jit(solution)/shard_map/ppermute | solution.py:227
  55.1 6.4 %collective-permute-start.17 = (f32[304,128]{1,0:T(8,128)S(1)}, f32[304,128]{1,0:T(8,128)S(1)}, u32[]{:S(2)}, u32[]{:S(2)}) collective-permute-start(f32[304,128]{1,0:T(8,128)S(1)} %get-tuple-element.66.refs_0_), channel_id=1, source_target_pairs={{0,16},{8,24},{16,0},{24,8},{1,17},{9,25},{17,1},{25,9},{2,18},{10... | collective-permute-start | bytes 466952 | tf_op jit(solution)/shard_map/ppermute | solution.py:227
  57.7 23.5 %collective-permute-start.18 = (f32[304,128]{1,0:T(8,128)S(1)}, f32[304,128]{1,0:T(8,128)S(1)}, u32[]{:S(2)}, u32[]{:S(2)}) collective-permute-start(f32[304,128]{1,0:T(8,128)S(1)} %get-tuple-element.66.refs_0_), channel_id=1, source_target_pairs={{0,24},{8,0},{16,8},{24,16},{1,25},{9,1},{17,9},{25,17},{2,26},{10... | collective-permute-start | bytes 466952 | tf_op jit(solution)/shard_map/ppermute | solution.py:227
  61.6 19.6 %collective-permute-start.19 = (f32[304,128]{1,0:T(8,128)S(1)}, f32[304,128]{1,0:T(8,128)S(1)}, u32[]{:S(2)}, u32[]{:S(2)}) collective-permute-start(f32[304,128]{1,0:T(8,128)S(1)} %get-tuple-element.66.refs_0_), channel_id=1, source_target_pairs={{0,4},{4,0},{1,5},{5,1},{2,6},{6,2},{3,7},{7,3},{8,12},{12,8},{9,1... | collective-permute-start | bytes 466952 | tf_op jit(solution)/shard_map/ppermute | solution.py:227
  67.6 59.5 %collective-permute-start.24 = (f32[304,512]{1,0:T(8,128)}, f32[304,512]{1,0:T(8,128)S(1)}, u32[]{:S(2)}, u32[]{:S(2)}) collective-permute-start(f32[304,512]{1,0:T(8,128)} %add.6), channel_id=1, source_target_pairs={{0,4},{4,8},{8,12},{12,16},{16,20},{20,24},{24,28},{1,5},{5,9},{9,... | collective-permute-start | bytes 1867784 | tf_op jit(solution)/shard_map/ppermute | solution.py:178
  70.9 56.2 %collective-permute-start.26 = (f32[304,512]{1,0:T(8,128)}, f32[304,512]{1,0:T(8,128)}, u32[]{:S(2)}, u32[]{:S(2)}) collective-permute-start(f32[304,512]{1,0:T(8,128)} %add.7), channel_id=1, source_target_pairs={{0,4},{4,8},{8,12},{12,16},{16,20},{20,24},{24,28},{1,5},{5,9},{9,... | collective-permute-start | bytes 1867784 | tf_op jit(solution)/shard_map/ppermute | solution.py:178
  81.1 11.0 %collective-permute-start.22 = (f32[304,128]{1,0:T(8,128)S(1)}, f32[304,128]{1,0:T(8,128)S(1)}, u32[]{:S(2)}, u32[]{:S(2)}) collective-permute-start(f32[304,128]{1,0:T(8,128)S(1)} %collective-permute-done.18.refs_3_), channel_id=1, source_target_pairs={{0,4},{4,0},{1,5},{5,1},{2,6},{6,2},{3,7},{7,3},{8,12},{12,8},{9,1... | collective-permute-start | bytes 466952 | tf_op jit(solution)/shard_map/ppermute | solution.py:227
  101.9 26.6 %collective-permute-start.28 = (f32[304,512]{1,0:T(8,128)S(1)}, f32[304,512]{1,0:T(8,128)S(1)}, u32[]{:S(2)}, u32[]{:S(2)}) collective-permute-start(f32[304,512]{1,0:T(8,128)S(1)} %get-tuple-element.79), channel_id=1, source_target_pairs={{0,2},{2,0},{1,3},{3,1},{4,6},{6,4},{5,7},{7,5},{8,10},{10,8},{9,1... | collective-permute-start | bytes 1867784 | tf_op jit(solution)/shard_map/ppermute | solution.py:175
  125.4 15.6 %collective-permute-start.27 = (f32[304,512]{1,0:T(8,128)S(1)}, f32[304,512]{1,0:T(8,128)S(1)}, u32[]{:S(2)}, u32[]{:S(2)}) collective-permute-start(f32[304,512]{1,0:T(8,128)S(1)} %bitcast.18), channel_id=1, source_target_pairs={{0,1},{1,0},{2,3},{3,2},{4,5},{5,4},{6,7},{7,6},{8,9},{9,8},{10,11... | collective-permute-start | bytes 1867784 | tf_op jit(solution)/shard_map/ppermute | solution.py:182
  125.6 28.9 %collective-permute-start.30 = (f32[304,512]{1,0:T(8,128)S(1)}, f32[304,512]{1,0:T(8,128)S(1)}, u32[]{:S(2)}, u32[]{:S(2)}) collective-permute-start(f32[304,512]{1,0:T(8,128)S(1)} %bitcast.17), channel_id=1, source_target_pairs={{0,3},{1,2},{2,1},{3,0},{4,7},{5,6},{6,5},{7,4},{8,11},{9,10},{10,... | collective-permute-start | bytes 1867784 | tf_op jit(solution)/shard_map/ppermute | solution.py:188
  128.3 26.2 %collective-permute-start.29 = (f32[304,512]{1,0:T(8,128)S(1)}, f32[304,512]{1,0:T(8,128)S(1)}, u32[]{:S(2)}, u32[]{:S(2)}) collective-permute-start(f32[304,512]{1,0:T(8,128)S(1)} %get-tuple-element.81), channel_id=1, source_target_pairs={{0,2},{2,0},{1,3},{3,1},{4,6},{6,4},{5,7},{7,5},{8,10},{10,8},{9,1... | collective-permute-start | bytes 1867784 | tf_op jit(solution)/shard_map/ppermute | solution.py:175
  (13 other events, 86.5 us)

commit v3 on v2

v3 whole, which is shorter than its diff:
```python
import functools

import jax
import jax.numpy as jnp
from jax import lax
from jax.experimental import pallas as pl
from jax.experimental.pallas import tpu as pltpu
from jax.sharding import Mesh, PartitionSpec as P

F32, BF16 = jnp.float32, jnp.bfloat16
VMEM_LIMIT = 28 * 2**20
SMEM_SPEC = pl.BlockSpec(memory_space=pltpu.SMEM)
VMEM_SPEC = pl.BlockSpec(memory_space=pltpu.VMEM)


def split(values):
    high = values.astype(BF16)
    return high, (values - high.astype(F32)).astype(BF16)


def call(kernel, name, shapes, operands, waits=(), flops=0, size=2**20, aliases=None):
    def body(*refs):
        kernel(*refs[: len(operands)], *refs[len(operands) + len(waits) :])

    return pl.pallas_call(
        body,
        out_shape=shapes,
        in_specs=[SMEM_SPEC] + [VMEM_SPEC] * (len(operands) - 1) + [pl.BlockSpec(memory_space=pl.ANY)] * len(waits),
        out_specs=[VMEM_SPEC] * len(shapes),
        input_output_aliases=aliases or {},
        compiler_params=pltpu.CompilerParams(vmem_limit_bytes=VMEM_LIMIT),
        cost_estimate=pl.CostEstimate(flops=flops, bytes_accessed=size, transcendentals=0),
        name=name,
    )(*operands, *waits)


def spread_kernel(info, own_ref, other_ref, *lag_refs):
    first = info[0] == 0
    half = lag_refs[0].shape[0]
    sensors = own_ref.shape[2]
    for lag, out_ref in enumerate(lag_refs):
        own, other = own_ref[lag], other_ref[lag]
        both = jnp.concatenate([jnp.where(first, own, other), jnp.where(first, other, own)], axis=0).T
        out_ref[...] = jnp.where(first, both[:half], both[sensors - half :])


def halves(info, model_ref, high_ref, low_ref, slot, lines, rows):
    spaces, depth, block = high_ref.shape[1:]
    width = depth // (lines * rows)
    for at in range(lines * rows):
        source = pl.ds(pl.multiple_of(chip_at(at, info, lines, rows) * width, width), width)
        target = slice(at * width, (at + 1) * width)
        for turn in range(spaces):
            columns = pl.ds(pl.multiple_of(lax.rem(info[1] + turn, spaces) * block, block), block)
            high_ref[slot, turn, target], low_ref[slot, turn, target] = split(model_ref[source, columns])


def own_halves_kernel(lines, rows, info, model_ref, far_ref, next_ref, high_ref, low_ref, far_out, next_out):
    far_out[...] = far_ref[...]
    next_out[...] = next_ref[...]
    halves(info, model_ref, high_ref, low_ref, info[0], lines, rows)


def other_halves_kernel(lines, rows, info, model_ref, high_in, low_in, high_ref, low_ref):
    halves(info, model_ref, high_ref, low_ref, 1 - info[0], lines, rows)


def line_shifts(lines):
    return [0] + sorted(range(1, lines), key=lambda shift: (min(shift, lines - shift), shift))


def chip_at(at, info, lines, rows):
    row_off, shift = at // lines, line_shifts(lines)[at % lines]
    return lax.rem(info[2] - shift + lines, lines) * rows + lax.rem(info[3] + row_off, rows)


def fill(blocks, pair_ref):
    half, width = pair_ref.shape[0] // 2, blocks[0].shape[1]
    at = 0
    for block in blocks:
        for start in range(0, block.shape[0], half):
            columns = slice(at * width, (at + 1) * width)
            pair_ref[:half, columns], pair_ref[half:, columns] = split(block[start : start + half])
            at += 1


def join_kernel(info, *refs):
    (*parts, out_ref) = refs
    start = 0
    for part in parts:
        out_ref[start : start + part.shape[0]] = part[...]
        start += part.shape[0]


def times(pair_ref, high_ref, low_ref, slot, turn, put):
    half = pair_ref.shape[0] // 2
    width = high_ref.shape[3]
    step = width if width % 256 else 256
    for start in range(0, width, step):
        columns = slice(start, start + step)
        both = jnp.dot(pair_ref[...], high_ref[slot, turn, :, columns], preferred_element_type=F32)
        low = jnp.dot(pair_ref[:half], low_ref[slot, turn, :, columns], preferred_element_type=F32)
        put(columns, both[:half] + (both[half:] + low))


def lead_two_kernel(info, high, low, next_block, *refs):
    blocks, (pair, send, next_out) = refs[:-3], refs[-3:]
    next_out[...] = next_block[...]
    fill(blocks, pair)
    for turn in range(1, high.shape[1]):

        def put(columns, total):
            send[turn - 1, :, columns] = total

        times(pair, high, low, 1, turn, put)


def rest_two_kernel(info, high, low, pair, keep, other):
    def put_keep(columns, total):
        keep[:, columns] = total

    times(pair, high, low, 1, 0, put_keep)
    for turn in range(high.shape[1]):

        def put(columns, total):
            other[turn, :, columns] = total

        times(pair, high, low, 0, turn, put)


def rest_one_kernel(info, high, low, pair, added, keep1, far, *refs):
    (*from1, keep, other, total1, far_out) = refs
    far_out[...] = far[...]
    total1[...] = functools.reduce(jnp.add, [keep1[...]] + [part[...] for part in from1])

    def put_keep(columns, total):
        keep[:, columns] = total + added[0, :, columns]

    times(pair, high, low, 1, 0, put_keep)
    for turn in range(high.shape[1]):

        def put(columns, total):
            other[turn, :, columns] = total

        times(pair, high, low, 0, turn, put)


def lead_one_kernel(count, info, high, low, added, *refs):
    blocks, next_blocks, (pair, send, next_out) = refs[: -count - 3], refs[-count - 3 : -3], refs[-3:]
    join_kernel(info, *next_blocks, next_out)
    fill(blocks, pair)
    for turn in range(1, high.shape[1]):

        def put(columns, total):
            send[turn - 1, :, columns] = total + added[turn, :, columns]

        times(pair, high, low, 1, turn, put)


def both_times(info, high, low, pair, added, turn, own_put, other_put):
    first = info[0] == 0
    early = {}

    def put_early(columns, total):
        early[columns.start] = total

    def put_late(columns, total):
        late = total + added[turn, :, columns]
        own_put(columns, jnp.where(first, early[columns.start], late))
        other_put(columns, jnp.where(first, late, early[columns.start]))

    times(pair, high, low, 0, turn, put_early)
    times(pair, high, low, 1, turn, put_late)


def lead_zero_kernel(info, high, low, added, *refs):
    blocks, (pair, send, cross) = refs[:-3], refs[-3:]
    fill(blocks, pair)
    for turn in range(1, high.shape[1]):

        def own_put(columns, total):
            send[turn - 1, :, columns] = total

        def other_put(columns, total):
            cross[turn - 1, :, columns] = total

        both_times(info, high, low, pair, added, turn, own_put, other_put)


def last_kernel(info, high, low, pair, added, keep, chip):
    def own_put(columns, total):
        keep[:, columns] = total

    def other_put(columns, total):
        chip[:, columns] = total

    both_times(info, high, low, pair, added, 0, own_put, other_put)


def totals_kernel(info, total1, keep0, *refs):
    (*from0, own_ref, other_ref) = refs
    first = info[0] == 0
    total0 = functools.reduce(jnp.add, [keep0[...]] + [part[...] for part in from0])
    own_ref[...] = jnp.where(first, total0, total1[...])
    other_ref[...] = jnp.where(first, total1[...], total0)


def finish_kernel(spaces, info, d_keep, d_chip, onward, *refs):
    (*parts, out_ref) = refs
    first = info[0] == 0
    sensors, half = out_ref.shape[0], d_keep.shape[0]
    own = d_keep[...] + onward[:half]
    other = d_chip[...] + onward[half:]
    for straight, cross in zip(parts[: spaces - 1], parts[spaces - 1 :]):
        own = own + straight[...]
        other = other + cross[...]
    out_ref[:half, :] = jnp.where(first, own, other)
    out_ref[half:, :] = jnp.where(first, other, own)[2 * half - sensors :, :]


def on_device(model, kernels, lines, rows, spaces):
    core = lax.axis_index("core")
    info = jnp.stack([core, lax.axis_index("space"), lax.axis_index("line"), lax.axis_index("row")]).astype(jnp.int32)
    own_model = model[0]
    depth, columns = own_model.shape
    lags, sensors, width = kernels.shape
    half = -(-sensors // 32) * 16
    block = columns // spaces

    def swap(values):
        return lax.ppermute(values, "core", [(0, 1), (1, 0)])

    def onward(values):
        return lax.ppermute(values, ("line", "row"), [(i, i + 1) for i in range(lines * rows - 1)])

    def over_space(sent):
        return [
            lax.ppermute(sent[d - 1], "space", [(i, (i + d) % spaces) for i in range(spaces)])
            for d in range(1, spaces)
        ]

    def over_space_and_core(sent):
        return [
            lax.ppermute(
                sent[d - 1],
                ("core", "space"),
                [(c * spaces + i, (1 - c) * spaces + (i + d) % spaces) for c in range(2) for i in range(spaces)],
            )
            for d in range(1, spaces)
        ]

    kernels_t = jnp.swapaxes(kernels, 1, 2)
    other_t = swap(kernels_t)
    lag_blocks = call(
        spread_kernel, "spread", [jax.ShapeDtypeStruct((half, 2 * width), F32)] * lags, [info, kernels_t, other_t]
    )

    def shifted(own_block):
        return [own_block] + [
            lax.ppermute(own_block, "line", [(i, (i + shift) % lines) for i in range(lines)])
            for shift in line_shifts(lines)[1:]
        ]

    def handed(blocks):
        return [
            lax.ppermute(values, "row", [(i, (i - off) % rows) for i in range(rows)])
            for off in range(1, rows)
            for values in blocks
        ]

    def joined(blocks, waits):
        shape = jax.ShapeDtypeStruct((half * len(blocks), blocks[0].shape[1]), F32)
        return call(join_kernel, "join", [shape], [info, *blocks], waits=waits)[0]

    pair = jax.ShapeDtypeStruct((2 * half, depth), BF16)
    one = jax.ShapeDtypeStruct((half, block), F32)
    sent = jax.ShapeDtypeStruct((spaces - 1, half, block), F32)
    whole = jax.ShapeDtypeStruct((spaces, half, block), F32)
    flops = 6 * half * depth * block

    line2 = shifted(lag_blocks[2])

    models = [jax.ShapeDtypeStruct((2, spaces, depth, block), BF16)] * 2
    small = jax.ShapeDtypeStruct((half, 2 * width), F32)
    late = min(2, lines - 1)
    high, low, late_block, block1 = call(
        functools.partial(own_halves_kernel, lines, rows),
        "own_halves",
        models + [small] * 2,
        [info, own_model, line2[late], lag_blocks[1]],
        size=1,
    )
    high, low = call(
        functools.partial(other_halves_kernel, lines, rows),
        "other_halves",
        models,
        [info, swap(own_model), high, low],
        size=1,
        aliases={2: 0, 3: 1},
    )
    row2 = handed(line2[:late] + [late_block] + line2[late + 1 :])
    pair2, send1, block0 = call(
        lead_two_kernel,
        "lead2",
        [pair, sent, small],
        [info, high, low, lag_blocks[0], *line2, *row2],
        flops=flops,
    )
    from1 = over_space(send1)
    keep1, early2 = call(rest_two_kernel, "rest2", [one, whole], [info, high, low, pair2], flops=3 * flops)

    line1, line0 = shifted(block1), shifted(block0)
    row1 = handed([joined(line1[:-1] or line1, [send1])] + line1[1:][-1:])
    near = line0[:-1] or line0
    pair1, send0, near0 = call(
        functools.partial(lead_one_kernel, len(near)),
        "lead1",
        [pair, sent, jax.ShapeDtypeStruct((half * len(near), 2 * width), F32)],
        [info, high, low, early2, *line1, *row1, *near],
        waits=from1,
        flops=flops,
    )
    from0 = over_space(send0)
    keep0, early1, total1, far0 = call(
        rest_one_kernel,
        "rest1",
        [one, whole, one, small],
        [info, high, low, pair1, early2, keep1, line0[-1], *from1],
        flops=3 * flops,
    )

    row0 = handed([near0, far0] if lines > 1 else [near0])
    pair0, d_send, d_cross = call(
        lead_zero_kernel, "lead0", [pair, sent, sent], [info, high, low, early1, *line0, *row0], flops=2 * flops
    )
    d_from, d_from_cross = over_space(d_send), over_space_and_core(d_cross)
    next_same, next_cross = call(totals_kernel, "totals", [one, one], [info, total1, keep0, *from0], waits=row0[-1:])
    arrived = onward(joined([next_same, swap(next_cross)], [d_send]))
    d_keep, d_chip = call(last_kernel, "last", [one, one], [info, high, low, pair0, early1], flops=2 * flops)
    (result,) = call(
        functools.partial(finish_kernel, spaces),
        "finish",
        [jax.ShapeDtypeStruct((sensors, block), F32)],
        [info, d_keep, swap(d_chip), arrived, *d_from, *d_from_cross],
    )
    return result[None]


def solution(mesh):
    chips, spaces = mesh.shape["tm"] // 2, mesh.shape["space"]
    rows = 1 if chips % 2 else 2
    lines = chips // rows
    grid = Mesh(mesh.devices.reshape(lines, rows, 2, spaces), ("line", "row", "core", "space"))
    return jax.shard_map(
        functools.partial(on_device, lines=lines, rows=rows, spaces=spaces),
        mesh=grid,
        in_specs=(P(("line", "row", "core"), "space", None), P(None, None, ("space", "line", "row", "core"))),
        out_specs=P(("line", "row", "core"), None, "space"),
        check_vma=False,
    )
```

time: 157 us -> 131 us (0.83)
  the two profiles are of different devices: /device:TPU:19 before, /device:TPU:21 now
where the time goes in v3:
time: 131 us; the launch traced here: 130 us
  waiting for transfers between devices  61.2 us (47%)
  starting transfers between devices  40.8 us (31%)
  Pallas kernels  24.8 us (19%)
  local copies, waits for them, and re-layouts  3.22 us (2%)
    pallas_call x13, Pallas kernels, call(): pl.pallas_call(body, out_shape=shapes, in_specs=[SMEM_SPEC] + [VMEM_SPEC]...  24.8 us
    ppermute x9, waiting for transfers between devices, shifted(): lax.ppermute(own_block, 'line', [(i, (i + shift) % lines) for i in range(...  22.7 us
    ppermute x3, waiting for transfers between devices, over_space(): lax.ppermute(sent[d - 1], 'space', [(i, (i + d) % spaces) for i in range(...  13.9 us
    ppermute x1, waiting for transfers between devices, over_space_and_core(): lax.ppermute(sent[d - 1], ('core', 'space'), [(c * spaces + i, (1 - c) *...  13.5 us
    ppermute x9, starting transfers between devices, shifted(): lax.ppermute(own_block, 'line', [(i, (i + shift) % lines) for i in range(...  11.4 us
    ppermute x1, starting transfers between devices, onward(): lax.ppermute(values, ('line', 'row'), [(i, i + 1) for i in range(lines *...  10.5 us
    ppermute x4, starting transfers between devices, swap(): return lax.ppermute(values, 'core', [(0, 1), (1, 0)])  9.6 us
    ppermute x4, waiting for transfers between devices, swap(): return lax.ppermute(values, 'core', [(0, 1), (1, 0)])  7.28 us
  transfers between devices with their start and end apart: 26, of which 12 were waited for; matrix products, arithmetic and copies ran while one was open for 0% of the time, Pallas kernels for 16%

profile of v3, /device:TPU:21, one launch (start us, length us, event | category | flops | bytes accessed | tf_op | source)
XLA Modules:
  0.0 130.3 jit_solution(10988302741585601301)
XLA Ops:
  0.8 7.3 %collective-permute-done.1.refs_2_ = f32[3,64,600]{2,1,0:T(8,128)S(1)} collective-permute-done((f32[3,64,600]{2,1,0:T(8,128)}, f32[3,64,600]{2,1,0:T(8,128)S(1)}, u32[]{:S(2)}, u32[]{:S(2)}) %collective-permute-start.1) | collective-permute-done | bytes 460832 | tf_op jit(solution)/shard_map/ppermute | solution.py:231
  11.5 1.9 %collective-permute-start.4 = (f32[304,128]{1,0:T(8,128)S(1)}, f32[304,128]{1,0:T(8,128)S(1)}, u32[]{:S(2)}, u32[]{:S(2)}) collective-permute-start(f32[304,128]{1,0:T(8,128)S(1)} %get-tuple-element.33.refs_4_), channel_id=1, source_target_pairs={{0,16},{8,24},{16,0},{24,8},{1,17},{9,25},{17,1},{25,9},{2,18},{10... | collective-permute-start | bytes 466952 | tf_op jit(solution)/shard_map/ppermute | solution.py:260
  13.6 1.9 %collective-permute-done.2.refs_2_.refs_6_ = f32[304,128]{1,0:T(8,128)S(1)} collective-permute-done((f32[304,128]{1,0:T(8,128)S(1)}, f32[304,128]{1,0:T(8,128)S(1)}, u32[]{:S(2)}, u32[]{:S(2)}) %collective-permute-start.2) | collective-permute-done | bytes 155680 | tf_op jit(solution)/shard_map/ppermute | solution.py:260
  15.5 2.2 %copy-done = f32[1,1024,1024]{2,1,0:T(8,128)S(1)} copy-done((f32[1,1024,1024]{2,1,0:T(8,128)S(1)}, f32[1,1024,1024]{2,1,0:T(8,128)}, u32[]{:S(2)}) %copy-start) | copy-done | bytes 4194328
  20.4 3.7 %collective-permute-done.4.refs_7_ = f32[304,128]{1,0:T(8,128)S(1)} collective-permute-done((f32[304,128]{1,0:T(8,128)S(1)}, f32[304,128]{1,0:T(8,128)S(1)}, u32[]{:S(2)}, u32[]{:S(2)}) %collective-permute-start.4) | collective-permute-done | bytes 155680 | tf_op jit(solution)/shard_map/ppermute | solution.py:260
  24.7 2.9 %other_halves.1 = (bf16[2,2,1024,512]{3,2,1,0:T(8,128)(2,1)S(1)}, bf16[2,2,1024,512]{3,2,1,0:T(8,128)(2,1)S(1)}) custom-call(s32[4]{0:T(128)S(1)} %pad_add_fusion.refs_0_, f32[1024,1024]{1,0:T(8,128)} %collective-permute-done.refs_1_, bf16[2,2,1024,512]{3,2,1,0:T(8,128)(2,1)S(1)} %get-tuple-element.35.refs_2_, ...), custom_call_target="tpu_custom_call", output_to_operand_aliasing={{0}: (2, {}), {1}: (3, {})} | custom-call | bytes 1 | tf_op jit(solution)/shard_map/other_halves/pallas_call | solution.py:25
  27.6 2.1 %collective-permute-start.9 = (f32[304,128]{1,0:T(8,128)S(1)}, f32[304,128]{1,0:T(8,128)S(1)}, u32[]{:S(2)}, u32[]{:S(2)}) collective-permute-start(f32[304,128]{1,0:T(8,128)S(1)} %get-tuple-element.43.refs_1_.refs_4_), channel_id=1, source_target_pairs={{0,8},{8,16},{16,24},{24,0},{1,9},{9,17},{17,25},{25,1},{2,10},{10... | collective-permute-start | bytes 466952 | tf_op jit(solution)/shard_map/ppermute | solution.py:260
  33.3 3.0 %collective-permute-done.9.refs_2_.refs_5_ = f32[304,128]{1,0:T(8,128)S(1)} collective-permute-done((f32[304,128]{1,0:T(8,128)S(1)}, f32[304,128]{1,0:T(8,128)S(1)}, u32[]{:S(2)}, u32[]{:S(2)}) %collective-permute-start.9) | collective-permute-done | bytes 155680 | tf_op jit(solution)/shard_map/ppermute | solution.py:260
  39.5 5.7 %collective-permute-done.11.refs_7_ = f32[304,128]{1,0:T(8,128)S(1)} collective-permute-done((f32[304,128]{1,0:T(8,128)S(1)}, f32[304,128]{1,0:T(8,128)S(1)}, u32[]{:S(2)}, u32[]{:S(2)}) %collective-permute-start.11) | collective-permute-done | bytes 155680 | tf_op jit(solution)/shard_map/ppermute | solution.py:260
  45.5 4.2 %collective-permute-start.14 = (f32[304,128]{1,0:T(8,128)S(1)}, f32[304,128]{1,0:T(8,128)S(1)}, u32[]{:S(2)}, u32[]{:S(2)}) collective-permute-start(f32[304,128]{1,0:T(8,128)S(1)} %get-tuple-element.45.refs_10_.refs_4_), channel_id=1, source_target_pairs={{0,8},{8,16},{16,24},{24,0},{1,9},{9,17},{17,25},{25,1},{2,10},{10... | collective-permute-start | bytes 466952 | tf_op jit(solution)/shard_map/ppermute | solution.py:260
  49.6 3.6 %rest2.1 = (f32[304,512]{1,0:T(8,128)S(1)}, f32[2,304,512]{2,1,0:T(8,128)S(1)}) custom-call(s32[4]{0:T(128)S(1)} %pad_add_fusion.refs_0_, bf16[2,2,1024,512]{3,2,1,0:T(8,128)(2,1)S(1)} %get-tuple-element.37.refs_1_, bf16[2,2,1024,512]{3,2,1,0:T(8,128)(2,1)S(1)} %get-tuple-element.38.refs_2_, bf16[608,1024]{1,0:T(8,128)(2,1)S(1)} %get-tuple-element.41.refs_3_), custom_call_target="tpu_custom_call" | custom-call | flops 2868903936 | bytes 1048576 | tf_op jit(solution)/shard_map/rest2/pallas_call | solution.py:25
  53.3 3.2 %collective-permute-done.15.refs_12_.refs_6_ = f32[304,128]{1,0:T(8,128)S(1)} collective-permute-done((f32[304,128]{1,0:T(8,128)S(1)}, f32[304,128]{1,0:T(8,128)S(1)}, u32[]{:S(2)}, u32[]{:S(2)}) %collective-permute-start.15) | collective-permute-done | bytes 155680 | tf_op jit(solution)/shard_map/ppermute | solution.py:260
  56.6 1.7 %lead1.1 = (bf16[608,1024]{1,0:T(8,128)(2,1)S(1)}, f32[1,304,512]{2,1,0:T(8,128)S(1)}, f32[912,128]{1,0:T(8,128)S(1)}) custom-call(s32[4]{0:T(128)S(1)} %pad_add_fusion.refs_0_, bf16[2,2,1024,512]{3,2,1,0:T(8,128)(2,1)S(1)} %get-tuple-element.37.refs_1_, bf16[2,2,1024,512]{3,2,1,0:T(8,128)(2,1)S(1)} %get-tuple-element.38.refs_2_, ...), custom_call_target="tpu_custom_call" | custom-call | flops 956301312 | bytes 1048576 | tf_op jit(solution)/shard_map/lead1/pallas_call | solution.py:25
  59.6 5.1 %collective-permute-done.17.refs_6_.refs_7_ = f32[304,128]{1,0:T(8,128)S(1)} collective-permute-done((f32[304,128]{1,0:T(8,128)S(1)}, f32[304,128]{1,0:T(8,128)S(1)}, u32[]{:S(2)}, u32[]{:S(2)}) %collective-permute-start.17) | collective-permute-done | bytes 155680 | tf_op jit(solution)/shard_map/ppermute | solution.py:260
  64.7 3.7 %rest1.1 = (f32[304,512]{1,0:T(8,128)S(1)}, f32[2,304,512]{2,1,0:T(8,128)S(1)}, f32[304,512]{1,0:T(8,128)S(1)}, f32[304,128]{1,0:T(8,128)S(1)}) custom-call(s32[4]{0:T(128)S(1)} %pad_add_fusion.refs_0_, bf16[2,2,1024,512]{3,2,1,0:T(8,128)(2,1)S(1)} %get-tuple-element.37.refs_1_, bf16[2,2,1024,512]{3,2,1,0:T(8,128)(2,1)S(1)} %get-tuple-element.38.refs_2_, ...), custom_call_target="tpu_custom_call" | custom-call | flops 2868903936 | bytes 1048576 | tf_op jit(solution)/shard_map/rest1/pallas_call | solution.py:25
  69.9 2.9 %collective-permute-done.19.refs_9_.refs_4_ = f32[304,128]{1,0:T(8,128)S(1)} collective-permute-done((f32[304,128]{1,0:T(8,128)S(1)}, f32[304,128]{1,0:T(8,128)S(1)}, u32[]{:S(2)}, u32[]{:S(2)}) %collective-permute-start.19) | collective-permute-done | bytes 155680 | tf_op jit(solution)/shard_map/ppermute | solution.py:266
  73.5 6.3 %collective-permute-start.22 = (f32[304,512]{1,0:T(8,128)S(1)}, f32[304,512]{1,0:T(8,128)S(1)}, u32[]{:S(2)}, u32[]{:S(2)}) collective-permute-start(f32[304,512]{1,0:T(8,128)S(1)} %get-tuple-element.58), channel_id=1, source_target_pairs={{0,2},{2,0},{1,3},{3,1},{4,6},{6,4},{5,7},{7,5},{8,10},{10,8},{9,1... | collective-permute-start | bytes 1867784 | tf_op jit(solution)/shard_map/ppermute | solution.py:231
  80.2 2.7 %lead0.1 = (bf16[608,1024]{1,0:T(8,128)(2,1)S(1)}, f32[1,304,512]{2,1,0:T(8,128)S(1)}, f32[1,304,512]{2,1,0:T(8,128)S(1)}) custom-call(s32[4]{0:T(128)S(1)} %pad_add_fusion.refs_0_, bf16[2,2,1024,512]{3,2,1,0:T(8,128)(2,1)S(1)} %get-tuple-element.37.refs_1_, bf16[2,2,1024,512]{3,2,1,0:T(8,128)(2,1)S(1)} %get-tuple-element.38.refs_2_, ...), custom_call_target="tpu_custom_call" | custom-call | flops 1912602624 | bytes 1048576 | tf_op jit(solution)/shard_map/lead0/pallas_call | solution.py:25
  83.5 10.5 %collective-permute-start.23 = (f32[608,512]{1,0:T(8,128)S(1)}, f32[608,512]{1,0:T(8,128)S(1)}, u32[]{:S(2)}, u32[]{:S(2)}) collective-permute-start(f32[608,512]{1,0:T(8,128)S(1)} %join.3), channel_id=1, source_target_pairs={{0,4},{4,8},{8,12},{12,16},{16,20},{20,24},{24,28},{1,5},{5,9},{9,... | collective-permute-start | bytes 3735560 | tf_op jit(solution)/shard_map/ppermute | solution.py:234
  94.1 2.7 %last.1 = (f32[304,512]{1,0:T(8,128)S(1)}, f32[304,512]{1,0:T(8,128)S(1)}) custom-call(s32[4]{0:T(128)S(1)} %pad_add_fusion.refs_0_, bf16[2,2,1024,512]{3,2,1,0:T(8,128)(2,1)S(1)} %get-tuple-element.37.refs_1_, bf16[2,2,1024,512]{3,2,1,0:T(8,128)(2,1)S(1)} %get-tuple-element.38.refs_2_, bf16[608,1024]{1,0:T(8,128)(2,1)S(1)} %get-tuple-element.51.refs_3_, ...), custom_call_target="tpu_custom_call" | custom-call | flops 1912602624 | bytes 1048576 | tf_op jit(solution)/shard_map/last/pallas_call | solution.py:25
  96.8 2.6 %collective-permute-start.20 = (f32[304,512]{1,0:T(8,128)S(1)}, f32[304,512]{1,0:T(8,128)S(1)}, u32[]{:S(2)}, u32[]{:S(2)}) collective-permute-start(f32[304,512]{1,0:T(8,128)S(1)} %get-tuple-element.53), channel_id=1, source_target_pairs={{0,2},{2,0},{1,3},{3,1},{4,6},{6,4},{5,7},{7,5},{8,10},{10,8},{9,1... | collective-permute-start | bytes 1867784 | tf_op jit(solution)/shard_map/ppermute | solution.py:231
  101.1 13.9 %collective-permute-done.24.refs_4_ = f32[304,512]{1,0:T(8,128)S(1)} collective-permute-done((f32[304,512]{1,0:T(8,128)S(1)}, f32[304,512]{1,0:T(8,128)S(1)}, u32[]{:S(2)}, u32[]{:S(2)}) %collective-permute-start.24) | collective-permute-done | bytes 622624 | tf_op jit(solution)/shard_map/ppermute | solution.py:238
  115.0 13.5 %collective-permute-done.25.refs_5_ = f32[304,512]{1,0:T(8,128)S(1)} collective-permute-done((f32[304,512]{1,0:T(8,128)S(1)}, f32[304,512]{1,0:T(8,128)S(1)}, u32[]{:S(2)}, u32[]{:S(2)}) %collective-permute-start.25) | collective-permute-done | bytes 622624 | tf_op jit(solution)/shard_map/ppermute | solution.py:244
  128.5 1.8 %finish.1 = f32[600,512]{1,0:T(8,128)} custom-call(s32[4]{0:T(128)S(1)} %pad_add_fusion.refs_0_, f32[304,512]{1,0:T(8,128)S(1)} %get-tuple-element.52.refs_1_, f32[304,512]{1,0:T(8,128)S(1)} %collective-permute-done.20.refs_2_, f32[608,512]{1,0:T(8,128)S(1)} %collective-permute-done.23.refs_3_, f32[304,512]{1,0:T(8,128)S(1)} %collective-permute-done.24.refs_4_, ...), custom_call_target="tpu_custom_call" | custom-call | bytes 1048576 | tf_op jit(solution)/shard_map/finish/pallas_call | solution.py:25
  (46 shorter events, 21.0 us)
Async XLA Ops:
  0.0 24.4 %collective-permute-start = (f32[1024,1024]{1,0:T(8,128)}, f32[1024,1024]{1,0:T(8,128)}, u32[]{:S(2)}, u32[]{:S(2)}) collective-permute-start(f32[1024,1024]{1,0:T(8,128)} %bitcast.11), channel_id=1, source_target_pairs={{0,2},{2,0},{1,3},{3,1},{4,6},{6,4},{5,7},{7,5},{8,10},{10,8},{9,1... | collective-permute-start | bytes 12582920 | tf_op jit(solution)/shard_map/ppermute | solution.py:231
  0.7 7.3 %collective-permute-start.1 = (f32[3,64,600]{2,1,0:T(8,128)}, f32[3,64,600]{2,1,0:T(8,128)S(1)}, u32[]{:S(2)}, u32[]{:S(2)}) collective-permute-start(f32[3,64,600]{2,1,0:T(8,128)} %bitcast.15), channel_id=1, source_target_pairs={{0,2},{2,0},{1,3},{3,1},{4,6},{6,4},{5,7},{7,5},{8,10},{10,8},{9,1... | collective-permute-start | bytes 1382408 | tf_op jit(solution)/shard_map/ppermute | solution.py:231
  9.9 5.5 %collective-permute-start.2 = (f32[304,128]{1,0:T(8,128)S(1)}, f32[304,128]{1,0:T(8,128)S(1)}, u32[]{:S(2)}, u32[]{:S(2)}) collective-permute-start(f32[304,128]{1,0:T(8,128)S(1)} %get-tuple-element.33.refs_4_), channel_id=1, source_target_pairs={{0,24},{8,0},{16,8},{24,16},{1,25},{9,1},{17,9},{25,17},{2,26},{10... | collective-permute-start | bytes 466952 | tf_op jit(solution)/shard_map/ppermute | solution.py:260
  10.2 9.0 %collective-permute-start.3 = (f32[304,128]{1,0:T(8,128)S(1)}, f32[304,128]{1,0:T(8,128)S(1)}, u32[]{:S(2)}, u32[]{:S(2)}) collective-permute-start(f32[304,128]{1,0:T(8,128)S(1)} %get-tuple-element.33.refs_4_), channel_id=1, source_target_pairs={{0,8},{8,16},{16,24},{24,0},{1,9},{9,17},{17,25},{25,1},{2,10},{10... | collective-permute-start | bytes 466952 | tf_op jit(solution)/shard_map/ppermute | solution.py:260
  11.5 12.7 %collective-permute-start.4 = (f32[304,128]{1,0:T(8,128)S(1)}, f32[304,128]{1,0:T(8,128)S(1)}, u32[]{:S(2)}, u32[]{:S(2)}) collective-permute-start(f32[304,128]{1,0:T(8,128)S(1)} %get-tuple-element.33.refs_4_), channel_id=1, source_target_pairs={{0,16},{8,24},{16,0},{24,8},{1,17},{9,25},{17,1},{25,9},{2,18},{10... | collective-permute-start | bytes 466952 | tf_op jit(solution)/shard_map/ppermute | solution.py:260
  13.4 14.2 %collective-permute-start.5 = (f32[304,128]{1,0:T(8,128)S(1)}, f32[304,128]{1,0:T(8,128)S(1)}, u32[]{:S(2)}, u32[]{:S(2)}) collective-permute-start(f32[304,128]{1,0:T(8,128)S(1)} %get-tuple-element.33.refs_4_), channel_id=1, source_target_pairs={{0,4},{4,0},{1,5},{5,1},{2,6},{6,2},{3,7},{7,3},{8,12},{12,8},{9,1... | collective-permute-start | bytes 466952 | tf_op jit(solution)/shard_map/ppermute | solution.py:266
  18.9 10.8 %collective-permute-start.7 = (f32[304,128]{1,0:T(8,128)S(1)}, f32[304,128]{1,0:T(8,128)S(1)}, u32[]{:S(2)}, u32[]{:S(2)}) collective-permute-start(f32[304,128]{1,0:T(8,128)S(1)} %get-tuple-element.40), channel_id=1, source_target_pairs={{0,4},{4,0},{1,5},{5,1},{2,6},{6,2},{3,7},{7,3},{8,12},{12,8},{9,1... | collective-permute-start | bytes 466952 | tf_op jit(solution)/shard_map/ppermute | solution.py:266
  19.2 10.5 %collective-permute-start.6 = (f32[304,128]{1,0:T(8,128)S(1)}, f32[304,128]{1,0:T(8,128)S(1)}, u32[]{:S(2)}, u32[]{:S(2)}) collective-permute-start(f32[304,128]{1,0:T(8,128)S(1)} %collective-permute-done.3.refs_5_), channel_id=1, source_target_pairs={{0,4},{4,0},{1,5},{5,1},{2,6},{6,2},{3,7},{7,3},{8,12},{12,8},{9,1... | collective-permute-start | bytes 466952 | tf_op jit(solution)/shard_map/ppermute | solution.py:266
  24.1 6.1 %collective-permute-start.8 = (f32[304,128]{1,0:T(8,128)S(1)}, f32[304,128]{1,0:T(8,128)S(1)}, u32[]{:S(2)}, u32[]{:S(2)}) collective-permute-start(f32[304,128]{1,0:T(8,128)S(1)} %collective-permute-done.4.refs_7_), channel_id=1, source_target_pairs={{0,4},{4,0},{1,5},{5,1},{2,6},{6,2},{3,7},{7,3},{8,12},{12,8},{9,1... | collective-permute-start | bytes 466952 | tf_op jit(solution)/shard_map/ppermute | solution.py:266
  24.4 8.9 %collective-permute-start.10 = (f32[304,128]{1,0:T(8,128)S(1)}, f32[304,128]{1,0:T(8,128)S(1)}, u32[]{:S(2)}, u32[]{:S(2)}) collective-permute-start(f32[304,128]{1,0:T(8,128)S(1)} %get-tuple-element.43.refs_1_.refs_4_), channel_id=1, source_target_pairs={{0,24},{8,0},{16,8},{24,16},{1,25},{9,1},{17,9},{25,17},{2,26},{10... | collective-permute-start | bytes 466952 | tf_op jit(solution)/shard_map/ppermute | solution.py:260
  27.6 8.7 %collective-permute-start.9 = (f32[304,128]{1,0:T(8,128)S(1)}, f32[304,128]{1,0:T(8,128)S(1)}, u32[]{:S(2)}, u32[]{:S(2)}) collective-permute-start(f32[304,128]{1,0:T(8,128)S(1)} %get-tuple-element.43.refs_1_.refs_4_), channel_id=1, source_target_pairs={{0,8},{8,16},{16,24},{24,0},{1,9},{9,17},{17,25},{25,1},{2,10},{10... | collective-permute-start | bytes 466952 | tf_op jit(solution)/shard_map/ppermute | solution.py:260
  32.0 24.6 %collective-permute-start.16 = (f32[304,512]{1,0:T(8,128)S(1)}, f32[304,512]{1,0:T(8,128)S(1)}, u32[]{:S(2)}, u32[]{:S(2)}) collective-permute-start(f32[304,512]{1,0:T(8,128)S(1)} %bitcast.14), channel_id=1, source_target_pairs={{0,1},{1,0},{2,3},{3,2},{4,5},{5,4},{6,7},{7,6},{8,9},{9,8},{10,11... | collective-permute-start | bytes 1867784 | tf_op jit(solution)/shard_map/ppermute | solution.py:238
  36.9 19.7 %collective-permute-start.12 = (f32[912,128]{1,0:T(8,128)S(1)}, f32[912,128]{1,0:T(8,128)S(1)}, u32[]{:S(2)}, u32[]{:S(2)}) collective-permute-start(f32[912,128]{1,0:T(8,128)S(1)} %join.2), channel_id=1, source_target_pairs={{0,4},{4,0},{1,5},{5,1},{2,6},{6,2},{3,7},{7,3},{8,12},{12,8},{9,1... | collective-permute-start | bytes 1400840 | tf_op jit(solution)/shard_map/ppermute | solution.py:266
  38.2 7.1 %collective-permute-start.11 = (f32[304,128]{1,0:T(8,128)S(1)}, f32[304,128]{1,0:T(8,128)S(1)}, u32[]{:S(2)}, u32[]{:S(2)}) collective-permute-start(f32[304,128]{1,0:T(8,128)S(1)} %get-tuple-element.43.refs_1_.refs_4_), channel_id=1, source_target_pairs={{0,16},{8,24},{16,0},{24,8},{1,17},{9,25},{17,1},{25,9},{2,18},{10... | collective-permute-start | bytes 466952 | tf_op jit(solution)/shard_map/ppermute | solution.py:260
  45.3 8.0 %collective-permute-start.13 = (f32[304,128]{1,0:T(8,128)S(1)}, f32[304,128]{1,0:T(8,128)S(1)}, u32[]{:S(2)}, u32[]{:S(2)}) collective-permute-start(f32[304,128]{1,0:T(8,128)S(1)} %collective-permute-done.11.refs_7_), channel_id=1, source_target_pairs={{0,4},{4,0},{1,5},{5,1},{2,6},{6,2},{3,7},{7,3},{8,12},{12,8},{9,1... | collective-permute-start | bytes 466952 | tf_op jit(solution)/shard_map/ppermute | solution.py:266
  45.5 7.8 %collective-permute-start.14 = (f32[304,128]{1,0:T(8,128)S(1)}, f32[304,128]{1,0:T(8,128)S(1)}, u32[]{:S(2)}, u32[]{:S(2)}) collective-permute-start(f32[304,128]{1,0:T(8,128)S(1)} %get-tuple-element.45.refs_10_.refs_4_), channel_id=1, source_target_pairs={{0,8},{8,16},{16,24},{24,0},{1,9},{9,17},{17,25},{25,1},{2,10},{10... | collective-permute-start | bytes 466952 | tf_op jit(solution)/shard_map/ppermute | solution.py:260
  49.6 6.9 %collective-permute-start.15 = (f32[304,128]{1,0:T(8,128)S(1)}, f32[304,128]{1,0:T(8,128)S(1)}, u32[]{:S(2)}, u32[]{:S(2)}) collective-permute-start(f32[304,128]{1,0:T(8,128)S(1)} %get-tuple-element.45.refs_10_.refs_4_), channel_id=1, source_target_pairs={{0,24},{8,0},{16,8},{24,16},{1,25},{9,1},{17,9},{25,17},{2,26},{10... | collective-permute-start | bytes 466952 | tf_op jit(solution)/shard_map/ppermute | solution.py:260
  58.3 14.5 %collective-permute-start.21 = (f32[304,512]{1,0:T(8,128)S(1)}, f32[304,512]{1,0:T(8,128)S(1)}, u32[]{:S(2)}, u32[]{:S(2)}) collective-permute-start(f32[304,512]{1,0:T(8,128)S(1)} %bitcast.18), channel_id=1, source_target_pairs={{0,1},{1,0},{2,3},{3,2},{4,5},{5,4},{6,7},{7,6},{8,9},{9,8},{10,11... | collective-permute-start | bytes 1867784 | tf_op jit(solution)/shard_map/ppermute | solution.py:238
  59.6 5.1 %collective-permute-start.17 = (f32[304,128]{1,0:T(8,128)S(1)}, f32[304,128]{1,0:T(8,128)S(1)}, u32[]{:S(2)}, u32[]{:S(2)}) collective-permute-start(f32[304,128]{1,0:T(8,128)S(1)} %get-tuple-element.45.refs_10_.refs_4_), channel_id=1, source_target_pairs={{0,16},{8,24},{16,0},{24,8},{1,17},{9,25},{17,1},{25,9},{2,18},{10... | collective-permute-start | bytes 466952 | tf_op jit(solution)/shard_map/ppermute | solution.py:260
  69.6 10.6 %collective-permute-start.18 = (f32[912,128]{1,0:T(8,128)S(1)}, f32[912,128]{1,0:T(8,128)S(1)}, u32[]{:S(2)}, u32[]{:S(2)}) collective-permute-start(f32[912,128]{1,0:T(8,128)S(1)} %get-tuple-element.49), channel_id=1, source_target_pairs={{0,4},{4,0},{1,5},{5,1},{2,6},{6,2},{3,7},{7,3},{8,12},{12,8},{9,1... | collective-permute-start | bytes 1400840 | tf_op jit(solution)/shard_map/ppermute | solution.py:266
  73.5 9.4 %collective-permute-start.22 = (f32[304,512]{1,0:T(8,128)S(1)}, f32[304,512]{1,0:T(8,128)S(1)}, u32[]{:S(2)}, u32[]{:S(2)}) collective-permute-start(f32[304,512]{1,0:T(8,128)S(1)} %get-tuple-element.58), channel_id=1, source_target_pairs={{0,2},{2,0},{1,3},{3,1},{4,6},{6,4},{5,7},{7,5},{8,10},{10,8},{9,1... | collective-permute-start | bytes 1867784 | tf_op jit(solution)/shard_map/ppermute | solution.py:231
  83.5 44.9 %collective-permute-start.23 = (f32[608,512]{1,0:T(8,128)S(1)}, f32[608,512]{1,0:T(8,128)S(1)}, u32[]{:S(2)}, u32[]{:S(2)}) collective-permute-start(f32[608,512]{1,0:T(8,128)S(1)} %join.3), channel_id=1, source_target_pairs={{0,4},{4,8},{8,12},{12,16},{16,20},{20,24},{24,28},{1,5},{5,9},{9,... | collective-permute-start | bytes 3735560 | tf_op jit(solution)/shard_map/ppermute | solution.py:234
  99.3 15.6 %collective-permute-start.24 = (f32[304,512]{1,0:T(8,128)S(1)}, f32[304,512]{1,0:T(8,128)S(1)}, u32[]{:S(2)}, u32[]{:S(2)}) collective-permute-start(f32[304,512]{1,0:T(8,128)S(1)} %bitcast.13), channel_id=1, source_target_pairs={{0,1},{1,0},{2,3},{3,2},{4,5},{5,4},{6,7},{7,6},{8,9},{9,8},{10,11... | collective-permute-start | bytes 1867784 | tf_op jit(solution)/shard_map/ppermute | solution.py:238
  99.6 28.8 %collective-permute-start.25 = (f32[304,512]{1,0:T(8,128)S(1)}, f32[304,512]{1,0:T(8,128)S(1)}, u32[]{:S(2)}, u32[]{:S(2)}) collective-permute-start(f32[304,512]{1,0:T(8,128)S(1)} %bitcast.17), channel_id=1, source_target_pairs={{0,3},{1,2},{2,1},{3,0},{4,7},{5,6},{6,5},{7,4},{8,11},{9,10},{10,... | collective-permute-start | bytes 1867784 | tf_op jit(solution)/shard_map/ppermute | solution.py:244
  (4 other events, 12.0 us)

commit v4 on v3

--- a/solution.py
+++ b/solution.py
@@ -18,15 +18,19 @@
     return high, (values - high.astype(F32)).astype(BF16)
 
 
-def call(kernel, name, shapes, operands, waits=(), flops=0, size=2**20, aliases=None):
+def call(kernel, name, shapes, operands, waits=(), flops=0, size=2**20, aliases=None, outside=(), scratch=()):
     def body(*refs):
         kernel(*refs[: len(operands)], *refs[len(operands) + len(waits) :])
+
+    anywhere = pl.BlockSpec(memory_space=pl.ANY)
+    specs = [SMEM_SPEC] + [pl.BlockSpec(memory_space=pltpu.HBM) if at in outside else VMEM_SPEC for at in range(1, len(operands))]
 
     return pl.pallas_call(
         body,
         out_shape=shapes,
-        in_specs=[SMEM_SPEC] + [VMEM_SPEC] * (len(operands) - 1) + [pl.BlockSpec(memory_space=pl.ANY)] * len(waits),
+        in_specs=specs + [anywhere] * len(waits),
         out_specs=[VMEM_SPEC] * len(shapes),
+        scratch_shapes=list(scratch),
         input_output_aliases=aliases or {},
         compiler_params=pltpu.CompilerParams(vmem_limit_bytes=VMEM_LIMIT),
         cost_estimate=pl.CostEstimate(flops=flops, bytes_accessed=size, transcendentals=0),
@@ -34,7 +38,16 @@
     )(*operands, *waits)
 
 
-def spread_kernel(info, own_ref, other_ref, *lag_refs):
+def stage_kernel(info, source_ref, out_ref, done):
+    copy = pltpu.make_async_copy(source_ref, out_ref, done)
+    copy.start()
+    copy.wait()
+
+
+def spread_kernel(info, own_ref, other_ref, model_ref, *refs):
+    (*lag_refs, model_out, done) = refs
+    copy = pltpu.make_async_copy(model_ref, model_out, done)
+    copy.start()
     first = info[0] == 0
     half = lag_refs[0].shape[0]
     sensors = own_ref.shape[2]
@@ -42,6 +55,7 @@
         own, other = own_ref[lag], other_ref[lag]
         both = jnp.concatenate([jnp.where(first, own, other), jnp.where(first, other, own)], axis=0).T
         out_ref[...] = jnp.where(first, both[:half], both[sensors - half :])
+    copy.wait()
 
 
 def halves(info, model_ref, high_ref, low_ref, slot, lines, rows):
@@ -65,23 +79,28 @@
     halves(info, model_ref, high_ref, low_ref, 1 - info[0], lines, rows)
 
 
-def line_shifts(lines):
+def near_first(lines):
     return [0] + sorted(range(1, lines), key=lambda shift: (min(shift, lines - shift), shift))
 
 
+def far_first(lines):
+    return [0] + near_first(lines)[:0:-1]
+
+
 def chip_at(at, info, lines, rows):
-    row_off, shift = at // lines, line_shifts(lines)[at % lines]
+    row_off, shift = at // lines, at % lines
     return lax.rem(info[2] - shift + lines, lines) * rows + lax.rem(info[3] + row_off, rows)
 
 
-def fill(blocks, pair_ref):
+def fill(blocks, shifts, pair_ref):
     half, width = pair_ref.shape[0] // 2, blocks[0].shape[1]
-    at = 0
+    count = 0
     for block in blocks:
         for start in range(0, block.shape[0], half):
+            at = count // len(shifts) * len(shifts) + shifts[count % len(shifts)]
             columns = slice(at * width, (at + 1) * width)
             pair_ref[:half, columns], pair_ref[half:, columns] = split(block[start : start + half])
-            at += 1
+            count += 1
 
 
 def join_kernel(info, *refs):
@@ -103,10 +122,10 @@
         put(columns, both[:half] + (both[half:] + low))
 
 
-def lead_two_kernel(info, high, low, next_block, *refs):
+def lead_two_kernel(shifts, info, high, low, next_block, *refs):
     blocks, (pair, send, next_out) = refs[:-3], refs[-3:]
     next_out[...] = next_block[...]
-    fill(blocks, pair)
+    fill(blocks, shifts, pair)
     for turn in range(1, high.shape[1]):
 
         def put(columns, total):
@@ -128,9 +147,8 @@
         times(pair, high, low, 0, turn, put)
 
 
-def rest_one_kernel(info, high, low, pair, added, keep1, far, *refs):
-    (*from1, keep, other, total1, far_out) = refs
-    far_out[...] = far[...]
+def rest_one_kernel(info, high, low, pair, added, keep1, *refs):
+    (*from1, keep, other, total1) = refs
     total1[...] = functools.reduce(jnp.add, [keep1[...]] + [part[...] for part in from1])
 
     def put_keep(columns, total):
@@ -145,10 +163,12 @@
         times(pair, high, low, 0, turn, put)
 
 
-def lead_one_kernel(count, info, high, low, added, *refs):
-    blocks, next_blocks, (pair, send, next_out) = refs[: -count - 3], refs[-count - 3 : -3], refs[-3:]
-    join_kernel(info, *next_blocks, next_out)
-    fill(blocks, pair)
+def lead_one_kernel(shifts, count, info, high, low, added, *refs):
+    if count:
+        (*refs, next_out) = refs
+        join_kernel(info, *refs[-count - 2 : -2], next_out)
+    blocks, (pair, send) = refs[: len(refs) - count - 2], refs[-2:]
+    fill(blocks, shifts, pair)
     for turn in range(1, high.shape[1]):
 
         def put(columns, total):
@@ -173,9 +193,9 @@
     times(pair, high, low, 1, turn, put_late)
 
 
-def lead_zero_kernel(info, high, low, added, *refs):
-    blocks, (pair, send, cross) = refs[:-3], refs[-3:]
-    fill(blocks, pair)
+def lead_zero_kernel(shifts, info, high, low, added, *refs):
+    blocks, (pair, send, cross, chip) = refs[:-4], refs[-4:]
+    fill(blocks, shifts, pair)
     for turn in range(1, high.shape[1]):
 
         def own_put(columns, total):
@@ -185,16 +205,21 @@
             cross[turn - 1, :, columns] = total
 
         both_times(info, high, low, pair, added, turn, own_put, other_put)
-
-
-def last_kernel(info, high, low, pair, added, keep, chip):
-    def own_put(columns, total):
-        keep[:, columns] = total
-
-    def other_put(columns, total):
-        chip[:, columns] = total
-
-    both_times(info, high, low, pair, added, 0, own_put, other_put)
+    later = jnp.where(info[0] == 0, 1.0, 0.0)
+
+    def put(columns, total):
+        chip[:, columns] = total + later * added[0, :, columns]
+
+    times(pair, high, low, 1 - info[0], 0, put)
+
+
+def last_kernel(info, high, low, pair, added, keep):
+    later = jnp.where(info[0] == 0, 0.0, 1.0)
+
+    def put(columns, total):
+        keep[:, columns] = total + later * added[0, :, columns]
+
+    times(pair, high, low, info[0], 0, put)
 
 
 def totals_kernel(info, total1, keep0, *refs):
@@ -205,12 +230,12 @@
     other_ref[...] = jnp.where(first, total1[...], total0)
 
 
-def finish_kernel(spaces, info, d_keep, d_chip, onward, *refs):
+def finish_kernel(spaces, info, d_keep, d_chip, next_own, next_other, *refs):
     (*parts, out_ref) = refs
     first = info[0] == 0
     sensors, half = out_ref.shape[0], d_keep.shape[0]
-    own = d_keep[...] + onward[:half]
-    other = d_chip[...] + onward[half:]
+    own = d_keep[...] + next_own[...]
+    other = d_chip[...] + next_other[...]
     for straight, cross in zip(parts[: spaces - 1], parts[spaces - 1 :]):
         own = own + straight[...]
         other = other + cross[...]
@@ -250,15 +275,28 @@
         ]
 
     kernels_t = jnp.swapaxes(kernels, 1, 2)
-    other_t = swap(kernels_t)
-    lag_blocks = call(
-        spread_kernel, "spread", [jax.ShapeDtypeStruct((half, 2 * width), F32)] * lags, [info, kernels_t, other_t]
-    )
-
-    def shifted(own_block):
+    copied = pltpu.SemaphoreType.DMA
+    (own_t,) = call(
+        stage_kernel,
+        "stage",
+        [jax.ShapeDtypeStruct(kernels_t.shape, F32)],
+        [info, kernels_t],
+        outside=[1],
+        scratch=[copied],
+    )
+    small = jax.ShapeDtypeStruct((half, 2 * width), F32)
+    *lag_blocks, staged = call(
+        spread_kernel,
+        "spread",
+        [small] * lags + [jax.ShapeDtypeStruct(own_model.shape, F32)],
+        [info, own_t, swap(kernels_t), own_model],
+        outside=[3],
+        scratch=[copied],
+    )
+
+    def shifted(own_block, shifts):
         return [own_block] + [
-            lax.ppermute(own_block, "line", [(i, (i + shift) % lines) for i in range(lines)])
-            for shift in line_shifts(lines)[1:]
+            lax.ppermute(own_block, "line", [(i, (i + shift) % lines) for i in range(lines)]) for shift in shifts[1:]
         ]
 
     def handed(blocks):
@@ -278,70 +316,79 @@
     whole = jax.ShapeDtypeStruct((spaces, half, block), F32)
     flops = 6 * half * depth * block
 
-    line2 = shifted(lag_blocks[2])
+    orders = near_first(lines), far_first(lines)
+    line2 = shifted(lag_blocks[2], orders[0])
 
     models = [jax.ShapeDtypeStruct((2, spaces, depth, block), BF16)] * 2
-    small = jax.ShapeDtypeStruct((half, 2 * width), F32)
     late = min(2, lines - 1)
     high, low, late_block, block1 = call(
         functools.partial(own_halves_kernel, lines, rows),
         "own_halves",
         models + [small] * 2,
-        [info, own_model, line2[late], lag_blocks[1]],
+        [info, staged, line2[late], lag_blocks[1]],
         size=1,
     )
     high, low = call(
         functools.partial(other_halves_kernel, lines, rows),
         "other_halves",
         models,
-        [info, swap(own_model), high, low],
+        [info, swap(staged), high, low],
         size=1,
         aliases={2: 0, 3: 1},
     )
     row2 = handed(line2[:late] + [late_block] + line2[late + 1 :])
+    line1 = shifted(block1, orders[1])
     pair2, send1, block0 = call(
-        lead_two_kernel,
+        functools.partial(lead_two_kernel, orders[0]),
         "lead2",
         [pair, sent, small],
         [info, high, low, lag_blocks[0], *line2, *row2],
+        waits=line1[1:2],
         flops=flops,
     )
     from1 = over_space(send1)
     keep1, early2 = call(rest_two_kernel, "rest2", [one, whole], [info, high, low, pair2], flops=3 * flops)
 
-    line1, line0 = shifted(block1), shifted(block0)
-    row1 = handed([joined(line1[:-1] or line1, [send1])] + line1[1:][-1:])
-    near = line0[:-1] or line0
-    pair1, send0, near0 = call(
-        functools.partial(lead_one_kernel, len(near)),
+    line0 = shifted(block0, orders[1])
+
+    def parts(line):
+        return [part for part in (line[:1], line[1:-1], line[1:][-1:]) if part]
+
+    row1 = handed([part[0] if len(part) == 1 else joined(part, [send1]) for part in parts(line1)])
+    between = line0[1:-1]
+    pair1, send0, *near0 = call(
+        functools.partial(lead_one_kernel, orders[1], len(between)),
         "lead1",
-        [pair, sent, jax.ShapeDtypeStruct((half * len(near), 2 * width), F32)],
-        [info, high, low, early2, *line1, *row1, *near],
+        [pair, sent] + [jax.ShapeDtypeStruct((half * len(between), 2 * width), F32)] * bool(between),
+        [info, high, low, early2, *line1, *row1, *between],
         waits=from1,
         flops=flops,
     )
     from0 = over_space(send0)
-    keep0, early1, total1, far0 = call(
+    row0 = handed(line0[:1] + near0 + line0[1:][-1:])
+    keep0, early1, total1 = call(
         rest_one_kernel,
         "rest1",
-        [one, whole, one, small],
-        [info, high, low, pair1, early2, keep1, line0[-1], *from1],
+        [one, whole, one],
+        [info, high, low, pair1, early2, keep1, *from1],
+        waits=row0[:2],
         flops=3 * flops,
     )
-
-    row0 = handed([near0, far0] if lines > 1 else [near0])
-    pair0, d_send, d_cross = call(
-        lead_zero_kernel, "lead0", [pair, sent, sent], [info, high, low, early1, *line0, *row0], flops=2 * flops
+    pair0, d_send, d_cross, d_chip = call(
+        functools.partial(lead_zero_kernel, orders[1]),
+        "lead0",
+        [pair, sent, sent, one],
+        [info, high, low, early1, *line0, *row0],
+        flops=3 * flops,
     )
     d_from, d_from_cross = over_space(d_send), over_space_and_core(d_cross)
     next_same, next_cross = call(totals_kernel, "totals", [one, one], [info, total1, keep0, *from0], waits=row0[-1:])
-    arrived = onward(joined([next_same, swap(next_cross)], [d_send]))
-    d_keep, d_chip = call(last_kernel, "last", [one, one], [info, high, low, pair0, early1], flops=2 * flops)
+    (d_keep,) = call(last_kernel, "last", [one], [info, high, low, pair0, early1], flops=flops)
     (result,) = call(
         functools.partial(finish_kernel, spaces),
         "finish",
         [jax.ShapeDtypeStruct((sensors, block), F32)],
-        [info, d_keep, swap(d_chip), arrived, *d_from, *d_from_cross],
+        [info, d_keep, swap(d_chip), onward(next_same), onward(swap(next_cross)), *d_from, *d_from_cross],
     )
     return result[None]
 

time: 131 us -> 115 us (0.88)
  the two profiles are of different devices: /device:TPU:21 before, /device:TPU:0 now
where the time goes in v4:
time: 115 us; the launch traced here: 113 us
  waiting for transfers between devices  43.6 us (38%)
  starting transfers between devices  42.4 us (37%)
  Pallas kernels  23.5 us (20%)
  local copies, waits for them, and re-layouts  3.21 us (3%)
    pallas_call x13, Pallas kernels, call(): pl.pallas_call(body, out_shape=shapes, in_specs=specs + [anywhere] * len(...  23.5 us
    ppermute x9, waiting for transfers between devices, shifted(): lax.ppermute(own_block, 'line', [(i, (i + shift) % lines) for i in range(...  18.6 us
    ppermute x9, starting transfers between devices, shifted(): lax.ppermute(own_block, 'line', [(i, (i + shift) % lines) for i in range(...  15.1 us
    ppermute x10, starting transfers between devices, handed(): lax.ppermute(values, 'row', [(i, (i - off) % rows) for i in range(rows)])  14.6 us
    ppermute x1, waiting for transfers between devices, over_space_and_core(): lax.ppermute(sent[d - 1], ('core', 'space'), [(c * spaces + i, (1 - c) *...  11.6 us
    ppermute x2, starting transfers between devices, onward(): lax.ppermute(values, ('line', 'row'), [(i, i + 1) for i in range(lines *...  7.82 us
    ppermute x3, waiting for transfers between devices, over_space(): lax.ppermute(sent[d - 1], 'space', [(i, (i + d) % spaces) for i in range(...  5.86 us
    ppermute x10, waiting for transfers between devices, handed(): lax.ppermute(values, 'row', [(i, (i - off) % rows) for i in range(rows)])  4.07 us
  transfers between devices with their start and end apart: 29, of which 14 were waited for; matrix products, arithmetic and copies ran while one was open for 0% of the time, Pallas kernels for 15%

profile of v4, /device:TPU:0, one launch (start us, length us, event | category | flops | bytes accessed | tf_op | source)
XLA Modules:
  0.0 113.1 jit_solution(2012678157185073493)
XLA Ops:
  2.5 2.2 %copy-done = f32[1,1024,1024]{2,1,0:T(8,128)S(1)} copy-done((f32[1,1024,1024]{2,1,0:T(8,128)S(1)}, f32[1,1024,1024]{2,1,0:T(8,128)}, u32[]{:S(2)}) %copy-start) | copy-done | bytes 4194328
  6.0 5.0 %collective-permute-start.2 = (f32[304,128]{1,0:T(8,128)S(1)}, f32[304,128]{1,0:T(8,128)S(1)}, u32[]{:S(2)}, u32[]{:S(2)}) collective-permute-start(f32[304,128]{1,0:T(8,128)S(1)} %get-tuple-element.33.refs_4_), channel_id=1, source_target_pairs={{0,24},{8,0},{16,8},{24,16},{1,25},{9,1},{17,9},{25,17},{2,26},{10... | collective-permute-start | bytes 466952 | tf_op jit(solution)/shard_map/ppermute | solution.py:299
  13.5 1.9 %collective-permute-done.2.refs_2_.refs_6_ = f32[304,128]{1,0:T(8,128)S(1)} collective-permute-done((f32[304,128]{1,0:T(8,128)S(1)}, f32[304,128]{1,0:T(8,128)S(1)}, u32[]{:S(2)}, u32[]{:S(2)}) %collective-permute-start.2) | collective-permute-done | bytes 155680 | tf_op jit(solution)/shard_map/ppermute | solution.py:299
  21.0 7.8 %collective-permute-done.4.refs_7_ = f32[304,128]{1,0:T(8,128)S(1)} collective-permute-done((f32[304,128]{1,0:T(8,128)S(1)}, f32[304,128]{1,0:T(8,128)S(1)}, u32[]{:S(2)}, u32[]{:S(2)}) %collective-permute-start.4) | collective-permute-done | bytes 155680 | tf_op jit(solution)/shard_map/ppermute | solution.py:299
  32.0 1.9 %collective-permute-done.6.refs_9_ = f32[304,128]{1,0:T(8,128)S(1)} collective-permute-done((f32[304,128]{1,0:T(8,128)S(1)}, f32[304,128]{1,0:T(8,128)S(1)}, u32[]{:S(2)}, u32[]{:S(2)}) %collective-permute-start.6) | collective-permute-done | bytes 155680 | tf_op jit(solution)/shard_map/ppermute | solution.py:304
  33.9 1.7 %collective-permute-done.8.refs_11_ = f32[304,128]{1,0:T(8,128)S(1)} collective-permute-done((f32[304,128]{1,0:T(8,128)S(1)}, f32[304,128]{1,0:T(8,128)S(1)}, u32[]{:S(2)}, u32[]{:S(2)}) %collective-permute-start.8) | collective-permute-done | bytes 155680 | tf_op jit(solution)/shard_map/ppermute | solution.py:304
  35.6 1.7 %lead2.1 = (bf16[608,1024]{1,0:T(8,128)(2,1)S(1)}, f32[1,304,512]{2,1,0:T(8,128)S(1)}, f32[304,128]{1,0:T(8,128)S(1)}) custom-call(s32[4]{0:T(128)S(1)} %pad_add_fusion.refs_0_, bf16[2,2,1024,512]{3,2,1,0:T(8,128)(2,1)S(1)} %get-tuple-element.37.refs_1_, bf16[2,2,1024,512]{3,2,1,0:T(8,128)(2,1)S(1)} %get-tuple-element.38.refs_2_, ...), custom_call_target="tpu_custom_call" | custom-call | flops 956301312 | bytes 1048576 | tf_op jit(solution)/shard_map/lead2/pallas_call | solution.py:28
  38.9 3.0 %collective-permute-start.10 = (f32[304,128]{1,0:T(8,128)S(1)}, f32[304,128]{1,0:T(8,128)S(1)}, u32[]{:S(2)}, u32[]{:S(2)}) collective-permute-start(f32[304,128]{1,0:T(8,128)S(1)} %get-tuple-element.41.refs_4_), channel_id=1, source_target_pairs={{0,24},{8,0},{16,8},{24,16},{1,25},{9,1},{17,9},{25,17},{2,26},{10... | collective-permute-start | bytes 466952 | tf_op jit(solution)/shard_map/ppermute | solution.py:299
  43.4 2.4 %collective-permute-done.10.refs_2_.refs_6_ = f32[304,128]{1,0:T(8,128)S(1)} collective-permute-done((f32[304,128]{1,0:T(8,128)S(1)}, f32[304,128]{1,0:T(8,128)S(1)}, u32[]{:S(2)}, u32[]{:S(2)}) %collective-permute-start.10) | collective-permute-done | bytes 155680 | tf_op jit(solution)/shard_map/ppermute | solution.py:299
  49.1 2.8 %collective-permute-start.14 = (f32[304,128]{1,0:T(8,128)S(1)}, f32[304,128]{1,0:T(8,128)S(1)}, u32[]{:S(2)}, u32[]{:S(2)}) collective-permute-start(f32[304,128]{1,0:T(8,128)S(1)} %collective-permute-done.11.refs_7_), channel_id=1, source_target_pairs={{0,4},{4,0},{1,5},{5,1},{2,6},{6,2},{3,7},{7,3},{8,12},{12,8},{9,1... | collective-permute-start | bytes 466952 | tf_op jit(solution)/shard_map/ppermute | solution.py:304
  53.4 3.6 %rest2.1 = (f32[304,512]{1,0:T(8,128)S(1)}, f32[2,304,512]{2,1,0:T(8,128)S(1)}) custom-call(s32[4]{0:T(128)S(1)} %pad_add_fusion.refs_0_, bf16[2,2,1024,512]{3,2,1,0:T(8,128)(2,1)S(1)} %get-tuple-element.37.refs_1_, bf16[2,2,1024,512]{3,2,1,0:T(8,128)(2,1)S(1)} %get-tuple-element.38.refs_2_, bf16[608,1024]{1,0:T(8,128)(2,1)S(1)} %get-tuple-element.42.refs_3_), custom_call_target="tpu_custom_call" | custom-call | flops 2868903936 | bytes 1048576 | tf_op jit(solution)/shard_map/rest2/pallas_call | solution.py:28
  58.8 1.7 %lead1.1 = (bf16[608,1024]{1,0:T(8,128)(2,1)S(1)}, f32[1,304,512]{2,1,0:T(8,128)S(1)}, f32[608,128]{1,0:T(8,128)S(1)}) custom-call(s32[4]{0:T(128)S(1)} %pad_add_fusion.refs_0_, bf16[2,2,1024,512]{3,2,1,0:T(8,128)(2,1)S(1)} %get-tuple-element.37.refs_1_, bf16[2,2,1024,512]{3,2,1,0:T(8,128)(2,1)S(1)} %get-tuple-element.38.refs_2_, ...), custom_call_target="tpu_custom_call" | custom-call | flops 956301312 | bytes 1048576 | tf_op jit(solution)/shard_map/lead1/pallas_call | solution.py:28
  61.2 3.4 %collective-permute-start.20 = (f32[304,128]{1,0:T(8,128)S(1)}, f32[304,128]{1,0:T(8,128)S(1)}, u32[]{:S(2)}, u32[]{:S(2)}) collective-permute-start(f32[304,128]{1,0:T(8,128)S(1)} %get-tuple-element.45.refs_4_), channel_id=1, source_target_pairs={{0,8},{8,16},{16,24},{24,0},{1,9},{9,17},{17,25},{25,1},{2,10},{10... | collective-permute-start | bytes 466952 | tf_op jit(solution)/shard_map/ppermute | solution.py:299
  66.1 2.1 %collective-permute-done.20.refs_7_ = f32[304,128]{1,0:T(8,128)S(1)} collective-permute-done((f32[304,128]{1,0:T(8,128)S(1)}, f32[304,128]{1,0:T(8,128)S(1)}, u32[]{:S(2)}, u32[]{:S(2)}) %collective-permute-start.20) | collective-permute-done | bytes 155680 | tf_op jit(solution)/shard_map/ppermute | solution.py:299
  68.2 2.0 %collective-permute-start.21 = (f32[304,128]{1,0:T(8,128)S(1)}, f32[304,128]{1,0:T(8,128)S(1)}, u32[]{:S(2)}, u32[]{:S(2)}) collective-permute-start(f32[304,128]{1,0:T(8,128)S(1)} %collective-permute-done.20.refs_7_), channel_id=1, source_target_pairs={{0,4},{4,0},{1,5},{5,1},{2,6},{6,2},{3,7},{7,3},{8,12},{12,8},{9,1... | collective-permute-start | bytes 466952 | tf_op jit(solution)/shard_map/ppermute | solution.py:304
  70.6 3.6 %rest1.1 = (f32[304,512]{1,0:T(8,128)S(1)}, f32[2,304,512]{2,1,0:T(8,128)S(1)}, f32[304,512]{1,0:T(8,128)S(1)}) custom-call(s32[4]{0:T(128)S(1)} %pad_add_fusion.refs_0_, bf16[2,2,1024,512]{3,2,1,0:T(8,128)(2,1)S(1)} %get-tuple-element.37.refs_1_, bf16[2,2,1024,512]{3,2,1,0:T(8,128)(2,1)S(1)} %get-tuple-element.38.refs_2_, ...), custom_call_target="tpu_custom_call" | custom-call | flops 2868903936 | bytes 1048576 | tf_op jit(solution)/shard_map/rest1/pallas_call | solution.py:28
  75.1 3.7 %lead0.1 = (bf16[608,1024]{1,0:T(8,128)(2,1)S(1)}, f32[1,304,512]{2,1,0:T(8,128)S(1)}, f32[1,304,512]{2,1,0:T(8,128)S(1)}, f32[304,512]{1,0:T(8,128)S(1)}) custom-call(s32[4]{0:T(128)S(1)} %pad_add_fusion.refs_0_, bf16[2,2,1024,512]{3,2,1,0:T(8,128)(2,1)S(1)} %get-tuple-element.37.refs_1_, bf16[2,2,1024,512]{3,2,1,0:T(8,128)(2,1)S(1)} %get-tuple-element.38.refs_2_, ...), custom_call_target="tpu_custom_call" | custom-call | flops 2868903936 | bytes 1048576 | tf_op jit(solution)/shard_map/lead0/pallas_call | solution.py:28
  80.8 3.1 %collective-permute-start.24 = (f32[304,512]{1,0:T(8,128)S(1)}, f32[304,512]{1,0:T(8,128)S(1)}, u32[]{:S(2)}, u32[]{:S(2)}) collective-permute-start(f32[304,512]{1,0:T(8,128)S(1)} %get-tuple-element.55), channel_id=1, source_target_pairs={{0,4},{4,8},{8,12},{12,16},{16,20},{20,24},{24,28},{1,5},{5,9},{9,... | collective-permute-start | bytes 1867784 | tf_op jit(solution)/shard_map/ppermute | solution.py:259
  84.0 4.7 %collective-permute-start.26 = (f32[304,512]{1,0:T(8,128)S(1)}, f32[304,512]{1,0:T(8,128)S(1)}, u32[]{:S(2)}, u32[]{:S(2)}) collective-permute-start(f32[304,512]{1,0:T(8,128)S(1)} %collective-permute-done.25), channel_id=1, source_target_pairs={{0,4},{4,8},{8,12},{12,16},{16,20},{20,24},{24,28},{1,5},{5,9},{9,... | collective-permute-start | bytes 1867784 | tf_op jit(solution)/shard_map/ppermute | solution.py:259
  88.7 1.7 %last.1.refs_1_ = f32[304,512]{1,0:T(8,128)S(1)} custom-call(s32[4]{0:T(128)S(1)} %pad_add_fusion.refs_0_, bf16[2,2,1024,512]{3,2,1,0:T(8,128)(2,1)S(1)} %get-tuple-element.37.refs_1_, bf16[2,2,1024,512]{3,2,1,0:T(8,128)(2,1)S(1)} %get-tuple-element.38.refs_2_, bf16[608,1024]{1,0:T(8,128)(2,1)S(1)} %get-tuple-element.50.refs_3_, ...), custom_call_target="tpu_custom_call" | custom-call | flops 956301312 | bytes 1048576 | tf_op jit(solution)/shard_map/last/pallas_call | solution.py:28
  90.4 5.9 %collective-permute-done.27.refs_5_ = f32[304,512]{1,0:T(8,128)S(1)} collective-permute-done((f32[304,512]{1,0:T(8,128)S(1)}, f32[304,512]{1,0:T(8,128)S(1)}, u32[]{:S(2)}, u32[]{:S(2)}) %collective-permute-start.27) | collective-permute-done | bytes 622624 | tf_op jit(solution)/shard_map/ppermute | solution.py:263
  96.2 11.6 %collective-permute-done.28.refs_6_ = f32[304,512]{1,0:T(8,128)S(1)} collective-permute-done((f32[304,512]{1,0:T(8,128)S(1)}, f32[304,512]{1,0:T(8,128)S(1)}, u32[]{:S(2)}, u32[]{:S(2)}) %collective-permute-start.28) | collective-permute-done | bytes 622624 | tf_op jit(solution)/shard_map/ppermute | solution.py:269
  107.8 3.4 %collective-permute-done.26.refs_4_ = f32[304,512]{1,0:T(8,128)S(1)} collective-permute-done((f32[304,512]{1,0:T(8,128)S(1)}, f32[304,512]{1,0:T(8,128)S(1)}, u32[]{:S(2)}, u32[]{:S(2)}) %collective-permute-start.26) | collective-permute-done | bytes 622624 | tf_op jit(solution)/shard_map/ppermute | solution.py:259
  111.3 1.8 %finish.1 = f32[600,512]{1,0:T(8,128)} custom-call(s32[4]{0:T(128)S(1)} %pad_add_fusion.refs_0_, f32[304,512]{1,0:T(8,128)S(1)} %last.1.refs_1_, f32[304,512]{1,0:T(8,128)S(1)} %collective-permute-done.22.refs_2_, f32[304,512]{1,0:T(8,128)S(1)} %collective-permute-done.24.refs_3_, f32[304,512]{1,0:T(8,128)S(1)} %collective-permute-done.26.refs_4_, ...), custom_call_target="tpu_custom_call" | custom-call | bytes 1048576 | tf_op jit(solution)/shard_map/finish/pallas_call | solution.py:28
  (52 shorter events, 30.4 us)
Async XLA Ops:
  5.8 24.4 %collective-permute-start.1 = (f32[1024,1024]{1,0:T(8,128)S(1)}, f32[1024,1024]{1,0:T(8,128)S(1)}, u32[]{:S(2)}, u32[]{:S(2)}) collective-permute-start(f32[1024,1024]{1,0:T(8,128)S(1)} %get-tuple-element.32.refs_1_), channel_id=1, source_target_pairs={{0,2},{2,0},{1,3},{3,1},{4,6},{6,4},{5,7},{7,5},{8,10},{10,8},{9,1... | collective-permute-start | bytes 12582920 | tf_op jit(solution)/shard_map/ppermute | solution.py:256
  6.0 9.5 %collective-permute-start.2 = (f32[304,128]{1,0:T(8,128)S(1)}, f32[304,128]{1,0:T(8,128)S(1)}, u32[]{:S(2)}, u32[]{:S(2)}) collective-permute-start(f32[304,128]{1,0:T(8,128)S(1)} %get-tuple-element.33.refs_4_), channel_id=1, source_target_pairs={{0,24},{8,0},{16,8},{24,16},{1,25},{9,1},{17,9},{25,17},{2,26},{10... | collective-permute-start | bytes 466952 | tf_op jit(solution)/shard_map/ppermute | solution.py:299
  11.0 8.8 %collective-permute-start.3 = (f32[304,128]{1,0:T(8,128)S(1)}, f32[304,128]{1,0:T(8,128)S(1)}, u32[]{:S(2)}, u32[]{:S(2)}) collective-permute-start(f32[304,128]{1,0:T(8,128)S(1)} %get-tuple-element.33.refs_4_), channel_id=1, source_target_pairs={{0,8},{8,16},{16,24},{24,0},{1,9},{9,17},{17,25},{25,1},{2,10},{10... | collective-permute-start | bytes 466952 | tf_op jit(solution)/shard_map/ppermute | solution.py:299
  11.0 17.7 %collective-permute-start.4 = (f32[304,128]{1,0:T(8,128)S(1)}, f32[304,128]{1,0:T(8,128)S(1)}, u32[]{:S(2)}, u32[]{:S(2)}) collective-permute-start(f32[304,128]{1,0:T(8,128)S(1)} %get-tuple-element.33.refs_4_), channel_id=1, source_target_pairs={{0,16},{8,24},{16,0},{24,8},{1,17},{9,25},{17,1},{25,9},{2,18},{10... | collective-permute-start | bytes 466952 | tf_op jit(solution)/shard_map/ppermute | solution.py:299
  12.0 20.0 %collective-permute-start.5 = (f32[304,128]{1,0:T(8,128)S(1)}, f32[304,128]{1,0:T(8,128)S(1)}, u32[]{:S(2)}, u32[]{:S(2)}) collective-permute-start(f32[304,128]{1,0:T(8,128)S(1)} %get-tuple-element.33.refs_4_), channel_id=1, source_target_pairs={{0,4},{4,0},{1,5},{5,1},{2,6},{6,2},{3,7},{7,3},{8,12},{12,8},{9,1... | collective-permute-start | bytes 466952 | tf_op jit(solution)/shard_map/ppermute | solution.py:304
  16.7 15.3 %collective-permute-start.7 = (f32[304,128]{1,0:T(8,128)S(1)}, f32[304,128]{1,0:T(8,128)S(1)}, u32[]{:S(2)}, u32[]{:S(2)}) collective-permute-start(f32[304,128]{1,0:T(8,128)S(1)} %get-tuple-element.40), channel_id=1, source_target_pairs={{0,4},{4,0},{1,5},{5,1},{2,6},{6,2},{3,7},{7,3},{8,12},{12,8},{9,1... | collective-permute-start | bytes 466952 | tf_op jit(solution)/shard_map/ppermute | solution.py:304
  19.8 12.2 %collective-permute-start.9 = (f32[304,128]{1,0:T(8,128)S(1)}, f32[304,128]{1,0:T(8,128)S(1)}, u32[]{:S(2)}, u32[]{:S(2)}) collective-permute-start(f32[304,128]{1,0:T(8,128)S(1)} %get-tuple-element.41.refs_4_), channel_id=1, source_target_pairs={{0,16},{8,24},{16,0},{24,8},{1,17},{9,25},{17,1},{25,9},{2,18},{10... | collective-permute-start | bytes 466952 | tf_op jit(solution)/shard_map/ppermute | solution.py:299
  37.3 21.5 %collective-permute-start.17 = (f32[304,512]{1,0:T(8,128)S(1)}, f32[304,512]{1,0:T(8,128)S(1)}, u32[]{:S(2)}, u32[]{:S(2)}) collective-permute-start(f32[304,512]{1,0:T(8,128)S(1)} %bitcast.12), channel_id=1, source_target_pairs={{0,1},{1,0},{2,3},{3,2},{4,5},{5,4},{6,7},{7,6},{8,9},{9,8},{10,11... | collective-permute-start | bytes 1867784 | tf_op jit(solution)/shard_map/ppermute | solution.py:263
  38.9 6.9 %collective-permute-start.10 = (f32[304,128]{1,0:T(8,128)S(1)}, f32[304,128]{1,0:T(8,128)S(1)}, u32[]{:S(2)}, u32[]{:S(2)}) collective-permute-start(f32[304,128]{1,0:T(8,128)S(1)} %get-tuple-element.41.refs_4_), channel_id=1, source_target_pairs={{0,24},{8,0},{16,8},{24,16},{1,25},{9,1},{17,9},{25,17},{2,26},{10... | collective-permute-start | bytes 466952 | tf_op jit(solution)/shard_map/ppermute | solution.py:299
  41.8 7.3 %collective-permute-start.11 = (f32[304,128]{1,0:T(8,128)S(1)}, f32[304,128]{1,0:T(8,128)S(1)}, u32[]{:S(2)}, u32[]{:S(2)}) collective-permute-start(f32[304,128]{1,0:T(8,128)S(1)} %get-tuple-element.41.refs_4_), channel_id=1, source_target_pairs={{0,8},{8,16},{16,24},{24,0},{1,9},{9,17},{17,25},{25,1},{2,10},{10... | collective-permute-start | bytes 466952 | tf_op jit(solution)/shard_map/ppermute | solution.py:299
  41.8 10.0 %collective-permute-start.12 = (f32[304,128]{1,0:T(8,128)S(1)}, f32[304,128]{1,0:T(8,128)S(1)}, u32[]{:S(2)}, u32[]{:S(2)}) collective-permute-start(f32[304,128]{1,0:T(8,128)S(1)} %get-tuple-element.41.refs_4_), channel_id=1, source_target_pairs={{0,4},{4,0},{1,5},{5,1},{2,6},{6,2},{3,7},{7,3},{8,12},{12,8},{9,1... | collective-permute-start | bytes 466952 | tf_op jit(solution)/shard_map/ppermute | solution.py:304
  46.3 12.5 %collective-permute-start.13 = (f32[608,128]{1,0:T(8,128)S(1)}, f32[608,128]{1,0:T(8,128)S(1)}, u32[]{:S(2)}, u32[]{:S(2)}) collective-permute-start(f32[608,128]{1,0:T(8,128)S(1)} %join.1), channel_id=1, source_target_pairs={{0,4},{4,0},{1,5},{5,1},{2,6},{6,2},{3,7},{7,3},{8,12},{12,8},{9,1... | collective-permute-start | bytes 933896 | tf_op jit(solution)/shard_map/ppermute | solution.py:304
  49.1 7.9 %collective-permute-start.14 = (f32[304,128]{1,0:T(8,128)S(1)}, f32[304,128]{1,0:T(8,128)S(1)}, u32[]{:S(2)}, u32[]{:S(2)}) collective-permute-start(f32[304,128]{1,0:T(8,128)S(1)} %collective-permute-done.11.refs_7_), channel_id=1, source_target_pairs={{0,4},{4,0},{1,5},{5,1},{2,6},{6,2},{3,7},{7,3},{8,12},{12,8},{9,1... | collective-permute-start | bytes 466952 | tf_op jit(solution)/shard_map/ppermute | solution.py:304
  51.9 6.5 %collective-permute-start.15 = (f32[304,128]{1,0:T(8,128)S(1)}, f32[304,128]{1,0:T(8,128)S(1)}, u32[]{:S(2)}, u32[]{:S(2)}) collective-permute-start(f32[304,128]{1,0:T(8,128)S(1)} %get-tuple-element.45.refs_4_), channel_id=1, source_target_pairs={{0,16},{8,24},{16,0},{24,8},{1,17},{9,25},{17,1},{25,9},{2,18},{10... | collective-permute-start | bytes 466952 | tf_op jit(solution)/shard_map/ppermute | solution.py:299
  51.9 6.9 %collective-permute-start.16 = (f32[304,128]{1,0:T(8,128)S(1)}, f32[304,128]{1,0:T(8,128)S(1)}, u32[]{:S(2)}, u32[]{:S(2)}) collective-permute-start(f32[304,128]{1,0:T(8,128)S(1)} %get-tuple-element.45.refs_4_), channel_id=1, source_target_pairs={{0,24},{8,0},{16,8},{24,16},{1,25},{9,1},{17,9},{25,17},{2,26},{10... | collective-permute-start | bytes 466952 | tf_op jit(solution)/shard_map/ppermute | solution.py:299
  60.5 13.8 %collective-permute-start.23 = (f32[304,512]{1,0:T(8,128)S(1)}, f32[304,512]{1,0:T(8,128)S(1)}, u32[]{:S(2)}, u32[]{:S(2)}) collective-permute-start(f32[304,512]{1,0:T(8,128)S(1)} %bitcast.15), channel_id=1, source_target_pairs={{0,1},{1,0},{2,3},{3,2},{4,5},{5,4},{6,7},{7,6},{8,9},{9,8},{10,11... | collective-permute-start | bytes 1867784 | tf_op jit(solution)/shard_map/ppermute | solution.py:263
  61.1 9.5 %collective-permute-start.19 = (f32[608,128]{1,0:T(8,128)S(1)}, f32[608,128]{1,0:T(8,128)S(1)}, u32[]{:S(2)}, u32[]{:S(2)}) collective-permute-start(f32[608,128]{1,0:T(8,128)S(1)} %get-tuple-element.48), channel_id=1, source_target_pairs={{0,4},{4,0},{1,5},{5,1},{2,6},{6,2},{3,7},{7,3},{8,12},{12,8},{9,1... | collective-permute-start | bytes 933896 | tf_op jit(solution)/shard_map/ppermute | solution.py:304
  61.2 7.0 %collective-permute-start.20 = (f32[304,128]{1,0:T(8,128)S(1)}, f32[304,128]{1,0:T(8,128)S(1)}, u32[]{:S(2)}, u32[]{:S(2)}) collective-permute-start(f32[304,128]{1,0:T(8,128)S(1)} %get-tuple-element.45.refs_4_), channel_id=1, source_target_pairs={{0,8},{8,16},{16,24},{24,0},{1,9},{9,17},{17,25},{25,1},{2,10},{10... | collective-permute-start | bytes 466952 | tf_op jit(solution)/shard_map/ppermute | solution.py:299
  75.0 8.9 %collective-permute-start.25 = (f32[304,512]{1,0:T(8,128)S(1)}, f32[304,512]{1,0:T(8,128)S(1)}, u32[]{:S(2)}, u32[]{:S(2)}) collective-permute-start(f32[304,512]{1,0:T(8,128)S(1)} %get-tuple-element.56), channel_id=1, source_target_pairs={{0,2},{2,0},{1,3},{3,1},{4,6},{6,4},{5,7},{7,5},{8,10},{10,8},{9,1... | collective-permute-start | bytes 1867784 | tf_op jit(solution)/shard_map/ppermute | solution.py:256
  78.8 11.6 %collective-permute-start.22 = (f32[304,512]{1,0:T(8,128)S(1)}, f32[304,512]{1,0:T(8,128)S(1)}, u32[]{:S(2)}, u32[]{:S(2)}) collective-permute-start(f32[304,512]{1,0:T(8,128)S(1)} %get-tuple-element.51), channel_id=1, source_target_pairs={{0,2},{2,0},{1,3},{3,1},{4,6},{6,4},{5,7},{7,5},{8,10},{10,8},{9,1... | collective-permute-start | bytes 1867784 | tf_op jit(solution)/shard_map/ppermute | solution.py:256
  79.3 16.9 %collective-permute-start.27 = (f32[304,512]{1,0:T(8,128)S(1)}, f32[304,512]{1,0:T(8,128)S(1)}, u32[]{:S(2)}, u32[]{:S(2)}) collective-permute-start(f32[304,512]{1,0:T(8,128)S(1)} %bitcast.17), channel_id=1, source_target_pairs={{0,1},{1,0},{2,3},{3,2},{4,5},{5,4},{6,7},{7,6},{8,9},{9,8},{10,11... | collective-permute-start | bytes 1867784 | tf_op jit(solution)/shard_map/ppermute | solution.py:263
  80.8 27.0 %collective-permute-start.28 = (f32[304,512]{1,0:T(8,128)S(1)}, f32[304,512]{1,0:T(8,128)S(1)}, u32[]{:S(2)}, u32[]{:S(2)}) collective-permute-start(f32[304,512]{1,0:T(8,128)S(1)} %bitcast.16), channel_id=1, source_target_pairs={{0,3},{1,2},{2,1},{3,0},{4,7},{5,6},{6,5},{7,4},{8,11},{9,10},{10,... | collective-permute-start | bytes 1867784 | tf_op jit(solution)/shard_map/ppermute | solution.py:269
  80.8 27.0 %collective-permute-start.24 = (f32[304,512]{1,0:T(8,128)S(1)}, f32[304,512]{1,0:T(8,128)S(1)}, u32[]{:S(2)}, u32[]{:S(2)}) collective-permute-start(f32[304,512]{1,0:T(8,128)S(1)} %get-tuple-element.55), channel_id=1, source_target_pairs={{0,4},{4,8},{8,12},{12,16},{16,20},{20,24},{24,28},{1,5},{5,9},{9,... | collective-permute-start | bytes 1867784 | tf_op jit(solution)/shard_map/ppermute | solution.py:259
  84.0 27.3 %collective-permute-start.26 = (f32[304,512]{1,0:T(8,128)S(1)}, f32[304,512]{1,0:T(8,128)S(1)}, u32[]{:S(2)}, u32[]{:S(2)}) collective-permute-start(f32[304,512]{1,0:T(8,128)S(1)} %collective-permute-done.25), channel_id=1, source_target_pairs={{0,4},{4,8},{8,12},{12,16},{16,20},{20,24},{24,28},{1,5},{5,9},{9,... | collective-permute-start | bytes 1867784 | tf_op jit(solution)/shard_map/ppermute | solution.py:259
  (7 other events, 28.4 us)

commit v5 on v4

--- a/solution.py
+++ b/solution.py
@@ -18,36 +18,27 @@
     return high, (values - high.astype(F32)).astype(BF16)
 
 
-def call(kernel, name, shapes, operands, waits=(), flops=0, size=2**20, aliases=None, outside=(), scratch=()):
+def call(kernel, name, shapes, operands, waits=(), flops=0, aliases=None):
     def body(*refs):
         kernel(*refs[: len(operands)], *refs[len(operands) + len(waits) :])
-
-    anywhere = pl.BlockSpec(memory_space=pl.ANY)
-    specs = [SMEM_SPEC] + [pl.BlockSpec(memory_space=pltpu.HBM) if at in outside else VMEM_SPEC for at in range(1, len(operands))]
 
     return pl.pallas_call(
         body,
         out_shape=shapes,
-        in_specs=specs + [anywhere] * len(waits),
+        in_specs=[SMEM_SPEC] + [VMEM_SPEC] * (len(operands) - 1) + [pl.BlockSpec(memory_space=pl.ANY)] * len(waits),
         out_specs=[VMEM_SPEC] * len(shapes),
-        scratch_shapes=list(scratch),
         input_output_aliases=aliases or {},
         compiler_params=pltpu.CompilerParams(vmem_limit_bytes=VMEM_LIMIT),
-        cost_estimate=pl.CostEstimate(flops=flops, bytes_accessed=size, transcendentals=0),
+        cost_estimate=pl.CostEstimate(flops=flops, bytes_accessed=1, transcendentals=0),
         name=name,
     )(*operands, *waits)
 
 
-def stage_kernel(info, source_ref, out_ref, done):
-    copy = pltpu.make_async_copy(source_ref, out_ref, done)
-    copy.start()
-    copy.wait()
-
-
-def spread_kernel(info, own_ref, other_ref, model_ref, *refs):
-    (*lag_refs, model_out, done) = refs
-    copy = pltpu.make_async_copy(model_ref, model_out, done)
-    copy.start()
+def stage_kernel(info, source_ref, out_ref):
+    out_ref[...] = source_ref[...]
+
+
+def spread_kernel(info, own_ref, other_ref, *lag_refs):
     first = info[0] == 0
     half = lag_refs[0].shape[0]
     sensors = own_ref.shape[2]
@@ -55,36 +46,30 @@
         own, other = own_ref[lag], other_ref[lag]
         both = jnp.concatenate([jnp.where(first, own, other), jnp.where(first, other, own)], axis=0).T
         out_ref[...] = jnp.where(first, both[:half], both[sensors - half :])
-    copy.wait()
-
-
-def halves(info, model_ref, high_ref, low_ref, slot, lines, rows):
+
+
+def own_halves_kernel(lines, rows, info, model_ref, next_ref, high_ref, low_ref, next_out, *staged_refs):
+    next_out[...] = next_ref[...]
     spaces, depth, block = high_ref.shape[1:]
     width = depth // (lines * rows)
-    for at in range(lines * rows):
-        source = pl.ds(pl.multiple_of(chip_at(at, info, lines, rows) * width, width), width)
-        target = slice(at * width, (at + 1) * width)
-        for turn in range(spaces):
-            columns = pl.ds(pl.multiple_of(lax.rem(info[1] + turn, spaces) * block, block), block)
-            high_ref[slot, turn, target], low_ref[slot, turn, target] = split(model_ref[source, columns])
-
-
-def own_halves_kernel(lines, rows, info, model_ref, far_ref, next_ref, high_ref, low_ref, far_out, next_out):
-    far_out[...] = far_ref[...]
-    next_out[...] = next_ref[...]
-    halves(info, model_ref, high_ref, low_ref, info[0], lines, rows)
-
-
-def other_halves_kernel(lines, rows, info, model_ref, high_in, low_in, high_ref, low_ref):
-    halves(info, model_ref, high_ref, low_ref, 1 - info[0], lines, rows)
+    for turn, staged_ref in enumerate(staged_refs):
+        columns = pl.ds(pl.multiple_of(lax.rem(info[1] + turn, spaces) * block, block), block)
+        for at in range(lines * rows):
+            source = pl.ds(pl.multiple_of(chip_at(at, info, lines, rows) * width, width), width)
+            target = slice(at * width, (at + 1) * width)
+            values = model_ref[source, columns]
+            staged_ref[target, :] = values
+            high_ref[info[0], turn, target], low_ref[info[0], turn, target] = split(values)
+
+
+def other_halves_kernel(info, high_in, low_in, *refs):
+    (*staged_refs, high_ref, low_ref) = refs
+    for turn, staged_ref in enumerate(staged_refs):
+        high_ref[1 - info[0], turn], low_ref[1 - info[0], turn] = split(staged_ref[...])
 
 
 def near_first(lines):
     return [0] + sorted(range(1, lines), key=lambda shift: (min(shift, lines - shift), shift))
-
-
-def far_first(lines):
-    return [0] + near_first(lines)[:0:-1]
 
 
 def chip_at(at, info, lines, rows):
@@ -92,12 +77,12 @@
     return lax.rem(info[2] - shift + lines, lines) * rows + lax.rem(info[3] + row_off, rows)
 
 
-def fill(blocks, shifts, pair_ref):
+def fill(lines, blocks, pair_ref):
     half, width = pair_ref.shape[0] // 2, blocks[0].shape[1]
     count = 0
     for block in blocks:
         for start in range(0, block.shape[0], half):
-            at = count // len(shifts) * len(shifts) + shifts[count % len(shifts)]
+            at = count // lines * lines + near_first(lines)[count % lines]
             columns = slice(at * width, (at + 1) * width)
             pair_ref[:half, columns], pair_ref[half:, columns] = split(block[start : start + half])
             count += 1
@@ -122,16 +107,27 @@
         put(columns, both[:half] + (both[half:] + low))
 
 
-def lead_two_kernel(shifts, info, high, low, next_block, *refs):
-    blocks, (pair, send, next_out) = refs[:-3], refs[-3:]
+def lead_two_kernel(lines, count, info, high, low, next_block, *refs):
+    (*refs, next_out) = refs
     next_out[...] = next_block[...]
-    fill(blocks, shifts, pair)
+    blocks, (pair, send) = lead(lines, count, refs)
     for turn in range(1, high.shape[1]):
 
         def put(columns, total):
             send[turn - 1, :, columns] = total
 
         times(pair, high, low, 1, turn, put)
+
+
+def lead(lines, count, refs):
+    if count:
+        (*refs, next_out) = refs
+    outputs = refs[-2:]
+    blocks, between = refs[: len(refs) - count - 2], refs[len(refs) - count - 2 : -2]
+    if count:
+        join_kernel(None, *between, next_out)
+    fill(lines, blocks, outputs[0])
+    return blocks, outputs
 
 
 def rest_two_kernel(info, high, low, pair, keep, other):
@@ -163,12 +159,8 @@
         times(pair, high, low, 0, turn, put)
 
 
-def lead_one_kernel(shifts, count, info, high, low, added, *refs):
-    if count:
-        (*refs, next_out) = refs
-        join_kernel(info, *refs[-count - 2 : -2], next_out)
-    blocks, (pair, send) = refs[: len(refs) - count - 2], refs[-2:]
-    fill(blocks, shifts, pair)
+def lead_one_kernel(lines, count, info, high, low, added, *refs):
+    blocks, (pair, send) = lead(lines, count, refs)
     for turn in range(1, high.shape[1]):
 
         def put(columns, total):
@@ -193,9 +185,9 @@
     times(pair, high, low, 1, turn, put_late)
 
 
-def lead_zero_kernel(shifts, info, high, low, added, *refs):
+def lead_zero_kernel(lines, info, high, low, added, *refs):
     blocks, (pair, send, cross, chip) = refs[:-4], refs[-4:]
-    fill(blocks, shifts, pair)
+    fill(lines, blocks, pair)
     for turn in range(1, high.shape[1]):
 
         def own_put(columns, total):
@@ -275,29 +267,16 @@
         ]
 
     kernels_t = jnp.swapaxes(kernels, 1, 2)
-    copied = pltpu.SemaphoreType.DMA
-    (own_t,) = call(
-        stage_kernel,
-        "stage",
-        [jax.ShapeDtypeStruct(kernels_t.shape, F32)],
-        [info, kernels_t],
-        outside=[1],
-        scratch=[copied],
-    )
+    (own_t,) = call(stage_kernel, "stage", [jax.ShapeDtypeStruct(kernels_t.shape, F32)], [info, kernels_t])
     small = jax.ShapeDtypeStruct((half, 2 * width), F32)
-    *lag_blocks, staged = call(
-        spread_kernel,
-        "spread",
-        [small] * lags + [jax.ShapeDtypeStruct(own_model.shape, F32)],
-        [info, own_t, swap(kernels_t), own_model],
-        outside=[3],
-        scratch=[copied],
-    )
-
-    def shifted(own_block, shifts):
-        return [own_block] + [
-            lax.ppermute(own_block, "line", [(i, (i + shift) % lines) for i in range(lines)]) for shift in shifts[1:]
-        ]
+    lag_blocks = call(spread_kernel, "spread", [small] * lags, [info, own_t, swap(kernels_t)])
+
+    def shifted(own_block):
+        moved = [
+            lax.ppermute(own_block, "line", [(i, (i + shift) % lines) for i in range(lines)])
+            for shift in near_first(lines)[1:]
+        ]
+        return [own_block], moved[:-1], moved[-1:]
 
     def handed(blocks):
         return [
@@ -306,9 +285,8 @@
             for values in blocks
         ]
 
-    def joined(blocks, waits):
-        shape = jax.ShapeDtypeStruct((half * len(blocks), blocks[0].shape[1]), F32)
-        return call(join_kernel, "join", [shape], [info, *blocks], waits=waits)[0]
+    between = max(lines - 2, 0)
+    joint = [jax.ShapeDtypeStruct((half * between, 2 * width), F32)] * bool(between)
 
     pair = jax.ShapeDtypeStruct((2 * half, depth), BF16)
     one = jax.ShapeDtypeStruct((half, block), F32)
@@ -316,56 +294,63 @@
     whole = jax.ShapeDtypeStruct((spaces, half, block), F32)
     flops = 6 * half * depth * block
 
-    orders = near_first(lines), far_first(lines)
-    line2 = shifted(lag_blocks[2], orders[0])
+    own2, near2, far2 = shifted(lag_blocks[2])
+    row2 = handed(own2)
 
     models = [jax.ShapeDtypeStruct((2, spaces, depth, block), BF16)] * 2
-    late = min(2, lines - 1)
-    high, low, late_block, block1 = call(
+    high, low, block1, *staged = call(
         functools.partial(own_halves_kernel, lines, rows),
         "own_halves",
-        models + [small] * 2,
-        [info, staged, line2[late], lag_blocks[1]],
-        size=1,
-    )
+        models + [small] + [jax.ShapeDtypeStruct((depth, block), F32)] * spaces,
+        [info, own_model, lag_blocks[1]],
+        waits=row2 + near2,
+    )
+    joint2 = call(join_kernel, "join2", joint, [info, *near2]) if joint else []
     high, low = call(
-        functools.partial(other_halves_kernel, lines, rows),
+        other_halves_kernel,
         "other_halves",
         models,
-        [info, swap(staged), high, low],
-        size=1,
-        aliases={2: 0, 3: 1},
-    )
-    row2 = handed(line2[:late] + [late_block] + line2[late + 1 :])
-    line1 = shifted(block1, orders[1])
-    pair2, send1, block0 = call(
-        functools.partial(lead_two_kernel, orders[0]),
+        [info, high, low] + [swap(part) for part in staged],
+        aliases={1: 0, 2: 1},
+    )
+
+    def gathered(own, near, far, row_own, near_joint):
+        return own + near + far, ordered(row_own, handed(near_joint), handed(far))
+
+    def ordered(*groups):
+        each = [len(group) // (rows - 1) if rows > 1 else 0 for group in groups]
+        return [
+            group[off * size + at] for off in range(rows - 1) for group, size in zip(groups, each) for at in range(size)
+        ]
+
+    line2, row2 = gathered(own2, near2, far2, row2, joint2)
+    own1, near1, far1 = shifted(block1)
+    row_own1 = handed(own1)
+    pair2, send1, *joint1, block0 = call(
+        functools.partial(lead_two_kernel, lines, between),
         "lead2",
-        [pair, sent, small],
-        [info, high, low, lag_blocks[0], *line2, *row2],
-        waits=line1[1:2],
+        [pair, sent] + joint + [small],
+        [info, high, low, lag_blocks[0], *line2, *row2, *near1],
+        waits=row_own1,
         flops=flops,
     )
     from1 = over_space(send1)
-    keep1, early2 = call(rest_two_kernel, "rest2", [one, whole], [info, high, low, pair2], flops=3 * flops)
-
-    line0 = shifted(block0, orders[1])
-
-    def parts(line):
-        return [part for part in (line[:1], line[1:-1], line[1:][-1:]) if part]
-
-    row1 = handed([part[0] if len(part) == 1 else joined(part, [send1]) for part in parts(line1)])
-    between = line0[1:-1]
-    pair1, send0, *near0 = call(
-        functools.partial(lead_one_kernel, orders[1], len(between)),
+    line1, row1 = gathered(own1, near1, far1, row_own1, joint1)
+    keep1, early2 = call(
+        rest_two_kernel, "rest2", [one, whole], [info, high, low, pair2], waits=row1[:2], flops=3 * flops
+    )
+    own0, near0, far0 = shifted(block0)
+    row_own0 = handed(own0)
+    pair1, send0, *joint0 = call(
+        functools.partial(lead_one_kernel, lines, between),
         "lead1",
-        [pair, sent] + [jax.ShapeDtypeStruct((half * len(between), 2 * width), F32)] * bool(between),
-        [info, high, low, early2, *line1, *row1, *between],
-        waits=from1,
+        [pair, sent] + joint,
+        [info, high, low, early2, *line1, *row1, *near0],
+        waits=from1 + row_own0,
         flops=flops,
     )
     from0 = over_space(send0)
-    row0 = handed(line0[:1] + near0 + line0[1:][-1:])
+    line0, row0 = gathered(own0, near0, far0, row_own0, joint0)
     keep0, early1, total1 = call(
         rest_one_kernel,
         "rest1",
@@ -375,7 +360,7 @@
         flops=3 * flops,
     )
     pair0, d_send, d_cross, d_chip = call(
-        functools.partial(lead_zero_kernel, orders[1]),
+        functools.partial(lead_zero_kernel, lines),
         "lead0",
         [pair, sent, sent, one],
         [info, high, low, early1, *line0, *row0],

time: 115 us -> 119 us (1.035); the launches traced: 113 us -> 118 us
  waiting for transfers between devices: 43.6 us -> 54.4 us
  starting transfers between devices: 42.4 us -> 37.5 us
    ppermute x9, waiting for transfers between devices: 18.6 us -> 29.9 us  [shifted(): lax.ppermute(own_block, 'line', [(i, (i + shift) % lines) for i in range(...]
    ppermute x10 -> x9, starting transfers between devices: 14.6 us -> 9.61 us  [handed(): lax.ppermute(values, 'row', [(i, (i - off) % rows) for i in range(rows)])]
    ppermute x10 -> x9, waiting for transfers between devices: 4.07 us -> 1.39 us  [handed(): lax.ppermute(values, 'row', [(i, (i - off) % rows) for i in range(rows)])]
    ppermute x3, waiting for transfers between devices: 5.86 us -> 8.39 us  [over_space(): lax.ppermute(sent[d - 1], 'space', [(i, (i + d) % spaces) for i in range(...]
    ppermute x2, starting transfers between devices: 7.82 us -> 5.3 us  [onward(): lax.ppermute(values, ('line', 'row'), [(i, i + 1) for i in range(lines *...]
    ppermute x9, starting transfers between devices: 15.1 us -> 17.3 us  [shifted(): lax.ppermute(own_block, 'line', [(i, (i + shift) % lines) for i in range(...]
  transfers between devices with their start and end apart: 29 -> 29, of which waited for: 14 -> 11; matrix products, arithmetic and copies ran while one was open for 0% -> 0% of each run, Pallas kernels for 15% -> 13%
where the time goes in v5:
time: 119 us; the launch traced here: 118 us
  waiting for transfers between devices  54.4 us (46%)
  starting transfers between devices  37.5 us (32%)
  Pallas kernels  23.1 us (19%)
  local copies, waits for them, and re-layouts  3.22 us (3%)
    ppermute x9, waiting for transfers between devices, shifted(): lax.ppermute(own_block, 'line', [(i, (i + shift) % lines) for i in range(...  29.9 us
    pallas_call x13, Pallas kernels, call(): pl.pallas_call(body, out_shape=shapes, in_specs=[SMEM_SPEC] + [VMEM_SPEC]...  23.1 us
    ppermute x9, starting transfers between devices, shifted(): lax.ppermute(own_block, 'line', [(i, (i + shift) % lines) for i in range(...  17.3 us
    ppermute x1, waiting for transfers between devices, over_space_and_core(): lax.ppermute(sent[d - 1], ('core', 'space'), [(c * spaces + i, (1 - c) *...  11.6 us
    ppermute x9, starting transfers between devices, handed(): lax.ppermute(values, 'row', [(i, (i - off) % rows) for i in range(rows)])  9.61 us
    ppermute x3, waiting for transfers between devices, over_space(): lax.ppermute(sent[d - 1], 'space', [(i, (i + d) % spaces) for i in range(...  8.39 us
    ppermute x2, starting transfers between devices, onward(): lax.ppermute(values, ('line', 'row'), [(i, i + 1) for i in range(lines *...  5.3 us
    ppermute x3, starting transfers between devices, over_space(): lax.ppermute(sent[d - 1], 'space', [(i, (i + d) % spaces) for i in range(...  3.65 us
  transfers between devices with their start and end apart: 29, of which 11 were waited for; matrix products, arithmetic and copies ran while one was open for 0% of the time, Pallas kernels for 13%

profile of v5, /device:TPU:0, one launch (start us, length us, event | category | flops | bytes accessed | tf_op | source)
XLA Modules:
  0.0 118.5 jit_solution(13222579345165802716)
XLA Ops:
  3.0 3.0 %collective-permute-start.2 = (f32[304,128]{1,0:T(8,128)S(1)}, f32[304,128]{1,0:T(8,128)S(1)}, u32[]{:S(2)}, u32[]{:S(2)}) collective-permute-start(f32[304,128]{1,0:T(8,128)S(1)} %get-tuple-element.34.refs_4_), channel_id=1, source_target_pairs={{0,8},{8,16},{16,24},{24,0},{1,9},{9,17},{17,25},{25,1},{2,10},{10... | collective-permute-start | bytes 466952 | tf_op jit(solution)/shard_map/ppermute | solution.py:276
  6.0 2.1 %collective-permute-start.3 = (f32[304,128]{1,0:T(8,128)S(1)}, f32[304,128]{1,0:T(8,128)S(1)}, u32[]{:S(2)}, u32[]{:S(2)}) collective-permute-start(f32[304,128]{1,0:T(8,128)S(1)} %get-tuple-element.34.refs_4_), channel_id=1, source_target_pairs={{0,24},{8,0},{16,8},{24,16},{1,25},{9,1},{17,9},{25,17},{2,26},{10... | collective-permute-start | bytes 466952 | tf_op jit(solution)/shard_map/ppermute | solution.py:276
  9.8 3.1 %collective-permute-done.2.refs_4_.refs_1_.refs_5_ = f32[304,128]{1,0:T(8,128)S(1)} collective-permute-done((f32[304,128]{1,0:T(8,128)S(1)}, f32[304,128]{1,0:T(8,128)S(1)}, u32[]{:S(2)}, u32[]{:S(2)}) %collective-permute-start.2) | collective-permute-done | bytes 155680 | tf_op jit(solution)/shard_map/ppermute | solution.py:276
  12.9 2.2 %collective-permute-done.3.refs_5_.refs_2_.refs_6_ = f32[304,128]{1,0:T(8,128)S(1)} collective-permute-done((f32[304,128]{1,0:T(8,128)S(1)}, f32[304,128]{1,0:T(8,128)S(1)}, u32[]{:S(2)}, u32[]{:S(2)}) %collective-permute-start.3) | collective-permute-done | bytes 155680 | tf_op jit(solution)/shard_map/ppermute | solution.py:276
  15.2 2.2 %copy-done = f32[1,1024,1024]{2,1,0:T(8,128)S(1)} copy-done((f32[1,1024,1024]{2,1,0:T(8,128)S(1)}, f32[1,1024,1024]{2,1,0:T(8,128)}, u32[]{:S(2)}) %copy-start) | copy-done | bytes 4194328
  22.7 2.2 %collective-permute-start.10 = (f32[304,128]{1,0:T(8,128)S(1)}, f32[304,128]{1,0:T(8,128)S(1)}, u32[]{:S(2)}, u32[]{:S(2)}) collective-permute-start(f32[304,128]{1,0:T(8,128)S(1)} %get-tuple-element.42.refs_4_), channel_id=1, source_target_pairs={{0,24},{8,0},{16,8},{24,16},{1,25},{9,1},{17,9},{25,17},{2,26},{10... | collective-permute-start | bytes 466952 | tf_op jit(solution)/shard_map/ppermute | solution.py:276
  24.9 5.3 %collective-permute-done.6.refs_7_ = f32[304,128]{1,0:T(8,128)S(1)} collective-permute-done((f32[304,128]{1,0:T(8,128)S(1)}, f32[304,128]{1,0:T(8,128)S(1)}, u32[]{:S(2)}, u32[]{:S(2)}) %collective-permute-start.6) | collective-permute-done | bytes 155680 | tf_op jit(solution)/shard_map/ppermute | solution.py:276
  31.7 2.0 %collective-permute-start.9 = (f32[304,128]{1,0:T(8,128)S(1)}, f32[304,128]{1,0:T(8,128)S(1)}, u32[]{:S(2)}, u32[]{:S(2)}) collective-permute-start(f32[304,128]{1,0:T(8,128)S(1)} %get-tuple-element.42.refs_4_), channel_id=1, source_target_pairs={{0,8},{8,16},{16,24},{24,0},{1,9},{9,17},{17,25},{25,1},{2,10},{10... | collective-permute-start | bytes 466952 | tf_op jit(solution)/shard_map/ppermute | solution.py:276
  35.5 5.0 %collective-permute-done.9.refs_11_.refs_5_ = f32[304,128]{1,0:T(8,128)S(1)} collective-permute-done((f32[304,128]{1,0:T(8,128)S(1)}, f32[304,128]{1,0:T(8,128)S(1)}, u32[]{:S(2)}, u32[]{:S(2)}) %collective-permute-start.9) | collective-permute-done | bytes 155680 | tf_op jit(solution)/shard_map/ppermute | solution.py:276
  40.5 1.7 %lead2.1 = (bf16[608,1024]{1,0:T(8,128)(2,1)S(1)}, f32[1,304,512]{2,1,0:T(8,128)S(1)}, f32[608,128]{1,0:T(8,128)S(1)}, f32[304,128]{1,0:T(8,128)S(1)}) custom-call(s32[4]{0:T(128)S(1)} %pad_add_fusion.refs_0_, bf16[2,2,1024,512]{3,2,1,0:T(8,128)(2,1)S(1)} %get-tuple-element.39.refs_1_, bf16[2,2,1024,512]{3,2,1,0:T(8,128)(2,1)S(1)} %get-tuple-element.40.refs_2_, ...), custom_call_target="tpu_custom_call" | custom-call | flops 956301312 | bytes 1 | tf_op jit(solution)/shard_map/lead2/pallas_call | solution.py:25
  44.3 2.0 %collective-permute-start.13 = (f32[304,128]{1,0:T(8,128)S(1)}, f32[304,128]{1,0:T(8,128)S(1)}, u32[]{:S(2)}, u32[]{:S(2)}) collective-permute-start(f32[304,128]{1,0:T(8,128)S(1)} %get-tuple-element.42.refs_4_), channel_id=1, source_target_pairs={{0,16},{8,24},{16,0},{24,8},{1,17},{9,25},{17,1},{25,9},{2,18},{10... | collective-permute-start | bytes 466952 | tf_op jit(solution)/shard_map/ppermute | solution.py:276
  46.3 7.3 %collective-permute-done.13.refs_7_ = f32[304,128]{1,0:T(8,128)S(1)} collective-permute-done((f32[304,128]{1,0:T(8,128)S(1)}, f32[304,128]{1,0:T(8,128)S(1)}, u32[]{:S(2)}, u32[]{:S(2)}) %collective-permute-start.13) | collective-permute-done | bytes 155680 | tf_op jit(solution)/shard_map/ppermute | solution.py:276
  54.6 3.8 %collective-permute-start.16 = (f32[304,128]{1,0:T(8,128)S(1)}, f32[304,128]{1,0:T(8,128)S(1)}, u32[]{:S(2)}, u32[]{:S(2)}) collective-permute-start(f32[304,128]{1,0:T(8,128)S(1)} %get-tuple-element.46.refs_4_), channel_id=1, source_target_pairs={{0,24},{8,0},{16,8},{24,16},{1,25},{9,1},{17,9},{25,17},{2,26},{10... | collective-permute-start | bytes 466952 | tf_op jit(solution)/shard_map/ppermute | solution.py:276
  59.5 3.6 %rest2.1 = (f32[304,512]{1,0:T(8,128)S(1)}, f32[2,304,512]{2,1,0:T(8,128)S(1)}) custom-call(s32[4]{0:T(128)S(1)} %pad_add_fusion.refs_0_, bf16[2,2,1024,512]{3,2,1,0:T(8,128)(2,1)S(1)} %get-tuple-element.39.refs_1_, bf16[2,2,1024,512]{3,2,1,0:T(8,128)(2,1)S(1)} %get-tuple-element.40.refs_2_, bf16[608,1024]{1,0:T(8,128)(2,1)S(1)} %get-tuple-element.43.refs_3_, ...), custom_call_target="tpu_custom_call" | custom-call | flops 2868903936 | bytes 1 | tf_op jit(solution)/shard_map/rest2/pallas_call | solution.py:25
  63.7 1.7 %lead1.1 = (bf16[608,1024]{1,0:T(8,128)(2,1)S(1)}, f32[1,304,512]{2,1,0:T(8,128)S(1)}, f32[608,128]{1,0:T(8,128)S(1)}) custom-call(s32[4]{0:T(128)S(1)} %pad_add_fusion.refs_0_, bf16[2,2,1024,512]{3,2,1,0:T(8,128)(2,1)S(1)} %get-tuple-element.39.refs_1_, bf16[2,2,1024,512]{3,2,1,0:T(8,128)(2,1)S(1)} %get-tuple-element.40.refs_2_, ...), custom_call_target="tpu_custom_call" | custom-call | flops 956301312 | bytes 1 | tf_op jit(solution)/shard_map/lead1/pallas_call | solution.py:25
  67.8 7.0 %collective-permute-done.20.refs_7_ = f32[304,128]{1,0:T(8,128)S(1)} collective-permute-done((f32[304,128]{1,0:T(8,128)S(1)}, f32[304,128]{1,0:T(8,128)S(1)}, u32[]{:S(2)}, u32[]{:S(2)}) %collective-permute-start.20) | collective-permute-done | bytes 155680 | tf_op jit(solution)/shard_map/ppermute | solution.py:276
  75.6 3.7 %rest1.1 = (f32[304,512]{1,0:T(8,128)S(1)}, f32[2,304,512]{2,1,0:T(8,128)S(1)}, f32[304,512]{1,0:T(8,128)S(1)}) custom-call(s32[4]{0:T(128)S(1)} %pad_add_fusion.refs_0_, bf16[2,2,1024,512]{3,2,1,0:T(8,128)(2,1)S(1)} %get-tuple-element.39.refs_1_, bf16[2,2,1024,512]{3,2,1,0:T(8,128)(2,1)S(1)} %get-tuple-element.40.refs_2_, ...), custom_call_target="tpu_custom_call" | custom-call | flops 2868903936 | bytes 1 | tf_op jit(solution)/shard_map/rest1/pallas_call | solution.py:25
  80.9 3.7 %lead0.1 = (bf16[608,1024]{1,0:T(8,128)(2,1)S(1)}, f32[1,304,512]{2,1,0:T(8,128)S(1)}, f32[1,304,512]{2,1,0:T(8,128)S(1)}, f32[304,512]{1,0:T(8,128)S(1)}) custom-call(s32[4]{0:T(128)S(1)} %pad_add_fusion.refs_0_, bf16[2,2,1024,512]{3,2,1,0:T(8,128)(2,1)S(1)} %get-tuple-element.39.refs_1_, bf16[2,2,1024,512]{3,2,1,0:T(8,128)(2,1)S(1)} %get-tuple-element.40.refs_2_, ...), custom_call_target="tpu_custom_call" | custom-call | flops 2868903936 | bytes 1 | tf_op jit(solution)/shard_map/lead0/pallas_call | solution.py:25
  86.6 2.7 %collective-permute-start.24 = (f32[304,512]{1,0:T(8,128)S(1)}, f32[304,512]{1,0:T(8,128)S(1)}, u32[]{:S(2)}, u32[]{:S(2)}) collective-permute-start(f32[304,512]{1,0:T(8,128)S(1)} %get-tuple-element.57), channel_id=1, source_target_pairs={{0,4},{4,8},{8,12},{12,16},{16,20},{20,24},{24,28},{1,5},{5,9},{9,... | collective-permute-start | bytes 1867784 | tf_op jit(solution)/shard_map/ppermute | solution.py:251
  89.3 2.6 %collective-permute-start.26 = (f32[304,512]{1,0:T(8,128)S(1)}, f32[304,512]{1,0:T(8,128)S(1)}, u32[]{:S(2)}, u32[]{:S(2)}) collective-permute-start(f32[304,512]{1,0:T(8,128)S(1)} %collective-permute-done.25), channel_id=1, source_target_pairs={{0,4},{4,8},{8,12},{12,16},{16,20},{20,24},{24,28},{1,5},{5,9},{9,... | collective-permute-start | bytes 1867784 | tf_op jit(solution)/shard_map/ppermute | solution.py:251
  93.6 8.4 %collective-permute-done.27.refs_5_ = f32[304,512]{1,0:T(8,128)S(1)} collective-permute-done((f32[304,512]{1,0:T(8,128)S(1)}, f32[304,512]{1,0:T(8,128)S(1)}, u32[]{:S(2)}, u32[]{:S(2)}) %collective-permute-start.27) | collective-permute-done | bytes 622624 | tf_op jit(solution)/shard_map/ppermute | solution.py:255
  102.0 11.6 %collective-permute-done.28.refs_6_ = f32[304,512]{1,0:T(8,128)S(1)} collective-permute-done((f32[304,512]{1,0:T(8,128)S(1)}, f32[304,512]{1,0:T(8,128)S(1)}, u32[]{:S(2)}, u32[]{:S(2)}) %collective-permute-start.28) | collective-permute-done | bytes 622624 | tf_op jit(solution)/shard_map/ppermute | solution.py:261
  113.6 3.1 %collective-permute-done.26.refs_4_ = f32[304,512]{1,0:T(8,128)S(1)} collective-permute-done((f32[304,512]{1,0:T(8,128)S(1)}, f32[304,512]{1,0:T(8,128)S(1)}, u32[]{:S(2)}, u32[]{:S(2)}) %collective-permute-start.26) | collective-permute-done | bytes 622624 | tf_op jit(solution)/shard_map/ppermute | solution.py:251
  116.7 1.8 %finish.1 = f32[600,512]{1,0:T(8,128)} custom-call(s32[4]{0:T(128)S(1)} %pad_add_fusion.refs_0_, f32[304,512]{1,0:T(8,128)S(1)} %last.1.refs_1_, f32[304,512]{1,0:T(8,128)S(1)} %collective-permute-done.22.refs_2_, f32[304,512]{1,0:T(8,128)S(1)} %collective-permute-done.24.refs_3_, f32[304,512]{1,0:T(8,128)S(1)} %collective-permute-done.26.refs_4_, ...), custom_call_target="tpu_custom_call" | custom-call | bytes 1 | tf_op jit(solution)/shard_map/finish/pallas_call | solution.py:25
  (52 shorter events, 26.5 us)
Async XLA Ops:
  3.0 9.9 %collective-permute-start.2 = (f32[304,128]{1,0:T(8,128)S(1)}, f32[304,128]{1,0:T(8,128)S(1)}, u32[]{:S(2)}, u32[]{:S(2)}) collective-permute-start(f32[304,128]{1,0:T(8,128)S(1)} %get-tuple-element.34.refs_4_), channel_id=1, source_target_pairs={{0,8},{8,16},{16,24},{24,0},{1,9},{9,17},{17,25},{25,1},{2,10},{10... | collective-permute-start | bytes 466952 | tf_op jit(solution)/shard_map/ppermute | solution.py:276
  6.0 9.1 %collective-permute-start.3 = (f32[304,128]{1,0:T(8,128)S(1)}, f32[304,128]{1,0:T(8,128)S(1)}, u32[]{:S(2)}, u32[]{:S(2)}) collective-permute-start(f32[304,128]{1,0:T(8,128)S(1)} %get-tuple-element.34.refs_4_), channel_id=1, source_target_pairs={{0,24},{8,0},{16,8},{24,16},{1,25},{9,1},{17,9},{25,17},{2,26},{10... | collective-permute-start | bytes 466952 | tf_op jit(solution)/shard_map/ppermute | solution.py:276
  8.1 7.0 %collective-permute-start.1 = (f32[304,128]{1,0:T(8,128)S(1)}, f32[304,128]{1,0:T(8,128)S(1)}, u32[]{:S(2)}, u32[]{:S(2)}) collective-permute-start(f32[304,128]{1,0:T(8,128)S(1)} %get-tuple-element.34.refs_4_), channel_id=1, source_target_pairs={{0,4},{4,0},{1,5},{5,1},{2,6},{6,2},{3,7},{7,3},{8,12},{12,8},{9,1... | collective-permute-start | bytes 466952 | tf_op jit(solution)/shard_map/ppermute | solution.py:283
  18.7 13.0 %collective-permute-start.4 = (f32[1024,512]{1,0:T(8,128)S(1)}, f32[1024,512]{1,0:T(8,128)S(1)}, u32[]{:S(2)}, u32[]{:S(2)}) collective-permute-start(f32[1024,512]{1,0:T(8,128)S(1)} %get-tuple-element.37), channel_id=1, source_target_pairs={{0,2},{2,0},{1,3},{3,1},{4,6},{6,4},{5,7},{7,5},{8,10},{10,8},{9,1... | collective-permute-start | bytes 6291464 | tf_op jit(solution)/shard_map/ppermute | solution.py:248
  18.8 15.0 %collective-permute-start.5 = (f32[1024,512]{1,0:T(8,128)S(1)}, f32[1024,512]{1,0:T(8,128)S(1)}, u32[]{:S(2)}, u32[]{:S(2)}) collective-permute-start(f32[1024,512]{1,0:T(8,128)S(1)} %get-tuple-element.38), channel_id=1, source_target_pairs={{0,2},{2,0},{1,3},{3,1},{4,6},{6,4},{5,7},{7,5},{8,10},{10,8},{9,1... | collective-permute-start | bytes 6291464 | tf_op jit(solution)/shard_map/ppermute | solution.py:248
  19.3 10.9 %collective-permute-start.6 = (f32[304,128]{1,0:T(8,128)S(1)}, f32[304,128]{1,0:T(8,128)S(1)}, u32[]{:S(2)}, u32[]{:S(2)}) collective-permute-start(f32[304,128]{1,0:T(8,128)S(1)} %get-tuple-element.34.refs_4_), channel_id=1, source_target_pairs={{0,16},{8,24},{16,0},{24,8},{1,17},{9,25},{17,1},{25,9},{2,18},{10... | collective-permute-start | bytes 466952 | tf_op jit(solution)/shard_map/ppermute | solution.py:276
  21.1 19.4 %collective-permute-start.7 = (f32[608,128]{1,0:T(8,128)S(1)}, f32[608,128]{1,0:T(8,128)S(1)}, u32[]{:S(2)}, u32[]{:S(2)}) collective-permute-start(f32[608,128]{1,0:T(8,128)S(1)} %join2.1), channel_id=1, source_target_pairs={{0,4},{4,0},{1,5},{5,1},{2,6},{6,2},{3,7},{7,3},{8,12},{12,8},{9,1... | collective-permute-start | bytes 933896 | tf_op jit(solution)/shard_map/ppermute | solution.py:283
  22.7 12.7 %collective-permute-start.10 = (f32[304,128]{1,0:T(8,128)S(1)}, f32[304,128]{1,0:T(8,128)S(1)}, u32[]{:S(2)}, u32[]{:S(2)}) collective-permute-start(f32[304,128]{1,0:T(8,128)S(1)} %get-tuple-element.42.refs_4_), channel_id=1, source_target_pairs={{0,24},{8,0},{16,8},{24,16},{1,25},{9,1},{17,9},{25,17},{2,26},{10... | collective-permute-start | bytes 466952 | tf_op jit(solution)/shard_map/ppermute | solution.py:276
  31.7 8.8 %collective-permute-start.9 = (f32[304,128]{1,0:T(8,128)S(1)}, f32[304,128]{1,0:T(8,128)S(1)}, u32[]{:S(2)}, u32[]{:S(2)}) collective-permute-start(f32[304,128]{1,0:T(8,128)S(1)} %get-tuple-element.42.refs_4_), channel_id=1, source_target_pairs={{0,8},{8,16},{16,24},{24,0},{1,9},{9,17},{17,25},{25,1},{2,10},{10... | collective-permute-start | bytes 466952 | tf_op jit(solution)/shard_map/ppermute | solution.py:276
  42.2 21.4 %collective-permute-start.17 = (f32[304,512]{1,0:T(8,128)S(1)}, f32[304,512]{1,0:T(8,128)S(1)}, u32[]{:S(2)}, u32[]{:S(2)}) collective-permute-start(f32[304,512]{1,0:T(8,128)S(1)} %bitcast.14), channel_id=1, source_target_pairs={{0,1},{1,0},{2,3},{3,2},{4,5},{5,4},{6,7},{7,6},{8,9},{9,8},{10,11... | collective-permute-start | bytes 1867784 | tf_op jit(solution)/shard_map/ppermute | solution.py:255
  43.8 14.6 %collective-permute-start.12 = (f32[608,128]{1,0:T(8,128)S(1)}, f32[608,128]{1,0:T(8,128)S(1)}, u32[]{:S(2)}, u32[]{:S(2)}) collective-permute-start(f32[608,128]{1,0:T(8,128)S(1)} %get-tuple-element.44), channel_id=1, source_target_pairs={{0,4},{4,0},{1,5},{5,1},{2,6},{6,2},{3,7},{7,3},{8,12},{12,8},{9,1... | collective-permute-start | bytes 933896 | tf_op jit(solution)/shard_map/ppermute | solution.py:283
  44.3 9.3 %collective-permute-start.13 = (f32[304,128]{1,0:T(8,128)S(1)}, f32[304,128]{1,0:T(8,128)S(1)}, u32[]{:S(2)}, u32[]{:S(2)}) collective-permute-start(f32[304,128]{1,0:T(8,128)S(1)} %get-tuple-element.42.refs_4_), channel_id=1, source_target_pairs={{0,16},{8,24},{16,0},{24,8},{1,17},{9,25},{17,1},{25,9},{2,18},{10... | collective-permute-start | bytes 466952 | tf_op jit(solution)/shard_map/ppermute | solution.py:276
  53.6 9.4 %collective-permute-start.14 = (f32[304,128]{1,0:T(8,128)S(1)}, f32[304,128]{1,0:T(8,128)S(1)}, u32[]{:S(2)}, u32[]{:S(2)}) collective-permute-start(f32[304,128]{1,0:T(8,128)S(1)} %collective-permute-done.13.refs_7_), channel_id=1, source_target_pairs={{0,4},{4,0},{1,5},{5,1},{2,6},{6,2},{3,7},{7,3},{8,12},{12,8},{9,1... | collective-permute-start | bytes 466952 | tf_op jit(solution)/shard_map/ppermute | solution.py:283
  54.6 8.5 %collective-permute-start.15 = (f32[304,128]{1,0:T(8,128)S(1)}, f32[304,128]{1,0:T(8,128)S(1)}, u32[]{:S(2)}, u32[]{:S(2)}) collective-permute-start(f32[304,128]{1,0:T(8,128)S(1)} %get-tuple-element.46.refs_4_), channel_id=1, source_target_pairs={{0,8},{8,16},{16,24},{24,0},{1,9},{9,17},{17,25},{25,1},{2,10},{10... | collective-permute-start | bytes 466952 | tf_op jit(solution)/shard_map/ppermute | solution.py:276
  54.6 8.5 %collective-permute-start.16 = (f32[304,128]{1,0:T(8,128)S(1)}, f32[304,128]{1,0:T(8,128)S(1)}, u32[]{:S(2)}, u32[]{:S(2)}) collective-permute-start(f32[304,128]{1,0:T(8,128)S(1)} %get-tuple-element.46.refs_4_), channel_id=1, source_target_pairs={{0,24},{8,0},{16,8},{24,16},{1,25},{9,1},{17,9},{25,17},{2,26},{10... | collective-permute-start | bytes 466952 | tf_op jit(solution)/shard_map/ppermute | solution.py:276
  65.4 14.7 %collective-permute-start.23 = (f32[304,512]{1,0:T(8,128)S(1)}, f32[304,512]{1,0:T(8,128)S(1)}, u32[]{:S(2)}, u32[]{:S(2)}) collective-permute-start(f32[304,512]{1,0:T(8,128)S(1)} %bitcast.16), channel_id=1, source_target_pairs={{0,1},{1,0},{2,3},{3,2},{4,5},{5,4},{6,7},{7,6},{8,9},{9,8},{10,11... | collective-permute-start | bytes 1867784 | tf_op jit(solution)/shard_map/ppermute | solution.py:255
  66.0 9.6 %collective-permute-start.19 = (f32[608,128]{1,0:T(8,128)S(1)}, f32[608,128]{1,0:T(8,128)S(1)}, u32[]{:S(2)}, u32[]{:S(2)}) collective-permute-start(f32[608,128]{1,0:T(8,128)S(1)} %get-tuple-element.50), channel_id=1, source_target_pairs={{0,4},{4,0},{1,5},{5,1},{2,6},{6,2},{3,7},{7,3},{8,12},{12,8},{9,1... | collective-permute-start | bytes 933896 | tf_op jit(solution)/shard_map/ppermute | solution.py:283
  67.0 7.8 %collective-permute-start.20 = (f32[304,128]{1,0:T(8,128)S(1)}, f32[304,128]{1,0:T(8,128)S(1)}, u32[]{:S(2)}, u32[]{:S(2)}) collective-permute-start(f32[304,128]{1,0:T(8,128)S(1)} %get-tuple-element.46.refs_4_), channel_id=1, source_target_pairs={{0,16},{8,24},{16,0},{24,8},{1,17},{9,25},{17,1},{25,9},{2,18},{10... | collective-permute-start | bytes 466952 | tf_op jit(solution)/shard_map/ppermute | solution.py:276
  80.8 8.5 %collective-permute-start.25 = (f32[304,512]{1,0:T(8,128)S(1)}, f32[304,512]{1,0:T(8,128)S(1)}, u32[]{:S(2)}, u32[]{:S(2)}) collective-permute-start(f32[304,512]{1,0:T(8,128)S(1)} %get-tuple-element.58), channel_id=1, source_target_pairs={{0,2},{2,0},{1,3},{3,1},{4,6},{6,4},{5,7},{7,5},{8,10},{10,8},{9,1... | collective-permute-start | bytes 1867784 | tf_op jit(solution)/shard_map/ppermute | solution.py:248
  84.5 9.1 %collective-permute-start.22 = (f32[304,512]{1,0:T(8,128)S(1)}, f32[304,512]{1,0:T(8,128)S(1)}, u32[]{:S(2)}, u32[]{:S(2)}) collective-permute-start(f32[304,512]{1,0:T(8,128)S(1)} %get-tuple-element.53), channel_id=1, source_target_pairs={{0,2},{2,0},{1,3},{3,1},{4,6},{6,4},{5,7},{7,5},{8,10},{10,8},{9,1... | collective-permute-start | bytes 1867784 | tf_op jit(solution)/shard_map/ppermute | solution.py:248
  85.1 16.9 %collective-permute-start.27 = (f32[304,512]{1,0:T(8,128)S(1)}, f32[304,512]{1,0:T(8,128)S(1)}, u32[]{:S(2)}, u32[]{:S(2)}) collective-permute-start(f32[304,512]{1,0:T(8,128)S(1)} %bitcast.17), channel_id=1, source_target_pairs={{0,1},{1,0},{2,3},{3,2},{4,5},{5,4},{6,7},{7,6},{8,9},{9,8},{10,11... | collective-permute-start | bytes 1867784 | tf_op jit(solution)/shard_map/ppermute | solution.py:255
  86.6 27.0 %collective-permute-start.28 = (f32[304,512]{1,0:T(8,128)S(1)}, f32[304,512]{1,0:T(8,128)S(1)}, u32[]{:S(2)}, u32[]{:S(2)}) collective-permute-start(f32[304,512]{1,0:T(8,128)S(1)} %bitcast.15), channel_id=1, source_target_pairs={{0,3},{1,2},{2,1},{3,0},{4,7},{5,6},{6,5},{7,4},{8,11},{9,10},{10,... | collective-permute-start | bytes 1867784 | tf_op jit(solution)/shard_map/ppermute | solution.py:261
  86.6 27.0 %collective-permute-start.24 = (f32[304,512]{1,0:T(8,128)S(1)}, f32[304,512]{1,0:T(8,128)S(1)}, u32[]{:S(2)}, u32[]{:S(2)}) collective-permute-start(f32[304,512]{1,0:T(8,128)S(1)} %get-tuple-element.57), channel_id=1, source_target_pairs={{0,4},{4,8},{8,12},{12,16},{16,20},{20,24},{24,28},{1,5},{5,9},{9,... | collective-permute-start | bytes 1867784 | tf_op jit(solution)/shard_map/ppermute | solution.py:251
  89.3 27.4 %collective-permute-start.26 = (f32[304,512]{1,0:T(8,128)S(1)}, f32[304,512]{1,0:T(8,128)S(1)}, u32[]{:S(2)}, u32[]{:S(2)}) collective-permute-start(f32[304,512]{1,0:T(8,128)S(1)} %collective-permute-done.25), channel_id=1, source_target_pairs={{0,4},{4,8},{8,12},{12,16},{16,20},{20,24},{24,28},{1,5},{5,9},{9,... | collective-permute-start | bytes 1867784 | tf_op jit(solution)/shard_map/ppermute | solution.py:251
  (7 other events, 27.9 us)

commit v6 on v5

--- a/solution.py
+++ b/solution.py
@@ -250,6 +250,10 @@
     def onward(values):
         return lax.ppermute(values, ("line", "row"), [(i, i + 1) for i in range(lines * rows - 1)])
 
+    def onward_across(values):
+        route = [(2 * i + core, 2 * i + 3 - core) for i in range(lines * rows - 1) for core in range(2)]
+        return lax.ppermute(values, ("line", "row", "core"), route)
+
     def over_space(sent):
         return [
             lax.ppermute(sent[d - 1], "space", [(i, (i + d) % spaces) for i in range(spaces)])
@@ -272,10 +276,11 @@
     lag_blocks = call(spread_kernel, "spread", [small] * lags, [info, own_t, swap(kernels_t)])
 
     def shifted(own_block):
-        moved = [
-            lax.ppermute(own_block, "line", [(i, (i + shift) % lines) for i in range(lines)])
-            for shift in near_first(lines)[1:]
-        ]
+        held = {0: own_block, lines: own_block}
+        for shift in near_first(lines)[1:]:
+            step = 1 if shift <= lines - shift else -1
+            held[shift] = lax.ppermute(held[shift - step], "line", [(i, (i + step) % lines) for i in range(lines)])
+        moved = [held[shift] for shift in near_first(lines)[1:]]
         return [own_block], moved[:-1], moved[-1:]
 
     def handed(blocks):
@@ -303,9 +308,8 @@
         "own_halves",
         models + [small] + [jax.ShapeDtypeStruct((depth, block), F32)] * spaces,
         [info, own_model, lag_blocks[1]],
-        waits=row2 + near2,
-    )
-    joint2 = call(join_kernel, "join2", joint, [info, *near2]) if joint else []
+    )
+    joint2 = call(join_kernel, "join2", joint, [info, *near2], waits=row2) if joint else []
     high, low = call(
         other_halves_kernel,
         "other_halves",
@@ -373,7 +377,7 @@
         functools.partial(finish_kernel, spaces),
         "finish",
         [jax.ShapeDtypeStruct((sensors, block), F32)],
-        [info, d_keep, swap(d_chip), onward(next_same), onward(swap(next_cross)), *d_from, *d_from_cross],
+        [info, d_keep, swap(d_chip), onward(next_same), onward_across(next_cross), *d_from, *d_from_cross],
     )
     return result[None]
 

time: 119 us -> 110 us (0.924)
  waiting for transfers between devices: 54.4 us -> 48.7 us
  starting transfers between devices: 37.5 us -> 34.6 us
    ppermute x9 -> x10, waiting for transfers between devices: 29.9 us -> 22.4 us  [the longest x9 19.6 us: shifted(): lax.ppermute(held[shift - step], 'line', [(i, (i + step) % lines) for i i...]
    ppermute x9, waiting for transfers between devices: 1.39 us -> 5.58 us  [handed(): lax.ppermute(values, 'row', [(i, (i - off) % rows) for i in range(rows)])]
    ppermute x2 -> x1, waiting for transfers between devices: 3.11 us -> 0.01 us  [onward(): lax.ppermute(values, ('line', 'row'), [(i, i + 1) for i in range(lines *...]
    ppermute x2 -> x1, starting transfers between devices: 5.3 us -> 2.43 us  [onward(): lax.ppermute(values, ('line', 'row'), [(i, i + 1) for i in range(lines *...]
    ppermute x9, starting transfers between devices: 9.61 us -> 10.8 us  [handed(): lax.ppermute(values, 'row', [(i, (i - off) % rows) for i in range(rows)])]
    ppermute x9 -> x10, starting transfers between devices: 17.3 us -> 16.2 us  [the longest x9 14.3 us: shifted(): lax.ppermute(held[shift - step], 'line', [(i, (i + step) % lines) for i i...]
  transfers between devices with their start and end apart: 29 -> 28, of which waited for: 11 -> 12; matrix products, arithmetic and copies ran while one was open for 0% -> 0% of each run, Pallas kernels for 13% -> 14%
where the time goes in v6:
time: 110 us
  waiting for transfers between devices  48.7 us (44%)
  starting transfers between devices  34.6 us (31%)
  Pallas kernels  23.1 us (21%)
  local copies, waits for them, and re-layouts  3.21 us (3%)
    pallas_call x13, Pallas kernels, call(): pl.pallas_call(body, out_shape=shapes, in_specs=[SMEM_SPEC] + [VMEM_SPEC]...  23.1 us
    ppermute x9, waiting for transfers between devices, shifted(): lax.ppermute(held[shift - step], 'line', [(i, (i + step) % lines) for i i...  19.6 us
    ppermute x9, starting transfers between devices, shifted(): lax.ppermute(held[shift - step], 'line', [(i, (i + step) % lines) for i i...  14.3 us
    ppermute x1, waiting for transfers between devices, over_space_and_core(): lax.ppermute(sent[d - 1], ('core', 'space'), [(c * spaces + i, (1 - c) *...  12.4 us
    ppermute x9, starting transfers between devices, handed(): lax.ppermute(values, 'row', [(i, (i - off) % rows) for i in range(rows)])  10.8 us
    ppermute x3, waiting for transfers between devices, over_space(): lax.ppermute(sent[d - 1], 'space', [(i, (i + d) % spaces) for i in range(...  8.31 us
    ppermute x9, waiting for transfers between devices, handed(): lax.ppermute(values, 'row', [(i, (i - off) % rows) for i in range(rows)])  5.58 us
    unnamed x4, local copies, waits for them, and re-layouts  3.21 us
  transfers between devices with their start and end apart: 28, of which 12 were waited for; matrix products, arithmetic and copies ran while one was open for 0% of the time, Pallas kernels for 14%

profile of v6, /device:TPU:0, one launch (start us, length us, event | category | flops | bytes accessed | tf_op | source)
XLA Modules:
  0.0 109.9 jit_solution(17680721901308924896)
XLA Ops:
  3.0 2.2 %copy-done = f32[1,1024,1024]{2,1,0:T(8,128)S(1)} copy-done((f32[1,1024,1024]{2,1,0:T(8,128)S(1)}, f32[1,1024,1024]{2,1,0:T(8,128)}, u32[]{:S(2)}) %copy-start) | copy-done | bytes 4194328
  7.2 2.9 %collective-permute-start.3 = (f32[304,128]{1,0:T(8,128)S(1)}, f32[304,128]{1,0:T(8,128)S(1)}, u32[]{:S(2)}, u32[]{:S(2)}) collective-permute-start(f32[304,128]{1,0:T(8,128)S(1)} %get-tuple-element.41.refs_4_), channel_id=1, source_target_pairs={{0,8},{8,16},{16,24},{24,0},{1,9},{9,17},{17,25},{25,1},{2,10},{10... | collective-permute-start | bytes 466952 | tf_op jit(solution)/shard_map/ppermute | solution.py:282
  10.1 2.0 %collective-permute-start.4 = (f32[304,128]{1,0:T(8,128)S(1)}, f32[304,128]{1,0:T(8,128)S(1)}, u32[]{:S(2)}, u32[]{:S(2)}) collective-permute-start(f32[304,128]{1,0:T(8,128)S(1)} %get-tuple-element.41.refs_4_), channel_id=1, source_target_pairs={{0,24},{8,0},{16,8},{24,16},{1,25},{9,1},{17,9},{25,17},{2,26},{10... | collective-permute-start | bytes 466952 | tf_op jit(solution)/shard_map/ppermute | solution.py:282
  12.1 1.7 %collective-permute-start.6 = (f32[304,128]{1,0:T(8,128)S(1)}, f32[304,128]{1,0:T(8,128)S(1)}, u32[]{:S(2)}, u32[]{:S(2)}) collective-permute-start(f32[304,128]{1,0:T(8,128)S(1)} %get-tuple-element.41.refs_4_), channel_id=1, source_target_pairs={{0,4},{4,0},{1,5},{5,1},{2,6},{6,2},{3,7},{7,3},{8,12},{12,8},{9,1... | collective-permute-start | bytes 466952 | tf_op jit(solution)/shard_map/ppermute | solution.py:288
  13.9 3.1 %collective-permute-done.3.refs_1_.refs_5_ = f32[304,128]{1,0:T(8,128)S(1)} collective-permute-done((f32[304,128]{1,0:T(8,128)S(1)}, f32[304,128]{1,0:T(8,128)S(1)}, u32[]{:S(2)}, u32[]{:S(2)}) %collective-permute-start.3) | collective-permute-done | bytes 155680 | tf_op jit(solution)/shard_map/ppermute | solution.py:282
  17.0 2.2 %collective-permute-done.4.refs_2_.refs_6_ = f32[304,128]{1,0:T(8,128)S(1)} collective-permute-done((f32[304,128]{1,0:T(8,128)S(1)}, f32[304,128]{1,0:T(8,128)S(1)}, u32[]{:S(2)}, u32[]{:S(2)}) %collective-permute-start.4) | collective-permute-done | bytes 155680 | tf_op jit(solution)/shard_map/ppermute | solution.py:282
  21.9 2.5 %collective-permute-done.5.refs_7_ = f32[304,128]{1,0:T(8,128)S(1)} collective-permute-done((f32[304,128]{1,0:T(8,128)S(1)}, f32[304,128]{1,0:T(8,128)S(1)}, u32[]{:S(2)}, u32[]{:S(2)}) %collective-permute-start.5) | collective-permute-done | bytes 155680 | tf_op jit(solution)/shard_map/ppermute | solution.py:282
  24.4 3.8 %collective-permute-start.10 = (f32[304,128]{1,0:T(8,128)S(1)}, f32[304,128]{1,0:T(8,128)S(1)}, u32[]{:S(2)}, u32[]{:S(2)}) collective-permute-start(f32[304,128]{1,0:T(8,128)S(1)} %get-tuple-element.42.refs_4_), channel_id=1, source_target_pairs={{0,24},{8,0},{16,8},{24,16},{1,25},{9,1},{17,9},{25,17},{2,26},{10... | collective-permute-start | bytes 466952 | tf_op jit(solution)/shard_map/ppermute | solution.py:282
  30.8 2.7 %collective-permute-done.11.refs_13_.refs_4_.refs_8_ = f32[304,128]{1,0:T(8,128)S(1)} collective-permute-done((f32[304,128]{1,0:T(8,128)S(1)}, f32[304,128]{1,0:T(8,128)S(1)}, u32[]{:S(2)}, u32[]{:S(2)}) %collective-permute-start.11) | collective-permute-done | bytes 155680 | tf_op jit(solution)/shard_map/ppermute | solution.py:288
  33.5 1.7 %collective-permute-done.8.refs_10_ = f32[304,128]{1,0:T(8,128)S(1)} collective-permute-done((f32[304,128]{1,0:T(8,128)S(1)}, f32[304,128]{1,0:T(8,128)S(1)}, u32[]{:S(2)}, u32[]{:S(2)}) %collective-permute-start.8) | collective-permute-done | bytes 155680 | tf_op jit(solution)/shard_map/ppermute | solution.py:288
  35.2 1.7 %lead2.1 = (bf16[608,1024]{1,0:T(8,128)(2,1)S(1)}, f32[1,304,512]{2,1,0:T(8,128)S(1)}, f32[608,128]{1,0:T(8,128)S(1)}, f32[304,128]{1,0:T(8,128)S(1)}) custom-call(s32[4]{0:T(128)S(1)} %pad_add_fusion.refs_0_, bf16[2,2,1024,512]{3,2,1,0:T(8,128)(2,1)S(1)} %get-tuple-element.38.refs_1_, bf16[2,2,1024,512]{3,2,1,0:T(8,128)(2,1)S(1)} %get-tuple-element.39.refs_2_, ...), custom_call_target="tpu_custom_call" | custom-call | flops 956301312 | bytes 1 | tf_op jit(solution)/shard_map/lead2/pallas_call | solution.py:25
  41.7 5.3 %collective-permute-done.13.refs_7_ = f32[304,128]{1,0:T(8,128)S(1)} collective-permute-done((f32[304,128]{1,0:T(8,128)S(1)}, f32[304,128]{1,0:T(8,128)S(1)}, u32[]{:S(2)}, u32[]{:S(2)}) %collective-permute-start.13) | collective-permute-done | bytes 155680 | tf_op jit(solution)/shard_map/ppermute | solution.py:282
  47.6 3.8 %collective-permute-start.16 = (f32[304,128]{1,0:T(8,128)S(1)}, f32[304,128]{1,0:T(8,128)S(1)}, u32[]{:S(2)}, u32[]{:S(2)}) collective-permute-start(f32[304,128]{1,0:T(8,128)S(1)} %get-tuple-element.46.refs_4_), channel_id=1, source_target_pairs={{0,24},{8,0},{16,8},{24,16},{1,25},{9,1},{17,9},{25,17},{2,26},{10... | collective-permute-start | bytes 466952 | tf_op jit(solution)/shard_map/ppermute | solution.py:282
  52.9 3.6 %rest2.1 = (f32[304,512]{1,0:T(8,128)S(1)}, f32[2,304,512]{2,1,0:T(8,128)S(1)}) custom-call(s32[4]{0:T(128)S(1)} %pad_add_fusion.refs_0_, bf16[2,2,1024,512]{3,2,1,0:T(8,128)(2,1)S(1)} %get-tuple-element.38.refs_1_, bf16[2,2,1024,512]{3,2,1,0:T(8,128)(2,1)S(1)} %get-tuple-element.39.refs_2_, bf16[608,1024]{1,0:T(8,128)(2,1)S(1)} %get-tuple-element.43.refs_3_, ...), custom_call_target="tpu_custom_call" | custom-call | flops 2868903936 | bytes 1 | tf_op jit(solution)/shard_map/rest2/pallas_call | solution.py:25
  56.6 1.7 %lead1.1 = (bf16[608,1024]{1,0:T(8,128)(2,1)S(1)}, f32[1,304,512]{2,1,0:T(8,128)S(1)}, f32[608,128]{1,0:T(8,128)S(1)}) custom-call(s32[4]{0:T(128)S(1)} %pad_add_fusion.refs_0_, bf16[2,2,1024,512]{3,2,1,0:T(8,128)(2,1)S(1)} %get-tuple-element.38.refs_1_, bf16[2,2,1024,512]{3,2,1,0:T(8,128)(2,1)S(1)} %get-tuple-element.39.refs_2_, ...), custom_call_target="tpu_custom_call" | custom-call | flops 956301312 | bytes 1 | tf_op jit(solution)/shard_map/lead1/pallas_call | solution.py:25
  60.6 6.4 %collective-permute-done.20.refs_7_ = f32[304,128]{1,0:T(8,128)S(1)} collective-permute-done((f32[304,128]{1,0:T(8,128)S(1)}, f32[304,128]{1,0:T(8,128)S(1)}, u32[]{:S(2)}, u32[]{:S(2)}) %collective-permute-start.20) | collective-permute-done | bytes 155680 | tf_op jit(solution)/shard_map/ppermute | solution.py:282
  67.5 3.7 %rest1.1 = (f32[304,512]{1,0:T(8,128)S(1)}, f32[2,304,512]{2,1,0:T(8,128)S(1)}, f32[304,512]{1,0:T(8,128)S(1)}) custom-call(s32[4]{0:T(128)S(1)} %pad_add_fusion.refs_0_, bf16[2,2,1024,512]{3,2,1,0:T(8,128)(2,1)S(1)} %get-tuple-element.38.refs_1_, bf16[2,2,1024,512]{3,2,1,0:T(8,128)(2,1)S(1)} %get-tuple-element.39.refs_2_, ...), custom_call_target="tpu_custom_call" | custom-call | flops 2868903936 | bytes 1 | tf_op jit(solution)/shard_map/rest1/pallas_call | solution.py:25
  72.2 3.7 %lead0.1 = (bf16[608,1024]{1,0:T(8,128)(2,1)S(1)}, f32[1,304,512]{2,1,0:T(8,128)S(1)}, f32[1,304,512]{2,1,0:T(8,128)S(1)}, f32[304,512]{1,0:T(8,128)S(1)}) custom-call(s32[4]{0:T(128)S(1)} %pad_add_fusion.refs_0_, bf16[2,2,1024,512]{3,2,1,0:T(8,128)(2,1)S(1)} %get-tuple-element.38.refs_1_, bf16[2,2,1024,512]{3,2,1,0:T(8,128)(2,1)S(1)} %get-tuple-element.39.refs_2_, ...), custom_call_target="tpu_custom_call" | custom-call | flops 2868903936 | bytes 1 | tf_op jit(solution)/shard_map/lead0/pallas_call | solution.py:25
  78.5 2.4 %collective-permute-start.24 = (f32[304,512]{1,0:T(8,128)S(1)}, f32[304,512]{1,0:T(8,128)S(1)}, u32[]{:S(2)}, u32[]{:S(2)}) collective-permute-start(f32[304,512]{1,0:T(8,128)S(1)} %get-tuple-element.57), channel_id=1, source_target_pairs={{0,4},{4,8},{8,12},{12,16},{16,20},{20,24},{24,28},{1,5},{5,9},{9,... | collective-permute-start | bytes 1867784 | tf_op jit(solution)/shard_map/ppermute | solution.py:251
  81.0 1.9 %collective-permute-start.25 = (f32[304,512]{1,0:T(8,128)S(1)}, f32[304,512]{1,0:T(8,128)S(1)}, u32[]{:S(2)}, u32[]{:S(2)}) collective-permute-start(f32[304,512]{1,0:T(8,128)S(1)} %get-tuple-element.58), channel_id=1, source_target_pairs={{0,6},{2,4},{4,10},{6,8},{8,14},{10,12},{12,18},{14,16},{16,22},{1... | collective-permute-start | bytes 1867784 | tf_op jit(solution)/shard_map/ppermute | solution.py:255
  84.6 8.3 %collective-permute-done.26.refs_5_ = f32[304,512]{1,0:T(8,128)S(1)} collective-permute-done((f32[304,512]{1,0:T(8,128)S(1)}, f32[304,512]{1,0:T(8,128)S(1)}, u32[]{:S(2)}, u32[]{:S(2)}) %collective-permute-start.26) | collective-permute-done | bytes 622624 | tf_op jit(solution)/shard_map/ppermute | solution.py:259
  92.9 12.4 %collective-permute-done.27.refs_6_ = f32[304,512]{1,0:T(8,128)S(1)} collective-permute-done((f32[304,512]{1,0:T(8,128)S(1)}, f32[304,512]{1,0:T(8,128)S(1)}, u32[]{:S(2)}, u32[]{:S(2)}) %collective-permute-start.27) | collective-permute-done | bytes 622624 | tf_op jit(solution)/shard_map/ppermute | solution.py:265
  105.3 2.8 %collective-permute-done.25.refs_4_ = f32[304,512]{1,0:T(8,128)S(1)} collective-permute-done((f32[304,512]{1,0:T(8,128)S(1)}, f32[304,512]{1,0:T(8,128)S(1)}, u32[]{:S(2)}, u32[]{:S(2)}) %collective-permute-start.25) | collective-permute-done | bytes 622624 | tf_op jit(solution)/shard_map/ppermute | solution.py:255
  108.1 1.8 %finish.1 = f32[600,512]{1,0:T(8,128)} custom-call(s32[4]{0:T(128)S(1)} %pad_add_fusion.refs_0_, f32[304,512]{1,0:T(8,128)S(1)} %last.1.refs_1_, f32[304,512]{1,0:T(8,128)S(1)} %collective-permute-done.22.refs_2_, f32[304,512]{1,0:T(8,128)S(1)} %collective-permute-done.24.refs_3_, f32[304,512]{1,0:T(8,128)S(1)} %collective-permute-done.25.refs_4_, ...), custom_call_target="tpu_custom_call" | custom-call | bytes 1 | tf_op jit(solution)/shard_map/finish/pallas_call | solution.py:25
  (50 shorter events, 25.2 us)
Async XLA Ops:
  6.6 17.9 %collective-permute-start.1 = (f32[1024,512]{1,0:T(8,128)S(1)}, f32[1024,512]{1,0:T(8,128)S(1)}, u32[]{:S(2)}, u32[]{:S(2)}) collective-permute-start(f32[1024,512]{1,0:T(8,128)S(1)} %get-tuple-element.36), channel_id=1, source_target_pairs={{0,2},{2,0},{1,3},{3,1},{4,6},{6,4},{5,7},{7,5},{8,10},{10,8},{9,1... | collective-permute-start | bytes 6291464 | tf_op jit(solution)/shard_map/ppermute | solution.py:248
  7.0 21.2 %collective-permute-start.2 = (f32[1024,512]{1,0:T(8,128)S(1)}, f32[1024,512]{1,0:T(8,128)S(1)}, u32[]{:S(2)}, u32[]{:S(2)}) collective-permute-start(f32[1024,512]{1,0:T(8,128)S(1)} %get-tuple-element.37), channel_id=1, source_target_pairs={{0,2},{2,0},{1,3},{3,1},{4,6},{6,4},{5,7},{7,5},{8,10},{10,8},{9,1... | collective-permute-start | bytes 6291464 | tf_op jit(solution)/shard_map/ppermute | solution.py:248
  7.2 9.8 %collective-permute-start.3 = (f32[304,128]{1,0:T(8,128)S(1)}, f32[304,128]{1,0:T(8,128)S(1)}, u32[]{:S(2)}, u32[]{:S(2)}) collective-permute-start(f32[304,128]{1,0:T(8,128)S(1)} %get-tuple-element.41.refs_4_), channel_id=1, source_target_pairs={{0,8},{8,16},{16,24},{24,0},{1,9},{9,17},{17,25},{25,1},{2,10},{10... | collective-permute-start | bytes 466952 | tf_op jit(solution)/shard_map/ppermute | solution.py:282
  10.1 9.1 %collective-permute-start.4 = (f32[304,128]{1,0:T(8,128)S(1)}, f32[304,128]{1,0:T(8,128)S(1)}, u32[]{:S(2)}, u32[]{:S(2)}) collective-permute-start(f32[304,128]{1,0:T(8,128)S(1)} %get-tuple-element.41.refs_4_), channel_id=1, source_target_pairs={{0,24},{8,0},{16,8},{24,16},{1,25},{9,1},{17,9},{25,17},{2,26},{10... | collective-permute-start | bytes 466952 | tf_op jit(solution)/shard_map/ppermute | solution.py:282
  12.1 7.1 %collective-permute-start.6 = (f32[304,128]{1,0:T(8,128)S(1)}, f32[304,128]{1,0:T(8,128)S(1)}, u32[]{:S(2)}, u32[]{:S(2)}) collective-permute-start(f32[304,128]{1,0:T(8,128)S(1)} %get-tuple-element.41.refs_4_), channel_id=1, source_target_pairs={{0,4},{4,0},{1,5},{5,1},{2,6},{6,2},{3,7},{7,3},{8,12},{12,8},{9,1... | collective-permute-start | bytes 466952 | tf_op jit(solution)/shard_map/ppermute | solution.py:288
  17.0 7.5 %collective-permute-start.5 = (f32[304,128]{1,0:T(8,128)S(1)}, f32[304,128]{1,0:T(8,128)S(1)}, u32[]{:S(2)}, u32[]{:S(2)}) collective-permute-start(f32[304,128]{1,0:T(8,128)S(1)} %collective-permute-done.3.refs_1_.refs_5_), channel_id=1, source_target_pairs={{0,8},{8,16},{16,24},{24,0},{1,9},{9,17},{17,25},{25,1},{2,10},{10... | collective-permute-start | bytes 466952 | tf_op jit(solution)/shard_map/ppermute | solution.py:282
  19.8 15.4 %collective-permute-start.7 = (f32[608,128]{1,0:T(8,128)S(1)}, f32[608,128]{1,0:T(8,128)S(1)}, u32[]{:S(2)}, u32[]{:S(2)}) collective-permute-start(f32[608,128]{1,0:T(8,128)S(1)} %join2.1), channel_id=1, source_target_pairs={{0,4},{4,0},{1,5},{5,1},{2,6},{6,2},{3,7},{7,3},{8,12},{12,8},{9,1... | collective-permute-start | bytes 933896 | tf_op jit(solution)/shard_map/ppermute | solution.py:288
  21.4 12.1 %collective-permute-start.11 = (f32[304,128]{1,0:T(8,128)S(1)}, f32[304,128]{1,0:T(8,128)S(1)}, u32[]{:S(2)}, u32[]{:S(2)}) collective-permute-start(f32[304,128]{1,0:T(8,128)S(1)} %get-tuple-element.42.refs_4_), channel_id=1, source_target_pairs={{0,4},{4,0},{1,5},{5,1},{2,6},{6,2},{3,7},{7,3},{8,12},{12,8},{9,1... | collective-permute-start | bytes 466952 | tf_op jit(solution)/shard_map/ppermute | solution.py:288
  24.4 9.1 %collective-permute-start.9 = (f32[304,128]{1,0:T(8,128)S(1)}, f32[304,128]{1,0:T(8,128)S(1)}, u32[]{:S(2)}, u32[]{:S(2)}) collective-permute-start(f32[304,128]{1,0:T(8,128)S(1)} %get-tuple-element.42.refs_4_), channel_id=1, source_target_pairs={{0,8},{8,16},{16,24},{24,0},{1,9},{9,17},{17,25},{25,1},{2,10},{10... | collective-permute-start | bytes 466952 | tf_op jit(solution)/shard_map/ppermute | solution.py:282
  24.4 9.1 %collective-permute-start.10 = (f32[304,128]{1,0:T(8,128)S(1)}, f32[304,128]{1,0:T(8,128)S(1)}, u32[]{:S(2)}, u32[]{:S(2)}) collective-permute-start(f32[304,128]{1,0:T(8,128)S(1)} %get-tuple-element.42.refs_4_), channel_id=1, source_target_pairs={{0,24},{8,0},{16,8},{24,16},{1,25},{9,1},{17,9},{25,17},{2,26},{10... | collective-permute-start | bytes 466952 | tf_op jit(solution)/shard_map/ppermute | solution.py:282
  37.0 19.7 %collective-permute-start.17 = (f32[304,512]{1,0:T(8,128)S(1)}, f32[304,512]{1,0:T(8,128)S(1)}, u32[]{:S(2)}, u32[]{:S(2)}) collective-permute-start(f32[304,512]{1,0:T(8,128)S(1)} %bitcast.15), channel_id=1, source_target_pairs={{0,1},{1,0},{2,3},{3,2},{4,5},{5,4},{6,7},{7,6},{8,9},{9,8},{10,11... | collective-permute-start | bytes 1867784 | tf_op jit(solution)/shard_map/ppermute | solution.py:259
  38.5 12.9 %collective-permute-start.12 = (f32[608,128]{1,0:T(8,128)S(1)}, f32[608,128]{1,0:T(8,128)S(1)}, u32[]{:S(2)}, u32[]{:S(2)}) collective-permute-start(f32[608,128]{1,0:T(8,128)S(1)} %get-tuple-element.44), channel_id=1, source_target_pairs={{0,4},{4,0},{1,5},{5,1},{2,6},{6,2},{3,7},{7,3},{8,12},{12,8},{9,1... | collective-permute-start | bytes 933896 | tf_op jit(solution)/shard_map/ppermute | solution.py:288
  40.0 7.0 %collective-permute-start.13 = (f32[304,128]{1,0:T(8,128)S(1)}, f32[304,128]{1,0:T(8,128)S(1)}, u32[]{:S(2)}, u32[]{:S(2)}) collective-permute-start(f32[304,128]{1,0:T(8,128)S(1)} %collective-permute-done.9.refs_11_.refs_5_), channel_id=1, source_target_pairs={{0,8},{8,16},{16,24},{24,0},{1,9},{9,17},{17,25},{25,1},{2,10},{10... | collective-permute-start | bytes 466952 | tf_op jit(solution)/shard_map/ppermute | solution.py:282
  47.1 9.4 %collective-permute-start.14 = (f32[304,128]{1,0:T(8,128)S(1)}, f32[304,128]{1,0:T(8,128)S(1)}, u32[]{:S(2)}, u32[]{:S(2)}) collective-permute-start(f32[304,128]{1,0:T(8,128)S(1)} %collective-permute-done.13.refs_7_), channel_id=1, source_target_pairs={{0,4},{4,0},{1,5},{5,1},{2,6},{6,2},{3,7},{7,3},{8,12},{12,8},{9,1... | collective-permute-start | bytes 466952 | tf_op jit(solution)/shard_map/ppermute | solution.py:288
  47.6 9.0 %collective-permute-start.15 = (f32[304,128]{1,0:T(8,128)S(1)}, f32[304,128]{1,0:T(8,128)S(1)}, u32[]{:S(2)}, u32[]{:S(2)}) collective-permute-start(f32[304,128]{1,0:T(8,128)S(1)} %get-tuple-element.46.refs_4_), channel_id=1, source_target_pairs={{0,8},{8,16},{16,24},{24,0},{1,9},{9,17},{17,25},{25,1},{2,10},{10... | collective-permute-start | bytes 466952 | tf_op jit(solution)/shard_map/ppermute | solution.py:282
  47.6 9.0 %collective-permute-start.16 = (f32[304,128]{1,0:T(8,128)S(1)}, f32[304,128]{1,0:T(8,128)S(1)}, u32[]{:S(2)}, u32[]{:S(2)}) collective-permute-start(f32[304,128]{1,0:T(8,128)S(1)} %get-tuple-element.46.refs_4_), channel_id=1, source_target_pairs={{0,24},{8,0},{16,8},{24,16},{1,25},{9,1},{17,9},{25,17},{2,26},{10... | collective-permute-start | bytes 466952 | tf_op jit(solution)/shard_map/ppermute | solution.py:282
  58.4 9.1 %collective-permute-start.19 = (f32[608,128]{1,0:T(8,128)S(1)}, f32[608,128]{1,0:T(8,128)S(1)}, u32[]{:S(2)}, u32[]{:S(2)}) collective-permute-start(f32[608,128]{1,0:T(8,128)S(1)} %get-tuple-element.50), channel_id=1, source_target_pairs={{0,4},{4,0},{1,5},{5,1},{2,6},{6,2},{3,7},{7,3},{8,12},{12,8},{9,1... | collective-permute-start | bytes 933896 | tf_op jit(solution)/shard_map/ppermute | solution.py:288
  60.0 7.0 %collective-permute-start.20 = (f32[304,128]{1,0:T(8,128)S(1)}, f32[304,128]{1,0:T(8,128)S(1)}, u32[]{:S(2)}, u32[]{:S(2)}) collective-permute-start(f32[304,128]{1,0:T(8,128)S(1)} %collective-permute-done.15.refs_11_.refs_5_), channel_id=1, source_target_pairs={{0,8},{8,16},{16,24},{24,0},{1,9},{9,17},{17,25},{25,1},{2,10},{10... | collective-permute-start | bytes 466952 | tf_op jit(solution)/shard_map/ppermute | solution.py:282
  60.0 17.9 %collective-permute-start.23 = (f32[304,512]{1,0:T(8,128)S(1)}, f32[304,512]{1,0:T(8,128)S(1)}, u32[]{:S(2)}, u32[]{:S(2)}) collective-permute-start(f32[304,512]{1,0:T(8,128)S(1)} %bitcast.14), channel_id=1, source_target_pairs={{0,1},{1,0},{2,3},{3,2},{4,5},{5,4},{6,7},{7,6},{8,9},{9,8},{10,11... | collective-permute-start | bytes 1867784 | tf_op jit(solution)/shard_map/ppermute | solution.py:259
  75.9 8.7 %collective-permute-start.22 = (f32[304,512]{1,0:T(8,128)S(1)}, f32[304,512]{1,0:T(8,128)S(1)}, u32[]{:S(2)}, u32[]{:S(2)}) collective-permute-start(f32[304,512]{1,0:T(8,128)S(1)} %get-tuple-element.53), channel_id=1, source_target_pairs={{0,2},{2,0},{1,3},{3,1},{4,6},{6,4},{5,7},{7,5},{8,10},{10,8},{9,1... | collective-permute-start | bytes 1867784 | tf_op jit(solution)/shard_map/ppermute | solution.py:248
  76.0 16.9 %collective-permute-start.26 = (f32[304,512]{1,0:T(8,128)S(1)}, f32[304,512]{1,0:T(8,128)S(1)}, u32[]{:S(2)}, u32[]{:S(2)}) collective-permute-start(f32[304,512]{1,0:T(8,128)S(1)} %bitcast.17), channel_id=1, source_target_pairs={{0,1},{1,0},{2,3},{3,2},{4,5},{5,4},{6,7},{7,6},{8,9},{9,8},{10,11... | collective-permute-start | bytes 1867784 | tf_op jit(solution)/shard_map/ppermute | solution.py:259
  76.7 28.6 %collective-permute-start.27 = (f32[304,512]{1,0:T(8,128)S(1)}, f32[304,512]{1,0:T(8,128)S(1)}, u32[]{:S(2)}, u32[]{:S(2)}) collective-permute-start(f32[304,512]{1,0:T(8,128)S(1)} %bitcast.16), channel_id=1, source_target_pairs={{0,3},{1,2},{2,1},{3,0},{4,7},{5,6},{6,5},{7,4},{8,11},{9,10},{10,... | collective-permute-start | bytes 1867784 | tf_op jit(solution)/shard_map/ppermute | solution.py:265
  78.5 26.7 %collective-permute-start.24 = (f32[304,512]{1,0:T(8,128)S(1)}, f32[304,512]{1,0:T(8,128)S(1)}, u32[]{:S(2)}, u32[]{:S(2)}) collective-permute-start(f32[304,512]{1,0:T(8,128)S(1)} %get-tuple-element.57), channel_id=1, source_target_pairs={{0,4},{4,8},{8,12},{12,16},{16,20},{20,24},{24,28},{1,5},{5,9},{9,... | collective-permute-start | bytes 1867784 | tf_op jit(solution)/shard_map/ppermute | solution.py:251
  81.0 27.1 %collective-permute-start.25 = (f32[304,512]{1,0:T(8,128)S(1)}, f32[304,512]{1,0:T(8,128)S(1)}, u32[]{:S(2)}, u32[]{:S(2)}) collective-permute-start(f32[304,512]{1,0:T(8,128)S(1)} %get-tuple-element.58), channel_id=1, source_target_pairs={{0,6},{2,4},{4,10},{6,8},{8,14},{10,12},{12,18},{14,16},{16,22},{1... | collective-permute-start | bytes 1867784 | tf_op jit(solution)/shard_map/ppermute | solution.py:255
  (6 other events, 22.8 us)

commit v7 on v6

--- a/solution.py
+++ b/solution.py
@@ -130,43 +130,41 @@
     return blocks, outputs
 
 
-def rest_two_kernel(info, high, low, pair, keep, other):
+def lead_one_kernel(lines, count, info, high, low, pair2, *refs):
+    blocks, (pair, send) = lead(lines, count, refs)
+    for turn in range(1, high.shape[1]):
+
+        def put(columns, total):
+            send[turn - 1, :, columns] = total
+
+        def add(columns, total):
+            send[turn - 1, :, columns] += total
+
+        times(pair2, high, low, 0, turn, put)
+        times(pair, high, low, 1, turn, add)
+
+
+def rest_one_kernel(info, high, low, pair2, pair1, *refs):
+    (*from1, keep, other, total1) = refs
+
+    def put_total(columns, total):
+        total1[:, columns] = functools.reduce(jnp.add, [total] + [part[:, columns] for part in from1])
+
     def put_keep(columns, total):
         keep[:, columns] = total
 
-    times(pair, high, low, 1, 0, put_keep)
+    def add_keep(columns, total):
+        keep[:, columns] += total
+
+    times(pair2, high, low, 1, 0, put_total)
+    times(pair2, high, low, 0, 0, put_keep)
+    times(pair1, high, low, 1, 0, add_keep)
     for turn in range(high.shape[1]):
 
         def put(columns, total):
             other[turn, :, columns] = total
 
-        times(pair, high, low, 0, turn, put)
-
-
-def rest_one_kernel(info, high, low, pair, added, keep1, *refs):
-    (*from1, keep, other, total1) = refs
-    total1[...] = functools.reduce(jnp.add, [keep1[...]] + [part[...] for part in from1])
-
-    def put_keep(columns, total):
-        keep[:, columns] = total + added[0, :, columns]
-
-    times(pair, high, low, 1, 0, put_keep)
-    for turn in range(high.shape[1]):
-
-        def put(columns, total):
-            other[turn, :, columns] = total
-
-        times(pair, high, low, 0, turn, put)
-
-
-def lead_one_kernel(lines, count, info, high, low, added, *refs):
-    blocks, (pair, send) = lead(lines, count, refs)
-    for turn in range(1, high.shape[1]):
-
-        def put(columns, total):
-            send[turn - 1, :, columns] = total + added[turn, :, columns]
-
-        times(pair, high, low, 1, turn, put)
+        times(pair1, high, low, 0, turn, put)
 
 
 def both_times(info, high, low, pair, added, turn, own_put, other_put):
@@ -225,12 +223,13 @@
 def finish_kernel(spaces, info, d_keep, d_chip, next_own, next_other, *refs):
     (*parts, out_ref) = refs
     first = info[0] == 0
-    sensors, half = out_ref.shape[0], d_keep.shape[0]
-    own = d_keep[...] + next_own[...]
-    other = d_chip[...] + next_other[...]
+    (sensors, step), half = out_ref.shape, d_keep.shape[0]
+    columns = pl.ds(pl.multiple_of(pl.program_id(0) * step, step), step)
+    own = d_keep[:, columns] + next_own[:, columns]
+    other = d_chip[:, columns] + next_other[:, columns]
     for straight, cross in zip(parts[: spaces - 1], parts[spaces - 1 :]):
-        own = own + straight[...]
-        other = other + cross[...]
+        own = own + straight[:, columns]
+        other = other + cross[:, columns]
     out_ref[:half, :] = jnp.where(first, own, other)
     out_ref[half:, :] = jnp.where(first, other, own)[2 * half - sensors :, :]
 
@@ -339,28 +338,26 @@
         flops=flops,
     )
     from1 = over_space(send1)
-    line1, row1 = gathered(own1, near1, far1, row_own1, joint1)
-    keep1, early2 = call(
-        rest_two_kernel, "rest2", [one, whole], [info, high, low, pair2], waits=row1[:2], flops=3 * flops
-    )
+    row_near1 = handed(joint1)
+    passed1 = list(call(join_kernel, "pass1", [small], [info, *far1], waits=row_near1)) if far1 else []
+    line1, row1 = own1 + near1 + far1, ordered(row_own1, row_near1, handed(passed1))
     own0, near0, far0 = shifted(block0)
-    row_own0 = handed(own0)
     pair1, send0, *joint0 = call(
-        functools.partial(lead_one_kernel, lines, between),
+        functools.partial(lead_one_kernel, lines, 1 + len(near0)),
         "lead1",
-        [pair, sent] + joint,
-        [info, high, low, early2, *line1, *row1, *near0],
-        waits=from1 + row_own0,
-        flops=flops,
+        [pair, sent, jax.ShapeDtypeStruct((half * (1 + len(near0)), 2 * width), F32)],
+        [info, high, low, pair2, *line1, *row1, *own0, *near0],
+        waits=from1,
+        flops=2 * flops,
     )
     from0 = over_space(send0)
-    line0, row0 = gathered(own0, near0, far0, row_own0, joint0)
+    line0, row0 = gathered(own0, near0, far0, [], joint0)
     keep0, early1, total1 = call(
         rest_one_kernel,
         "rest1",
         [one, whole, one],
-        [info, high, low, pair1, early2, keep1, *from1],
-        waits=row0[:2],
+        [info, high, low, pair2, pair1, *from1],
+        waits=row0[:1],
         flops=3 * flops,
     )
     pair0, d_send, d_cross, d_chip = call(
@@ -373,12 +370,17 @@
     d_from, d_from_cross = over_space(d_send), over_space_and_core(d_cross)
     next_same, next_cross = call(totals_kernel, "totals", [one, one], [info, total1, keep0, *from0], waits=row0[-1:])
     (d_keep,) = call(last_kernel, "last", [one], [info, high, low, pair0, early1], flops=flops)
-    (result,) = call(
+    operands = [d_keep, swap(d_chip), onward(next_same), onward_across(next_cross), *d_from, *d_from_cross]
+    step = block if block % 128 else 128
+    result = pl.pallas_call(
         functools.partial(finish_kernel, spaces),
-        "finish",
-        [jax.ShapeDtypeStruct((sensors, block), F32)],
-        [info, d_keep, swap(d_chip), onward(next_same), onward_across(next_cross), *d_from, *d_from_cross],
-    )
+        grid=(block // step,),
+        out_shape=jax.ShapeDtypeStruct((sensors, block), F32),
+        in_specs=[SMEM_SPEC] + [VMEM_SPEC] * len(operands),
+        out_specs=pl.BlockSpec((sensors, step), lambda at: (0, at)),
+        compiler_params=pltpu.CompilerParams(vmem_limit_bytes=VMEM_LIMIT),
+        name="finish",
+    )(info, *operands)
     return result[None]
 
 

time: 110 us -> 113 us (1.027); the launches traced: 110 us -> 111 us
  starting transfers between devices: 34.6 us -> 36.3 us
    ppermute x9 -> x8, waiting for transfers between devices: 5.58 us -> 8.13 us  [handed(): lax.ppermute(values, 'row', [(i, (i - off) % rows) for i in range(rows)])]
    pallas_call x0 -> x1, Pallas kernels: none -> 2.38 us  [on_device(): pl.pallas_call(functools.partial(finish_kernel, spaces), grid=(block // s...]
    pallas_call x13 -> x12, Pallas kernels: 23.1 us -> 21 us  [call(): pl.pallas_call(body, out_shape=shapes, in_specs=[SMEM_SPEC] + [VMEM_SPEC]...]
    ppermute x3, waiting for transfers between devices: 8.31 us -> 6.34 us  [over_space(): lax.ppermute(sent[d - 1], 'space', [(i, (i + d) % spaces) for i in range(...]
    ppermute x1, starting transfers between devices: 1.87 us -> 3.68 us  [onward_across(): return lax.ppermute(values, ('line', 'row', 'core'), route)]
    ppermute x9 -> x8, starting transfers between devices: 10.8 us -> 9.53 us  [handed(): lax.ppermute(values, 'row', [(i, (i - off) % rows) for i in range(rows)])]
    ppermute x9, waiting for transfers between devices: 19.6 us -> 18.4 us  [shifted(): lax.ppermute(held[shift - step], 'line', [(i, (i + step) % lines) for i i...]
  transfers between devices with their start and end apart: 28 -> 27, of which waited for: 12 -> 14; matrix products, arithmetic and copies ran while one was open for 0% -> 0% of each run, Pallas kernels for 14% -> 13%
where the time goes in v7:
time: 113 us; the launch traced here: 111 us
  waiting for transfers between devices  48.2 us (43%)
  starting transfers between devices  36.3 us (32%)
  Pallas kernels  23.4 us (21%)
  local copies, waits for them, and re-layouts  3.21 us (3%)
    pallas_call x12, Pallas kernels, call(): pl.pallas_call(body, out_shape=shapes, in_specs=[SMEM_SPEC] + [VMEM_SPEC]...  21 us
    ppermute x9, waiting for transfers between devices, shifted(): lax.ppermute(held[shift - step], 'line', [(i, (i + step) % lines) for i i...  18.4 us
    ppermute x9, starting transfers between devices, shifted(): lax.ppermute(held[shift - step], 'line', [(i, (i + step) % lines) for i i...  15 us
    ppermute x1, waiting for transfers between devices, over_space_and_core(): lax.ppermute(sent[d - 1], ('core', 'space'), [(c * spaces + i, (1 - c) *...  12.4 us
    ppermute x8, starting transfers between devices, handed(): lax.ppermute(values, 'row', [(i, (i - off) % rows) for i in range(rows)])  9.53 us
    ppermute x8, waiting for transfers between devices, handed(): lax.ppermute(values, 'row', [(i, (i - off) % rows) for i in range(rows)])  8.13 us
    ppermute x3, waiting for transfers between devices, over_space(): lax.ppermute(sent[d - 1], 'space', [(i, (i + d) % spaces) for i in range(...  6.34 us
    ppermute x3, starting transfers between devices, over_space(): lax.ppermute(sent[d - 1], 'space', [(i, (i + d) % spaces) for i in range(...  3.7 us
  transfers between devices with their start and end apart: 27, of which 14 were waited for; matrix products, arithmetic and copies ran while one was open for 0% of the time, Pallas kernels for 13%

profile of v7, /device:TPU:0, one launch (start us, length us, event | category | flops | bytes accessed | tf_op | source)
XLA Modules:
  0.0 111.3 jit_solution(17804711998229823090)
XLA Ops:
  3.0 2.2 %copy-done = f32[1,1024,1024]{2,1,0:T(8,128)S(1)} copy-done((f32[1,1024,1024]{2,1,0:T(8,128)S(1)}, f32[1,1024,1024]{2,1,0:T(8,128)}, u32[]{:S(2)}) %copy-start) | copy-done | bytes 4194328
  7.1 2.9 %collective-permute-start.3 = (f32[304,128]{1,0:T(8,128)S(1)}, f32[304,128]{1,0:T(8,128)S(1)}, u32[]{:S(2)}, u32[]{:S(2)}) collective-permute-start(f32[304,128]{1,0:T(8,128)S(1)} %get-tuple-element.39.refs_4_), channel_id=1, source_target_pairs={{0,8},{8,16},{16,24},{24,0},{1,9},{9,17},{17,25},{25,1},{2,10},{10... | collective-permute-start | bytes 466952 | tf_op jit(solution)/shard_map/ppermute | solution.py:281
  10.1 2.0 %collective-permute-start.4 = (f32[304,128]{1,0:T(8,128)S(1)}, f32[304,128]{1,0:T(8,128)S(1)}, u32[]{:S(2)}, u32[]{:S(2)}) collective-permute-start(f32[304,128]{1,0:T(8,128)S(1)} %get-tuple-element.39.refs_4_), channel_id=1, source_target_pairs={{0,24},{8,0},{16,8},{24,16},{1,25},{9,1},{17,9},{25,17},{2,26},{10... | collective-permute-start | bytes 466952 | tf_op jit(solution)/shard_map/ppermute | solution.py:281
  12.1 1.7 %collective-permute-start.6 = (f32[304,128]{1,0:T(8,128)S(1)}, f32[304,128]{1,0:T(8,128)S(1)}, u32[]{:S(2)}, u32[]{:S(2)}) collective-permute-start(f32[304,128]{1,0:T(8,128)S(1)} %get-tuple-element.39.refs_4_), channel_id=1, source_target_pairs={{0,4},{4,0},{1,5},{5,1},{2,6},{6,2},{3,7},{7,3},{8,12},{12,8},{9,1... | collective-permute-start | bytes 466952 | tf_op jit(solution)/shard_map/ppermute | solution.py:287
  13.8 3.1 %collective-permute-done.3.refs_1_.refs_5_ = f32[304,128]{1,0:T(8,128)S(1)} collective-permute-done((f32[304,128]{1,0:T(8,128)S(1)}, f32[304,128]{1,0:T(8,128)S(1)}, u32[]{:S(2)}, u32[]{:S(2)}) %collective-permute-start.3) | collective-permute-done | bytes 155680 | tf_op jit(solution)/shard_map/ppermute | solution.py:281
  17.0 2.2 %collective-permute-done.4.refs_2_.refs_6_ = f32[304,128]{1,0:T(8,128)S(1)} collective-permute-done((f32[304,128]{1,0:T(8,128)S(1)}, f32[304,128]{1,0:T(8,128)S(1)}, u32[]{:S(2)}, u32[]{:S(2)}) %collective-permute-start.4) | collective-permute-done | bytes 155680 | tf_op jit(solution)/shard_map/ppermute | solution.py:281
  22.5 1.9 %collective-permute-done.5.refs_7_ = f32[304,128]{1,0:T(8,128)S(1)} collective-permute-done((f32[304,128]{1,0:T(8,128)S(1)}, f32[304,128]{1,0:T(8,128)S(1)}, u32[]{:S(2)}, u32[]{:S(2)}) %collective-permute-start.5) | collective-permute-done | bytes 155680 | tf_op jit(solution)/shard_map/ppermute | solution.py:281
  24.4 3.3 %collective-permute-start.10 = (f32[304,128]{1,0:T(8,128)S(1)}, f32[304,128]{1,0:T(8,128)S(1)}, u32[]{:S(2)}, u32[]{:S(2)}) collective-permute-start(f32[304,128]{1,0:T(8,128)S(1)} %get-tuple-element.40.refs_4_), channel_id=1, source_target_pairs={{0,24},{8,0},{16,8},{24,16},{1,25},{9,1},{17,9},{25,17},{2,26},{10... | collective-permute-start | bytes 466952 | tf_op jit(solution)/shard_map/ppermute | solution.py:281
  31.2 2.3 %collective-permute-done.11.refs_13_.refs_8_ = f32[304,128]{1,0:T(8,128)S(1)} collective-permute-done((f32[304,128]{1,0:T(8,128)S(1)}, f32[304,128]{1,0:T(8,128)S(1)}, u32[]{:S(2)}, u32[]{:S(2)}) %collective-permute-start.11) | collective-permute-done | bytes 155680 | tf_op jit(solution)/shard_map/ppermute | solution.py:287
  35.2 1.7 %lead2.1 = (bf16[608,1024]{1,0:T(8,128)(2,1)S(1)}, f32[1,304,512]{2,1,0:T(8,128)S(1)}, f32[608,128]{1,0:T(8,128)S(1)}, f32[304,128]{1,0:T(8,128)S(1)}) custom-call(s32[4]{0:T(128)S(1)} %pad_add_fusion.refs_0_.info, bf16[2,2,1024,512]{3,2,1,0:T(8,128)(2,1)S(1)} %get-tuple-element.36.refs_1_, bf16[2,2,1024,512]{3,2,1,0:T(8,128)(2,1)S(1)} %get-tuple-element.37.refs_2_, ...), custom_call_target="tpu_custom_call" | custom-call | flops 956301312 | bytes 1 | tf_op jit(solution)/shard_map/lead2/pallas_call | solution.py:25
  41.8 3.8 %collective-permute-start.16 = (f32[304,128]{1,0:T(8,128)S(1)}, f32[304,128]{1,0:T(8,128)S(1)}, u32[]{:S(2)}, u32[]{:S(2)}) collective-permute-start(f32[304,128]{1,0:T(8,128)S(1)} %get-tuple-element.43.refs_11_.refs_4_), channel_id=1, source_target_pairs={{0,24},{8,0},{16,8},{24,16},{1,25},{9,1},{17,9},{25,17},{2,26},{10... | collective-permute-start | bytes 466952 | tf_op jit(solution)/shard_map/ppermute | solution.py:281
  45.5 3.2 %collective-permute-done.12.refs_1_.refs_7_ = f32[304,128]{1,0:T(8,128)S(1)} collective-permute-done((f32[304,128]{1,0:T(8,128)S(1)}, f32[304,128]{1,0:T(8,128)S(1)}, u32[]{:S(2)}, u32[]{:S(2)}) %collective-permute-start.12) | collective-permute-done | bytes 155680 | tf_op jit(solution)/shard_map/ppermute | solution.py:281
  51.5 4.1 %collective-permute-done.14.refs_10_ = f32[304,128]{1,0:T(8,128)S(1)} collective-permute-done((f32[304,128]{1,0:T(8,128)S(1)}, f32[304,128]{1,0:T(8,128)S(1)}, u32[]{:S(2)}, u32[]{:S(2)}) %collective-permute-start.14) | collective-permute-done | bytes 155680 | tf_op jit(solution)/shard_map/ppermute | solution.py:287
  55.6 2.7 %lead1.1 = (bf16[608,1024]{1,0:T(8,128)(2,1)S(1)}, f32[1,304,512]{2,1,0:T(8,128)S(1)}, f32[912,128]{1,0:T(8,128)S(1)}) custom-call(s32[4]{0:T(128)S(1)} %pad_add_fusion.refs_0_.info, bf16[2,2,1024,512]{3,2,1,0:T(8,128)(2,1)S(1)} %get-tuple-element.36.refs_1_, bf16[2,2,1024,512]{3,2,1,0:T(8,128)(2,1)S(1)} %get-tuple-element.37.refs_2_, ...), custom_call_target="tpu_custom_call" | custom-call | flops 1912602624 | bytes 1 | tf_op jit(solution)/shard_map/lead1/pallas_call | solution.py:25
  59.5 6.1 %collective-permute-done.19.refs_7_ = f32[304,128]{1,0:T(8,128)S(1)} collective-permute-done((f32[304,128]{1,0:T(8,128)S(1)}, f32[304,128]{1,0:T(8,128)S(1)}, u32[]{:S(2)}, u32[]{:S(2)}) %collective-permute-start.19) | collective-permute-done | bytes 155680 | tf_op jit(solution)/shard_map/ppermute | solution.py:281
  65.6 1.8 %collective-permute-start.20 = (f32[304,128]{1,0:T(8,128)S(1)}, f32[304,128]{1,0:T(8,128)S(1)}, u32[]{:S(2)}, u32[]{:S(2)}) collective-permute-start(f32[304,128]{1,0:T(8,128)S(1)} %collective-permute-done.19.refs_7_), channel_id=1, source_target_pairs={{0,4},{4,0},{1,5},{5,1},{2,6},{6,2},{3,7},{7,3},{8,12},{12,8},{9,1... | collective-permute-start | bytes 466952 | tf_op jit(solution)/shard_map/ppermute | solution.py:287
  67.4 5.5 %rest1.1 = (f32[304,512]{1,0:T(8,128)S(1)}, f32[2,304,512]{2,1,0:T(8,128)S(1)}, f32[304,512]{1,0:T(8,128)S(1)}) custom-call(s32[4]{0:T(128)S(1)} %pad_add_fusion.refs_0_.info, bf16[2,2,1024,512]{3,2,1,0:T(8,128)(2,1)S(1)} %get-tuple-element.36.refs_1_, bf16[2,2,1024,512]{3,2,1,0:T(8,128)(2,1)S(1)} %get-tuple-element.37.refs_2_, ...), custom_call_target="tpu_custom_call" | custom-call | flops 2868903936 | bytes 1 | tf_op jit(solution)/shard_map/rest1/pallas_call | solution.py:25
  72.9 3.7 %lead0.1 = (bf16[608,1024]{1,0:T(8,128)(2,1)S(1)}, f32[1,304,512]{2,1,0:T(8,128)S(1)}, f32[1,304,512]{2,1,0:T(8,128)S(1)}, f32[304,512]{1,0:T(8,128)S(1)}) custom-call(s32[4]{0:T(128)S(1)} %pad_add_fusion.refs_0_.info, bf16[2,2,1024,512]{3,2,1,0:T(8,128)(2,1)S(1)} %get-tuple-element.36.refs_1_, bf16[2,2,1024,512]{3,2,1,0:T(8,128)(2,1)S(1)} %get-tuple-element.37.refs_2_, ...), custom_call_target="tpu_custom_call" | custom-call | flops 2868903936 | bytes 1 | tf_op jit(solution)/shard_map/lead0/pallas_call | solution.py:25
  79.3 2.6 %collective-permute-start.23 = (f32[304,512]{1,0:T(8,128)S(1)}, f32[304,512]{1,0:T(8,128)S(1)}, u32[]{:S(2)}, u32[]{:S(2)}) collective-permute-start(f32[304,512]{1,0:T(8,128)S(1)} %get-tuple-element.53), channel_id=1, source_target_pairs={{0,4},{4,8},{8,12},{12,16},{16,20},{20,24},{24,28},{1,5},{5,9},{9,... | collective-permute-start | bytes 1867784 | tf_op jit(solution)/shard_map/ppermute | solution.py:250
  81.9 3.7 %collective-permute-start.24 = (f32[304,512]{1,0:T(8,128)S(1)}, f32[304,512]{1,0:T(8,128)S(1)}, u32[]{:S(2)}, u32[]{:S(2)}) collective-permute-start(f32[304,512]{1,0:T(8,128)S(1)} %get-tuple-element.54), channel_id=1, source_target_pairs={{0,6},{2,4},{4,10},{6,8},{8,14},{10,12},{12,18},{14,16},{16,22},{1... | collective-permute-start | bytes 1867784 | tf_op jit(solution)/shard_map/ppermute | solution.py:254
  87.3 6.3 %collective-permute-done.25.refs_0_ = f32[304,512]{1,0:T(8,128)S(1)} collective-permute-done((f32[304,512]{1,0:T(8,128)S(1)}, f32[304,512]{1,0:T(8,128)S(1)}, u32[]{:S(2)}, u32[]{:S(2)}) %collective-permute-start.25) | collective-permute-done | bytes 622624 | tf_op jit(solution)/shard_map/ppermute | solution.py:258
  93.6 12.4 %collective-permute-done.26.refs_1_ = f32[304,512]{1,0:T(8,128)S(1)} collective-permute-done((f32[304,512]{1,0:T(8,128)S(1)}, f32[304,512]{1,0:T(8,128)S(1)}, u32[]{:S(2)}, u32[]{:S(2)}) %collective-permute-start.26) | collective-permute-done | bytes 622624 | tf_op jit(solution)/shard_map/ppermute | solution.py:264
  106.0 2.9 %collective-permute-done.24.next_other = f32[304,512]{1,0:T(8,128)S(1)} collective-permute-done((f32[304,512]{1,0:T(8,128)S(1)}, f32[304,512]{1,0:T(8,128)S(1)}, u32[]{:S(2)}, u32[]{:S(2)}) %collective-permute-start.24) | collective-permute-done | bytes 622624 | tf_op jit(solution)/shard_map/ppermute | solution.py:254
  109.0 2.4 %finish.1 = f32[600,512]{1,0:T(8,128)} custom-call(s32[4]{0:T(128)S(1)} %pad_add_fusion.refs_0_.info, f32[304,512]{1,0:T(8,128)S(1)} %last.1.d_keep, f32[304,512]{1,0:T(8,128)S(1)} %collective-permute-done.21.d_chip, f32[304,512]{1,0:T(8,128)S(1)} %collective-permute-done.23.next_own, f32[304,512]{1,0:T(8,128)S(1)} %collective-permute-done.24.next_other, ...), custom_call_target="tpu_custom_call" | custom-call | tf_op jit(solution)/shard_map/finish/pallas_call | solution.py:375
  (48 shorter events, 26.5 us)
Async XLA Ops:
  6.6 21.2 %collective-permute-start.1 = (f32[1024,512]{1,0:T(8,128)S(1)}, f32[1024,512]{1,0:T(8,128)S(1)}, u32[]{:S(2)}, u32[]{:S(2)}) collective-permute-start(f32[1024,512]{1,0:T(8,128)S(1)} %get-tuple-element.34), channel_id=1, source_target_pairs={{0,2},{2,0},{1,3},{3,1},{4,6},{6,4},{5,7},{7,5},{8,10},{10,8},{9,1... | collective-permute-start | bytes 6291464 | tf_op jit(solution)/shard_map/ppermute | solution.py:247
  7.0 22.0 %collective-permute-start.2 = (f32[1024,512]{1,0:T(8,128)S(1)}, f32[1024,512]{1,0:T(8,128)S(1)}, u32[]{:S(2)}, u32[]{:S(2)}) collective-permute-start(f32[1024,512]{1,0:T(8,128)S(1)} %get-tuple-element.35), channel_id=1, source_target_pairs={{0,2},{2,0},{1,3},{3,1},{4,6},{6,4},{5,7},{7,5},{8,10},{10,8},{9,1... | collective-permute-start | bytes 6291464 | tf_op jit(solution)/shard_map/ppermute | solution.py:247
  7.1 9.8 %collective-permute-start.3 = (f32[304,128]{1,0:T(8,128)S(1)}, f32[304,128]{1,0:T(8,128)S(1)}, u32[]{:S(2)}, u32[]{:S(2)}) collective-permute-start(f32[304,128]{1,0:T(8,128)S(1)} %get-tuple-element.39.refs_4_), channel_id=1, source_target_pairs={{0,8},{8,16},{16,24},{24,0},{1,9},{9,17},{17,25},{25,1},{2,10},{10... | collective-permute-start | bytes 466952 | tf_op jit(solution)/shard_map/ppermute | solution.py:281
  10.1 9.1 %collective-permute-start.4 = (f32[304,128]{1,0:T(8,128)S(1)}, f32[304,128]{1,0:T(8,128)S(1)}, u32[]{:S(2)}, u32[]{:S(2)}) collective-permute-start(f32[304,128]{1,0:T(8,128)S(1)} %get-tuple-element.39.refs_4_), channel_id=1, source_target_pairs={{0,24},{8,0},{16,8},{24,16},{1,25},{9,1},{17,9},{25,17},{2,26},{10... | collective-permute-start | bytes 466952 | tf_op jit(solution)/shard_map/ppermute | solution.py:281
  12.1 7.1 %collective-permute-start.6 = (f32[304,128]{1,0:T(8,128)S(1)}, f32[304,128]{1,0:T(8,128)S(1)}, u32[]{:S(2)}, u32[]{:S(2)}) collective-permute-start(f32[304,128]{1,0:T(8,128)S(1)} %get-tuple-element.39.refs_4_), channel_id=1, source_target_pairs={{0,4},{4,0},{1,5},{5,1},{2,6},{6,2},{3,7},{7,3},{8,12},{12,8},{9,1... | collective-permute-start | bytes 466952 | tf_op jit(solution)/shard_map/ppermute | solution.py:287
  17.0 7.5 %collective-permute-start.5 = (f32[304,128]{1,0:T(8,128)S(1)}, f32[304,128]{1,0:T(8,128)S(1)}, u32[]{:S(2)}, u32[]{:S(2)}) collective-permute-start(f32[304,128]{1,0:T(8,128)S(1)} %collective-permute-done.3.refs_1_.refs_5_), channel_id=1, source_target_pairs={{0,8},{8,16},{16,24},{24,0},{1,9},{9,17},{17,25},{25,1},{2,10},{10... | collective-permute-start | bytes 466952 | tf_op jit(solution)/shard_map/ppermute | solution.py:281
  19.8 15.4 %collective-permute-start.7 = (f32[608,128]{1,0:T(8,128)S(1)}, f32[608,128]{1,0:T(8,128)S(1)}, u32[]{:S(2)}, u32[]{:S(2)}) collective-permute-start(f32[608,128]{1,0:T(8,128)S(1)} %join2.1), channel_id=1, source_target_pairs={{0,4},{4,0},{1,5},{5,1},{2,6},{6,2},{3,7},{7,3},{8,12},{12,8},{9,1... | collective-permute-start | bytes 933896 | tf_op jit(solution)/shard_map/ppermute | solution.py:287
  21.4 9.6 %collective-permute-start.9 = (f32[304,128]{1,0:T(8,128)S(1)}, f32[304,128]{1,0:T(8,128)S(1)}, u32[]{:S(2)}, u32[]{:S(2)}) collective-permute-start(f32[304,128]{1,0:T(8,128)S(1)} %get-tuple-element.40.refs_4_), channel_id=1, source_target_pairs={{0,8},{8,16},{16,24},{24,0},{1,9},{9,17},{17,25},{25,1},{2,10},{10... | collective-permute-start | bytes 466952 | tf_op jit(solution)/shard_map/ppermute | solution.py:281
  24.4 6.8 %collective-permute-start.10 = (f32[304,128]{1,0:T(8,128)S(1)}, f32[304,128]{1,0:T(8,128)S(1)}, u32[]{:S(2)}, u32[]{:S(2)}) collective-permute-start(f32[304,128]{1,0:T(8,128)S(1)} %get-tuple-element.40.refs_4_), channel_id=1, source_target_pairs={{0,24},{8,0},{16,8},{24,16},{1,25},{9,1},{17,9},{25,17},{2,26},{10... | collective-permute-start | bytes 466952 | tf_op jit(solution)/shard_map/ppermute | solution.py:281
  36.9 18.7 %collective-permute-start.17 = (f32[304,512]{1,0:T(8,128)S(1)}, f32[304,512]{1,0:T(8,128)S(1)}, u32[]{:S(2)}, u32[]{:S(2)}) collective-permute-start(f32[304,512]{1,0:T(8,128)S(1)} %bitcast.15), channel_id=1, source_target_pairs={{0,1},{1,0},{2,3},{3,2},{4,5},{5,4},{6,7},{7,6},{8,9},{9,8},{10,11... | collective-permute-start | bytes 1867784 | tf_op jit(solution)/shard_map/ppermute | solution.py:258
  38.5 10.2 %collective-permute-start.13 = (f32[608,128]{1,0:T(8,128)S(1)}, f32[608,128]{1,0:T(8,128)S(1)}, u32[]{:S(2)}, u32[]{:S(2)}) collective-permute-start(f32[608,128]{1,0:T(8,128)S(1)} %get-tuple-element.42), channel_id=1, source_target_pairs={{0,4},{4,0},{1,5},{5,1},{2,6},{6,2},{3,7},{7,3},{8,12},{12,8},{9,1... | collective-permute-start | bytes 933896 | tf_op jit(solution)/shard_map/ppermute | solution.py:287
  40.0 8.7 %collective-permute-start.12 = (f32[304,128]{1,0:T(8,128)S(1)}, f32[304,128]{1,0:T(8,128)S(1)}, u32[]{:S(2)}, u32[]{:S(2)}) collective-permute-start(f32[304,128]{1,0:T(8,128)S(1)} %collective-permute-done.9.refs_11_.refs_5_), channel_id=1, source_target_pairs={{0,8},{8,16},{16,24},{24,0},{1,9},{9,17},{17,25},{25,1},{2,10},{10... | collective-permute-start | bytes 466952 | tf_op jit(solution)/shard_map/ppermute | solution.py:281
  41.7 9.5 %collective-permute-start.15 = (f32[304,128]{1,0:T(8,128)S(1)}, f32[304,128]{1,0:T(8,128)S(1)}, u32[]{:S(2)}, u32[]{:S(2)}) collective-permute-start(f32[304,128]{1,0:T(8,128)S(1)} %get-tuple-element.43.refs_11_.refs_4_), channel_id=1, source_target_pairs={{0,8},{8,16},{16,24},{24,0},{1,9},{9,17},{17,25},{25,1},{2,10},{10... | collective-permute-start | bytes 466952 | tf_op jit(solution)/shard_map/ppermute | solution.py:281
  41.8 9.7 %collective-permute-start.16 = (f32[304,128]{1,0:T(8,128)S(1)}, f32[304,128]{1,0:T(8,128)S(1)}, u32[]{:S(2)}, u32[]{:S(2)}) collective-permute-start(f32[304,128]{1,0:T(8,128)S(1)} %get-tuple-element.43.refs_11_.refs_4_), channel_id=1, source_target_pairs={{0,24},{8,0},{16,8},{24,16},{1,25},{9,1},{17,9},{25,17},{2,26},{10... | collective-permute-start | bytes 466952 | tf_op jit(solution)/shard_map/ppermute | solution.py:281
  49.3 6.3 %collective-permute-start.14 = (f32[304,128]{1,0:T(8,128)S(1)}, f32[304,128]{1,0:T(8,128)S(1)}, u32[]{:S(2)}, u32[]{:S(2)}) collective-permute-start(f32[304,128]{1,0:T(8,128)S(1)} %pass1.1), channel_id=1, source_target_pairs={{0,4},{4,0},{1,5},{5,1},{2,6},{6,2},{3,7},{7,3},{8,12},{12,8},{9,1... | collective-permute-start | bytes 466952 | tf_op jit(solution)/shard_map/ppermute | solution.py:287
  58.3 9.1 %collective-permute-start.18 = (f32[912,128]{1,0:T(8,128)S(1)}, f32[912,128]{1,0:T(8,128)S(1)}, u32[]{:S(2)}, u32[]{:S(2)}) collective-permute-start(f32[912,128]{1,0:T(8,128)S(1)} %get-tuple-element.46), channel_id=1, source_target_pairs={{0,4},{4,0},{1,5},{5,1},{2,6},{6,2},{3,7},{7,3},{8,12},{12,8},{9,1... | collective-permute-start | bytes 1400840 | tf_op jit(solution)/shard_map/ppermute | solution.py:287
  58.6 7.0 %collective-permute-start.19 = (f32[304,128]{1,0:T(8,128)S(1)}, f32[304,128]{1,0:T(8,128)S(1)}, u32[]{:S(2)}, u32[]{:S(2)}) collective-permute-start(f32[304,128]{1,0:T(8,128)S(1)} %collective-permute-done.15.refs_12_.refs_5_), channel_id=1, source_target_pairs={{0,8},{8,16},{16,24},{24,0},{1,9},{9,17},{17,25},{25,1},{2,10},{10... | collective-permute-start | bytes 466952 | tf_op jit(solution)/shard_map/ppermute | solution.py:281
  58.6 20.0 %collective-permute-start.22 = (f32[304,512]{1,0:T(8,128)S(1)}, f32[304,512]{1,0:T(8,128)S(1)}, u32[]{:S(2)}, u32[]{:S(2)}) collective-permute-start(f32[304,512]{1,0:T(8,128)S(1)} %bitcast.14), channel_id=1, source_target_pairs={{0,1},{1,0},{2,3},{3,2},{4,5},{5,4},{6,7},{7,6},{8,9},{9,8},{10,11... | collective-permute-start | bytes 1867784 | tf_op jit(solution)/shard_map/ppermute | solution.py:258
  65.6 7.3 %collective-permute-start.20 = (f32[304,128]{1,0:T(8,128)S(1)}, f32[304,128]{1,0:T(8,128)S(1)}, u32[]{:S(2)}, u32[]{:S(2)}) collective-permute-start(f32[304,128]{1,0:T(8,128)S(1)} %collective-permute-done.19.refs_7_), channel_id=1, source_target_pairs={{0,4},{4,0},{1,5},{5,1},{2,6},{6,2},{3,7},{7,3},{8,12},{12,8},{9,1... | collective-permute-start | bytes 466952 | tf_op jit(solution)/shard_map/ppermute | solution.py:287
  76.6 10.6 %collective-permute-start.21 = (f32[304,512]{1,0:T(8,128)S(1)}, f32[304,512]{1,0:T(8,128)S(1)}, u32[]{:S(2)}, u32[]{:S(2)}) collective-permute-start(f32[304,512]{1,0:T(8,128)S(1)} %get-tuple-element.49), channel_id=1, source_target_pairs={{0,2},{2,0},{1,3},{3,1},{4,6},{6,4},{5,7},{7,5},{8,10},{10,8},{9,1... | collective-permute-start | bytes 1867784 | tf_op jit(solution)/shard_map/ppermute | solution.py:247
  76.7 16.9 %collective-permute-start.25 = (f32[304,512]{1,0:T(8,128)S(1)}, f32[304,512]{1,0:T(8,128)S(1)}, u32[]{:S(2)}, u32[]{:S(2)}) collective-permute-start(f32[304,512]{1,0:T(8,128)S(1)} %bitcast.17), channel_id=1, source_target_pairs={{0,1},{1,0},{2,3},{3,2},{4,5},{5,4},{6,7},{7,6},{8,9},{9,8},{10,11... | collective-permute-start | bytes 1867784 | tf_op jit(solution)/shard_map/ppermute | solution.py:258
  77.9 28.1 %collective-permute-start.26 = (f32[304,512]{1,0:T(8,128)S(1)}, f32[304,512]{1,0:T(8,128)S(1)}, u32[]{:S(2)}, u32[]{:S(2)}) collective-permute-start(f32[304,512]{1,0:T(8,128)S(1)} %bitcast.16), channel_id=1, source_target_pairs={{0,3},{1,2},{2,1},{3,0},{4,7},{5,6},{6,5},{7,4},{8,11},{9,10},{10,... | collective-permute-start | bytes 1867784 | tf_op jit(solution)/shard_map/ppermute | solution.py:264
  79.3 26.8 %collective-permute-start.23 = (f32[304,512]{1,0:T(8,128)S(1)}, f32[304,512]{1,0:T(8,128)S(1)}, u32[]{:S(2)}, u32[]{:S(2)}) collective-permute-start(f32[304,512]{1,0:T(8,128)S(1)} %get-tuple-element.53), channel_id=1, source_target_pairs={{0,4},{4,8},{8,12},{12,16},{16,20},{20,24},{24,28},{1,5},{5,9},{9,... | collective-permute-start | bytes 1867784 | tf_op jit(solution)/shard_map/ppermute | solution.py:250
  81.9 27.1 %collective-permute-start.24 = (f32[304,512]{1,0:T(8,128)S(1)}, f32[304,512]{1,0:T(8,128)S(1)}, u32[]{:S(2)}, u32[]{:S(2)}) collective-permute-start(f32[304,512]{1,0:T(8,128)S(1)} %get-tuple-element.54), channel_id=1, source_target_pairs={{0,6},{2,4},{4,10},{6,8},{8,14},{10,12},{12,18},{14,16},{16,22},{1... | collective-permute-start | bytes 1867784 | tf_op jit(solution)/shard_map/ppermute | solution.py:254
  (5 other events, 17.4 us)

commit v8 on v7

--- a/solution.py
+++ b/solution.py
@@ -220,16 +220,17 @@
     other_ref[...] = jnp.where(first, total1[...], total0)
 
 
-def finish_kernel(spaces, info, d_keep, d_chip, next_own, next_other, *refs):
-    (*parts, out_ref) = refs
+def add_kernel(info, *refs):
+    count = len(refs) // 2 - 1
+    for terms, out_ref in ((refs[:count], refs[-2]), (refs[count:-2], refs[-1])):
+        out_ref[...] = functools.reduce(jnp.add, [term[...] for term in terms])
+
+
+def finish_kernel(info, own_sum, other_sum, next_own, next_other, out_ref):
     first = info[0] == 0
-    (sensors, step), half = out_ref.shape, d_keep.shape[0]
-    columns = pl.ds(pl.multiple_of(pl.program_id(0) * step, step), step)
-    own = d_keep[:, columns] + next_own[:, columns]
-    other = d_chip[:, columns] + next_other[:, columns]
-    for straight, cross in zip(parts[: spaces - 1], parts[spaces - 1 :]):
-        own = own + straight[:, columns]
-        other = other + cross[:, columns]
+    sensors, half = out_ref.shape[0], own_sum.shape[0]
+    own = own_sum[...] + next_own[...]
+    other = other_sum[...] + next_other[...]
     out_ref[:half, :] = jnp.where(first, own, other)
     out_ref[half:, :] = jnp.where(first, other, own)[2 * half - sensors :, :]
 
@@ -334,13 +335,11 @@
         "lead2",
         [pair, sent] + joint + [small],
         [info, high, low, lag_blocks[0], *line2, *row2, *near1],
-        waits=row_own1,
+        waits=row_own1 + far1,
         flops=flops,
     )
     from1 = over_space(send1)
-    row_near1 = handed(joint1)
-    passed1 = list(call(join_kernel, "pass1", [small], [info, *far1], waits=row_near1)) if far1 else []
-    line1, row1 = own1 + near1 + far1, ordered(row_own1, row_near1, handed(passed1))
+    line1, row1 = gathered(own1, near1, far1, row_own1, joint1)
     own0, near0, far0 = shifted(block0)
     pair1, send0, *joint0 = call(
         functools.partial(lead_one_kernel, lines, 1 + len(near0)),
@@ -351,15 +350,15 @@
         flops=2 * flops,
     )
     from0 = over_space(send0)
-    line0, row0 = gathered(own0, near0, far0, [], joint0)
     keep0, early1, total1 = call(
         rest_one_kernel,
         "rest1",
         [one, whole, one],
         [info, high, low, pair2, pair1, *from1],
-        waits=row0[:1],
         flops=3 * flops,
     )
+    passed0 = list(call(join_kernel, "pass0", [small], [info, *far0], waits=[early1])) if far0 else []
+    line0, row0 = own0 + near0 + far0, ordered(handed(joint0), handed(passed0))
     pair0, d_send, d_cross, d_chip = call(
         functools.partial(lead_zero_kernel, lines),
         "lead0",
@@ -370,17 +369,13 @@
     d_from, d_from_cross = over_space(d_send), over_space_and_core(d_cross)
     next_same, next_cross = call(totals_kernel, "totals", [one, one], [info, total1, keep0, *from0], waits=row0[-1:])
     (d_keep,) = call(last_kernel, "last", [one], [info, high, low, pair0, early1], flops=flops)
-    operands = [d_keep, swap(d_chip), onward(next_same), onward_across(next_cross), *d_from, *d_from_cross]
-    step = block if block % 128 else 128
-    result = pl.pallas_call(
-        functools.partial(finish_kernel, spaces),
-        grid=(block // step,),
-        out_shape=jax.ShapeDtypeStruct((sensors, block), F32),
-        in_specs=[SMEM_SPEC] + [VMEM_SPEC] * len(operands),
-        out_specs=pl.BlockSpec((sensors, step), lambda at: (0, at)),
-        compiler_params=pltpu.CompilerParams(vmem_limit_bytes=VMEM_LIMIT),
-        name="finish",
-    )(info, *operands)
+    sums = call(add_kernel, "add", [one, one], [info, d_keep, *d_from, swap(d_chip), *d_from_cross])
+    (result,) = call(
+        finish_kernel,
+        "finish",
+        [jax.ShapeDtypeStruct((sensors, block), F32)],
+        [info, *sums, onward(next_same), onward_across(next_cross)],
+    )
     return result[None]
 
 

time: 113 us -> 109 us (0.965)
  starting transfers between devices: 36.3 us -> 32.6 us
    ppermute x1, waiting for transfers between devices: 12.4 us -> 7.08 us  [over_space_and_core(): lax.ppermute(sent[d - 1], ('core', 'space'), [(c * spaces + i, (1 - c) *...]
    ppermute x9, waiting for transfers between devices: 18.4 us -> 14 us  [shifted(): lax.ppermute(held[shift - step], 'line', [(i, (i + step) % lines) for i i...]
    ppermute x1, waiting for transfers between devices: 2.94 us -> 7.29 us  [onward_across(): return lax.ppermute(values, ('line', 'row', 'core'), route)]
    ppermute x9, starting transfers between devices: 15 us -> 11.5 us  [shifted(): lax.ppermute(held[shift - step], 'line', [(i, (i + step) % lines) for i i...]
    ppermute x3, waiting for transfers between devices: 6.34 us -> 8.94 us  [over_space(): lax.ppermute(sent[d - 1], 'space', [(i, (i + d) % spaces) for i in range(...]
    pallas_call x12 -> x14, Pallas kernels: 21 us -> 23.4 us  [call(): pl.pallas_call(body, out_shape=shapes, in_specs=[SMEM_SPEC] + [VMEM_SPEC]...]
    pallas_call x1 -> x0, Pallas kernels: 2.38 us -> none  [on_device(): pl.pallas_call(functools.partial(finish_kernel, spaces), grid=(block // s...]
    ppermute x8, waiting for transfers between devices: 8.13 us -> 10.4 us  [handed(): lax.ppermute(values, 'row', [(i, (i - off) % rows) for i in range(rows)])]
  transfers between devices with their start and end apart: 27 -> 27, of which waited for: 14 -> 13; matrix products, arithmetic and copies ran while one was open for 0% -> 0% of each run, Pallas kernels for 13% -> 14%
where the time goes in v8:
time: 109 us; the launch traced here: 107 us
  waiting for transfers between devices  47.7 us (44%)
  starting transfers between devices  32.6 us (30%)
  Pallas kernels  23.4 us (21%)
  local copies, waits for them, and re-layouts  3.21 us (3%)
    pallas_call x14, Pallas kernels, call(): pl.pallas_call(body, out_shape=shapes, in_specs=[SMEM_SPEC] + [VMEM_SPEC]...  23.4 us
    ppermute x9, waiting for transfers between devices, shifted(): lax.ppermute(held[shift - step], 'line', [(i, (i + step) % lines) for i i...  14 us
    ppermute x9, starting transfers between devices, shifted(): lax.ppermute(held[shift - step], 'line', [(i, (i + step) % lines) for i i...  11.5 us
    ppermute x8, waiting for transfers between devices, handed(): lax.ppermute(values, 'row', [(i, (i - off) % rows) for i in range(rows)])  10.4 us
    ppermute x8, starting transfers between devices, handed(): lax.ppermute(values, 'row', [(i, (i - off) % rows) for i in range(rows)])  9.61 us
    ppermute x3, waiting for transfers between devices, over_space(): lax.ppermute(sent[d - 1], 'space', [(i, (i + d) % spaces) for i in range(...  8.94 us
    ppermute x1, waiting for transfers between devices, onward_across(): return lax.ppermute(values, ('line', 'row', 'core'), route)  7.29 us
    ppermute x1, waiting for transfers between devices, over_space_and_core(): lax.ppermute(sent[d - 1], ('core', 'space'), [(c * spaces + i, (1 - c) *...  7.08 us
  transfers between devices with their start and end apart: 27, of which 13 were waited for; matrix products, arithmetic and copies ran while one was open for 0% of the time, Pallas kernels for 14%

profile of v8, /device:TPU:0, one launch (start us, length us, event | category | flops | bytes accessed | tf_op | source)
XLA Modules:
  0.0 107.2 jit_solution(16797909433180514211)
XLA Ops:
  3.0 2.2 %copy-done = f32[1,1024,1024]{2,1,0:T(8,128)S(1)} copy-done((f32[1,1024,1024]{2,1,0:T(8,128)S(1)}, f32[1,1024,1024]{2,1,0:T(8,128)}, u32[]{:S(2)}) %copy-start) | copy-done | bytes 4194328
  7.2 2.9 %collective-permute-start.3 = (f32[304,128]{1,0:T(8,128)S(1)}, f32[304,128]{1,0:T(8,128)S(1)}, u32[]{:S(2)}, u32[]{:S(2)}) collective-permute-start(f32[304,128]{1,0:T(8,128)S(1)} %get-tuple-element.41.refs_4_), channel_id=1, source_target_pairs={{0,8},{8,16},{16,24},{24,0},{1,9},{9,17},{17,25},{25,1},{2,10},{10... | collective-permute-start | bytes 466952 | tf_op jit(solution)/shard_map/ppermute | solution.py:282
  10.1 2.0 %collective-permute-start.4 = (f32[304,128]{1,0:T(8,128)S(1)}, f32[304,128]{1,0:T(8,128)S(1)}, u32[]{:S(2)}, u32[]{:S(2)}) collective-permute-start(f32[304,128]{1,0:T(8,128)S(1)} %get-tuple-element.41.refs_4_), channel_id=1, source_target_pairs={{0,24},{8,0},{16,8},{24,16},{1,25},{9,1},{17,9},{25,17},{2,26},{10... | collective-permute-start | bytes 466952 | tf_op jit(solution)/shard_map/ppermute | solution.py:282
  12.1 1.7 %collective-permute-start.6 = (f32[304,128]{1,0:T(8,128)S(1)}, f32[304,128]{1,0:T(8,128)S(1)}, u32[]{:S(2)}, u32[]{:S(2)}) collective-permute-start(f32[304,128]{1,0:T(8,128)S(1)} %get-tuple-element.41.refs_4_), channel_id=1, source_target_pairs={{0,4},{4,0},{1,5},{5,1},{2,6},{6,2},{3,7},{7,3},{8,12},{12,8},{9,1... | collective-permute-start | bytes 466952 | tf_op jit(solution)/shard_map/ppermute | solution.py:288
  13.9 3.1 %collective-permute-done.3.refs_1_.refs_5_ = f32[304,128]{1,0:T(8,128)S(1)} collective-permute-done((f32[304,128]{1,0:T(8,128)S(1)}, f32[304,128]{1,0:T(8,128)S(1)}, u32[]{:S(2)}, u32[]{:S(2)}) %collective-permute-start.3) | collective-permute-done | bytes 155680 | tf_op jit(solution)/shard_map/ppermute | solution.py:282
  17.0 2.2 %collective-permute-done.4.refs_2_.refs_6_ = f32[304,128]{1,0:T(8,128)S(1)} collective-permute-done((f32[304,128]{1,0:T(8,128)S(1)}, f32[304,128]{1,0:T(8,128)S(1)}, u32[]{:S(2)}, u32[]{:S(2)}) %collective-permute-start.4) | collective-permute-done | bytes 155680 | tf_op jit(solution)/shard_map/ppermute | solution.py:282
  22.6 3.4 %collective-permute-done.9.refs_11_.refs_5_ = f32[304,128]{1,0:T(8,128)S(1)} collective-permute-done((f32[304,128]{1,0:T(8,128)S(1)}, f32[304,128]{1,0:T(8,128)S(1)}, u32[]{:S(2)}, u32[]{:S(2)}) %collective-permute-start.9) | collective-permute-done | bytes 155680 | tf_op jit(solution)/shard_map/ppermute | solution.py:282
  26.6 2.6 %collective-permute-done.5.refs_7_ = f32[304,128]{1,0:T(8,128)S(1)} collective-permute-done((f32[304,128]{1,0:T(8,128)S(1)}, f32[304,128]{1,0:T(8,128)S(1)}, u32[]{:S(2)}, u32[]{:S(2)}) %collective-permute-start.5) | collective-permute-done | bytes 155680 | tf_op jit(solution)/shard_map/ppermute | solution.py:282
  32.5 2.5 %collective-permute-done.11.refs_13_.refs_8_ = f32[304,128]{1,0:T(8,128)S(1)} collective-permute-done((f32[304,128]{1,0:T(8,128)S(1)}, f32[304,128]{1,0:T(8,128)S(1)}, u32[]{:S(2)}, u32[]{:S(2)}) %collective-permute-start.11) | collective-permute-done | bytes 155680 | tf_op jit(solution)/shard_map/ppermute | solution.py:288
  35.0 2.5 %collective-permute-done.12.refs_14_.refs_7_ = f32[304,128]{1,0:T(8,128)S(1)} collective-permute-done((f32[304,128]{1,0:T(8,128)S(1)}, f32[304,128]{1,0:T(8,128)S(1)}, u32[]{:S(2)}, u32[]{:S(2)}) %collective-permute-start.12) | collective-permute-done | bytes 155680 | tf_op jit(solution)/shard_map/ppermute | solution.py:282
  42.8 3.8 %collective-permute-start.16 = (f32[304,128]{1,0:T(8,128)S(1)}, f32[304,128]{1,0:T(8,128)S(1)}, u32[]{:S(2)}, u32[]{:S(2)}) collective-permute-start(f32[304,128]{1,0:T(8,128)S(1)} %get-tuple-element.45.refs_11_.refs_4_), channel_id=1, source_target_pairs={{0,24},{8,0},{16,8},{24,16},{1,25},{9,1},{17,9},{25,17},{2,26},{10... | collective-permute-start | bytes 466952 | tf_op jit(solution)/shard_map/ppermute | solution.py:282
  46.6 3.2 %collective-permute-done.14.refs_10_ = f32[304,128]{1,0:T(8,128)S(1)} collective-permute-done((f32[304,128]{1,0:T(8,128)S(1)}, f32[304,128]{1,0:T(8,128)S(1)}, u32[]{:S(2)}, u32[]{:S(2)}) %collective-permute-start.14) | collective-permute-done | bytes 155680 | tf_op jit(solution)/shard_map/ppermute | solution.py:288
  49.9 1.8 %collective-permute-done.17.refs_14_.refs_5_ = f32[304,512]{1,0:T(8,128)S(1)} collective-permute-done((f32[304,512]{1,0:T(8,128)S(1)}, f32[304,512]{1,0:T(8,128)S(1)}, u32[]{:S(2)}, u32[]{:S(2)}) %collective-permute-start.17) | collective-permute-done | bytes 622624 | tf_op jit(solution)/shard_map/ppermute | solution.py:259
  51.7 2.7 %lead1.1 = (bf16[608,1024]{1,0:T(8,128)(2,1)S(1)}, f32[1,304,512]{2,1,0:T(8,128)S(1)}, f32[912,128]{1,0:T(8,128)S(1)}) custom-call(s32[4]{0:T(128)S(1)} %pad_add_fusion.refs_0_, bf16[2,2,1024,512]{3,2,1,0:T(8,128)(2,1)S(1)} %get-tuple-element.38.refs_1_, bf16[2,2,1024,512]{3,2,1,0:T(8,128)(2,1)S(1)} %get-tuple-element.39.refs_2_, ...), custom_call_target="tpu_custom_call" | custom-call | flops 1912602624 | bytes 1 | tf_op jit(solution)/shard_map/lead1/pallas_call | solution.py:25
  54.4 1.8 %collective-permute-start.19 = (f32[912,128]{1,0:T(8,128)S(1)}, f32[912,128]{1,0:T(8,128)S(1)}, u32[]{:S(2)}, u32[]{:S(2)}) collective-permute-start(f32[912,128]{1,0:T(8,128)S(1)} %get-tuple-element.49), channel_id=1, source_target_pairs={{0,4},{4,0},{1,5},{5,1},{2,6},{6,2},{3,7},{7,3},{8,12},{12,8},{9,1... | collective-permute-start | bytes 1400840 | tf_op jit(solution)/shard_map/ppermute | solution.py:288
  58.3 5.5 %rest1.1 = (f32[304,512]{1,0:T(8,128)S(1)}, f32[2,304,512]{2,1,0:T(8,128)S(1)}, f32[304,512]{1,0:T(8,128)S(1)}) custom-call(s32[4]{0:T(128)S(1)} %pad_add_fusion.refs_0_, bf16[2,2,1024,512]{3,2,1,0:T(8,128)(2,1)S(1)} %get-tuple-element.38.refs_1_, bf16[2,2,1024,512]{3,2,1,0:T(8,128)(2,1)S(1)} %get-tuple-element.39.refs_2_, ...), custom_call_target="tpu_custom_call" | custom-call | flops 2868903936 | bytes 1 | tf_op jit(solution)/shard_map/rest1/pallas_call | solution.py:25
  65.0 4.7 %collective-permute-done.20.refs_9_.refs_4_ = f32[304,128]{1,0:T(8,128)S(1)} collective-permute-done((f32[304,128]{1,0:T(8,128)S(1)}, f32[304,128]{1,0:T(8,128)S(1)}, u32[]{:S(2)}, u32[]{:S(2)}) %collective-permute-start.20) | collective-permute-done | bytes 155680 | tf_op jit(solution)/shard_map/ppermute | solution.py:288
  69.7 3.7 %lead0.1 = (bf16[608,1024]{1,0:T(8,128)(2,1)S(1)}, f32[1,304,512]{2,1,0:T(8,128)S(1)}, f32[1,304,512]{2,1,0:T(8,128)S(1)}, f32[304,512]{1,0:T(8,128)S(1)}) custom-call(s32[4]{0:T(128)S(1)} %pad_add_fusion.refs_0_, bf16[2,2,1024,512]{3,2,1,0:T(8,128)(2,1)S(1)} %get-tuple-element.38.refs_1_, bf16[2,2,1024,512]{3,2,1,0:T(8,128)(2,1)S(1)} %get-tuple-element.39.refs_2_, ...), custom_call_target="tpu_custom_call" | custom-call | flops 2868903936 | bytes 1 | tf_op jit(solution)/shard_map/lead0/pallas_call | solution.py:25
  76.3 2.5 %collective-permute-start.25 = (f32[304,512]{1,0:T(8,128)S(1)}, f32[304,512]{1,0:T(8,128)S(1)}, u32[]{:S(2)}, u32[]{:S(2)}) collective-permute-start(f32[304,512]{1,0:T(8,128)S(1)} %get-tuple-element.59), channel_id=1, source_target_pairs={{0,4},{4,8},{8,12},{12,16},{16,20},{20,24},{24,28},{1,5},{5,9},{9,... | collective-permute-start | bytes 1867784 | tf_op jit(solution)/shard_map/ppermute | solution.py:251
  78.7 2.8 %collective-permute-start.26 = (f32[304,512]{1,0:T(8,128)S(1)}, f32[304,512]{1,0:T(8,128)S(1)}, u32[]{:S(2)}, u32[]{:S(2)}) collective-permute-start(f32[304,512]{1,0:T(8,128)S(1)} %get-tuple-element.60), channel_id=1, source_target_pairs={{0,6},{2,4},{4,10},{6,8},{8,14},{10,12},{12,18},{14,16},{16,22},{1... | collective-permute-start | bytes 1867784 | tf_op jit(solution)/shard_map/ppermute | solution.py:255
  83.2 7.2 %collective-permute-done.21.refs_2_ = f32[304,512]{1,0:T(8,128)S(1)} collective-permute-done((f32[304,512]{1,0:T(8,128)S(1)}, f32[304,512]{1,0:T(8,128)S(1)}, u32[]{:S(2)}, u32[]{:S(2)}) %collective-permute-start.21) | collective-permute-done | bytes 622624 | tf_op jit(solution)/shard_map/ppermute | solution.py:259
  90.4 7.1 %collective-permute-done.23.refs_4_ = f32[304,512]{1,0:T(8,128)S(1)} collective-permute-done((f32[304,512]{1,0:T(8,128)S(1)}, f32[304,512]{1,0:T(8,128)S(1)}, u32[]{:S(2)}, u32[]{:S(2)}) %collective-permute-start.23) | collective-permute-done | bytes 622624 | tf_op jit(solution)/shard_map/ppermute | solution.py:265
  98.2 7.3 %collective-permute-done.26.refs_4_ = f32[304,512]{1,0:T(8,128)S(1)} collective-permute-done((f32[304,512]{1,0:T(8,128)S(1)}, f32[304,512]{1,0:T(8,128)S(1)}, u32[]{:S(2)}, u32[]{:S(2)}) %collective-permute-start.26) | collective-permute-done | bytes 622624 | tf_op jit(solution)/shard_map/ppermute | solution.py:255
  105.5 1.7 %finish.1 = f32[600,512]{1,0:T(8,128)} custom-call(s32[4]{0:T(128)S(1)} %pad_add_fusion.refs_0_, f32[304,512]{1,0:T(8,128)S(1)} %get-tuple-element.54.refs_1_, f32[304,512]{1,0:T(8,128)S(1)} %get-tuple-element.55.refs_2_, f32[304,512]{1,0:T(8,128)S(1)} %collective-permute-done.25.refs_3_, f32[304,512]{1,0:T(8,128)S(1)} %collective-permute-done.26.refs_4_), custom_call_target="tpu_custom_call" | custom-call | bytes 1 | tf_op jit(solution)/shard_map/finish/pallas_call | solution.py:25
  (49 shorter events, 26.1 us)
Async XLA Ops:
  6.6 23.9 %collective-permute-start.1 = (f32[1024,512]{1,0:T(8,128)S(1)}, f32[1024,512]{1,0:T(8,128)S(1)}, u32[]{:S(2)}, u32[]{:S(2)}) collective-permute-start(f32[1024,512]{1,0:T(8,128)S(1)} %get-tuple-element.36), channel_id=1, source_target_pairs={{0,2},{2,0},{1,3},{3,1},{4,6},{6,4},{5,7},{7,5},{8,10},{10,8},{9,1... | collective-permute-start | bytes 6291464 | tf_op jit(solution)/shard_map/ppermute | solution.py:248
  7.0 23.4 %collective-permute-start.2 = (f32[1024,512]{1,0:T(8,128)S(1)}, f32[1024,512]{1,0:T(8,128)S(1)}, u32[]{:S(2)}, u32[]{:S(2)}) collective-permute-start(f32[1024,512]{1,0:T(8,128)S(1)} %get-tuple-element.37), channel_id=1, source_target_pairs={{0,2},{2,0},{1,3},{3,1},{4,6},{6,4},{5,7},{7,5},{8,10},{10,8},{9,1... | collective-permute-start | bytes 6291464 | tf_op jit(solution)/shard_map/ppermute | solution.py:248
  7.2 9.8 %collective-permute-start.3 = (f32[304,128]{1,0:T(8,128)S(1)}, f32[304,128]{1,0:T(8,128)S(1)}, u32[]{:S(2)}, u32[]{:S(2)}) collective-permute-start(f32[304,128]{1,0:T(8,128)S(1)} %get-tuple-element.41.refs_4_), channel_id=1, source_target_pairs={{0,8},{8,16},{16,24},{24,0},{1,9},{9,17},{17,25},{25,1},{2,10},{10... | collective-permute-start | bytes 466952 | tf_op jit(solution)/shard_map/ppermute | solution.py:282
  10.1 9.1 %collective-permute-start.4 = (f32[304,128]{1,0:T(8,128)S(1)}, f32[304,128]{1,0:T(8,128)S(1)}, u32[]{:S(2)}, u32[]{:S(2)}) collective-permute-start(f32[304,128]{1,0:T(8,128)S(1)} %get-tuple-element.41.refs_4_), channel_id=1, source_target_pairs={{0,24},{8,0},{16,8},{24,16},{1,25},{9,1},{17,9},{25,17},{2,26},{10... | collective-permute-start | bytes 466952 | tf_op jit(solution)/shard_map/ppermute | solution.py:282
  12.1 8.5 %collective-permute-start.6 = (f32[304,128]{1,0:T(8,128)S(1)}, f32[304,128]{1,0:T(8,128)S(1)}, u32[]{:S(2)}, u32[]{:S(2)}) collective-permute-start(f32[304,128]{1,0:T(8,128)S(1)} %get-tuple-element.41.refs_4_), channel_id=1, source_target_pairs={{0,4},{4,0},{1,5},{5,1},{2,6},{6,2},{3,7},{7,3},{8,12},{12,8},{9,1... | collective-permute-start | bytes 466952 | tf_op jit(solution)/shard_map/ppermute | solution.py:288
  17.0 9.0 %collective-permute-start.9 = (f32[304,128]{1,0:T(8,128)S(1)}, f32[304,128]{1,0:T(8,128)S(1)}, u32[]{:S(2)}, u32[]{:S(2)}) collective-permute-start(f32[304,128]{1,0:T(8,128)S(1)} %get-tuple-element.42.refs_4_), channel_id=1, source_target_pairs={{0,8},{8,16},{16,24},{24,0},{1,9},{9,17},{17,25},{25,1},{2,10},{10... | collective-permute-start | bytes 466952 | tf_op jit(solution)/shard_map/ppermute | solution.py:282
  19.2 10.0 %collective-permute-start.5 = (f32[304,128]{1,0:T(8,128)S(1)}, f32[304,128]{1,0:T(8,128)S(1)}, u32[]{:S(2)}, u32[]{:S(2)}) collective-permute-start(f32[304,128]{1,0:T(8,128)S(1)} %collective-permute-done.3.refs_1_.refs_5_), channel_id=1, source_target_pairs={{0,8},{8,16},{16,24},{24,0},{1,9},{9,17},{17,25},{25,1},{2,10},{10... | collective-permute-start | bytes 466952 | tf_op jit(solution)/shard_map/ppermute | solution.py:282
  21.2 16.3 %collective-permute-start.7 = (f32[608,128]{1,0:T(8,128)S(1)}, f32[608,128]{1,0:T(8,128)S(1)}, u32[]{:S(2)}, u32[]{:S(2)}) collective-permute-start(f32[608,128]{1,0:T(8,128)S(1)} %join2.1), channel_id=1, source_target_pairs={{0,4},{4,0},{1,5},{5,1},{2,6},{6,2},{3,7},{7,3},{8,12},{12,8},{9,1... | collective-permute-start | bytes 933896 | tf_op jit(solution)/shard_map/ppermute | solution.py:288
  26.0 6.5 %collective-permute-start.10 = (f32[304,128]{1,0:T(8,128)S(1)}, f32[304,128]{1,0:T(8,128)S(1)}, u32[]{:S(2)}, u32[]{:S(2)}) collective-permute-start(f32[304,128]{1,0:T(8,128)S(1)} %get-tuple-element.42.refs_4_), channel_id=1, source_target_pairs={{0,24},{8,0},{16,8},{24,16},{1,25},{9,1},{17,9},{25,17},{2,26},{10... | collective-permute-start | bytes 466952 | tf_op jit(solution)/shard_map/ppermute | solution.py:282
  30.4 7.0 %collective-permute-start.12 = (f32[304,128]{1,0:T(8,128)S(1)}, f32[304,128]{1,0:T(8,128)S(1)}, u32[]{:S(2)}, u32[]{:S(2)}) collective-permute-start(f32[304,128]{1,0:T(8,128)S(1)} %collective-permute-done.9.refs_11_.refs_5_), channel_id=1, source_target_pairs={{0,8},{8,16},{16,24},{24,0},{1,9},{9,17},{17,25},{25,1},{2,10},{10... | collective-permute-start | bytes 466952 | tf_op jit(solution)/shard_map/ppermute | solution.py:282
  30.5 7.0 %collective-permute-start.8 = (f32[304,128]{1,0:T(8,128)S(1)}, f32[304,128]{1,0:T(8,128)S(1)}, u32[]{:S(2)}, u32[]{:S(2)}) collective-permute-start(f32[304,128]{1,0:T(8,128)S(1)} %collective-permute-done.5.refs_7_), channel_id=1, source_target_pairs={{0,4},{4,0},{1,5},{5,1},{2,6},{6,2},{3,7},{7,3},{8,12},{12,8},{9,1... | collective-permute-start | bytes 466952 | tf_op jit(solution)/shard_map/ppermute | solution.py:288
  39.2 12.5 %collective-permute-start.17 = (f32[304,512]{1,0:T(8,128)S(1)}, f32[304,512]{1,0:T(8,128)S(1)}, u32[]{:S(2)}, u32[]{:S(2)}) collective-permute-start(f32[304,512]{1,0:T(8,128)S(1)} %bitcast.17), channel_id=1, source_target_pairs={{0,1},{1,0},{2,3},{3,2},{4,5},{5,4},{6,7},{7,6},{8,9},{9,8},{10,11... | collective-permute-start | bytes 1867784 | tf_op jit(solution)/shard_map/ppermute | solution.py:259
  40.8 9.2 %collective-permute-start.13 = (f32[608,128]{1,0:T(8,128)S(1)}, f32[608,128]{1,0:T(8,128)S(1)}, u32[]{:S(2)}, u32[]{:S(2)}) collective-permute-start(f32[608,128]{1,0:T(8,128)S(1)} %get-tuple-element.44), channel_id=1, source_target_pairs={{0,4},{4,0},{1,5},{5,1},{2,6},{6,2},{3,7},{7,3},{8,12},{12,8},{9,1... | collective-permute-start | bytes 933896 | tf_op jit(solution)/shard_map/ppermute | solution.py:288
  41.5 8.3 %collective-permute-start.14 = (f32[304,128]{1,0:T(8,128)S(1)}, f32[304,128]{1,0:T(8,128)S(1)}, u32[]{:S(2)}, u32[]{:S(2)}) collective-permute-start(f32[304,128]{1,0:T(8,128)S(1)} %collective-permute-done.12.refs_14_.refs_7_), channel_id=1, source_target_pairs={{0,4},{4,0},{1,5},{5,1},{2,6},{6,2},{3,7},{7,3},{8,12},{12,8},{9,1... | collective-permute-start | bytes 466952 | tf_op jit(solution)/shard_map/ppermute | solution.py:288
  42.8 7.1 %collective-permute-start.15 = (f32[304,128]{1,0:T(8,128)S(1)}, f32[304,128]{1,0:T(8,128)S(1)}, u32[]{:S(2)}, u32[]{:S(2)}) collective-permute-start(f32[304,128]{1,0:T(8,128)S(1)} %get-tuple-element.45.refs_11_.refs_4_), channel_id=1, source_target_pairs={{0,8},{8,16},{16,24},{24,0},{1,9},{9,17},{17,25},{25,1},{2,10},{10... | collective-permute-start | bytes 466952 | tf_op jit(solution)/shard_map/ppermute | solution.py:282
  42.8 7.1 %collective-permute-start.16 = (f32[304,128]{1,0:T(8,128)S(1)}, f32[304,128]{1,0:T(8,128)S(1)}, u32[]{:S(2)}, u32[]{:S(2)}) collective-permute-start(f32[304,128]{1,0:T(8,128)S(1)} %get-tuple-element.45.refs_11_.refs_4_), channel_id=1, source_target_pairs={{0,24},{8,0},{16,8},{24,16},{1,25},{9,1},{17,9},{25,17},{2,26},{10... | collective-permute-start | bytes 466952 | tf_op jit(solution)/shard_map/ppermute | solution.py:282
  54.4 15.3 %collective-permute-start.19 = (f32[912,128]{1,0:T(8,128)S(1)}, f32[912,128]{1,0:T(8,128)S(1)}, u32[]{:S(2)}, u32[]{:S(2)}) collective-permute-start(f32[912,128]{1,0:T(8,128)S(1)} %get-tuple-element.49), channel_id=1, source_target_pairs={{0,4},{4,0},{1,5},{5,1},{2,6},{6,2},{3,7},{7,3},{8,12},{12,8},{9,1... | collective-permute-start | bytes 1400840 | tf_op jit(solution)/shard_map/ppermute | solution.py:288
  56.2 7.6 %collective-permute-start.18 = (f32[304,128]{1,0:T(8,128)S(1)}, f32[304,128]{1,0:T(8,128)S(1)}, u32[]{:S(2)}, u32[]{:S(2)}) collective-permute-start(f32[304,128]{1,0:T(8,128)S(1)} %collective-permute-done.15.refs_12_.refs_5_), channel_id=1, source_target_pairs={{0,8},{8,16},{16,24},{24,0},{1,9},{9,17},{17,25},{25,1},{2,10},{10... | collective-permute-start | bytes 466952 | tf_op jit(solution)/shard_map/ppermute | solution.py:282
  56.8 18.7 %collective-permute-start.24 = (f32[304,512]{1,0:T(8,128)S(1)}, f32[304,512]{1,0:T(8,128)S(1)}, u32[]{:S(2)}, u32[]{:S(2)}) collective-permute-start(f32[304,512]{1,0:T(8,128)S(1)} %bitcast.14), channel_id=1, source_target_pairs={{0,1},{1,0},{2,3},{3,2},{4,5},{5,4},{6,7},{7,6},{8,9},{9,8},{10,11... | collective-permute-start | bytes 1867784 | tf_op jit(solution)/shard_map/ppermute | solution.py:259
  73.4 17.0 %collective-permute-start.21 = (f32[304,512]{1,0:T(8,128)S(1)}, f32[304,512]{1,0:T(8,128)S(1)}, u32[]{:S(2)}, u32[]{:S(2)}) collective-permute-start(f32[304,512]{1,0:T(8,128)S(1)} %bitcast.16), channel_id=1, source_target_pairs={{0,1},{1,0},{2,3},{3,2},{4,5},{5,4},{6,7},{7,6},{8,9},{9,8},{10,11... | collective-permute-start | bytes 1867784 | tf_op jit(solution)/shard_map/ppermute | solution.py:259
  74.3 16.1 %collective-permute-start.22 = (f32[304,512]{1,0:T(8,128)S(1)}, f32[304,512]{1,0:T(8,128)S(1)}, u32[]{:S(2)}, u32[]{:S(2)}) collective-permute-start(f32[304,512]{1,0:T(8,128)S(1)} %get-tuple-element.52), channel_id=1, source_target_pairs={{0,2},{2,0},{1,3},{3,1},{4,6},{6,4},{5,7},{7,5},{8,10},{10,8},{9,1... | collective-permute-start | bytes 1867784 | tf_op jit(solution)/shard_map/ppermute | solution.py:248
  74.3 23.2 %collective-permute-start.23 = (f32[304,512]{1,0:T(8,128)S(1)}, f32[304,512]{1,0:T(8,128)S(1)}, u32[]{:S(2)}, u32[]{:S(2)}) collective-permute-start(f32[304,512]{1,0:T(8,128)S(1)} %bitcast.15), channel_id=1, source_target_pairs={{0,3},{1,2},{2,1},{3,0},{4,7},{5,6},{6,5},{7,4},{8,11},{9,10},{10,... | collective-permute-start | bytes 1867784 | tf_op jit(solution)/shard_map/ppermute | solution.py:265
  76.3 21.9 %collective-permute-start.25 = (f32[304,512]{1,0:T(8,128)S(1)}, f32[304,512]{1,0:T(8,128)S(1)}, u32[]{:S(2)}, u32[]{:S(2)}) collective-permute-start(f32[304,512]{1,0:T(8,128)S(1)} %get-tuple-element.59), channel_id=1, source_target_pairs={{0,4},{4,8},{8,12},{12,16},{16,20},{20,24},{24,28},{1,5},{5,9},{9,... | collective-permute-start | bytes 1867784 | tf_op jit(solution)/shard_map/ppermute | solution.py:251
  78.7 26.7 %collective-permute-start.26 = (f32[304,512]{1,0:T(8,128)S(1)}, f32[304,512]{1,0:T(8,128)S(1)}, u32[]{:S(2)}, u32[]{:S(2)}) collective-permute-start(f32[304,512]{1,0:T(8,128)S(1)} %get-tuple-element.60), channel_id=1, source_target_pairs={{0,6},{2,4},{4,10},{6,8},{8,14},{10,12},{12,18},{14,16},{16,22},{1... | collective-permute-start | bytes 1867784 | tf_op jit(solution)/shard_map/ppermute | solution.py:255
  (5 other events, 16.5 us)

commit v9 on v8

--- a/solution.py
+++ b/solution.py
@@ -212,12 +212,14 @@
     times(pair, high, low, info[0], 0, put)
 
 
-def totals_kernel(info, total1, keep0, *refs):
-    (*from0, own_ref, other_ref) = refs
-    first = info[0] == 0
-    total0 = functools.reduce(jnp.add, [keep0[...]] + [part[...] for part in from0])
-    own_ref[...] = jnp.where(first, total0, total1[...])
-    other_ref[...] = jnp.where(first, total1[...], total0)
+def total_kernel(info, *refs):
+    refs[-1][...] = functools.reduce(jnp.add, [term[...] for term in refs[:-1]])
+
+
+def pass_kernel(info, *refs):
+    count = len(refs) // 2
+    for source, target in zip(refs[:count], refs[count:]):
+        target[...] = source[...]
 
 
 def add_kernel(info, *refs):
@@ -247,12 +249,12 @@
     def swap(values):
         return lax.ppermute(values, "core", [(0, 1), (1, 0)])
 
-    def onward(values):
-        return lax.ppermute(values, ("line", "row"), [(i, i + 1) for i in range(lines * rows - 1)])
-
-    def onward_across(values):
-        route = [(2 * i + core, 2 * i + 3 - core) for i in range(lines * rows - 1) for core in range(2)]
-        return lax.ppermute(values, ("line", "row", "core"), route)
+    def onward(values, target):
+        def from_core(source):
+            route = [(2 * i + source, 2 * i + 2 + target) for i in range(lines * rows - 1)]
+            return lax.ppermute(values, ("line", "row", "core"), route)
+
+        return from_core(target), from_core(1 - target)
 
     def over_space(sent):
         return [
@@ -355,10 +357,10 @@
         "rest1",
         [one, whole, one],
         [info, high, low, pair2, pair1, *from1],
+        waits=far0,
         flops=3 * flops,
     )
-    passed0 = list(call(join_kernel, "pass0", [small], [info, *far0], waits=[early1])) if far0 else []
-    line0, row0 = own0 + near0 + far0, ordered(handed(joint0), handed(passed0))
+    line0, row0 = gathered(own0, near0, far0, [], joint0)
     pair0, d_send, d_cross, d_chip = call(
         functools.partial(lead_zero_kernel, lines),
         "lead0",
@@ -367,14 +369,19 @@
         flops=3 * flops,
     )
     d_from, d_from_cross = over_space(d_send), over_space_and_core(d_cross)
-    next_same, next_cross = call(totals_kernel, "totals", [one, one], [info, total1, keep0, *from0], waits=row0[-1:])
+    (total0,) = call(total_kernel, "total0", [one], [info, keep0, *from0], waits=row0[-1:])
+    (passed1,) = call(pass_kernel, "pass1", [one], [info, total1], waits=row0)
+    same1, cross1 = onward(passed1, 1)
+    same0, cross0 = onward(total0, 0)
     (d_keep,) = call(last_kernel, "last", [one], [info, high, low, pair0, early1], flops=flops)
-    sums = call(add_kernel, "add", [one, one], [info, d_keep, *d_from, swap(d_chip), *d_from_cross])
+    sums = call(
+        add_kernel, "add", [one, one], [info, d_keep, same1, *d_from, swap(d_chip), cross1, *d_from_cross]
+    )
     (result,) = call(
         finish_kernel,
         "finish",
         [jax.ShapeDtypeStruct((sensors, block), F32)],
-        [info, *sums, onward(next_same), onward_across(next_cross)],
+        [info, *sums, same0, cross0],
     )
     return result[None]
 

time: 109 us -> 105 us (0.963)
  waiting for transfers between devices: 47.7 us -> 43 us
    ppermute x2 -> x4, waiting for transfers between devices: 7.3 us -> 0.01 us  [from_core(): return lax.ppermute(values, ('line', 'row', 'core'), route)]
    ppermute x9, waiting for transfers between devices: 14 us -> 20.3 us  [shifted(): lax.ppermute(held[shift - step], 'line', [(i, (i + step) % lines) for i i...]
    ppermute x8, waiting for transfers between devices: 10.4 us -> 5.71 us  [handed(): lax.ppermute(values, 'row', [(i, (i - off) % rows) for i in range(rows)])]
    ppermute x3, waiting for transfers between devices: 8.94 us -> 10.1 us  [over_space(): lax.ppermute(sent[d - 1], 'space', [(i, (i + d) % spaces) for i in range(...]
    ppermute x2 -> x4, starting transfers between devices: 5.24 us -> 6.19 us  [from_core(): return lax.ppermute(values, ('line', 'row', 'core'), route)]
  transfers between devices with their start and end apart: 27 -> 29, of which waited for: 13 -> 12; matrix products, arithmetic and copies ran while one was open for 0% -> 0% of each run, Pallas kernels for 14% -> 15%
where the time goes in v9:
time: 105 us; the launch traced here: 103 us
  waiting for transfers between devices  43 us (41%)
  starting transfers between devices  33.5 us (32%)
  Pallas kernels  23.4 us (22%)
  local copies, waits for them, and re-layouts  3.21 us (3%)
    pallas_call x14, Pallas kernels, call(): pl.pallas_call(body, out_shape=shapes, in_specs=[SMEM_SPEC] + [VMEM_SPEC]...  23.4 us
    ppermute x9, waiting for transfers between devices, shifted(): lax.ppermute(held[shift - step], 'line', [(i, (i + step) % lines) for i i...  20.3 us
    ppermute x9, starting transfers between devices, shifted(): lax.ppermute(held[shift - step], 'line', [(i, (i + step) % lines) for i i...  11.5 us
    ppermute x3, waiting for transfers between devices, over_space(): lax.ppermute(sent[d - 1], 'space', [(i, (i + d) % spaces) for i in range(...  10.1 us
    ppermute x8, starting transfers between devices, handed(): lax.ppermute(values, 'row', [(i, (i - off) % rows) for i in range(rows)])  9.28 us
    ppermute x1, waiting for transfers between devices, over_space_and_core(): lax.ppermute(sent[d - 1], ('core', 'space'), [(c * spaces + i, (1 - c) *...  6.82 us
    ppermute x4, starting transfers between devices, from_core(): return lax.ppermute(values, ('line', 'row', 'core'), route)  6.19 us
    ppermute x8, waiting for transfers between devices, handed(): lax.ppermute(values, 'row', [(i, (i - off) % rows) for i in range(rows)])  5.71 us
  transfers between devices with their start and end apart: 29, of which 12 were waited for; matrix products, arithmetic and copies ran while one was open for 0% of the time, Pallas kernels for 15%

profile of v9, /device:TPU:0, one launch (start us, length us, event | category | flops | bytes accessed | tf_op | source)
XLA Modules:
  0.0 103.4 jit_solution(1449092271209797409)
XLA Ops:
  3.0 2.2 %copy-done = f32[1,1024,1024]{2,1,0:T(8,128)S(1)} copy-done((f32[1,1024,1024]{2,1,0:T(8,128)S(1)}, f32[1,1024,1024]{2,1,0:T(8,128)}, u32[]{:S(2)}) %copy-start) | copy-done | bytes 4194328
  7.2 2.9 %collective-permute-start.3 = (f32[304,128]{1,0:T(8,128)S(1)}, f32[304,128]{1,0:T(8,128)S(1)}, u32[]{:S(2)}, u32[]{:S(2)}) collective-permute-start(f32[304,128]{1,0:T(8,128)S(1)} %get-tuple-element.39.refs_4_), channel_id=1, source_target_pairs={{0,8},{8,16},{16,24},{24,0},{1,9},{9,17},{17,25},{25,1},{2,10},{10... | collective-permute-start | bytes 466952 | tf_op jit(solution)/shard_map/ppermute | solution.py:284
  10.1 2.0 %collective-permute-start.4 = (f32[304,128]{1,0:T(8,128)S(1)}, f32[304,128]{1,0:T(8,128)S(1)}, u32[]{:S(2)}, u32[]{:S(2)}) collective-permute-start(f32[304,128]{1,0:T(8,128)S(1)} %get-tuple-element.39.refs_4_), channel_id=1, source_target_pairs={{0,24},{8,0},{16,8},{24,16},{1,25},{9,1},{17,9},{25,17},{2,26},{10... | collective-permute-start | bytes 466952 | tf_op jit(solution)/shard_map/ppermute | solution.py:284
  12.1 1.7 %collective-permute-start.6 = (f32[304,128]{1,0:T(8,128)S(1)}, f32[304,128]{1,0:T(8,128)S(1)}, u32[]{:S(2)}, u32[]{:S(2)}) collective-permute-start(f32[304,128]{1,0:T(8,128)S(1)} %get-tuple-element.39.refs_4_), channel_id=1, source_target_pairs={{0,4},{4,0},{1,5},{5,1},{2,6},{6,2},{3,7},{7,3},{8,12},{12,8},{9,1... | collective-permute-start | bytes 466952 | tf_op jit(solution)/shard_map/ppermute | solution.py:290
  13.9 3.1 %collective-permute-done.3.refs_1_.refs_5_ = f32[304,128]{1,0:T(8,128)S(1)} collective-permute-done((f32[304,128]{1,0:T(8,128)S(1)}, f32[304,128]{1,0:T(8,128)S(1)}, u32[]{:S(2)}, u32[]{:S(2)}) %collective-permute-start.3) | collective-permute-done | bytes 155680 | tf_op jit(solution)/shard_map/ppermute | solution.py:284
  17.0 2.2 %collective-permute-done.4.refs_2_.refs_6_ = f32[304,128]{1,0:T(8,128)S(1)} collective-permute-done((f32[304,128]{1,0:T(8,128)S(1)}, f32[304,128]{1,0:T(8,128)S(1)}, u32[]{:S(2)}, u32[]{:S(2)}) %collective-permute-start.4) | collective-permute-done | bytes 155680 | tf_op jit(solution)/shard_map/ppermute | solution.py:284
  22.6 3.4 %collective-permute-done.9.refs_11_.refs_5_ = f32[304,128]{1,0:T(8,128)S(1)} collective-permute-done((f32[304,128]{1,0:T(8,128)S(1)}, f32[304,128]{1,0:T(8,128)S(1)}, u32[]{:S(2)}, u32[]{:S(2)}) %collective-permute-start.9) | collective-permute-done | bytes 155680 | tf_op jit(solution)/shard_map/ppermute | solution.py:284
  26.6 2.6 %collective-permute-done.5.refs_7_ = f32[304,128]{1,0:T(8,128)S(1)} collective-permute-done((f32[304,128]{1,0:T(8,128)S(1)}, f32[304,128]{1,0:T(8,128)S(1)}, u32[]{:S(2)}, u32[]{:S(2)}) %collective-permute-start.5) | collective-permute-done | bytes 155680 | tf_op jit(solution)/shard_map/ppermute | solution.py:284
  32.5 2.5 %collective-permute-done.11.refs_13_.refs_8_ = f32[304,128]{1,0:T(8,128)S(1)} collective-permute-done((f32[304,128]{1,0:T(8,128)S(1)}, f32[304,128]{1,0:T(8,128)S(1)}, u32[]{:S(2)}, u32[]{:S(2)}) %collective-permute-start.11) | collective-permute-done | bytes 155680 | tf_op jit(solution)/shard_map/ppermute | solution.py:290
  35.0 2.5 %collective-permute-done.12.refs_14_.refs_7_ = f32[304,128]{1,0:T(8,128)S(1)} collective-permute-done((f32[304,128]{1,0:T(8,128)S(1)}, f32[304,128]{1,0:T(8,128)S(1)}, u32[]{:S(2)}, u32[]{:S(2)}) %collective-permute-start.12) | collective-permute-done | bytes 155680 | tf_op jit(solution)/shard_map/ppermute | solution.py:284
  42.8 3.8 %collective-permute-start.16 = (f32[304,128]{1,0:T(8,128)S(1)}, f32[304,128]{1,0:T(8,128)S(1)}, u32[]{:S(2)}, u32[]{:S(2)}) collective-permute-start(f32[304,128]{1,0:T(8,128)S(1)} %get-tuple-element.43.refs_11_.refs_4_), channel_id=1, source_target_pairs={{0,24},{8,0},{16,8},{24,16},{1,25},{9,1},{17,9},{25,17},{2,26},{10... | collective-permute-start | bytes 466952 | tf_op jit(solution)/shard_map/ppermute | solution.py:284
  46.6 3.2 %collective-permute-done.14.refs_10_ = f32[304,128]{1,0:T(8,128)S(1)} collective-permute-done((f32[304,128]{1,0:T(8,128)S(1)}, f32[304,128]{1,0:T(8,128)S(1)}, u32[]{:S(2)}, u32[]{:S(2)}) %collective-permute-start.14) | collective-permute-done | bytes 155680 | tf_op jit(solution)/shard_map/ppermute | solution.py:290
  49.9 1.8 %collective-permute-done.17.refs_14_.refs_5_ = f32[304,512]{1,0:T(8,128)S(1)} collective-permute-done((f32[304,512]{1,0:T(8,128)S(1)}, f32[304,512]{1,0:T(8,128)S(1)}, u32[]{:S(2)}, u32[]{:S(2)}) %collective-permute-start.17) | collective-permute-done | bytes 622624 | tf_op jit(solution)/shard_map/ppermute | solution.py:261
  51.7 2.7 %lead1.1 = (bf16[608,1024]{1,0:T(8,128)(2,1)S(1)}, f32[1,304,512]{2,1,0:T(8,128)S(1)}, f32[912,128]{1,0:T(8,128)S(1)}) custom-call(s32[4]{0:T(128)S(1)} %pad_add_fusion.refs_0_, bf16[2,2,1024,512]{3,2,1,0:T(8,128)(2,1)S(1)} %get-tuple-element.36.refs_1_, bf16[2,2,1024,512]{3,2,1,0:T(8,128)(2,1)S(1)} %get-tuple-element.37.refs_2_, ...), custom_call_target="tpu_custom_call" | custom-call | flops 1912602624 | bytes 1 | tf_op jit(solution)/shard_map/lead1/pallas_call | solution.py:25
  54.4 1.8 %collective-permute-start.19 = (f32[912,128]{1,0:T(8,128)S(1)}, f32[912,128]{1,0:T(8,128)S(1)}, u32[]{:S(2)}, u32[]{:S(2)}) collective-permute-start(f32[912,128]{1,0:T(8,128)S(1)} %get-tuple-element.47), channel_id=1, source_target_pairs={{0,4},{4,0},{1,5},{5,1},{2,6},{6,2},{3,7},{7,3},{8,12},{12,8},{9,1... | collective-permute-start | bytes 1400840 | tf_op jit(solution)/shard_map/ppermute | solution.py:290
  56.8 6.4 %collective-permute-done.18.refs_6_.refs_7_ = f32[304,128]{1,0:T(8,128)S(1)} collective-permute-done((f32[304,128]{1,0:T(8,128)S(1)}, f32[304,128]{1,0:T(8,128)S(1)}, u32[]{:S(2)}, u32[]{:S(2)}) %collective-permute-start.18) | collective-permute-done | bytes 155680 | tf_op jit(solution)/shard_map/ppermute | solution.py:284
  63.5 1.7 %collective-permute-start.26 = (f32[304,512]{1,0:T(8,128)S(1)}, f32[304,512]{1,0:T(8,128)S(1)}, u32[]{:S(2)}, u32[]{:S(2)}) collective-permute-start(f32[304,512]{1,0:T(8,128)S(1)} %bitcast.14), channel_id=1, source_target_pairs={{0,1},{1,0},{2,3},{3,2},{4,5},{5,4},{6,7},{7,6},{8,9},{9,8},{10,11... | collective-permute-start | bytes 1867784 | tf_op jit(solution)/shard_map/ppermute | solution.py:261
  65.2 5.5 %rest1.1 = (f32[304,512]{1,0:T(8,128)S(1)}, f32[2,304,512]{2,1,0:T(8,128)S(1)}, f32[304,512]{1,0:T(8,128)S(1)}) custom-call(s32[4]{0:T(128)S(1)} %pad_add_fusion.refs_0_, bf16[2,2,1024,512]{3,2,1,0:T(8,128)(2,1)S(1)} %get-tuple-element.36.refs_1_, bf16[2,2,1024,512]{3,2,1,0:T(8,128)(2,1)S(1)} %get-tuple-element.37.refs_2_, ...), custom_call_target="tpu_custom_call" | custom-call | flops 2868903936 | bytes 1 | tf_op jit(solution)/shard_map/rest1/pallas_call | solution.py:25
  73.4 3.7 %lead0.1 = (bf16[608,1024]{1,0:T(8,128)(2,1)S(1)}, f32[1,304,512]{2,1,0:T(8,128)S(1)}, f32[1,304,512]{2,1,0:T(8,128)S(1)}, f32[304,512]{1,0:T(8,128)S(1)}) custom-call(s32[4]{0:T(128)S(1)} %pad_add_fusion.refs_0_, bf16[2,2,1024,512]{3,2,1,0:T(8,128)(2,1)S(1)} %get-tuple-element.36.refs_1_, bf16[2,2,1024,512]{3,2,1,0:T(8,128)(2,1)S(1)} %get-tuple-element.37.refs_2_, ...), custom_call_target="tpu_custom_call" | custom-call | flops 2868903936 | bytes 1 | tf_op jit(solution)/shard_map/lead0/pallas_call | solution.py:25
  77.4 1.9 %collective-permute-start.25 = (f32[304,512]{1,0:T(8,128)S(1)}, f32[304,512]{1,0:T(8,128)S(1)}, u32[]{:S(2)}, u32[]{:S(2)}) collective-permute-start(f32[304,512]{1,0:T(8,128)S(1)} %bitcast.15), channel_id=1, source_target_pairs={{0,3},{1,2},{2,1},{3,0},{4,7},{5,6},{6,5},{7,4},{8,11},{9,10},{10,... | collective-permute-start | bytes 1867784 | tf_op jit(solution)/shard_map/ppermute | solution.py:267
  79.9 3.5 %collective-permute-start.27 = (f32[304,512]{1,0:T(8,128)S(1)}, f32[304,512]{1,0:T(8,128)S(1)}, u32[]{:S(2)}, u32[]{:S(2)}) collective-permute-start(f32[304,512]{1,0:T(8,128)S(1)} %total0.1), channel_id=1, source_target_pairs={{0,4},{4,8},{8,12},{12,16},{16,20},{20,24},{24,28},{1,5},{5,9},{9,... | collective-permute-start | bytes 1867784 | tf_op jit(solution)/shard_map/ppermute | solution.py:255
  85.8 8.3 %collective-permute-done.22.refs_3_ = f32[304,512]{1,0:T(8,128)S(1)} collective-permute-done((f32[304,512]{1,0:T(8,128)S(1)}, f32[304,512]{1,0:T(8,128)S(1)}, u32[]{:S(2)}, u32[]{:S(2)}) %collective-permute-start.22) | collective-permute-done | bytes 622624 | tf_op jit(solution)/shard_map/ppermute | solution.py:261
  94.1 6.8 %collective-permute-done.25.refs_6_ = f32[304,512]{1,0:T(8,128)S(1)} collective-permute-done((f32[304,512]{1,0:T(8,128)S(1)}, f32[304,512]{1,0:T(8,128)S(1)}, u32[]{:S(2)}, u32[]{:S(2)}) %collective-permute-start.25) | collective-permute-done | bytes 622624 | tf_op jit(solution)/shard_map/ppermute | solution.py:267
  101.7 1.8 %finish.1 = f32[600,512]{1,0:T(8,128)} custom-call(s32[4]{0:T(128)S(1)} %pad_add_fusion.refs_0_, f32[304,512]{1,0:T(8,128)S(1)} %get-tuple-element.53.refs_1_, f32[304,512]{1,0:T(8,128)S(1)} %get-tuple-element.54.refs_2_, f32[304,512]{1,0:T(8,128)S(1)} %collective-permute-done.27.refs_3_, f32[304,512]{1,0:T(8,128)S(1)} %collective-permute-done.28.refs_4_), custom_call_target="tpu_custom_call" | custom-call | bytes 1 | tf_op jit(solution)/shard_map/finish/pallas_call | solution.py:25
  (53 shorter events, 25.2 us)
Async XLA Ops:
  6.6 23.9 %collective-permute-start.1 = (f32[1024,512]{1,0:T(8,128)S(1)}, f32[1024,512]{1,0:T(8,128)S(1)}, u32[]{:S(2)}, u32[]{:S(2)}) collective-permute-start(f32[1024,512]{1,0:T(8,128)S(1)} %get-tuple-element.34), channel_id=1, source_target_pairs={{0,2},{2,0},{1,3},{3,1},{4,6},{6,4},{5,7},{7,5},{8,10},{10,8},{9,1... | collective-permute-start | bytes 6291464 | tf_op jit(solution)/shard_map/ppermute | solution.py:250
  7.0 23.4 %collective-permute-start.2 = (f32[1024,512]{1,0:T(8,128)S(1)}, f32[1024,512]{1,0:T(8,128)S(1)}, u32[]{:S(2)}, u32[]{:S(2)}) collective-permute-start(f32[1024,512]{1,0:T(8,128)S(1)} %get-tuple-element.35), channel_id=1, source_target_pairs={{0,2},{2,0},{1,3},{3,1},{4,6},{6,4},{5,7},{7,5},{8,10},{10,8},{9,1... | collective-permute-start | bytes 6291464 | tf_op jit(solution)/shard_map/ppermute | solution.py:250
  7.2 9.8 %collective-permute-start.3 = (f32[304,128]{1,0:T(8,128)S(1)}, f32[304,128]{1,0:T(8,128)S(1)}, u32[]{:S(2)}, u32[]{:S(2)}) collective-permute-start(f32[304,128]{1,0:T(8,128)S(1)} %get-tuple-element.39.refs_4_), channel_id=1, source_target_pairs={{0,8},{8,16},{16,24},{24,0},{1,9},{9,17},{17,25},{25,1},{2,10},{10... | collective-permute-start | bytes 466952 | tf_op jit(solution)/shard_map/ppermute | solution.py:284
  10.1 9.1 %collective-permute-start.4 = (f32[304,128]{1,0:T(8,128)S(1)}, f32[304,128]{1,0:T(8,128)S(1)}, u32[]{:S(2)}, u32[]{:S(2)}) collective-permute-start(f32[304,128]{1,0:T(8,128)S(1)} %get-tuple-element.39.refs_4_), channel_id=1, source_target_pairs={{0,24},{8,0},{16,8},{24,16},{1,25},{9,1},{17,9},{25,17},{2,26},{10... | collective-permute-start | bytes 466952 | tf_op jit(solution)/shard_map/ppermute | solution.py:284
  12.1 8.5 %collective-permute-start.6 = (f32[304,128]{1,0:T(8,128)S(1)}, f32[304,128]{1,0:T(8,128)S(1)}, u32[]{:S(2)}, u32[]{:S(2)}) collective-permute-start(f32[304,128]{1,0:T(8,128)S(1)} %get-tuple-element.39.refs_4_), channel_id=1, source_target_pairs={{0,4},{4,0},{1,5},{5,1},{2,6},{6,2},{3,7},{7,3},{8,12},{12,8},{9,1... | collective-permute-start | bytes 466952 | tf_op jit(solution)/shard_map/ppermute | solution.py:290
  17.0 9.0 %collective-permute-start.9 = (f32[304,128]{1,0:T(8,128)S(1)}, f32[304,128]{1,0:T(8,128)S(1)}, u32[]{:S(2)}, u32[]{:S(2)}) collective-permute-start(f32[304,128]{1,0:T(8,128)S(1)} %get-tuple-element.40.refs_4_), channel_id=1, source_target_pairs={{0,8},{8,16},{16,24},{24,0},{1,9},{9,17},{17,25},{25,1},{2,10},{10... | collective-permute-start | bytes 466952 | tf_op jit(solution)/shard_map/ppermute | solution.py:284
  19.2 10.0 %collective-permute-start.5 = (f32[304,128]{1,0:T(8,128)S(1)}, f32[304,128]{1,0:T(8,128)S(1)}, u32[]{:S(2)}, u32[]{:S(2)}) collective-permute-start(f32[304,128]{1,0:T(8,128)S(1)} %collective-permute-done.3.refs_1_.refs_5_), channel_id=1, source_target_pairs={{0,8},{8,16},{16,24},{24,0},{1,9},{9,17},{17,25},{25,1},{2,10},{10... | collective-permute-start | bytes 466952 | tf_op jit(solution)/shard_map/ppermute | solution.py:284
  21.2 16.3 %collective-permute-start.7 = (f32[608,128]{1,0:T(8,128)S(1)}, f32[608,128]{1,0:T(8,128)S(1)}, u32[]{:S(2)}, u32[]{:S(2)}) collective-permute-start(f32[608,128]{1,0:T(8,128)S(1)} %join2.1), channel_id=1, source_target_pairs={{0,4},{4,0},{1,5},{5,1},{2,6},{6,2},{3,7},{7,3},{8,12},{12,8},{9,1... | collective-permute-start | bytes 933896 | tf_op jit(solution)/shard_map/ppermute | solution.py:290
  30.4 7.0 %collective-permute-start.12 = (f32[304,128]{1,0:T(8,128)S(1)}, f32[304,128]{1,0:T(8,128)S(1)}, u32[]{:S(2)}, u32[]{:S(2)}) collective-permute-start(f32[304,128]{1,0:T(8,128)S(1)} %collective-permute-done.9.refs_11_.refs_5_), channel_id=1, source_target_pairs={{0,8},{8,16},{16,24},{24,0},{1,9},{9,17},{17,25},{25,1},{2,10},{10... | collective-permute-start | bytes 466952 | tf_op jit(solution)/shard_map/ppermute | solution.py:284
  39.2 12.5 %collective-permute-start.17 = (f32[304,512]{1,0:T(8,128)S(1)}, f32[304,512]{1,0:T(8,128)S(1)}, u32[]{:S(2)}, u32[]{:S(2)}) collective-permute-start(f32[304,512]{1,0:T(8,128)S(1)} %bitcast.17), channel_id=1, source_target_pairs={{0,1},{1,0},{2,3},{3,2},{4,5},{5,4},{6,7},{7,6},{8,9},{9,8},{10,11... | collective-permute-start | bytes 1867784 | tf_op jit(solution)/shard_map/ppermute | solution.py:261
  40.8 9.2 %collective-permute-start.13 = (f32[608,128]{1,0:T(8,128)S(1)}, f32[608,128]{1,0:T(8,128)S(1)}, u32[]{:S(2)}, u32[]{:S(2)}) collective-permute-start(f32[608,128]{1,0:T(8,128)S(1)} %get-tuple-element.42), channel_id=1, source_target_pairs={{0,4},{4,0},{1,5},{5,1},{2,6},{6,2},{3,7},{7,3},{8,12},{12,8},{9,1... | collective-permute-start | bytes 933896 | tf_op jit(solution)/shard_map/ppermute | solution.py:290
  41.5 8.4 %collective-permute-start.14 = (f32[304,128]{1,0:T(8,128)S(1)}, f32[304,128]{1,0:T(8,128)S(1)}, u32[]{:S(2)}, u32[]{:S(2)}) collective-permute-start(f32[304,128]{1,0:T(8,128)S(1)} %collective-permute-done.12.refs_14_.refs_7_), channel_id=1, source_target_pairs={{0,4},{4,0},{1,5},{5,1},{2,6},{6,2},{3,7},{7,3},{8,12},{12,8},{9,1... | collective-permute-start | bytes 466952 | tf_op jit(solution)/shard_map/ppermute | solution.py:290
  42.8 7.1 %collective-permute-start.15 = (f32[304,128]{1,0:T(8,128)S(1)}, f32[304,128]{1,0:T(8,128)S(1)}, u32[]{:S(2)}, u32[]{:S(2)}) collective-permute-start(f32[304,128]{1,0:T(8,128)S(1)} %get-tuple-element.43.refs_11_.refs_4_), channel_id=1, source_target_pairs={{0,8},{8,16},{16,24},{24,0},{1,9},{9,17},{17,25},{25,1},{2,10},{10... | collective-permute-start | bytes 466952 | tf_op jit(solution)/shard_map/ppermute | solution.py:284
  42.8 7.1 %collective-permute-start.16 = (f32[304,128]{1,0:T(8,128)S(1)}, f32[304,128]{1,0:T(8,128)S(1)}, u32[]{:S(2)}, u32[]{:S(2)}) collective-permute-start(f32[304,128]{1,0:T(8,128)S(1)} %get-tuple-element.43.refs_11_.refs_4_), channel_id=1, source_target_pairs={{0,24},{8,0},{16,8},{24,16},{1,25},{9,1},{17,9},{25,17},{2,26},{10... | collective-permute-start | bytes 466952 | tf_op jit(solution)/shard_map/ppermute | solution.py:284
  54.4 16.4 %collective-permute-start.19 = (f32[912,128]{1,0:T(8,128)S(1)}, f32[912,128]{1,0:T(8,128)S(1)}, u32[]{:S(2)}, u32[]{:S(2)}) collective-permute-start(f32[912,128]{1,0:T(8,128)S(1)} %get-tuple-element.47), channel_id=1, source_target_pairs={{0,4},{4,0},{1,5},{5,1},{2,6},{6,2},{3,7},{7,3},{8,12},{12,8},{9,1... | collective-permute-start | bytes 1400840 | tf_op jit(solution)/shard_map/ppermute | solution.py:290
  63.2 7.5 %collective-permute-start.20 = (f32[304,128]{1,0:T(8,128)S(1)}, f32[304,128]{1,0:T(8,128)S(1)}, u32[]{:S(2)}, u32[]{:S(2)}) collective-permute-start(f32[304,128]{1,0:T(8,128)S(1)} %collective-permute-done.18.refs_6_.refs_7_), channel_id=1, source_target_pairs={{0,4},{4,0},{1,5},{5,1},{2,6},{6,2},{3,7},{7,3},{8,12},{12,8},{9,1... | collective-permute-start | bytes 466952 | tf_op jit(solution)/shard_map/ppermute | solution.py:290
  63.5 13.9 %collective-permute-start.26 = (f32[304,512]{1,0:T(8,128)S(1)}, f32[304,512]{1,0:T(8,128)S(1)}, u32[]{:S(2)}, u32[]{:S(2)}) collective-permute-start(f32[304,512]{1,0:T(8,128)S(1)} %bitcast.14), channel_id=1, source_target_pairs={{0,1},{1,0},{2,3},{3,2},{4,5},{5,4},{6,7},{7,6},{8,9},{9,8},{10,11... | collective-permute-start | bytes 1867784 | tf_op jit(solution)/shard_map/ppermute | solution.py:261
  71.3 8.5 %collective-permute-start.21 = (f32[304,512]{1,0:T(8,128)S(1)}, f32[304,512]{1,0:T(8,128)S(1)}, u32[]{:S(2)}, u32[]{:S(2)}) collective-permute-start(f32[304,512]{1,0:T(8,128)S(1)} %pass1.1), channel_id=1, source_target_pairs={{2,6},{6,10},{10,14},{14,18},{18,22},{22,26},{26,30},{3,7},{7,11},... | collective-permute-start | bytes 1867784 | tf_op jit(solution)/shard_map/ppermute | solution.py:255
  72.1 11.3 %collective-permute-start.24 = (f32[304,512]{1,0:T(8,128)S(1)}, f32[304,512]{1,0:T(8,128)S(1)}, u32[]{:S(2)}, u32[]{:S(2)}) collective-permute-start(f32[304,512]{1,0:T(8,128)S(1)} %pass1.1), channel_id=1, source_target_pairs={{0,6},{4,10},{8,14},{12,18},{16,22},{20,26},{24,30},{1,7},{5,11},{... | collective-permute-start | bytes 1867784 | tf_op jit(solution)/shard_map/ppermute | solution.py:255
  77.1 17.0 %collective-permute-start.22 = (f32[304,512]{1,0:T(8,128)S(1)}, f32[304,512]{1,0:T(8,128)S(1)}, u32[]{:S(2)}, u32[]{:S(2)}) collective-permute-start(f32[304,512]{1,0:T(8,128)S(1)} %bitcast.16), channel_id=1, source_target_pairs={{0,1},{1,0},{2,3},{3,2},{4,5},{5,4},{6,7},{7,6},{8,9},{9,8},{10,11... | collective-permute-start | bytes 1867784 | tf_op jit(solution)/shard_map/ppermute | solution.py:261
  77.4 16.7 %collective-permute-start.23 = (f32[304,512]{1,0:T(8,128)S(1)}, f32[304,512]{1,0:T(8,128)S(1)}, u32[]{:S(2)}, u32[]{:S(2)}) collective-permute-start(f32[304,512]{1,0:T(8,128)S(1)} %get-tuple-element.51), channel_id=1, source_target_pairs={{0,2},{2,0},{1,3},{3,1},{4,6},{6,4},{5,7},{7,5},{8,10},{10,8},{9,1... | collective-permute-start | bytes 1867784 | tf_op jit(solution)/shard_map/ppermute | solution.py:250
  77.4 23.5 %collective-permute-start.25 = (f32[304,512]{1,0:T(8,128)S(1)}, f32[304,512]{1,0:T(8,128)S(1)}, u32[]{:S(2)}, u32[]{:S(2)}) collective-permute-start(f32[304,512]{1,0:T(8,128)S(1)} %bitcast.15), channel_id=1, source_target_pairs={{0,3},{1,2},{2,1},{3,0},{4,7},{5,6},{6,5},{7,4},{8,11},{9,10},{10,... | collective-permute-start | bytes 1867784 | tf_op jit(solution)/shard_map/ppermute | solution.py:267
  79.9 21.8 %collective-permute-start.27 = (f32[304,512]{1,0:T(8,128)S(1)}, f32[304,512]{1,0:T(8,128)S(1)}, u32[]{:S(2)}, u32[]{:S(2)}) collective-permute-start(f32[304,512]{1,0:T(8,128)S(1)} %total0.1), channel_id=1, source_target_pairs={{0,4},{4,8},{8,12},{12,16},{16,20},{20,24},{24,28},{1,5},{5,9},{9,... | collective-permute-start | bytes 1867784 | tf_op jit(solution)/shard_map/ppermute | solution.py:255
  83.4 18.3 %collective-permute-start.28 = (f32[304,512]{1,0:T(8,128)S(1)}, f32[304,512]{1,0:T(8,128)S(1)}, u32[]{:S(2)}, u32[]{:S(2)}) collective-permute-start(f32[304,512]{1,0:T(8,128)S(1)} %total0.1), channel_id=1, source_target_pairs={{2,4},{6,8},{10,12},{14,16},{18,20},{22,24},{26,28},{3,5},{7,9},{1... | collective-permute-start | bytes 1867784 | tf_op jit(solution)/shard_map/ppermute | solution.py:255
  (7 other events, 31.8 us)

commit v10 on v9

--- a/solution.py
+++ b/solution.py
@@ -145,20 +145,12 @@
 
 
 def rest_one_kernel(info, high, low, pair2, pair1, *refs):
-    (*from1, keep, other, total1) = refs
+    (*from1, other, total1) = refs
 
     def put_total(columns, total):
         total1[:, columns] = functools.reduce(jnp.add, [total] + [part[:, columns] for part in from1])
 
-    def put_keep(columns, total):
-        keep[:, columns] = total
-
-    def add_keep(columns, total):
-        keep[:, columns] += total
-
     times(pair2, high, low, 1, 0, put_total)
-    times(pair2, high, low, 0, 0, put_keep)
-    times(pair1, high, low, 1, 0, add_keep)
     for turn in range(high.shape[1]):
 
         def put(columns, total):
@@ -212,8 +204,17 @@
     times(pair, high, low, info[0], 0, put)
 
 
-def total_kernel(info, *refs):
-    refs[-1][...] = functools.reduce(jnp.add, [term[...] for term in refs[:-1]])
+def total_kernel(info, high, low, pair2, pair1, *refs):
+    (*from0, total0) = refs
+
+    def put(columns, total):
+        total0[:, columns] = functools.reduce(jnp.add, [total] + [part[:, columns] for part in from0])
+
+    def add(columns, total):
+        total0[:, columns] += total
+
+    times(pair2, high, low, 0, 0, put)
+    times(pair1, high, low, 1, 0, add)
 
 
 def pass_kernel(info, *refs):
@@ -222,17 +223,17 @@
         target[...] = source[...]
 
 
-def add_kernel(info, *refs):
-    count = len(refs) // 2 - 1
+def add_kernel(count, info, *refs):
     for terms, out_ref in ((refs[:count], refs[-2]), (refs[count:-2], refs[-1])):
         out_ref[...] = functools.reduce(jnp.add, [term[...] for term in terms])
 
 
-def finish_kernel(info, own_sum, other_sum, next_own, next_other, out_ref):
+def finish_kernel(info, own_sum, other_sum, next_own, next_other, *refs):
+    (*crossed, out_ref) = refs
     first = info[0] == 0
     sensors, half = out_ref.shape[0], own_sum.shape[0]
     own = own_sum[...] + next_own[...]
-    other = other_sum[...] + next_other[...]
+    other = functools.reduce(jnp.add, [other_sum[...] + next_other[...]] + [part[...] for part in crossed])
     out_ref[:half, :] = jnp.where(first, own, other)
     out_ref[half:, :] = jnp.where(first, other, own)[2 * half - sensors :, :]
 
@@ -352,10 +353,10 @@
         flops=2 * flops,
     )
     from0 = over_space(send0)
-    keep0, early1, total1 = call(
+    early1, total1 = call(
         rest_one_kernel,
         "rest1",
-        [one, whole, one],
+        [whole, one],
         [info, high, low, pair2, pair1, *from1],
         waits=far0,
         flops=3 * flops,
@@ -369,19 +370,18 @@
         flops=3 * flops,
     )
     d_from, d_from_cross = over_space(d_send), over_space_and_core(d_cross)
-    (total0,) = call(total_kernel, "total0", [one], [info, keep0, *from0], waits=row0[-1:])
+    (total0,) = call(total_kernel, "total0", [one], [info, high, low, pair2, pair1, *from0], waits=row0[-1:])
     (passed1,) = call(pass_kernel, "pass1", [one], [info, total1], waits=row0)
     same1, cross1 = onward(passed1, 1)
     same0, cross0 = onward(total0, 0)
     (d_keep,) = call(last_kernel, "last", [one], [info, high, low, pair0, early1], flops=flops)
-    sums = call(
-        add_kernel, "add", [one, one], [info, d_keep, same1, *d_from, swap(d_chip), cross1, *d_from_cross]
-    )
+    owns, others = [d_keep, same1, *d_from], [swap(d_chip), cross1]
+    sums = call(functools.partial(add_kernel, len(owns)), "add", [one, one], [info, *owns, *others])
     (result,) = call(
         finish_kernel,
         "finish",
         [jax.ShapeDtypeStruct((sensors, block), F32)],
-        [info, *sums, same0, cross0],
+        [info, *sums, same0, cross0, *d_from_cross],
     )
     return result[None]
 

time: 105 us -> 102 us (0.971); the launches traced: 103 us -> 102 us
  waiting for transfers between devices: 43 us -> 41.4 us
    ppermute x3, waiting for transfers between devices: 10.1 us -> 8.09 us  [over_space(): lax.ppermute(sent[d - 1], 'space', [(i, (i + d) % spaces) for i in range(...]
where the time goes in v10:
time: 102 us
  waiting for transfers between devices  41.4 us (41%)
  starting transfers between devices  33.5 us (33%)
  Pallas kernels  23.6 us (23%)
  local copies, waits for them, and re-layouts  3.21 us (3%)
    pallas_call x14, Pallas kernels, call(): pl.pallas_call(body, out_shape=shapes, in_specs=[SMEM_SPEC] + [VMEM_SPEC]...  23.6 us
    ppermute x9, waiting for transfers between devices, shifted(): lax.ppermute(held[shift - step], 'line', [(i, (i + step) % lines) for i i...  20.3 us
    ppermute x9, starting transfers between devices, shifted(): lax.ppermute(held[shift - step], 'line', [(i, (i + step) % lines) for i i...  11.5 us
    ppermute x8, starting transfers between devices, handed(): lax.ppermute(values, 'row', [(i, (i - off) % rows) for i in range(rows)])  9.28 us
    ppermute x3, waiting for transfers between devices, over_space(): lax.ppermute(sent[d - 1], 'space', [(i, (i + d) % spaces) for i in range(...  8.09 us
    ppermute x1, waiting for transfers between devices, over_space_and_core(): lax.ppermute(sent[d - 1], ('core', 'space'), [(c * spaces + i, (1 - c) *...  7.24 us
    ppermute x4, starting transfers between devices, from_core(): return lax.ppermute(values, ('line', 'row', 'core'), route)  6.19 us
    ppermute x8, waiting for transfers between devices, handed(): lax.ppermute(values, 'row', [(i, (i - off) % rows) for i in range(rows)])  5.71 us
  transfers between devices with their start and end apart: 29, of which 12 were waited for; matrix products, arithmetic and copies ran while one was open for 0% of the time, Pallas kernels for 15%

profile of v10, /device:TPU:0, one launch (start us, length us, event | category | flops | bytes accessed | tf_op | source)
XLA Modules:
  0.0 101.9 jit_solution(16977686175725715307)
XLA Ops:
  3.0 2.2 %copy-done = f32[1,1024,1024]{2,1,0:T(8,128)S(1)} copy-done((f32[1,1024,1024]{2,1,0:T(8,128)S(1)}, f32[1,1024,1024]{2,1,0:T(8,128)}, u32[]{:S(2)}) %copy-start) | copy-done | bytes 4194328
  7.2 2.9 %collective-permute-start.3 = (f32[304,128]{1,0:T(8,128)S(1)}, f32[304,128]{1,0:T(8,128)S(1)}, u32[]{:S(2)}, u32[]{:S(2)}) collective-permute-start(f32[304,128]{1,0:T(8,128)S(1)} %get-tuple-element.38.refs_4_), channel_id=1, source_target_pairs={{0,8},{8,16},{16,24},{24,0},{1,9},{9,17},{17,25},{25,1},{2,10},{10... | collective-permute-start | bytes 466952 | tf_op jit(solution)/shard_map/ppermute | solution.py:285
  10.1 2.0 %collective-permute-start.4 = (f32[304,128]{1,0:T(8,128)S(1)}, f32[304,128]{1,0:T(8,128)S(1)}, u32[]{:S(2)}, u32[]{:S(2)}) collective-permute-start(f32[304,128]{1,0:T(8,128)S(1)} %get-tuple-element.38.refs_4_), channel_id=1, source_target_pairs={{0,24},{8,0},{16,8},{24,16},{1,25},{9,1},{17,9},{25,17},{2,26},{10... | collective-permute-start | bytes 466952 | tf_op jit(solution)/shard_map/ppermute | solution.py:285
  12.1 1.7 %collective-permute-start.6 = (f32[304,128]{1,0:T(8,128)S(1)}, f32[304,128]{1,0:T(8,128)S(1)}, u32[]{:S(2)}, u32[]{:S(2)}) collective-permute-start(f32[304,128]{1,0:T(8,128)S(1)} %get-tuple-element.38.refs_4_), channel_id=1, source_target_pairs={{0,4},{4,0},{1,5},{5,1},{2,6},{6,2},{3,7},{7,3},{8,12},{12,8},{9,1... | collective-permute-start | bytes 466952 | tf_op jit(solution)/shard_map/ppermute | solution.py:291
  13.9 3.1 %collective-permute-done.3.refs_1_.refs_5_ = f32[304,128]{1,0:T(8,128)S(1)} collective-permute-done((f32[304,128]{1,0:T(8,128)S(1)}, f32[304,128]{1,0:T(8,128)S(1)}, u32[]{:S(2)}, u32[]{:S(2)}) %collective-permute-start.3) | collective-permute-done | bytes 155680 | tf_op jit(solution)/shard_map/ppermute | solution.py:285
  17.0 2.2 %collective-permute-done.4.refs_2_.refs_6_ = f32[304,128]{1,0:T(8,128)S(1)} collective-permute-done((f32[304,128]{1,0:T(8,128)S(1)}, f32[304,128]{1,0:T(8,128)S(1)}, u32[]{:S(2)}, u32[]{:S(2)}) %collective-permute-start.4) | collective-permute-done | bytes 155680 | tf_op jit(solution)/shard_map/ppermute | solution.py:285
  22.6 3.4 %collective-permute-done.9.refs_11_.refs_5_ = f32[304,128]{1,0:T(8,128)S(1)} collective-permute-done((f32[304,128]{1,0:T(8,128)S(1)}, f32[304,128]{1,0:T(8,128)S(1)}, u32[]{:S(2)}, u32[]{:S(2)}) %collective-permute-start.9) | collective-permute-done | bytes 155680 | tf_op jit(solution)/shard_map/ppermute | solution.py:285
  26.6 2.6 %collective-permute-done.5.refs_7_ = f32[304,128]{1,0:T(8,128)S(1)} collective-permute-done((f32[304,128]{1,0:T(8,128)S(1)}, f32[304,128]{1,0:T(8,128)S(1)}, u32[]{:S(2)}, u32[]{:S(2)}) %collective-permute-start.5) | collective-permute-done | bytes 155680 | tf_op jit(solution)/shard_map/ppermute | solution.py:285
  32.5 2.5 %collective-permute-done.11.refs_13_.refs_8_ = f32[304,128]{1,0:T(8,128)S(1)} collective-permute-done((f32[304,128]{1,0:T(8,128)S(1)}, f32[304,128]{1,0:T(8,128)S(1)}, u32[]{:S(2)}, u32[]{:S(2)}) %collective-permute-start.11) | collective-permute-done | bytes 155680 | tf_op jit(solution)/shard_map/ppermute | solution.py:291
  35.0 2.5 %collective-permute-done.12.refs_14_.refs_7_ = f32[304,128]{1,0:T(8,128)S(1)} collective-permute-done((f32[304,128]{1,0:T(8,128)S(1)}, f32[304,128]{1,0:T(8,128)S(1)}, u32[]{:S(2)}, u32[]{:S(2)}) %collective-permute-start.12) | collective-permute-done | bytes 155680 | tf_op jit(solution)/shard_map/ppermute | solution.py:285
  42.8 3.8 %collective-permute-start.16 = (f32[304,128]{1,0:T(8,128)S(1)}, f32[304,128]{1,0:T(8,128)S(1)}, u32[]{:S(2)}, u32[]{:S(2)}) collective-permute-start(f32[304,128]{1,0:T(8,128)S(1)} %get-tuple-element.42.refs_11_.refs_4_), channel_id=1, source_target_pairs={{0,24},{8,0},{16,8},{24,16},{1,25},{9,1},{17,9},{25,17},{2,26},{10... | collective-permute-start | bytes 466952 | tf_op jit(solution)/shard_map/ppermute | solution.py:285
  46.6 3.2 %collective-permute-done.14.refs_10_ = f32[304,128]{1,0:T(8,128)S(1)} collective-permute-done((f32[304,128]{1,0:T(8,128)S(1)}, f32[304,128]{1,0:T(8,128)S(1)}, u32[]{:S(2)}, u32[]{:S(2)}) %collective-permute-start.14) | collective-permute-done | bytes 155680 | tf_op jit(solution)/shard_map/ppermute | solution.py:291
  49.9 1.8 %collective-permute-done.17.refs_14_.refs_5_ = f32[304,512]{1,0:T(8,128)S(1)} collective-permute-done((f32[304,512]{1,0:T(8,128)S(1)}, f32[304,512]{1,0:T(8,128)S(1)}, u32[]{:S(2)}, u32[]{:S(2)}) %collective-permute-start.17) | collective-permute-done | bytes 622624 | tf_op jit(solution)/shard_map/ppermute | solution.py:262
  51.7 2.7 %lead1.1 = (bf16[608,1024]{1,0:T(8,128)(2,1)S(1)}, f32[1,304,512]{2,1,0:T(8,128)S(1)}, f32[912,128]{1,0:T(8,128)S(1)}) custom-call(s32[4]{0:T(128)S(1)} %pad_add_fusion.refs_0_, bf16[2,2,1024,512]{3,2,1,0:T(8,128)(2,1)S(1)} %get-tuple-element.35.refs_1_, bf16[2,2,1024,512]{3,2,1,0:T(8,128)(2,1)S(1)} %get-tuple-element.36.refs_2_, ...), custom_call_target="tpu_custom_call" | custom-call | flops 1912602624 | bytes 1 | tf_op jit(solution)/shard_map/lead1/pallas_call | solution.py:25
  54.4 1.8 %collective-permute-start.19 = (f32[912,128]{1,0:T(8,128)S(1)}, f32[912,128]{1,0:T(8,128)S(1)}, u32[]{:S(2)}, u32[]{:S(2)}) collective-permute-start(f32[912,128]{1,0:T(8,128)S(1)} %get-tuple-element.46), channel_id=1, source_target_pairs={{0,4},{4,0},{1,5},{5,1},{2,6},{6,2},{3,7},{7,3},{8,12},{12,8},{9,1... | collective-permute-start | bytes 1400840 | tf_op jit(solution)/shard_map/ppermute | solution.py:291
  56.8 6.4 %collective-permute-done.18.refs_6_.refs_7_ = f32[304,128]{1,0:T(8,128)S(1)} collective-permute-done((f32[304,128]{1,0:T(8,128)S(1)}, f32[304,128]{1,0:T(8,128)S(1)}, u32[]{:S(2)}, u32[]{:S(2)}) %collective-permute-start.18) | collective-permute-done | bytes 155680 | tf_op jit(solution)/shard_map/ppermute | solution.py:285
  63.5 1.7 %collective-permute-start.25 = (f32[304,512]{1,0:T(8,128)S(1)}, f32[304,512]{1,0:T(8,128)S(1)}, u32[]{:S(2)}, u32[]{:S(2)}) collective-permute-start(f32[304,512]{1,0:T(8,128)S(1)} %bitcast.14), channel_id=1, source_target_pairs={{0,1},{1,0},{2,3},{3,2},{4,5},{5,4},{6,7},{7,6},{8,9},{9,8},{10,11... | collective-permute-start | bytes 1867784 | tf_op jit(solution)/shard_map/ppermute | solution.py:262
  65.2 3.6 %rest1.1 = (f32[2,304,512]{2,1,0:T(8,128)S(1)}, f32[304,512]{1,0:T(8,128)S(1)}) custom-call(s32[4]{0:T(128)S(1)} %pad_add_fusion.refs_0_, bf16[2,2,1024,512]{3,2,1,0:T(8,128)(2,1)S(1)} %get-tuple-element.35.refs_1_, bf16[2,2,1024,512]{3,2,1,0:T(8,128)(2,1)S(1)} %get-tuple-element.36.refs_2_, bf16[608,1024]{1,0:T(8,128)(2,1)S(1)} %get-tuple-element.40.refs_3_, ...), custom_call_target="tpu_custom_call" | custom-call | flops 2868903936 | bytes 1 | tf_op jit(solution)/shard_map/rest1/pallas_call | solution.py:25
  71.5 3.7 %lead0.1 = (bf16[608,1024]{1,0:T(8,128)(2,1)S(1)}, f32[1,304,512]{2,1,0:T(8,128)S(1)}, f32[1,304,512]{2,1,0:T(8,128)S(1)}, f32[304,512]{1,0:T(8,128)S(1)}) custom-call(s32[4]{0:T(128)S(1)} %pad_add_fusion.refs_0_, bf16[2,2,1024,512]{3,2,1,0:T(8,128)(2,1)S(1)} %get-tuple-element.35.refs_1_, bf16[2,2,1024,512]{3,2,1,0:T(8,128)(2,1)S(1)} %get-tuple-element.36.refs_2_, ...), custom_call_target="tpu_custom_call" | custom-call | flops 2868903936 | bytes 1 | tf_op jit(solution)/shard_map/lead0/pallas_call | solution.py:25
  77.3 2.6 %total0.1 = f32[304,512]{1,0:T(8,128)S(1)} custom-call(s32[4]{0:T(128)S(1)} %pad_add_fusion.refs_0_, bf16[2,2,1024,512]{3,2,1,0:T(8,128)(2,1)S(1)} %get-tuple-element.35.refs_1_, bf16[2,2,1024,512]{3,2,1,0:T(8,128)(2,1)S(1)} %get-tuple-element.36.refs_2_, bf16[608,1024]{1,0:T(8,128)(2,1)S(1)} %get-tuple-element.40.refs_3_, ...), custom_call_target="tpu_custom_call" | custom-call | bytes 1 | tf_op jit(solution)/shard_map/total0/pallas_call | solution.py:25
  80.0 3.5 %collective-permute-start.26 = (f32[304,512]{1,0:T(8,128)S(1)}, f32[304,512]{1,0:T(8,128)S(1)}, u32[]{:S(2)}, u32[]{:S(2)}) collective-permute-start(f32[304,512]{1,0:T(8,128)S(1)} %total0.1), channel_id=1, source_target_pairs={{0,4},{4,8},{8,12},{12,16},{16,20},{20,24},{24,28},{1,5},{5,9},{9,... | collective-permute-start | bytes 1867784 | tf_op jit(solution)/shard_map/ppermute | solution.py:256
  85.8 6.3 %collective-permute-done.22.refs_3_ = f32[304,512]{1,0:T(8,128)S(1)} collective-permute-done((f32[304,512]{1,0:T(8,128)S(1)}, f32[304,512]{1,0:T(8,128)S(1)}, u32[]{:S(2)}, u32[]{:S(2)}) %collective-permute-start.22) | collective-permute-done | bytes 622624 | tf_op jit(solution)/shard_map/ppermute | solution.py:262
  92.9 7.2 %collective-permute-done.28.refs_5_ = f32[304,512]{1,0:T(8,128)S(1)} collective-permute-done((f32[304,512]{1,0:T(8,128)S(1)}, f32[304,512]{1,0:T(8,128)S(1)}, u32[]{:S(2)}, u32[]{:S(2)}) %collective-permute-start.28) | collective-permute-done | bytes 622624 | tf_op jit(solution)/shard_map/ppermute | solution.py:268
  100.1 1.8 %finish.1 = f32[600,512]{1,0:T(8,128)} custom-call(s32[4]{0:T(128)S(1)} %pad_add_fusion.refs_0_, f32[304,512]{1,0:T(8,128)S(1)} %get-tuple-element.51.refs_1_, f32[304,512]{1,0:T(8,128)S(1)} %get-tuple-element.52.refs_2_, f32[304,512]{1,0:T(8,128)S(1)} %collective-permute-done.26.refs_3_, f32[304,512]{1,0:T(8,128)S(1)} %collective-permute-done.27.refs_4_, ...), custom_call_target="tpu_custom_call" | custom-call | bytes 1 | tf_op jit(solution)/shard_map/finish/pallas_call | solution.py:25
  (53 shorter events, 26.4 us)
Async XLA Ops:
  6.6 23.9 %collective-permute-start.1 = (f32[1024,512]{1,0:T(8,128)S(1)}, f32[1024,512]{1,0:T(8,128)S(1)}, u32[]{:S(2)}, u32[]{:S(2)}) collective-permute-start(f32[1024,512]{1,0:T(8,128)S(1)} %get-tuple-element.33), channel_id=1, source_target_pairs={{0,2},{2,0},{1,3},{3,1},{4,6},{6,4},{5,7},{7,5},{8,10},{10,8},{9,1... | collective-permute-start | bytes 6291464 | tf_op jit(solution)/shard_map/ppermute | solution.py:251
  7.0 23.4 %collective-permute-start.2 = (f32[1024,512]{1,0:T(8,128)S(1)}, f32[1024,512]{1,0:T(8,128)S(1)}, u32[]{:S(2)}, u32[]{:S(2)}) collective-permute-start(f32[1024,512]{1,0:T(8,128)S(1)} %get-tuple-element.34), channel_id=1, source_target_pairs={{0,2},{2,0},{1,3},{3,1},{4,6},{6,4},{5,7},{7,5},{8,10},{10,8},{9,1... | collective-permute-start | bytes 6291464 | tf_op jit(solution)/shard_map/ppermute | solution.py:251
  7.2 9.8 %collective-permute-start.3 = (f32[304,128]{1,0:T(8,128)S(1)}, f32[304,128]{1,0:T(8,128)S(1)}, u32[]{:S(2)}, u32[]{:S(2)}) collective-permute-start(f32[304,128]{1,0:T(8,128)S(1)} %get-tuple-element.38.refs_4_), channel_id=1, source_target_pairs={{0,8},{8,16},{16,24},{24,0},{1,9},{9,17},{17,25},{25,1},{2,10},{10... | collective-permute-start | bytes 466952 | tf_op jit(solution)/shard_map/ppermute | solution.py:285
  10.1 9.1 %collective-permute-start.4 = (f32[304,128]{1,0:T(8,128)S(1)}, f32[304,128]{1,0:T(8,128)S(1)}, u32[]{:S(2)}, u32[]{:S(2)}) collective-permute-start(f32[304,128]{1,0:T(8,128)S(1)} %get-tuple-element.38.refs_4_), channel_id=1, source_target_pairs={{0,24},{8,0},{16,8},{24,16},{1,25},{9,1},{17,9},{25,17},{2,26},{10... | collective-permute-start | bytes 466952 | tf_op jit(solution)/shard_map/ppermute | solution.py:285
  12.1 8.5 %collective-permute-start.6 = (f32[304,128]{1,0:T(8,128)S(1)}, f32[304,128]{1,0:T(8,128)S(1)}, u32[]{:S(2)}, u32[]{:S(2)}) collective-permute-start(f32[304,128]{1,0:T(8,128)S(1)} %get-tuple-element.38.refs_4_), channel_id=1, source_target_pairs={{0,4},{4,0},{1,5},{5,1},{2,6},{6,2},{3,7},{7,3},{8,12},{12,8},{9,1... | collective-permute-start | bytes 466952 | tf_op jit(solution)/shard_map/ppermute | solution.py:291
  17.0 9.0 %collective-permute-start.9 = (f32[304,128]{1,0:T(8,128)S(1)}, f32[304,128]{1,0:T(8,128)S(1)}, u32[]{:S(2)}, u32[]{:S(2)}) collective-permute-start(f32[304,128]{1,0:T(8,128)S(1)} %get-tuple-element.39.refs_4_), channel_id=1, source_target_pairs={{0,8},{8,16},{16,24},{24,0},{1,9},{9,17},{17,25},{25,1},{2,10},{10... | collective-permute-start | bytes 466952 | tf_op jit(solution)/shard_map/ppermute | solution.py:285
  19.2 10.0 %collective-permute-start.5 = (f32[304,128]{1,0:T(8,128)S(1)}, f32[304,128]{1,0:T(8,128)S(1)}, u32[]{:S(2)}, u32[]{:S(2)}) collective-permute-start(f32[304,128]{1,0:T(8,128)S(1)} %collective-permute-done.3.refs_1_.refs_5_), channel_id=1, source_target_pairs={{0,8},{8,16},{16,24},{24,0},{1,9},{9,17},{17,25},{25,1},{2,10},{10... | collective-permute-start | bytes 466952 | tf_op jit(solution)/shard_map/ppermute | solution.py:285
  21.2 16.3 %collective-permute-start.7 = (f32[608,128]{1,0:T(8,128)S(1)}, f32[608,128]{1,0:T(8,128)S(1)}, u32[]{:S(2)}, u32[]{:S(2)}) collective-permute-start(f32[608,128]{1,0:T(8,128)S(1)} %join2.1), channel_id=1, source_target_pairs={{0,4},{4,0},{1,5},{5,1},{2,6},{6,2},{3,7},{7,3},{8,12},{12,8},{9,1... | collective-permute-start | bytes 933896 | tf_op jit(solution)/shard_map/ppermute | solution.py:291
  30.4 7.0 %collective-permute-start.12 = (f32[304,128]{1,0:T(8,128)S(1)}, f32[304,128]{1,0:T(8,128)S(1)}, u32[]{:S(2)}, u32[]{:S(2)}) collective-permute-start(f32[304,128]{1,0:T(8,128)S(1)} %collective-permute-done.9.refs_11_.refs_5_), channel_id=1, source_target_pairs={{0,8},{8,16},{16,24},{24,0},{1,9},{9,17},{17,25},{25,1},{2,10},{10... | collective-permute-start | bytes 466952 | tf_op jit(solution)/shard_map/ppermute | solution.py:285
  39.2 12.5 %collective-permute-start.17 = (f32[304,512]{1,0:T(8,128)S(1)}, f32[304,512]{1,0:T(8,128)S(1)}, u32[]{:S(2)}, u32[]{:S(2)}) collective-permute-start(f32[304,512]{1,0:T(8,128)S(1)} %bitcast.17), channel_id=1, source_target_pairs={{0,1},{1,0},{2,3},{3,2},{4,5},{5,4},{6,7},{7,6},{8,9},{9,8},{10,11... | collective-permute-start | bytes 1867784 | tf_op jit(solution)/shard_map/ppermute | solution.py:262
  40.8 9.2 %collective-permute-start.13 = (f32[608,128]{1,0:T(8,128)S(1)}, f32[608,128]{1,0:T(8,128)S(1)}, u32[]{:S(2)}, u32[]{:S(2)}) collective-permute-start(f32[608,128]{1,0:T(8,128)S(1)} %get-tuple-element.41), channel_id=1, source_target_pairs={{0,4},{4,0},{1,5},{5,1},{2,6},{6,2},{3,7},{7,3},{8,12},{12,8},{9,1... | collective-permute-start | bytes 933896 | tf_op jit(solution)/shard_map/ppermute | solution.py:291
  41.5 8.4 %collective-permute-start.14 = (f32[304,128]{1,0:T(8,128)S(1)}, f32[304,128]{1,0:T(8,128)S(1)}, u32[]{:S(2)}, u32[]{:S(2)}) collective-permute-start(f32[304,128]{1,0:T(8,128)S(1)} %collective-permute-done.12.refs_14_.refs_7_), channel_id=1, source_target_pairs={{0,4},{4,0},{1,5},{5,1},{2,6},{6,2},{3,7},{7,3},{8,12},{12,8},{9,1... | collective-permute-start | bytes 466952 | tf_op jit(solution)/shard_map/ppermute | solution.py:291
  42.8 7.1 %collective-permute-start.15 = (f32[304,128]{1,0:T(8,128)S(1)}, f32[304,128]{1,0:T(8,128)S(1)}, u32[]{:S(2)}, u32[]{:S(2)}) collective-permute-start(f32[304,128]{1,0:T(8,128)S(1)} %get-tuple-element.42.refs_11_.refs_4_), channel_id=1, source_target_pairs={{0,8},{8,16},{16,24},{24,0},{1,9},{9,17},{17,25},{25,1},{2,10},{10... | collective-permute-start | bytes 466952 | tf_op jit(solution)/shard_map/ppermute | solution.py:285
  42.8 7.1 %collective-permute-start.16 = (f32[304,128]{1,0:T(8,128)S(1)}, f32[304,128]{1,0:T(8,128)S(1)}, u32[]{:S(2)}, u32[]{:S(2)}) collective-permute-start(f32[304,128]{1,0:T(8,128)S(1)} %get-tuple-element.42.refs_11_.refs_4_), channel_id=1, source_target_pairs={{0,24},{8,0},{16,8},{24,16},{1,25},{9,1},{17,9},{25,17},{2,26},{10... | collective-permute-start | bytes 466952 | tf_op jit(solution)/shard_map/ppermute | solution.py:285
  54.4 14.5 %collective-permute-start.19 = (f32[912,128]{1,0:T(8,128)S(1)}, f32[912,128]{1,0:T(8,128)S(1)}, u32[]{:S(2)}, u32[]{:S(2)}) collective-permute-start(f32[912,128]{1,0:T(8,128)S(1)} %get-tuple-element.46), channel_id=1, source_target_pairs={{0,4},{4,0},{1,5},{5,1},{2,6},{6,2},{3,7},{7,3},{8,12},{12,8},{9,1... | collective-permute-start | bytes 1400840 | tf_op jit(solution)/shard_map/ppermute | solution.py:291
  56.2 7.0 %collective-permute-start.18 = (f32[304,128]{1,0:T(8,128)S(1)}, f32[304,128]{1,0:T(8,128)S(1)}, u32[]{:S(2)}, u32[]{:S(2)}) collective-permute-start(f32[304,128]{1,0:T(8,128)S(1)} %collective-permute-done.15.refs_12_.refs_5_), channel_id=1, source_target_pairs={{0,8},{8,16},{16,24},{24,0},{1,9},{9,17},{17,25},{25,1},{2,10},{10... | collective-permute-start | bytes 466952 | tf_op jit(solution)/shard_map/ppermute | solution.py:285
  63.5 12.8 %collective-permute-start.25 = (f32[304,512]{1,0:T(8,128)S(1)}, f32[304,512]{1,0:T(8,128)S(1)}, u32[]{:S(2)}, u32[]{:S(2)}) collective-permute-start(f32[304,512]{1,0:T(8,128)S(1)} %bitcast.14), channel_id=1, source_target_pairs={{0,1},{1,0},{2,3},{3,2},{4,5},{5,4},{6,7},{7,6},{8,9},{9,8},{10,11... | collective-permute-start | bytes 1867784 | tf_op jit(solution)/shard_map/ppermute | solution.py:262
  69.4 10.6 %collective-permute-start.21 = (f32[304,512]{1,0:T(8,128)S(1)}, f32[304,512]{1,0:T(8,128)S(1)}, u32[]{:S(2)}, u32[]{:S(2)}) collective-permute-start(f32[304,512]{1,0:T(8,128)S(1)} %pass1.1), channel_id=1, source_target_pairs={{2,6},{6,10},{10,14},{14,18},{18,22},{22,26},{26,30},{3,7},{7,11},... | collective-permute-start | bytes 1867784 | tf_op jit(solution)/shard_map/ppermute | solution.py:256
  70.1 13.3 %collective-permute-start.24 = (f32[304,512]{1,0:T(8,128)S(1)}, f32[304,512]{1,0:T(8,128)S(1)}, u32[]{:S(2)}, u32[]{:S(2)}) collective-permute-start(f32[304,512]{1,0:T(8,128)S(1)} %pass1.1), channel_id=1, source_target_pairs={{0,6},{4,10},{8,14},{12,18},{16,22},{20,26},{24,30},{1,7},{5,11},{... | collective-permute-start | bytes 1867784 | tf_op jit(solution)/shard_map/ppermute | solution.py:256
  75.1 17.0 %collective-permute-start.22 = (f32[304,512]{1,0:T(8,128)S(1)}, f32[304,512]{1,0:T(8,128)S(1)}, u32[]{:S(2)}, u32[]{:S(2)}) collective-permute-start(f32[304,512]{1,0:T(8,128)S(1)} %bitcast.16), channel_id=1, source_target_pairs={{0,1},{1,0},{2,3},{3,2},{4,5},{5,4},{6,7},{7,6},{8,9},{9,8},{10,11... | collective-permute-start | bytes 1867784 | tf_op jit(solution)/shard_map/ppermute | solution.py:262
  76.3 15.9 %collective-permute-start.23 = (f32[304,512]{1,0:T(8,128)S(1)}, f32[304,512]{1,0:T(8,128)S(1)}, u32[]{:S(2)}, u32[]{:S(2)}) collective-permute-start(f32[304,512]{1,0:T(8,128)S(1)} %get-tuple-element.50), channel_id=1, source_target_pairs={{0,2},{2,0},{1,3},{3,1},{4,6},{6,4},{5,7},{7,5},{8,10},{10,8},{9,1... | collective-permute-start | bytes 1867784 | tf_op jit(solution)/shard_map/ppermute | solution.py:251
  76.3 23.8 %collective-permute-start.28 = (f32[304,512]{1,0:T(8,128)S(1)}, f32[304,512]{1,0:T(8,128)S(1)}, u32[]{:S(2)}, u32[]{:S(2)}) collective-permute-start(f32[304,512]{1,0:T(8,128)S(1)} %bitcast.15), channel_id=1, source_target_pairs={{0,3},{1,2},{2,1},{3,0},{4,7},{5,6},{6,5},{7,4},{8,11},{9,10},{10,... | collective-permute-start | bytes 1867784 | tf_op jit(solution)/shard_map/ppermute | solution.py:268
  80.0 20.1 %collective-permute-start.26 = (f32[304,512]{1,0:T(8,128)S(1)}, f32[304,512]{1,0:T(8,128)S(1)}, u32[]{:S(2)}, u32[]{:S(2)}) collective-permute-start(f32[304,512]{1,0:T(8,128)S(1)} %total0.1), channel_id=1, source_target_pairs={{0,4},{4,8},{8,12},{12,16},{16,20},{20,24},{24,28},{1,5},{5,9},{9,... | collective-permute-start | bytes 1867784 | tf_op jit(solution)/shard_map/ppermute | solution.py:256
  83.5 16.7 %collective-permute-start.27 = (f32[304,512]{1,0:T(8,128)S(1)}, f32[304,512]{1,0:T(8,128)S(1)}, u32[]{:S(2)}, u32[]{:S(2)}) collective-permute-start(f32[304,512]{1,0:T(8,128)S(1)} %total0.1), channel_id=1, source_target_pairs={{2,4},{6,8},{10,12},{14,16},{18,20},{22,24},{26,28},{3,5},{7,9},{1... | collective-permute-start | bytes 1867784 | tf_op jit(solution)/shard_map/ppermute | solution.py:256
  (7 other events, 30.3 us)

commit v11 on v10

--- a/solution.py
+++ b/solution.py
@@ -176,7 +176,7 @@
 
 
 def lead_zero_kernel(lines, info, high, low, added, *refs):
-    blocks, (pair, send, cross, chip) = refs[:-4], refs[-4:]
+    blocks, (pair, send, cross) = refs[:-3], refs[-3:]
     fill(lines, blocks, pair)
     for turn in range(1, high.shape[1]):
 
@@ -187,12 +187,6 @@
             cross[turn - 1, :, columns] = total
 
         both_times(info, high, low, pair, added, turn, own_put, other_put)
-    later = jnp.where(info[0] == 0, 1.0, 0.0)
-
-    def put(columns, total):
-        chip[:, columns] = total + later * added[0, :, columns]
-
-    times(pair, high, low, 1 - info[0], 0, put)
 
 
 def last_kernel(info, high, low, pair, added, keep):
@@ -204,8 +198,14 @@
     times(pair, high, low, info[0], 0, put)
 
 
-def total_kernel(info, high, low, pair2, pair1, *refs):
-    (*from0, total0) = refs
+def total_kernel(info, high, low, pair2, pair1, pair0, added, *refs):
+    (*from0, total0, chip) = refs
+    later = jnp.where(info[0] == 0, 1.0, 0.0)
+
+    def put_chip(columns, total):
+        chip[:, columns] = total + later * added[0, :, columns]
+
+    times(pair0, high, low, 1 - info[0], 0, put_chip)
 
     def put(columns, total):
         total0[:, columns] = functools.reduce(jnp.add, [total] + [part[:, columns] for part in from0])
@@ -362,15 +362,17 @@
         flops=3 * flops,
     )
     line0, row0 = gathered(own0, near0, far0, [], joint0)
-    pair0, d_send, d_cross, d_chip = call(
+    pair0, d_send, d_cross = call(
         functools.partial(lead_zero_kernel, lines),
         "lead0",
-        [pair, sent, sent, one],
+        [pair, sent, sent],
         [info, high, low, early1, *line0, *row0],
         flops=3 * flops,
     )
     d_from, d_from_cross = over_space(d_send), over_space_and_core(d_cross)
-    (total0,) = call(total_kernel, "total0", [one], [info, high, low, pair2, pair1, *from0], waits=row0[-1:])
+    total0, d_chip = call(
+        total_kernel, "total0", [one] * 2, [info, high, low, pair2, pair1, pair0, early1, *from0]
+    )
     (passed1,) = call(pass_kernel, "pass1", [one], [info, total1], waits=row0)
     same1, cross1 = onward(passed1, 1)
     same0, cross0 = onward(total0, 0)

time: 102 us -> 102 us (level)
    ppermute x4, starting transfers between devices: 1.03 us -> 2.11 us  [swap(): return lax.ppermute(values, 'core', [(0, 1), (1, 0)])]
    ppermute x1, starting transfers between devices: 1.03 us -> 0.01 us  [over_space_and_core(): lax.ppermute(sent[d - 1], ('core', 'space'), [(c * spaces + i, (1 - c) *...]
where the time goes in v11:
time: 102 us
  waiting for transfers between devices  41.4 us (41%)
  starting transfers between devices  33.5 us (33%)
  Pallas kernels  23.6 us (23%)
  local copies, waits for them, and re-layouts  3.21 us (3%)
    pallas_call x14, Pallas kernels, call(): pl.pallas_call(body, out_shape=shapes, in_specs=[SMEM_SPEC] + [VMEM_SPEC]...  23.6 us
    ppermute x9, waiting for transfers between devices, shifted(): lax.ppermute(held[shift - step], 'line', [(i, (i + step) % lines) for i i...  20.3 us
    ppermute x9, starting transfers between devices, shifted(): lax.ppermute(held[shift - step], 'line', [(i, (i + step) % lines) for i i...  11.5 us
    ppermute x8, starting transfers between devices, handed(): lax.ppermute(values, 'row', [(i, (i - off) % rows) for i in range(rows)])  9.28 us
    ppermute x1, waiting for transfers between devices, over_space_and_core(): lax.ppermute(sent[d - 1], ('core', 'space'), [(c * spaces + i, (1 - c) *...  8.19 us
    ppermute x3, waiting for transfers between devices, over_space(): lax.ppermute(sent[d - 1], 'space', [(i, (i + d) % spaces) for i in range(...  7.09 us
    ppermute x4, starting transfers between devices, from_core(): return lax.ppermute(values, ('line', 'row', 'core'), route)  6.18 us
    ppermute x8, waiting for transfers between devices, handed(): lax.ppermute(values, 'row', [(i, (i - off) % rows) for i in range(rows)])  5.71 us
  transfers between devices with their start and end apart: 29, of which 12 were waited for; matrix products, arithmetic and copies ran while one was open for 0% of the time, Pallas kernels for 15%

profile of v11, /device:TPU:0, one launch (start us, length us, event | category | flops | bytes accessed | tf_op | source)
XLA Modules:
  0.0 101.9 jit_solution(10001569999106514013)
XLA Ops:
  3.0 2.2 %copy-done = f32[1,1024,1024]{2,1,0:T(8,128)S(1)} copy-done((f32[1,1024,1024]{2,1,0:T(8,128)S(1)}, f32[1,1024,1024]{2,1,0:T(8,128)}, u32[]{:S(2)}) %copy-start) | copy-done | bytes 4194328
  7.2 2.9 %collective-permute-start.3 = (f32[304,128]{1,0:T(8,128)S(1)}, f32[304,128]{1,0:T(8,128)S(1)}, u32[]{:S(2)}, u32[]{:S(2)}) collective-permute-start(f32[304,128]{1,0:T(8,128)S(1)} %get-tuple-element.39.refs_4_), channel_id=1, source_target_pairs={{0,8},{8,16},{16,24},{24,0},{1,9},{9,17},{17,25},{25,1},{2,10},{10... | collective-permute-start | bytes 466952 | tf_op jit(solution)/shard_map/ppermute | solution.py:285
  10.1 2.0 %collective-permute-start.4 = (f32[304,128]{1,0:T(8,128)S(1)}, f32[304,128]{1,0:T(8,128)S(1)}, u32[]{:S(2)}, u32[]{:S(2)}) collective-permute-start(f32[304,128]{1,0:T(8,128)S(1)} %get-tuple-element.39.refs_4_), channel_id=1, source_target_pairs={{0,24},{8,0},{16,8},{24,16},{1,25},{9,1},{17,9},{25,17},{2,26},{10... | collective-permute-start | bytes 466952 | tf_op jit(solution)/shard_map/ppermute | solution.py:285
  12.1 1.7 %collective-permute-start.6 = (f32[304,128]{1,0:T(8,128)S(1)}, f32[304,128]{1,0:T(8,128)S(1)}, u32[]{:S(2)}, u32[]{:S(2)}) collective-permute-start(f32[304,128]{1,0:T(8,128)S(1)} %get-tuple-element.39.refs_4_), channel_id=1, source_target_pairs={{0,4},{4,0},{1,5},{5,1},{2,6},{6,2},{3,7},{7,3},{8,12},{12,8},{9,1... | collective-permute-start | bytes 466952 | tf_op jit(solution)/shard_map/ppermute | solution.py:291
  13.9 3.1 %collective-permute-done.3.refs_1_.refs_5_ = f32[304,128]{1,0:T(8,128)S(1)} collective-permute-done((f32[304,128]{1,0:T(8,128)S(1)}, f32[304,128]{1,0:T(8,128)S(1)}, u32[]{:S(2)}, u32[]{:S(2)}) %collective-permute-start.3) | collective-permute-done | bytes 155680 | tf_op jit(solution)/shard_map/ppermute | solution.py:285
  17.0 2.2 %collective-permute-done.4.refs_2_.refs_6_ = f32[304,128]{1,0:T(8,128)S(1)} collective-permute-done((f32[304,128]{1,0:T(8,128)S(1)}, f32[304,128]{1,0:T(8,128)S(1)}, u32[]{:S(2)}, u32[]{:S(2)}) %collective-permute-start.4) | collective-permute-done | bytes 155680 | tf_op jit(solution)/shard_map/ppermute | solution.py:285
  22.6 3.4 %collective-permute-done.9.refs_11_.refs_5_ = f32[304,128]{1,0:T(8,128)S(1)} collective-permute-done((f32[304,128]{1,0:T(8,128)S(1)}, f32[304,128]{1,0:T(8,128)S(1)}, u32[]{:S(2)}, u32[]{:S(2)}) %collective-permute-start.9) | collective-permute-done | bytes 155680 | tf_op jit(solution)/shard_map/ppermute | solution.py:285
  26.6 2.6 %collective-permute-done.5.refs_7_ = f32[304,128]{1,0:T(8,128)S(1)} collective-permute-done((f32[304,128]{1,0:T(8,128)S(1)}, f32[304,128]{1,0:T(8,128)S(1)}, u32[]{:S(2)}, u32[]{:S(2)}) %collective-permute-start.5) | collective-permute-done | bytes 155680 | tf_op jit(solution)/shard_map/ppermute | solution.py:285
  32.5 2.5 %collective-permute-done.11.refs_13_.refs_8_ = f32[304,128]{1,0:T(8,128)S(1)} collective-permute-done((f32[304,128]{1,0:T(8,128)S(1)}, f32[304,128]{1,0:T(8,128)S(1)}, u32[]{:S(2)}, u32[]{:S(2)}) %collective-permute-start.11) | collective-permute-done | bytes 155680 | tf_op jit(solution)/shard_map/ppermute | solution.py:291
  35.0 2.5 %collective-permute-done.12.refs_14_.refs_7_ = f32[304,128]{1,0:T(8,128)S(1)} collective-permute-done((f32[304,128]{1,0:T(8,128)S(1)}, f32[304,128]{1,0:T(8,128)S(1)}, u32[]{:S(2)}, u32[]{:S(2)}) %collective-permute-start.12) | collective-permute-done | bytes 155680 | tf_op jit(solution)/shard_map/ppermute | solution.py:285
  42.8 3.8 %collective-permute-start.16 = (f32[304,128]{1,0:T(8,128)S(1)}, f32[304,128]{1,0:T(8,128)S(1)}, u32[]{:S(2)}, u32[]{:S(2)}) collective-permute-start(f32[304,128]{1,0:T(8,128)S(1)} %get-tuple-element.43.refs_11_.refs_4_), channel_id=1, source_target_pairs={{0,24},{8,0},{16,8},{24,16},{1,25},{9,1},{17,9},{25,17},{2,26},{10... | collective-permute-start | bytes 466952 | tf_op jit(solution)/shard_map/ppermute | solution.py:285
  46.6 3.2 %collective-permute-done.14.refs_10_ = f32[304,128]{1,0:T(8,128)S(1)} collective-permute-done((f32[304,128]{1,0:T(8,128)S(1)}, f32[304,128]{1,0:T(8,128)S(1)}, u32[]{:S(2)}, u32[]{:S(2)}) %collective-permute-start.14) | collective-permute-done | bytes 155680 | tf_op jit(solution)/shard_map/ppermute | solution.py:291
  49.9 1.8 %collective-permute-done.17.refs_14_.refs_5_ = f32[304,512]{1,0:T(8,128)S(1)} collective-permute-done((f32[304,512]{1,0:T(8,128)S(1)}, f32[304,512]{1,0:T(8,128)S(1)}, u32[]{:S(2)}, u32[]{:S(2)}) %collective-permute-start.17) | collective-permute-done | bytes 622624 | tf_op jit(solution)/shard_map/ppermute | solution.py:262
  51.7 2.7 %lead1.1 = (bf16[608,1024]{1,0:T(8,128)(2,1)S(1)}, f32[1,304,512]{2,1,0:T(8,128)S(1)}, f32[912,128]{1,0:T(8,128)S(1)}) custom-call(s32[4]{0:T(128)S(1)} %pad_add_fusion.refs_0_, bf16[2,2,1024,512]{3,2,1,0:T(8,128)(2,1)S(1)} %get-tuple-element.36.refs_1_, bf16[2,2,1024,512]{3,2,1,0:T(8,128)(2,1)S(1)} %get-tuple-element.37.refs_2_, ...), custom_call_target="tpu_custom_call" | custom-call | flops 1912602624 | bytes 1 | tf_op jit(solution)/shard_map/lead1/pallas_call | solution.py:25
  54.4 1.8 %collective-permute-start.19 = (f32[912,128]{1,0:T(8,128)S(1)}, f32[912,128]{1,0:T(8,128)S(1)}, u32[]{:S(2)}, u32[]{:S(2)}) collective-permute-start(f32[912,128]{1,0:T(8,128)S(1)} %get-tuple-element.47), channel_id=1, source_target_pairs={{0,4},{4,0},{1,5},{5,1},{2,6},{6,2},{3,7},{7,3},{8,12},{12,8},{9,1... | collective-permute-start | bytes 1400840 | tf_op jit(solution)/shard_map/ppermute | solution.py:291
  56.8 6.4 %collective-permute-done.18.refs_6_.refs_7_ = f32[304,128]{1,0:T(8,128)S(1)} collective-permute-done((f32[304,128]{1,0:T(8,128)S(1)}, f32[304,128]{1,0:T(8,128)S(1)}, u32[]{:S(2)}, u32[]{:S(2)}) %collective-permute-start.18) | collective-permute-done | bytes 155680 | tf_op jit(solution)/shard_map/ppermute | solution.py:285
  63.5 1.7 %collective-permute-start.23 = (f32[304,512]{1,0:T(8,128)S(1)}, f32[304,512]{1,0:T(8,128)S(1)}, u32[]{:S(2)}, u32[]{:S(2)}) collective-permute-start(f32[304,512]{1,0:T(8,128)S(1)} %bitcast.14), channel_id=1, source_target_pairs={{0,1},{1,0},{2,3},{3,2},{4,5},{5,4},{6,7},{7,6},{8,9},{9,8},{10,11... | collective-permute-start | bytes 1867784 | tf_op jit(solution)/shard_map/ppermute | solution.py:262
  65.2 3.6 %rest1.1 = (f32[2,304,512]{2,1,0:T(8,128)S(1)}, f32[304,512]{1,0:T(8,128)S(1)}) custom-call(s32[4]{0:T(128)S(1)} %pad_add_fusion.refs_0_, bf16[2,2,1024,512]{3,2,1,0:T(8,128)(2,1)S(1)} %get-tuple-element.36.refs_1_, bf16[2,2,1024,512]{3,2,1,0:T(8,128)(2,1)S(1)} %get-tuple-element.37.refs_2_, bf16[608,1024]{1,0:T(8,128)(2,1)S(1)} %get-tuple-element.41.refs_3_, ...), custom_call_target="tpu_custom_call" | custom-call | flops 2868903936 | bytes 1 | tf_op jit(solution)/shard_map/rest1/pallas_call | solution.py:25
  71.5 2.7 %lead0.1 = (bf16[608,1024]{1,0:T(8,128)(2,1)S(1)}, f32[1,304,512]{2,1,0:T(8,128)S(1)}, f32[1,304,512]{2,1,0:T(8,128)S(1)}) custom-call(s32[4]{0:T(128)S(1)} %pad_add_fusion.refs_0_, bf16[2,2,1024,512]{3,2,1,0:T(8,128)(2,1)S(1)} %get-tuple-element.36.refs_1_, bf16[2,2,1024,512]{3,2,1,0:T(8,128)(2,1)S(1)} %get-tuple-element.37.refs_2_, ...), custom_call_target="tpu_custom_call" | custom-call | flops 2868903936 | bytes 1 | tf_op jit(solution)/shard_map/lead0/pallas_call | solution.py:25
  75.4 3.6 %total0.1 = (f32[304,512]{1,0:T(8,128)S(1)}, f32[304,512]{1,0:T(8,128)S(1)}) custom-call(s32[4]{0:T(128)S(1)} %pad_add_fusion.refs_0_, bf16[2,2,1024,512]{3,2,1,0:T(8,128)(2,1)S(1)} %get-tuple-element.36.refs_1_, bf16[2,2,1024,512]{3,2,1,0:T(8,128)(2,1)S(1)} %get-tuple-element.37.refs_2_, bf16[608,1024]{1,0:T(8,128)(2,1)S(1)} %get-tuple-element.41.refs_3_, ...), custom_call_target="tpu_custom_call" | custom-call | bytes 1 | tf_op jit(solution)/shard_map/total0/pallas_call | solution.py:25
  80.0 3.4 %collective-permute-start.26 = (f32[304,512]{1,0:T(8,128)S(1)}, f32[304,512]{1,0:T(8,128)S(1)}, u32[]{:S(2)}, u32[]{:S(2)}) collective-permute-start(f32[304,512]{1,0:T(8,128)S(1)} %get-tuple-element.55), channel_id=1, source_target_pairs={{0,4},{4,8},{8,12},{12,16},{16,20},{20,24},{24,28},{1,5},{5,9},{9,... | collective-permute-start | bytes 1867784 | tf_op jit(solution)/shard_map/ppermute | solution.py:256
  85.9 5.3 %collective-permute-done.22.refs_3_ = f32[304,512]{1,0:T(8,128)S(1)} collective-permute-done((f32[304,512]{1,0:T(8,128)S(1)}, f32[304,512]{1,0:T(8,128)S(1)}, u32[]{:S(2)}, u32[]{:S(2)}) %collective-permute-start.22) | collective-permute-done | bytes 622624 | tf_op jit(solution)/shard_map/ppermute | solution.py:262
  91.9 8.2 %collective-permute-done.28.refs_5_ = f32[304,512]{1,0:T(8,128)S(1)} collective-permute-done((f32[304,512]{1,0:T(8,128)S(1)}, f32[304,512]{1,0:T(8,128)S(1)}, u32[]{:S(2)}, u32[]{:S(2)}) %collective-permute-start.28) | collective-permute-done | bytes 622624 | tf_op jit(solution)/shard_map/ppermute | solution.py:268
  100.1 1.8 %finish.1 = f32[600,512]{1,0:T(8,128)} custom-call(s32[4]{0:T(128)S(1)} %pad_add_fusion.refs_0_, f32[304,512]{1,0:T(8,128)S(1)} %get-tuple-element.53.refs_1_, f32[304,512]{1,0:T(8,128)S(1)} %get-tuple-element.54.refs_2_, f32[304,512]{1,0:T(8,128)S(1)} %collective-permute-done.26.refs_3_, f32[304,512]{1,0:T(8,128)S(1)} %collective-permute-done.27.refs_4_, ...), custom_call_target="tpu_custom_call" | custom-call | bytes 1 | tf_op jit(solution)/shard_map/finish/pallas_call | solution.py:25
  (53 shorter events, 26.5 us)
Async XLA Ops:
  6.6 23.9 %collective-permute-start.1 = (f32[1024,512]{1,0:T(8,128)S(1)}, f32[1024,512]{1,0:T(8,128)S(1)}, u32[]{:S(2)}, u32[]{:S(2)}) collective-permute-start(f32[1024,512]{1,0:T(8,128)S(1)} %get-tuple-element.34), channel_id=1, source_target_pairs={{0,2},{2,0},{1,3},{3,1},{4,6},{6,4},{5,7},{7,5},{8,10},{10,8},{9,1... | collective-permute-start | bytes 6291464 | tf_op jit(solution)/shard_map/ppermute | solution.py:251
  7.0 23.4 %collective-permute-start.2 = (f32[1024,512]{1,0:T(8,128)S(1)}, f32[1024,512]{1,0:T(8,128)S(1)}, u32[]{:S(2)}, u32[]{:S(2)}) collective-permute-start(f32[1024,512]{1,0:T(8,128)S(1)} %get-tuple-element.35), channel_id=1, source_target_pairs={{0,2},{2,0},{1,3},{3,1},{4,6},{6,4},{5,7},{7,5},{8,10},{10,8},{9,1... | collective-permute-start | bytes 6291464 | tf_op jit(solution)/shard_map/ppermute | solution.py:251
  7.2 9.8 %collective-permute-start.3 = (f32[304,128]{1,0:T(8,128)S(1)}, f32[304,128]{1,0:T(8,128)S(1)}, u32[]{:S(2)}, u32[]{:S(2)}) collective-permute-start(f32[304,128]{1,0:T(8,128)S(1)} %get-tuple-element.39.refs_4_), channel_id=1, source_target_pairs={{0,8},{8,16},{16,24},{24,0},{1,9},{9,17},{17,25},{25,1},{2,10},{10... | collective-permute-start | bytes 466952 | tf_op jit(solution)/shard_map/ppermute | solution.py:285
  10.1 9.1 %collective-permute-start.4 = (f32[304,128]{1,0:T(8,128)S(1)}, f32[304,128]{1,0:T(8,128)S(1)}, u32[]{:S(2)}, u32[]{:S(2)}) collective-permute-start(f32[304,128]{1,0:T(8,128)S(1)} %get-tuple-element.39.refs_4_), channel_id=1, source_target_pairs={{0,24},{8,0},{16,8},{24,16},{1,25},{9,1},{17,9},{25,17},{2,26},{10... | collective-permute-start | bytes 466952 | tf_op jit(solution)/shard_map/ppermute | solution.py:285
  12.1 8.5 %collective-permute-start.6 = (f32[304,128]{1,0:T(8,128)S(1)}, f32[304,128]{1,0:T(8,128)S(1)}, u32[]{:S(2)}, u32[]{:S(2)}) collective-permute-start(f32[304,128]{1,0:T(8,128)S(1)} %get-tuple-element.39.refs_4_), channel_id=1, source_target_pairs={{0,4},{4,0},{1,5},{5,1},{2,6},{6,2},{3,7},{7,3},{8,12},{12,8},{9,1... | collective-permute-start | bytes 466952 | tf_op jit(solution)/shard_map/ppermute | solution.py:291
  17.0 9.0 %collective-permute-start.9 = (f32[304,128]{1,0:T(8,128)S(1)}, f32[304,128]{1,0:T(8,128)S(1)}, u32[]{:S(2)}, u32[]{:S(2)}) collective-permute-start(f32[304,128]{1,0:T(8,128)S(1)} %get-tuple-element.40.refs_4_), channel_id=1, source_target_pairs={{0,8},{8,16},{16,24},{24,0},{1,9},{9,17},{17,25},{25,1},{2,10},{10... | collective-permute-start | bytes 466952 | tf_op jit(solution)/shard_map/ppermute | solution.py:285
  19.2 10.0 %collective-permute-start.5 = (f32[304,128]{1,0:T(8,128)S(1)}, f32[304,128]{1,0:T(8,128)S(1)}, u32[]{:S(2)}, u32[]{:S(2)}) collective-permute-start(f32[304,128]{1,0:T(8,128)S(1)} %collective-permute-done.3.refs_1_.refs_5_), channel_id=1, source_target_pairs={{0,8},{8,16},{16,24},{24,0},{1,9},{9,17},{17,25},{25,1},{2,10},{10... | collective-permute-start | bytes 466952 | tf_op jit(solution)/shard_map/ppermute | solution.py:285
  21.2 16.3 %collective-permute-start.7 = (f32[608,128]{1,0:T(8,128)S(1)}, f32[608,128]{1,0:T(8,128)S(1)}, u32[]{:S(2)}, u32[]{:S(2)}) collective-permute-start(f32[608,128]{1,0:T(8,128)S(1)} %join2.1), channel_id=1, source_target_pairs={{0,4},{4,0},{1,5},{5,1},{2,6},{6,2},{3,7},{7,3},{8,12},{12,8},{9,1... | collective-permute-start | bytes 933896 | tf_op jit(solution)/shard_map/ppermute | solution.py:291
  30.4 7.0 %collective-permute-start.12 = (f32[304,128]{1,0:T(8,128)S(1)}, f32[304,128]{1,0:T(8,128)S(1)}, u32[]{:S(2)}, u32[]{:S(2)}) collective-permute-start(f32[304,128]{1,0:T(8,128)S(1)} %collective-permute-done.9.refs_11_.refs_5_), channel_id=1, source_target_pairs={{0,8},{8,16},{16,24},{24,0},{1,9},{9,17},{17,25},{25,1},{2,10},{10... | collective-permute-start | bytes 466952 | tf_op jit(solution)/shard_map/ppermute | solution.py:285
  39.2 12.5 %collective-permute-start.17 = (f32[304,512]{1,0:T(8,128)S(1)}, f32[304,512]{1,0:T(8,128)S(1)}, u32[]{:S(2)}, u32[]{:S(2)}) collective-permute-start(f32[304,512]{1,0:T(8,128)S(1)} %bitcast.17), channel_id=1, source_target_pairs={{0,1},{1,0},{2,3},{3,2},{4,5},{5,4},{6,7},{7,6},{8,9},{9,8},{10,11... | collective-permute-start | bytes 1867784 | tf_op jit(solution)/shard_map/ppermute | solution.py:262
  40.8 9.2 %collective-permute-start.13 = (f32[608,128]{1,0:T(8,128)S(1)}, f32[608,128]{1,0:T(8,128)S(1)}, u32[]{:S(2)}, u32[]{:S(2)}) collective-permute-start(f32[608,128]{1,0:T(8,128)S(1)} %get-tuple-element.42), channel_id=1, source_target_pairs={{0,4},{4,0},{1,5},{5,1},{2,6},{6,2},{3,7},{7,3},{8,12},{12,8},{9,1... | collective-permute-start | bytes 933896 | tf_op jit(solution)/shard_map/ppermute | solution.py:291
  41.5 8.4 %collective-permute-start.14 = (f32[304,128]{1,0:T(8,128)S(1)}, f32[304,128]{1,0:T(8,128)S(1)}, u32[]{:S(2)}, u32[]{:S(2)}) collective-permute-start(f32[304,128]{1,0:T(8,128)S(1)} %collective-permute-done.12.refs_14_.refs_7_), channel_id=1, source_target_pairs={{0,4},{4,0},{1,5},{5,1},{2,6},{6,2},{3,7},{7,3},{8,12},{12,8},{9,1... | collective-permute-start | bytes 466952 | tf_op jit(solution)/shard_map/ppermute | solution.py:291
  42.8 7.1 %collective-permute-start.15 = (f32[304,128]{1,0:T(8,128)S(1)}, f32[304,128]{1,0:T(8,128)S(1)}, u32[]{:S(2)}, u32[]{:S(2)}) collective-permute-start(f32[304,128]{1,0:T(8,128)S(1)} %get-tuple-element.43.refs_11_.refs_4_), channel_id=1, source_target_pairs={{0,8},{8,16},{16,24},{24,0},{1,9},{9,17},{17,25},{25,1},{2,10},{10... | collective-permute-start | bytes 466952 | tf_op jit(solution)/shard_map/ppermute | solution.py:285
  42.8 7.1 %collective-permute-start.16 = (f32[304,128]{1,0:T(8,128)S(1)}, f32[304,128]{1,0:T(8,128)S(1)}, u32[]{:S(2)}, u32[]{:S(2)}) collective-permute-start(f32[304,128]{1,0:T(8,128)S(1)} %get-tuple-element.43.refs_11_.refs_4_), channel_id=1, source_target_pairs={{0,24},{8,0},{16,8},{24,16},{1,25},{9,1},{17,9},{25,17},{2,26},{10... | collective-permute-start | bytes 466952 | tf_op jit(solution)/shard_map/ppermute | solution.py:285
  54.4 14.5 %collective-permute-start.19 = (f32[912,128]{1,0:T(8,128)S(1)}, f32[912,128]{1,0:T(8,128)S(1)}, u32[]{:S(2)}, u32[]{:S(2)}) collective-permute-start(f32[912,128]{1,0:T(8,128)S(1)} %get-tuple-element.47), channel_id=1, source_target_pairs={{0,4},{4,0},{1,5},{5,1},{2,6},{6,2},{3,7},{7,3},{8,12},{12,8},{9,1... | collective-permute-start | bytes 1400840 | tf_op jit(solution)/shard_map/ppermute | solution.py:291
  56.2 7.0 %collective-permute-start.18 = (f32[304,128]{1,0:T(8,128)S(1)}, f32[304,128]{1,0:T(8,128)S(1)}, u32[]{:S(2)}, u32[]{:S(2)}) collective-permute-start(f32[304,128]{1,0:T(8,128)S(1)} %collective-permute-done.15.refs_12_.refs_5_), channel_id=1, source_target_pairs={{0,8},{8,16},{16,24},{24,0},{1,9},{9,17},{17,25},{25,1},{2,10},{10... | collective-permute-start | bytes 466952 | tf_op jit(solution)/shard_map/ppermute | solution.py:285
  63.5 11.9 %collective-permute-start.23 = (f32[304,512]{1,0:T(8,128)S(1)}, f32[304,512]{1,0:T(8,128)S(1)}, u32[]{:S(2)}, u32[]{:S(2)}) collective-permute-start(f32[304,512]{1,0:T(8,128)S(1)} %bitcast.14), channel_id=1, source_target_pairs={{0,1},{1,0},{2,3},{3,2},{4,5},{5,4},{6,7},{7,6},{8,9},{9,8},{10,11... | collective-permute-start | bytes 1867784 | tf_op jit(solution)/shard_map/ppermute | solution.py:262
  69.4 10.6 %collective-permute-start.21 = (f32[304,512]{1,0:T(8,128)S(1)}, f32[304,512]{1,0:T(8,128)S(1)}, u32[]{:S(2)}, u32[]{:S(2)}) collective-permute-start(f32[304,512]{1,0:T(8,128)S(1)} %pass1.1), channel_id=1, source_target_pairs={{2,6},{6,10},{10,14},{14,18},{18,22},{22,26},{26,30},{3,7},{7,11},... | collective-permute-start | bytes 1867784 | tf_op jit(solution)/shard_map/ppermute | solution.py:256
  70.1 13.4 %collective-permute-start.25 = (f32[304,512]{1,0:T(8,128)S(1)}, f32[304,512]{1,0:T(8,128)S(1)}, u32[]{:S(2)}, u32[]{:S(2)}) collective-permute-start(f32[304,512]{1,0:T(8,128)S(1)} %pass1.1), channel_id=1, source_target_pairs={{0,6},{4,10},{8,14},{12,18},{16,22},{20,26},{24,30},{1,7},{5,11},{... | collective-permute-start | bytes 1867784 | tf_op jit(solution)/shard_map/ppermute | solution.py:256
  74.2 17.0 %collective-permute-start.22 = (f32[304,512]{1,0:T(8,128)S(1)}, f32[304,512]{1,0:T(8,128)S(1)}, u32[]{:S(2)}, u32[]{:S(2)}) collective-permute-start(f32[304,512]{1,0:T(8,128)S(1)} %bitcast.16), channel_id=1, source_target_pairs={{0,1},{1,0},{2,3},{3,2},{4,5},{5,4},{6,7},{7,6},{8,9},{9,8},{10,11... | collective-permute-start | bytes 1867784 | tf_op jit(solution)/shard_map/ppermute | solution.py:262
  75.3 24.8 %collective-permute-start.28 = (f32[304,512]{1,0:T(8,128)S(1)}, f32[304,512]{1,0:T(8,128)S(1)}, u32[]{:S(2)}, u32[]{:S(2)}) collective-permute-start(f32[304,512]{1,0:T(8,128)S(1)} %bitcast.15), channel_id=1, source_target_pairs={{0,3},{1,2},{2,1},{3,0},{4,7},{5,6},{6,5},{7,4},{8,11},{9,10},{10,... | collective-permute-start | bytes 1867784 | tf_op jit(solution)/shard_map/ppermute | solution.py:268
  78.9 12.2 %collective-permute-start.24 = (f32[304,512]{1,0:T(8,128)S(1)}, f32[304,512]{1,0:T(8,128)S(1)}, u32[]{:S(2)}, u32[]{:S(2)}) collective-permute-start(f32[304,512]{1,0:T(8,128)S(1)} %get-tuple-element.52), channel_id=1, source_target_pairs={{0,2},{2,0},{1,3},{3,1},{4,6},{6,4},{5,7},{7,5},{8,10},{10,8},{9,1... | collective-permute-start | bytes 1867784 | tf_op jit(solution)/shard_map/ppermute | solution.py:251
  80.0 20.1 %collective-permute-start.26 = (f32[304,512]{1,0:T(8,128)S(1)}, f32[304,512]{1,0:T(8,128)S(1)}, u32[]{:S(2)}, u32[]{:S(2)}) collective-permute-start(f32[304,512]{1,0:T(8,128)S(1)} %get-tuple-element.55), channel_id=1, source_target_pairs={{0,4},{4,8},{8,12},{12,16},{16,20},{20,24},{24,28},{1,5},{5,9},{9,... | collective-permute-start | bytes 1867784 | tf_op jit(solution)/shard_map/ppermute | solution.py:256
  83.5 16.6 %collective-permute-start.27 = (f32[304,512]{1,0:T(8,128)S(1)}, f32[304,512]{1,0:T(8,128)S(1)}, u32[]{:S(2)}, u32[]{:S(2)}) collective-permute-start(f32[304,512]{1,0:T(8,128)S(1)} %get-tuple-element.55), channel_id=1, source_target_pairs={{2,4},{6,8},{10,12},{14,16},{18,20},{22,24},{26,28},{3,5},{7,9},{1... | collective-permute-start | bytes 1867784 | tf_op jit(solution)/shard_map/ppermute | solution.py:256
  (7 other events, 30.3 us)

commit v12 on v11

--- a/solution.py
+++ b/solution.py
@@ -373,8 +373,7 @@
     total0, d_chip = call(
         total_kernel, "total0", [one] * 2, [info, high, low, pair2, pair1, pair0, early1, *from0]
     )
-    (passed1,) = call(pass_kernel, "pass1", [one], [info, total1], waits=row0)
-    same1, cross1 = onward(passed1, 1)
+    same1, cross1 = onward(total1, 1)
     same0, cross0 = onward(total0, 0)
     (d_keep,) = call(last_kernel, "last", [one], [info, high, low, pair0, early1], flops=flops)
     owns, others = [d_keep, same1, *d_from], [swap(d_chip), cross1]

time: 102 us -> 112 us (1.098)
  the two profiles are of different devices: /device:TPU:0 before, /device:TPU:25 now
where the time goes in v12:
time: 112 us
  waiting for transfers between devices  50.2 us (45%)
  starting transfers between devices  35.3 us (32%)
  Pallas kernels  23 us (21%)
  local copies, waits for them, and re-layouts  3.21 us (3%)
    ppermute x8, waiting for transfers between devices, handed(): lax.ppermute(values, 'row', [(i, (i - off) % rows) for i in range(rows)])  24.3 us
    pallas_call x13, Pallas kernels, call(): pl.pallas_call(body, out_shape=shapes, in_specs=[SMEM_SPEC] + [VMEM_SPEC]...  23 us
    ppermute x1, waiting for transfers between devices, over_space_and_core(): lax.ppermute(sent[d - 1], ('core', 'space'), [(c * spaces + i, (1 - c) *...  14 us
    ppermute x9, starting transfers between devices, shifted(): lax.ppermute(held[shift - step], 'line', [(i, (i + step) % lines) for i i...  12.9 us
    ppermute x9, waiting for transfers between devices, shifted(): lax.ppermute(held[shift - step], 'line', [(i, (i + step) % lines) for i i...  8.67 us
    ppermute x4, starting transfers between devices, from_core(): return lax.ppermute(values, ('line', 'row', 'core'), route)  8.34 us
    ppermute x8, starting transfers between devices, handed(): lax.ppermute(values, 'row', [(i, (i - off) % rows) for i in range(rows)])  7.41 us
    unnamed x4, local copies, waits for them, and re-layouts  3.21 us
  transfers between devices with their start and end apart: 29, of which 12 were waited for; matrix products, arithmetic and copies ran while one was open for 0% of the time, Pallas kernels for 15%

profile of v12, /device:TPU:25, one launch (start us, length us, event | category | flops | bytes accessed | tf_op | source)
XLA Modules:
  0.0 112.0 jit_solution(10157335185264051007)
XLA Ops:
  3.3 2.2 %copy-done = f32[1,1024,1024]{2,1,0:T(8,128)S(1)} copy-done((f32[1,1024,1024]{2,1,0:T(8,128)S(1)}, f32[1,1024,1024]{2,1,0:T(8,128)}, u32[]{:S(2)}) %copy-start) | copy-done | bytes 4194328
  7.4 1.5 %collective-permute-start.4 = (f32[304,128]{1,0:T(8,128)S(1)}, f32[304,128]{1,0:T(8,128)S(1)}, u32[]{:S(2)}, u32[]{:S(2)}) collective-permute-start(f32[304,128]{1,0:T(8,128)S(1)} %get-tuple-element.39.refs_4_), channel_id=1, source_target_pairs={{0,24},{8,0},{16,8},{24,16},{1,25},{9,1},{17,9},{25,17},{2,26},{10... | collective-permute-start | bytes 466952 | tf_op jit(solution)/shard_map/ppermute | solution.py:285
  10.1 2.7 %collective-permute-done.3.refs_1_.refs_5_ = f32[304,128]{1,0:T(8,128)S(1)} collective-permute-done((f32[304,128]{1,0:T(8,128)S(1)}, f32[304,128]{1,0:T(8,128)S(1)}, u32[]{:S(2)}, u32[]{:S(2)}) %collective-permute-start.3) | collective-permute-done | bytes 155680 | tf_op jit(solution)/shard_map/ppermute | solution.py:285
  12.8 1.9 %collective-permute-start.9 = (f32[304,128]{1,0:T(8,128)S(1)}, f32[304,128]{1,0:T(8,128)S(1)}, u32[]{:S(2)}, u32[]{:S(2)}) collective-permute-start(f32[304,128]{1,0:T(8,128)S(1)} %get-tuple-element.40.refs_4_), channel_id=1, source_target_pairs={{0,8},{8,16},{16,24},{24,0},{1,9},{9,17},{17,25},{25,1},{2,10},{10... | collective-permute-start | bytes 466952 | tf_op jit(solution)/shard_map/ppermute | solution.py:285
  15.8 1.6 %collective-permute-start.5 = (f32[304,128]{1,0:T(8,128)S(1)}, f32[304,128]{1,0:T(8,128)S(1)}, u32[]{:S(2)}, u32[]{:S(2)}) collective-permute-start(f32[304,128]{1,0:T(8,128)S(1)} %collective-permute-done.3.refs_1_.refs_5_), channel_id=1, source_target_pairs={{0,8},{8,16},{16,24},{24,0},{1,9},{9,17},{17,25},{25,1},{2,10},{10... | collective-permute-start | bytes 466952 | tf_op jit(solution)/shard_map/ppermute | solution.py:285
  19.2 2.0 %collective-permute-done.5.refs_7_ = f32[304,128]{1,0:T(8,128)S(1)} collective-permute-done((f32[304,128]{1,0:T(8,128)S(1)}, f32[304,128]{1,0:T(8,128)S(1)}, u32[]{:S(2)}, u32[]{:S(2)}) %collective-permute-start.5) | collective-permute-done | bytes 155680 | tf_op jit(solution)/shard_map/ppermute | solution.py:285
  22.4 4.0 %collective-permute-start.12 = (f32[304,128]{1,0:T(8,128)S(1)}, f32[304,128]{1,0:T(8,128)S(1)}, u32[]{:S(2)}, u32[]{:S(2)}) collective-permute-start(f32[304,128]{1,0:T(8,128)S(1)} %collective-permute-done.9.refs_11_.refs_5_), channel_id=1, source_target_pairs={{0,8},{8,16},{16,24},{24,0},{1,9},{9,17},{17,25},{25,1},{2,10},{10... | collective-permute-start | bytes 466952 | tf_op jit(solution)/shard_map/ppermute | solution.py:285
  28.8 3.4 %collective-permute-done.8.refs_10_ = f32[304,128]{1,0:T(8,128)S(1)} collective-permute-done((f32[304,128]{1,0:T(8,128)S(1)}, f32[304,128]{1,0:T(8,128)S(1)}, u32[]{:S(2)}, u32[]{:S(2)}) %collective-permute-start.8) | collective-permute-done | bytes 155680 | tf_op jit(solution)/shard_map/ppermute | solution.py:291
  32.2 1.7 %lead2.1 = (bf16[608,1024]{1,0:T(8,128)(2,1)S(1)}, f32[1,304,512]{2,1,0:T(8,128)S(1)}, f32[608,128]{1,0:T(8,128)S(1)}, f32[304,128]{1,0:T(8,128)S(1)}) custom-call(s32[4]{0:T(128)S(1)} %pad_add_fusion.refs_0_, bf16[2,2,1024,512]{3,2,1,0:T(8,128)(2,1)S(1)} %get-tuple-element.36.refs_1_, bf16[2,2,1024,512]{3,2,1,0:T(8,128)(2,1)S(1)} %get-tuple-element.37.refs_2_, ...), custom_call_target="tpu_custom_call" | custom-call | flops 956301312 | bytes 1 | tf_op jit(solution)/shard_map/lead2/pallas_call | solution.py:25
  38.1 2.6 %collective-permute-done.15.refs_12_.refs_5_ = f32[304,128]{1,0:T(8,128)S(1)} collective-permute-done((f32[304,128]{1,0:T(8,128)S(1)}, f32[304,128]{1,0:T(8,128)S(1)}, u32[]{:S(2)}, u32[]{:S(2)}) %collective-permute-start.15) | collective-permute-done | bytes 155680 | tf_op jit(solution)/shard_map/ppermute | solution.py:285
  40.8 2.4 %collective-permute-start.18 = (f32[304,128]{1,0:T(8,128)S(1)}, f32[304,128]{1,0:T(8,128)S(1)}, u32[]{:S(2)}, u32[]{:S(2)}) collective-permute-start(f32[304,128]{1,0:T(8,128)S(1)} %collective-permute-done.15.refs_12_.refs_5_), channel_id=1, source_target_pairs={{0,8},{8,16},{16,24},{24,0},{1,9},{9,17},{17,25},{25,1},{2,10},{10... | collective-permute-start | bytes 466952 | tf_op jit(solution)/shard_map/ppermute | solution.py:285
  44.5 2.1 %collective-permute-done.17.refs_14_.refs_5_ = f32[304,512]{1,0:T(8,128)S(1)} collective-permute-done((f32[304,512]{1,0:T(8,128)S(1)}, f32[304,512]{1,0:T(8,128)S(1)}, u32[]{:S(2)}, u32[]{:S(2)}) %collective-permute-start.17) | collective-permute-done | bytes 622624 | tf_op jit(solution)/shard_map/ppermute | solution.py:262
  46.6 2.7 %lead1.1 = (bf16[608,1024]{1,0:T(8,128)(2,1)S(1)}, f32[1,304,512]{2,1,0:T(8,128)S(1)}, f32[912,128]{1,0:T(8,128)S(1)}) custom-call(s32[4]{0:T(128)S(1)} %pad_add_fusion.refs_0_, bf16[2,2,1024,512]{3,2,1,0:T(8,128)(2,1)S(1)} %get-tuple-element.36.refs_1_, bf16[2,2,1024,512]{3,2,1,0:T(8,128)(2,1)S(1)} %get-tuple-element.37.refs_2_, ...), custom_call_target="tpu_custom_call" | custom-call | flops 1912602624 | bytes 1 | tf_op jit(solution)/shard_map/lead1/pallas_call | solution.py:25
  49.3 1.9 %collective-permute-start.19 = (f32[912,128]{1,0:T(8,128)S(1)}, f32[912,128]{1,0:T(8,128)S(1)}, u32[]{:S(2)}, u32[]{:S(2)}) collective-permute-start(f32[912,128]{1,0:T(8,128)S(1)} %get-tuple-element.47), channel_id=1, source_target_pairs={{0,4},{4,0},{1,5},{5,1},{2,6},{6,2},{3,7},{7,3},{8,12},{12,8},{9,1... | collective-permute-start | bytes 1400840 | tf_op jit(solution)/shard_map/ppermute | solution.py:291
  52.4 3.6 %rest1.1 = (f32[2,304,512]{2,1,0:T(8,128)S(1)}, f32[304,512]{1,0:T(8,128)S(1)}) custom-call(s32[4]{0:T(128)S(1)} %pad_add_fusion.refs_0_, bf16[2,2,1024,512]{3,2,1,0:T(8,128)(2,1)S(1)} %get-tuple-element.36.refs_1_, bf16[2,2,1024,512]{3,2,1,0:T(8,128)(2,1)S(1)} %get-tuple-element.37.refs_2_, bf16[608,1024]{1,0:T(8,128)(2,1)S(1)} %get-tuple-element.41.refs_3_, ...), custom_call_target="tpu_custom_call" | custom-call | flops 2868903936 | bytes 1 | tf_op jit(solution)/shard_map/rest1/pallas_call | solution.py:25
  56.0 2.0 %collective-permute-start.21 = (f32[304,512]{1,0:T(8,128)S(1)}, f32[304,512]{1,0:T(8,128)S(1)}, u32[]{:S(2)}, u32[]{:S(2)}) collective-permute-start(f32[304,512]{1,0:T(8,128)S(1)} %get-tuple-element.49), channel_id=1, source_target_pairs={{2,6},{6,10},{10,14},{14,18},{18,22},{22,26},{26,30},{3,7},{7,11},... | collective-permute-start | bytes 1867784 | tf_op jit(solution)/shard_map/ppermute | solution.py:256
  59.3 19.0 %collective-permute-done.20.refs_9_ = f32[304,128]{1,0:T(8,128)S(1)} collective-permute-done((f32[304,128]{1,0:T(8,128)S(1)}, f32[304,128]{1,0:T(8,128)S(1)}, u32[]{:S(2)}, u32[]{:S(2)}) %collective-permute-start.20) | collective-permute-done | bytes 155680 | tf_op jit(solution)/shard_map/ppermute | solution.py:291
  78.3 2.7 %lead0.1 = (bf16[608,1024]{1,0:T(8,128)(2,1)S(1)}, f32[1,304,512]{2,1,0:T(8,128)S(1)}, f32[1,304,512]{2,1,0:T(8,128)S(1)}) custom-call(s32[4]{0:T(128)S(1)} %pad_add_fusion.refs_0_, bf16[2,2,1024,512]{3,2,1,0:T(8,128)(2,1)S(1)} %get-tuple-element.36.refs_1_, bf16[2,2,1024,512]{3,2,1,0:T(8,128)(2,1)S(1)} %get-tuple-element.37.refs_2_, ...), custom_call_target="tpu_custom_call" | custom-call | flops 2868903936 | bytes 1 | tf_op jit(solution)/shard_map/lead0/pallas_call | solution.py:25
  81.3 2.6 %collective-permute-start.28 = (f32[304,512]{1,0:T(8,128)S(1)}, f32[304,512]{1,0:T(8,128)S(1)}, u32[]{:S(2)}, u32[]{:S(2)}) collective-permute-start(f32[304,512]{1,0:T(8,128)S(1)} %bitcast.14), channel_id=1, source_target_pairs={{0,3},{1,2},{2,1},{3,0},{4,7},{5,6},{6,5},{7,4},{8,11},{9,10},{10,... | collective-permute-start | bytes 1867784 | tf_op jit(solution)/shard_map/ppermute | solution.py:268
  83.9 3.6 %total0.1 = (f32[304,512]{1,0:T(8,128)S(1)}, f32[304,512]{1,0:T(8,128)S(1)}) custom-call(s32[4]{0:T(128)S(1)} %pad_add_fusion.refs_0_, bf16[2,2,1024,512]{3,2,1,0:T(8,128)(2,1)S(1)} %get-tuple-element.36.refs_1_, bf16[2,2,1024,512]{3,2,1,0:T(8,128)(2,1)S(1)} %get-tuple-element.37.refs_2_, bf16[608,1024]{1,0:T(8,128)(2,1)S(1)} %get-tuple-element.41.refs_3_, ...), custom_call_target="tpu_custom_call" | custom-call | bytes 1 | tf_op jit(solution)/shard_map/total0/pallas_call | solution.py:25
  88.3 4.4 %collective-permute-start.27 = (f32[304,512]{1,0:T(8,128)S(1)}, f32[304,512]{1,0:T(8,128)S(1)}, u32[]{:S(2)}, u32[]{:S(2)}) collective-permute-start(f32[304,512]{1,0:T(8,128)S(1)} %get-tuple-element.55), channel_id=1, source_target_pairs={{2,4},{6,8},{10,12},{14,16},{18,20},{22,24},{26,28},{3,5},{7,9},{1... | collective-permute-start | bytes 1867784 | tf_op jit(solution)/shard_map/ppermute | solution.py:256
  92.7 1.7 %last.1.refs_1_ = f32[304,512]{1,0:T(8,128)S(1)} custom-call(s32[4]{0:T(128)S(1)} %pad_add_fusion.refs_0_, bf16[2,2,1024,512]{3,2,1,0:T(8,128)(2,1)S(1)} %get-tuple-element.36.refs_1_, bf16[2,2,1024,512]{3,2,1,0:T(8,128)(2,1)S(1)} %get-tuple-element.37.refs_2_, bf16[608,1024]{1,0:T(8,128)(2,1)S(1)} %get-tuple-element.48.refs_3_.refs_5_, ...), custom_call_target="tpu_custom_call" | custom-call | flops 956301312 | bytes 1 | tf_op jit(solution)/shard_map/last/pallas_call | solution.py:25
  96.1 14.0 %collective-permute-done.28.refs_5_ = f32[304,512]{1,0:T(8,128)S(1)} collective-permute-done((f32[304,512]{1,0:T(8,128)S(1)}, f32[304,512]{1,0:T(8,128)S(1)}, u32[]{:S(2)}, u32[]{:S(2)}) %collective-permute-start.28) | collective-permute-done | bytes 622624 | tf_op jit(solution)/shard_map/ppermute | solution.py:268
  110.2 1.8 %finish.1 = f32[600,512]{1,0:T(8,128)} custom-call(s32[4]{0:T(128)S(1)} %pad_add_fusion.refs_0_, f32[304,512]{1,0:T(8,128)S(1)} %get-tuple-element.53.refs_1_, f32[304,512]{1,0:T(8,128)S(1)} %get-tuple-element.54.refs_2_, f32[304,512]{1,0:T(8,128)S(1)} %collective-permute-done.26.refs_3_, f32[304,512]{1,0:T(8,128)S(1)} %collective-permute-done.27.refs_4_, ...), custom_call_target="tpu_custom_call" | custom-call | bytes 1 | tf_op jit(solution)/shard_map/finish/pallas_call | solution.py:25
  (52 shorter events, 23.8 us)
Async XLA Ops:
  6.8 15.6 %collective-permute-start.1 = (f32[1024,512]{1,0:T(8,128)S(1)}, f32[1024,512]{1,0:T(8,128)S(1)}, u32[]{:S(2)}, u32[]{:S(2)}) collective-permute-start(f32[1024,512]{1,0:T(8,128)S(1)} %get-tuple-element.34), channel_id=1, source_target_pairs={{0,2},{2,0},{1,3},{3,1},{4,6},{6,4},{5,7},{7,5},{8,10},{10,8},{9,1... | collective-permute-start | bytes 6291464 | tf_op jit(solution)/shard_map/ppermute | solution.py:251
  7.2 19.1 %collective-permute-start.2 = (f32[1024,512]{1,0:T(8,128)S(1)}, f32[1024,512]{1,0:T(8,128)S(1)}, u32[]{:S(2)}, u32[]{:S(2)}) collective-permute-start(f32[1024,512]{1,0:T(8,128)S(1)} %get-tuple-element.35), channel_id=1, source_target_pairs={{0,2},{2,0},{1,3},{3,1},{4,6},{6,4},{5,7},{7,5},{8,10},{10,8},{9,1... | collective-permute-start | bytes 6291464 | tf_op jit(solution)/shard_map/ppermute | solution.py:251
  7.4 8.4 %collective-permute-start.4 = (f32[304,128]{1,0:T(8,128)S(1)}, f32[304,128]{1,0:T(8,128)S(1)}, u32[]{:S(2)}, u32[]{:S(2)}) collective-permute-start(f32[304,128]{1,0:T(8,128)S(1)} %get-tuple-element.39.refs_4_), channel_id=1, source_target_pairs={{0,24},{8,0},{16,8},{24,16},{1,25},{9,1},{17,9},{25,17},{2,26},{10... | collective-permute-start | bytes 466952 | tf_op jit(solution)/shard_map/ppermute | solution.py:285
  8.9 8.5 %collective-permute-start.6 = (f32[304,128]{1,0:T(8,128)S(1)}, f32[304,128]{1,0:T(8,128)S(1)}, u32[]{:S(2)}, u32[]{:S(2)}) collective-permute-start(f32[304,128]{1,0:T(8,128)S(1)} %get-tuple-element.39.refs_4_), channel_id=1, source_target_pairs={{0,4},{4,0},{1,5},{5,1},{2,6},{6,2},{3,7},{7,3},{8,12},{12,8},{9,1... | collective-permute-start | bytes 466952 | tf_op jit(solution)/shard_map/ppermute | solution.py:291
  12.8 6.4 %collective-permute-start.9 = (f32[304,128]{1,0:T(8,128)S(1)}, f32[304,128]{1,0:T(8,128)S(1)}, u32[]{:S(2)}, u32[]{:S(2)}) collective-permute-start(f32[304,128]{1,0:T(8,128)S(1)} %get-tuple-element.40.refs_4_), channel_id=1, source_target_pairs={{0,8},{8,16},{16,24},{24,0},{1,9},{9,17},{17,25},{25,1},{2,10},{10... | collective-permute-start | bytes 466952 | tf_op jit(solution)/shard_map/ppermute | solution.py:285
  17.9 14.3 %collective-permute-start.7 = (f32[608,128]{1,0:T(8,128)S(1)}, f32[608,128]{1,0:T(8,128)S(1)}, u32[]{:S(2)}, u32[]{:S(2)}) collective-permute-start(f32[608,128]{1,0:T(8,128)S(1)} %join2.1), channel_id=1, source_target_pairs={{0,4},{4,0},{1,5},{5,1},{2,6},{6,2},{3,7},{7,3},{8,12},{12,8},{9,1... | collective-permute-start | bytes 933896 | tf_op jit(solution)/shard_map/ppermute | solution.py:291
  19.2 8.7 %collective-permute-start.10 = (f32[304,128]{1,0:T(8,128)S(1)}, f32[304,128]{1,0:T(8,128)S(1)}, u32[]{:S(2)}, u32[]{:S(2)}) collective-permute-start(f32[304,128]{1,0:T(8,128)S(1)} %get-tuple-element.40.refs_4_), channel_id=1, source_target_pairs={{0,24},{8,0},{16,8},{24,16},{1,25},{9,1},{17,9},{25,17},{2,26},{10... | collective-permute-start | bytes 466952 | tf_op jit(solution)/shard_map/ppermute | solution.py:285
  21.2 7.6 %collective-permute-start.11 = (f32[304,128]{1,0:T(8,128)S(1)}, f32[304,128]{1,0:T(8,128)S(1)}, u32[]{:S(2)}, u32[]{:S(2)}) collective-permute-start(f32[304,128]{1,0:T(8,128)S(1)} %get-tuple-element.40.refs_4_), channel_id=1, source_target_pairs={{0,4},{4,0},{1,5},{5,1},{2,6},{6,2},{3,7},{7,3},{8,12},{12,8},{9,1... | collective-permute-start | bytes 466952 | tf_op jit(solution)/shard_map/ppermute | solution.py:291
  22.4 6.4 %collective-permute-start.12 = (f32[304,128]{1,0:T(8,128)S(1)}, f32[304,128]{1,0:T(8,128)S(1)}, u32[]{:S(2)}, u32[]{:S(2)}) collective-permute-start(f32[304,128]{1,0:T(8,128)S(1)} %collective-permute-done.9.refs_11_.refs_5_), channel_id=1, source_target_pairs={{0,8},{8,16},{16,24},{24,0},{1,9},{9,17},{17,25},{25,1},{2,10},{10... | collective-permute-start | bytes 466952 | tf_op jit(solution)/shard_map/ppermute | solution.py:285
  33.9 12.7 %collective-permute-start.17 = (f32[304,512]{1,0:T(8,128)S(1)}, f32[304,512]{1,0:T(8,128)S(1)}, u32[]{:S(2)}, u32[]{:S(2)}) collective-permute-start(f32[304,512]{1,0:T(8,128)S(1)} %bitcast.17), channel_id=1, source_target_pairs={{0,1},{1,0},{2,3},{3,2},{4,5},{5,4},{6,7},{7,6},{8,9},{9,8},{10,11... | collective-permute-start | bytes 1867784 | tf_op jit(solution)/shard_map/ppermute | solution.py:262
  35.2 9.3 %collective-permute-start.13 = (f32[608,128]{1,0:T(8,128)S(1)}, f32[608,128]{1,0:T(8,128)S(1)}, u32[]{:S(2)}, u32[]{:S(2)}) collective-permute-start(f32[608,128]{1,0:T(8,128)S(1)} %get-tuple-element.42), channel_id=1, source_target_pairs={{0,4},{4,0},{1,5},{5,1},{2,6},{6,2},{3,7},{7,3},{8,12},{12,8},{9,1... | collective-permute-start | bytes 933896 | tf_op jit(solution)/shard_map/ppermute | solution.py:291
  37.1 7.1 %collective-permute-start.14 = (f32[304,128]{1,0:T(8,128)S(1)}, f32[304,128]{1,0:T(8,128)S(1)}, u32[]{:S(2)}, u32[]{:S(2)}) collective-permute-start(f32[304,128]{1,0:T(8,128)S(1)} %collective-permute-done.12.refs_14_.refs_7_), channel_id=1, source_target_pairs={{0,4},{4,0},{1,5},{5,1},{2,6},{6,2},{3,7},{7,3},{8,12},{12,8},{9,1... | collective-permute-start | bytes 466952 | tf_op jit(solution)/shard_map/ppermute | solution.py:291
  37.3 7.1 %collective-permute-start.16 = (f32[304,128]{1,0:T(8,128)S(1)}, f32[304,128]{1,0:T(8,128)S(1)}, u32[]{:S(2)}, u32[]{:S(2)}) collective-permute-start(f32[304,128]{1,0:T(8,128)S(1)} %get-tuple-element.43.refs_11_.refs_4_), channel_id=1, source_target_pairs={{0,24},{8,0},{16,8},{24,16},{1,25},{9,1},{17,9},{25,17},{2,26},{10... | collective-permute-start | bytes 466952 | tf_op jit(solution)/shard_map/ppermute | solution.py:285
  40.8 11.6 %collective-permute-start.18 = (f32[304,128]{1,0:T(8,128)S(1)}, f32[304,128]{1,0:T(8,128)S(1)}, u32[]{:S(2)}, u32[]{:S(2)}) collective-permute-start(f32[304,128]{1,0:T(8,128)S(1)} %collective-permute-done.15.refs_12_.refs_5_), channel_id=1, source_target_pairs={{0,8},{8,16},{16,24},{24,0},{1,9},{9,17},{17,25},{25,1},{2,10},{10... | collective-permute-start | bytes 466952 | tf_op jit(solution)/shard_map/ppermute | solution.py:285
  49.3 29.0 %collective-permute-start.19 = (f32[912,128]{1,0:T(8,128)S(1)}, f32[912,128]{1,0:T(8,128)S(1)}, u32[]{:S(2)}, u32[]{:S(2)}) collective-permute-start(f32[912,128]{1,0:T(8,128)S(1)} %get-tuple-element.47), channel_id=1, source_target_pairs={{0,4},{4,0},{1,5},{5,1},{2,6},{6,2},{3,7},{7,3},{8,12},{12,8},{9,1... | collective-permute-start | bytes 1400840 | tf_op jit(solution)/shard_map/ppermute | solution.py:291
  51.2 32.7 %collective-permute-start.23 = (f32[304,512]{1,0:T(8,128)S(1)}, f32[304,512]{1,0:T(8,128)S(1)}, u32[]{:S(2)}, u32[]{:S(2)}) collective-permute-start(f32[304,512]{1,0:T(8,128)S(1)} %bitcast.15), channel_id=1, source_target_pairs={{0,1},{1,0},{2,3},{3,2},{4,5},{5,4},{6,7},{7,6},{8,9},{9,8},{10,11... | collective-permute-start | bytes 1867784 | tf_op jit(solution)/shard_map/ppermute | solution.py:262
  56.0 31.6 %collective-permute-start.21 = (f32[304,512]{1,0:T(8,128)S(1)}, f32[304,512]{1,0:T(8,128)S(1)}, u32[]{:S(2)}, u32[]{:S(2)}) collective-permute-start(f32[304,512]{1,0:T(8,128)S(1)} %get-tuple-element.49), channel_id=1, source_target_pairs={{2,6},{6,10},{10,14},{14,18},{18,22},{22,26},{26,30},{3,7},{7,11},... | collective-permute-start | bytes 1867784 | tf_op jit(solution)/shard_map/ppermute | solution.py:256
  58.0 30.3 %collective-permute-start.25 = (f32[304,512]{1,0:T(8,128)S(1)}, f32[304,512]{1,0:T(8,128)S(1)}, u32[]{:S(2)}, u32[]{:S(2)}) collective-permute-start(f32[304,512]{1,0:T(8,128)S(1)} %get-tuple-element.49), channel_id=1, source_target_pairs={{0,6},{4,10},{8,14},{12,18},{16,22},{20,26},{24,30},{1,7},{5,11},{... | collective-permute-start | bytes 1867784 | tf_op jit(solution)/shard_map/ppermute | solution.py:256
  59.3 19.0 %collective-permute-start.20 = (f32[304,128]{1,0:T(8,128)S(1)}, f32[304,128]{1,0:T(8,128)S(1)}, u32[]{:S(2)}, u32[]{:S(2)}) collective-permute-start(f32[304,128]{1,0:T(8,128)S(1)} %collective-permute-done.18.refs_6_.refs_7_), channel_id=1, source_target_pairs={{0,4},{4,0},{1,5},{5,1},{2,6},{6,2},{3,7},{7,3},{8,12},{12,8},{9,1... | collective-permute-start | bytes 466952 | tf_op jit(solution)/shard_map/ppermute | solution.py:291
  81.0 14.4 %collective-permute-start.22 = (f32[304,512]{1,0:T(8,128)S(1)}, f32[304,512]{1,0:T(8,128)S(1)}, u32[]{:S(2)}, u32[]{:S(2)}) collective-permute-start(f32[304,512]{1,0:T(8,128)S(1)} %bitcast.16), channel_id=1, source_target_pairs={{0,1},{1,0},{2,3},{3,2},{4,5},{5,4},{6,7},{7,6},{8,9},{9,8},{10,11... | collective-permute-start | bytes 1867784 | tf_op jit(solution)/shard_map/ppermute | solution.py:262
  81.3 28.8 %collective-permute-start.28 = (f32[304,512]{1,0:T(8,128)S(1)}, f32[304,512]{1,0:T(8,128)S(1)}, u32[]{:S(2)}, u32[]{:S(2)}) collective-permute-start(f32[304,512]{1,0:T(8,128)S(1)} %bitcast.14), channel_id=1, source_target_pairs={{0,3},{1,2},{2,1},{3,0},{4,7},{5,6},{6,5},{7,4},{8,11},{9,10},{10,... | collective-permute-start | bytes 1867784 | tf_op jit(solution)/shard_map/ppermute | solution.py:268
  87.5 7.9 %collective-permute-start.24 = (f32[304,512]{1,0:T(8,128)S(1)}, f32[304,512]{1,0:T(8,128)S(1)}, u32[]{:S(2)}, u32[]{:S(2)}) collective-permute-start(f32[304,512]{1,0:T(8,128)S(1)} %get-tuple-element.52), channel_id=1, source_target_pairs={{0,2},{2,0},{1,3},{3,1},{4,6},{6,4},{5,7},{7,5},{8,10},{10,8},{9,1... | collective-permute-start | bytes 1867784 | tf_op jit(solution)/shard_map/ppermute | solution.py:251
  87.6 22.6 %collective-permute-start.26 = (f32[304,512]{1,0:T(8,128)S(1)}, f32[304,512]{1,0:T(8,128)S(1)}, u32[]{:S(2)}, u32[]{:S(2)}) collective-permute-start(f32[304,512]{1,0:T(8,128)S(1)} %get-tuple-element.55), channel_id=1, source_target_pairs={{0,4},{4,8},{8,12},{12,16},{16,20},{20,24},{24,28},{1,5},{5,9},{9,... | collective-permute-start | bytes 1867784 | tf_op jit(solution)/shard_map/ppermute | solution.py:256
  88.3 21.9 %collective-permute-start.27 = (f32[304,512]{1,0:T(8,128)S(1)}, f32[304,512]{1,0:T(8,128)S(1)}, u32[]{:S(2)}, u32[]{:S(2)}) collective-permute-start(f32[304,512]{1,0:T(8,128)S(1)} %get-tuple-element.55), channel_id=1, source_target_pairs={{2,4},{6,8},{10,12},{14,16},{18,20},{22,24},{26,28},{3,5},{7,9},{1... | collective-permute-start | bytes 1867784 | tf_op jit(solution)/shard_map/ppermute | solution.py:256
  (7 other events, 26.7 us)
